TPU v7x, 128 devices: a whole 4x4x4 slice. The times are simulated.
128 devices in a mesh: dp: 128 (over x, y, z, core).
Axes of the slice: x: 4, y: 4, z: 4, core: 2. Of those that a mesh axis runs over, the one named last changes fastest.
Arguments:
- latent: bfloat16 [512, 6, 6, 6, 256], P('dp'), may hold values from -6 to 6
- out_grad: bfloat16 [512, 3, 3, 3, 256], P('dp'), may hold values from -6 to 6
- first_kernel: float32 [27, 65536], P(None, 'dp'), may hold values from -0.078125 to 0.078125
- first_mean: float32 [27, 65536], P(None, 'dp'), may hold values from -0.15625 to 0.15625
- first_square: float32 [27, 65536], P(None, 'dp'), may hold values from 0.0001 to 0.01
- second_kernel: float32 [27, 65536], P(None, 'dp'), may hold values from -0.078125 to 0.078125
- second_mean: float32 [27, 65536], P(None, 'dp'), may hold values from -0.15625 to 0.15625
- second_square: float32 [27, 65536], P(None, 'dp'), may hold values from 0.0001 to 0.01
Outputs:
- block_out: bfloat16 [512, 3, 3, 3, 256], P('dp')
- first_kernel_new: float32 [27, 65536], P(None, 'dp')
- first_mean_new: float32 [27, 65536], P(None, 'dp')
- first_square_new: float32 [27, 65536], P(None, 'dp')
- second_kernel_new: float32 [27, 65536], P(None, 'dp')
- second_mean_new: float32 [27, 65536], P(None, 'dp')
- second_square_new: float32 [27, 65536], P(None, 'dp')
All inputs are finite; a program needn't handle non-finite values.
Results may differ from a plain program's by a relative error of at most 0.0042.
Values may be sent and summed in bfloat16 or wider, within the bound.
No kernel may reach another device: no remote copies, remote signals or barrier semaphores. Data moves between devices by JAX's collectives and lax.ppermute only.
A program may use at most 128 MiB of HBM per device.

v0:
```python
import jax
import jax.numpy as jnp
from jax import lax
from jax.sharding import PartitionSpec as P


def slope(value):
    sigma = jax.nn.sigmoid(value)
    return sigma * (1.0 + value * (1.0 - sigma))


def adam_update(weight, first, second, grad):
    first_new = 0.9 * first + 0.1 * grad
    second_new = 0.999 * second + 0.001 * grad * grad
    fix_first = 1.0 - 0.9**10
    fix_second = 1.0 - 0.999**10
    weight_new = weight - 0.05 * (first_new / fix_first) / (
        jnp.sqrt(second_new / fix_second) + 1e-08
    )
    return (weight_new, first_new, second_new)


def tap_offsets(offset):
    return (offset // 9, offset // 3 % 3, offset % 3)


def window_same(padded, offset, edge):
    di, dj, dl = tap_offsets(offset)
    piece = padded[:, di : di + edge, dj : dj + edge, dl : dl + edge, :]
    return piece.reshape(-1, padded.shape[-1])


def window_strided(padded, offset, outer):
    di, dj, dl = tap_offsets(offset)
    span = 2 * outer - 1
    piece = padded[:, di : di + span : 2, dj : dj + span : 2, dl : dl + span : 2, :]
    return piece.reshape(-1, padded.shape[-1])


def outer_sum(left, right):
    return lax.dot_general(
        left, right, (((0,), (0,)), ((), ())), preferred_element_type=jnp.float32
    )


def body(
    latent,
    out_grad,
    first_kernel,
    first_mean,
    first_square,
    second_kernel,
    second_mean,
    second_square,
):
    samples = latent.shape[0]
    edge = latent.shape[1]
    outer = out_grad.shape[1]
    chans = latent.shape[-1]
    total_samples = samples * lax.axis_size("dp")
    kernel1 = lax.all_gather(first_kernel.astype(jnp.bfloat16), "dp", axis=1, tiled=True).reshape(
        27, chans, chans
    )
    kernel2 = lax.all_gather(second_kernel.astype(jnp.bfloat16), "dp", axis=1, tiled=True).reshape(
        27, chans, chans
    )
    pad_width = ((0, 0), (1, 1), (1, 1), (1, 1), (0, 0))
    latent_pad = jnp.pad(latent, pad_width)
    act = jnp.zeros((samples * edge**3, chans), jnp.float32)
    for offset in range(27):
        act = act + jnp.dot(
            window_same(latent_pad, offset, edge),
            kernel1[offset],
            preferred_element_type=jnp.float32,
        )
    hidden = jax.nn.silu(act).astype(jnp.bfloat16)
    hidden_pad = jnp.pad(hidden.reshape(samples, edge, edge, edge, chans), pad_width)
    conv = jnp.zeros((samples * outer**3, chans), jnp.float32)
    for offset in range(27):
        conv = conv + jnp.dot(
            window_strided(hidden_pad, offset, outer),
            kernel2[offset],
            preferred_element_type=jnp.float32,
        )
    skipped = latent[:, ::2, ::2, ::2, :].reshape(-1, chans).astype(jnp.float32)
    pre = conv + skipped
    block_out = jax.nn.silu(pre).astype(jnp.bfloat16).reshape(samples, outer, outer, outer, chans)
    grad_pre = (out_grad.reshape(-1, chans).astype(jnp.float32) * slope(pre)).astype(jnp.bfloat16)
    grad2 = jnp.stack(
        [outer_sum(window_strided(hidden_pad, offset, outer), grad_pre) for offset in range(27)]
    )
    grad2 = grad2.reshape(27, chans * chans)
    summed2 = lax.psum_scatter(grad2, "dp", scatter_dimension=1, tiled=True)
    kernel_back = lax.all_gather(
        second_kernel.astype(jnp.bfloat16), "dp", axis=1, tiled=True
    ).reshape(27, chans, chans)
    grad_pad = jnp.zeros((samples, edge + 2, edge + 2, edge + 2, chans), jnp.float32)
    span = 2 * outer - 1
    for offset in range(27):
        di, dj, dl = tap_offsets(offset)
        term = lax.dot_general(
            grad_pre,
            kernel_back[offset],
            (((1,), (1,)), ((), ())),
            preferred_element_type=jnp.float32,
        )
        term = term.reshape(samples, outer, outer, outer, chans)
        grad_pad = grad_pad.at[
            :, di : di + span : 2, dj : dj + span : 2, dl : dl + span : 2, :
        ].add(term)
    grad_hidden = grad_pad[:, 1 : edge + 1, 1 : edge + 1, 1 : edge + 1, :].reshape(-1, chans)
    grad_act = (grad_hidden * slope(act)).astype(jnp.bfloat16)
    grad1 = jnp.stack(
        [outer_sum(window_same(latent_pad, offset, edge), grad_act) for offset in range(27)]
    )
    grad1 = grad1.reshape(27, chans * chans)
    summed1 = lax.psum_scatter(grad1, "dp", scatter_dimension=1, tiled=True)
    new_one = adam_update(first_kernel, first_mean, first_square, summed1 / total_samples)
    new_two = adam_update(second_kernel, second_mean, second_square, summed2 / total_samples)
    return (block_out, new_one[0], new_one[1], new_one[2], new_two[0], new_two[1], new_two[2])


def solution(mesh):
    placed = (
        P("dp", None, None, None, None),
        P("dp", None, None, None, None),
        P(None, "dp"),
        P(None, "dp"),
        P(None, "dp"),
        P(None, "dp"),
        P(None, "dp"),
        P(None, "dp"),
    )
    return jax.shard_map(
        body,
        mesh=mesh,
        in_specs=placed,
        out_specs=(
            P("dp", None, None, None, None),
            P(None, "dp"),
            P(None, "dp"),
            P(None, "dp"),
            P(None, "dp"),
            P(None, "dp"),
            P(None, "dp"),
        ),
        check_vma=False,
    )
```

profile of v0, /device:TPU:0, one launch (start us, length us, event | category | flops | bytes accessed | tf_op | source)
XLA Modules:
  0.0 2136.8 jit_solution(10609896950951869958)
XLA Ops:
  11.2 3.7 pad_slice_fusion.1
  14.9 4.7 pad_slice_fusion
  138.7 13.0 slice_reduce_fusion.46
  164.5 28.6 %slice_reduce_fusion.27 = (bf16[65536]{0:T(1024)(128)(2,1)}, bf16[65536]{0:T(1024)(128)(2,1)}, bf16[65536]{0:T(1024)(128)(2,1)}, bf16[65536]{0:T(1024)(128)(2,1)...) fusion(bf16[27,65536]{1,0:T(8,128)(2,1)} %all-gather.3.cloned.1, ...), kind=kLoop, calls=%fused_computation.190 | loop fusion | bytes 4980736 | tf_op jit(solution)/shard_map/slice | solution.py:73
  240.0 10.8 slice.516
  250.8 10.8 slice.518
  261.6 10.8 slice.520
  272.4 10.8 slice.522
  283.2 10.8 slice.524
  294.0 10.8 slice.526
  304.8 10.7 slice.528
  315.5 10.8 slice.530
  326.3 10.8 slice.532
  337.1 10.8 slice.534
  347.9 10.8 slice.536
  358.7 10.7 slice.538
  369.4 10.7 slice.540
  380.1 10.8 slice.542
  390.9 10.8 slice.544
  401.7 10.8 slice.546
  412.5 10.7 slice.548
  423.2 10.7 slice.550
  433.9 10.8 slice.552
  444.7 10.7 slice.554
  455.5 10.8 slice.556
  466.2 10.8 slice.558
  477.1 10.8 slice.560
  487.9 10.7 slice.562
  498.6 10.8 slice.564
  509.4 10.8 slice.566
  520.2 10.7 slice.568
  530.9 12.0 slice_reduce_fusion.19
  554.0 27.8 %slice_reduce_fusion = (bf16[65536]{0:T(1024)(128)(2,1)S(1)}, bf16[65536]{0:T(1024)(128)(2,1)S(1)}, bf16[65536]{0:T(1024)(128)(2,1)S(1)}, bf16[65536]{0:T(1024)(...) fusion(bf16[27,65536]{1,0:T(8,128)(2,1)} %all-gather.5.cloned.1, ...), kind=kLoop, calls=%fused_computation.163 | loop fusion | bytes 4980736 | tf_op jit(solution)/shard_map/slice | solution.py:82
  679.9 3.0 scatter_fusion
  682.9 3.0 scatter_fusion.1
  685.9 3.0 scatter_fusion.2
  688.9 3.0 scatter_fusion.3
  691.9 3.4 scatter_fusion.4
  719.1 3.0 scatter_fusion.13
  722.1 3.0 scatter_fusion.14
  728.1 3.1 scatter_fusion.16
  731.2 3.0 scatter_fusion.17
  734.2 3.0 scatter_fusion.18
  758.0 3.4 scatter_fusion.26
  806.3 22.8 %stack.195 = f32[27,65536]{1,0:T(8,128)} concatenate(f32[1,65536]{1,0:T(1,128)S(1)} %bitcast.693, f32[1,65536]{1,0:T(1,128)S(1)} %bitcast.695, f32[1,65536]{1,0:T(1,128)S(1)} %bitcast.696, f32[1,65536]{1,0:T(1,128)S(1)} %bitcast.697, f32[1,65536]{1,0:T(1,128)S(1)} %bitcast.699, f32[1,65536]{1,0:T(1,128)S(1)} %bitcast.700, f32[1,65536]{1,0:T(1,128)S(1)} %bitcast.701, ...), dimensions={0} | concatenate | bytes 14155776 | tf_op jit(solution)/shard_map/stack | solution.py:113
  853.2 22.9 %stack.223 = f32[27,65536]{1,0:T(8,128)} concatenate(f32[1,65536]{1,0:T(1,128)S(1)} %bitcast.676, f32[1,65536]{1,0:T(1,128)S(1)} %bitcast.677, f32[1,65536]{1,0:T(1,128)S(1)} %bitcast.678, f32[1,65536]{1,0:T(1,128)S(1)} %bitcast.679, f32[1,65536]{1,0:T(1,128)S(1)} %bitcast.680, f32[1,65536]{1,0:T(1,128)S(1)} %bitcast.681, f32[1,65536]{1,0:T(1,128)S(1)} %bitcast.682, ...), dimensions={0} | concatenate | bytes 14155776 | tf_op jit(solution)/shard_map/stack | solution.py:89
  877.6 604.7 %reduce-scatter.3.cloned.1.call-done = f32[27,512]{1,0:T(8,128)} async-done(((f32[27,65536]{1,0:T(8,128)}), f32[27,512]{1,0:T(8,128)}) %reduce-scatter.3.cloned.1.call-update) | async-done | bytes 55312 | tf_op jit(solution)/shard_map/reduce_scatter | solution.py:117
  1483.8 644.8 %reduce-scatter.5.cloned.1.call-done = f32[27,512]{1,0:T(8,128)} async-done(((f32[27,65536]{1,0:T(8,128)}), f32[27,512]{1,0:T(8,128)}) %reduce-scatter.5.cloned.1.call-update) | async-done | bytes 55312 | tf_op jit(solution)/shard_map/reduce_scatter | solution.py:93
  (885 shorter events, 410.4 us)
Async XLA Ops:
  7.2 131.5 %all-gather.3.cloned.1.call-start = ((), (), s32[]{:S(2)}) async-start(), calls=%async_computation.2 | async-start | bytes 4227072 | tf_op jit(solution)/shard_map/all_gather | solution.py:61
  8.8 522.2 %all-gather.5.cloned.1.call-start = ((), (), s32[]{:S(2)}) async-start(), calls=%async_computation.3 | async-start | bytes 4227072 | tf_op jit(solution)/shard_map/all_gather | solution.py:64
  10.3 1472.0 %reduce-scatter.3.cloned.1.call-start = ((), (), s32[]{:S(2)}) async-start(), calls=%async_computation.4 | async-start | bytes 8454144 | tf_op jit(solution)/shard_map/reduce_scatter | solution.py:117
  27.0 199.2 %copy-start.1 = (bf16[864,256]{1,0:T(8,128)(2,1)}, bf16[864,256]{1,0:T(8,128)(2,1)S(1)}, u32[]{:S(2)}) copy-start(bf16[864,256]{1,0:T(8,128)(2,1)S(1)} %reshape.523) | copy-start | bytes 1327108
  27.2 199.2 %copy-start.3 = (bf16[864,256]{1,0:T(8,128)(2,1)}, bf16[864,256]{1,0:T(8,128)(2,1)S(1)}, u32[]{:S(2)}) copy-start(bf16[864,256]{1,0:T(8,128)(2,1)S(1)} %reshape.524) | copy-start | bytes 1327108
  28.7 198.4 %copy-start.5 = (bf16[864,256]{1,0:T(8,128)(2,1)}, bf16[864,256]{1,0:T(8,128)(2,1)S(1)}, u32[]{:S(2)}) copy-start(bf16[864,256]{1,0:T(8,128)(2,1)S(1)} %reshape.525) | copy-start | bytes 1327108
  32.0 195.4 %copy-start.7 = (bf16[864,256]{1,0:T(8,128)(2,1)}, bf16[864,256]{1,0:T(8,128)(2,1)S(1)}, u32[]{:S(2)}) copy-start(bf16[864,256]{1,0:T(8,128)(2,1)S(1)} %reshape.526) | copy-start | bytes 1327108
  102.8 135.3 %copy-start.47 = (bf16[864,256]{1,0:T(8,128)(2,1)}, bf16[864,256]{1,0:T(8,128)(2,1)S(1)}, u32[]{:S(2)}) copy-start(bf16[864,256]{1,0:T(8,128)(2,1)S(1)} %reshape.546) | copy-start | bytes 1327108
  600.4 25.7 %copy-start.211 = (bf16[4,3,3,3,256]{4,3,2,1,0:T(4,128)(2,1)S(1)}, bf16[4,3,3,3,256]{4,3,2,1,0:T(4,128)(2,1)}, u32[]{:S(2)}) copy-start(bf16[4,3,3,3,256]{4,3,2,1,0:T(4,128)(2,1)} %slice.540) | copy-start | bytes 165892
  601.8 28.2 %copy-start.210 = (bf16[4,3,3,3,256]{4,3,2,1,0:T(4,128)(2,1)S(1)}, bf16[4,3,3,3,256]{4,3,2,1,0:T(4,128)(2,1)}, u32[]{:S(2)}) copy-start(bf16[4,3,3,3,256]{4,3,2,1,0:T(4,128)(2,1)} %slice.546) | copy-start | bytes 165892
  603.2 32.2 %copy-start.209 = (bf16[4,3,3,3,256]{4,3,2,1,0:T(4,128)(2,1)S(1)}, bf16[4,3,3,3,256]{4,3,2,1,0:T(4,128)(2,1)}, u32[]{:S(2)}) copy-start(bf16[4,3,3,3,256]{4,3,2,1,0:T(4,128)(2,1)} %slice.554) | copy-start | bytes 165892
  603.9 35.3 %copy-start.208 = (bf16[4,3,3,3,256]{4,3,2,1,0:T(4,128)(2,1)S(1)}, bf16[4,3,3,3,256]{4,3,2,1,0:T(4,128)(2,1)}, u32[]{:S(2)}) copy-start(bf16[4,3,3,3,256]{4,3,2,1,0:T(4,128)(2,1)} %slice.560) | copy-start | bytes 165892
  605.3 37.7 %copy-start.207 = (bf16[4,3,3,3,256]{4,3,2,1,0:T(4,128)(2,1)S(1)}, bf16[4,3,3,3,256]{4,3,2,1,0:T(4,128)(2,1)}, u32[]{:S(2)}) copy-start(bf16[4,3,3,3,256]{4,3,2,1,0:T(4,128)(2,1)} %slice.566) | copy-start | bytes 165892
  606.7 39.7 %copy-start.92 = (bf16[256,256]{1,0:T(8,128)(2,1)S(1)}, bf16[256,256]{1,0:T(8,128)(2,1)}, u32[]{:S(2)}) copy-start(bf16[256,256]{1,0:T(8,128)(2,1)} %squeeze.217) | copy-start | bytes 393220
  607.4 40.0 %copy-start.93 = (bf16[256,256]{1,0:T(8,128)(2,1)S(1)}, bf16[256,256]{1,0:T(8,128)(2,1)}, u32[]{:S(2)}) copy-start(bf16[256,256]{1,0:T(8,128)(2,1)} %squeeze.218) | copy-start | bytes 393220
  613.7 34.8 %copy-start.94 = (bf16[256,256]{1,0:T(8,128)(2,1)S(1)}, bf16[256,256]{1,0:T(8,128)(2,1)}, u32[]{:S(2)}) copy-start(bf16[256,256]{1,0:T(8,128)(2,1)} %squeeze.219) | copy-start | bytes 393220
  618.3 31.1 %copy-start.95 = (bf16[256,256]{1,0:T(8,128)(2,1)S(1)}, bf16[256,256]{1,0:T(8,128)(2,1)}, u32[]{:S(2)}) copy-start(bf16[256,256]{1,0:T(8,128)(2,1)} %squeeze.220) | copy-start | bytes 393220
  623.0 27.5 %copy-start.96 = (bf16[256,256]{1,0:T(8,128)(2,1)S(1)}, bf16[256,256]{1,0:T(8,128)(2,1)}, u32[]{:S(2)}) copy-start(bf16[256,256]{1,0:T(8,128)(2,1)} %squeeze.221) | copy-start | bytes 393220
  626.8 24.7 %copy-start.97 = (bf16[256,256]{1,0:T(8,128)(2,1)S(1)}, bf16[256,256]{1,0:T(8,128)(2,1)}, u32[]{:S(2)}) copy-start(bf16[256,256]{1,0:T(8,128)(2,1)} %squeeze.222) | copy-start | bytes 393220
  630.7 21.0 copy-start.98
  679.4 18.8 copy-start.85
  679.9 21.3 copy-start.84
  679.9 24.3 %copy-start.83 = (s32[27]{0:T(128)S(1)}, s32[27]{0:T(128)}, u32[]{:S(2)}) copy-start(s32[27]{0:T(128)} %reshape.627) | copy-start | bytes 328
  679.9 27.3 %copy-start.82 = (s32[27]{0:T(128)S(1)}, s32[27]{0:T(128)}, u32[]{:S(2)}) copy-start(s32[27]{0:T(128)} %reshape.633) | copy-start | bytes 328
  682.9 27.3 %copy-start.81 = (s32[27]{0:T(128)S(1)}, s32[27]{0:T(128)}, u32[]{:S(2)}) copy-start(s32[27]{0:T(128)} %reshape.639) | copy-start | bytes 328
  685.9 27.3 %copy-start.80 = (s32[27]{0:T(128)S(1)}, s32[27]{0:T(128)}, u32[]{:S(2)}) copy-start(s32[27]{0:T(128)} %reshape.645) | copy-start | bytes 328
  688.8 27.3 %copy-start.79 = (s32[27]{0:T(128)S(1)}, s32[27]{0:T(128)}, u32[]{:S(2)}) copy-start(s32[27]{0:T(128)} %reshape.651) | copy-start | bytes 328
  691.8 27.3 %copy-start.78 = (s32[27]{0:T(128)S(1)}, s32[27]{0:T(128)}, u32[]{:S(2)}) copy-start(s32[27]{0:T(128)} %reshape.657) | copy-start | bytes 328
  695.2 26.9 %copy-start.77 = (s32[27]{0:T(128)S(1)}, s32[27]{0:T(128)}, u32[]{:S(2)}) copy-start(s32[27]{0:T(128)} %reshape.663) | copy-start | bytes 328
  698.2 26.9 %copy-start.76 = (s32[27]{0:T(128)S(1)}, s32[27]{0:T(128)}, u32[]{:S(2)}) copy-start(s32[27]{0:T(128)} %reshape.669) | copy-start | bytes 328
  701.2 26.9 %copy-start.75 = (s32[27]{0:T(128)S(1)}, s32[27]{0:T(128)}, u32[]{:S(2)}) copy-start(s32[27]{0:T(128)} %reshape.675) | copy-start | bytes 328
  704.2 27.0 %copy-start.74 = (s32[27]{0:T(128)S(1)}, s32[27]{0:T(128)}, u32[]{:S(2)}) copy-start(s32[27]{0:T(128)} %reshape.681) | copy-start | bytes 328
  707.2 27.0 %copy-start.73 = (s32[27]{0:T(128)S(1)}, s32[27]{0:T(128)}, u32[]{:S(2)}) copy-start(s32[27]{0:T(128)} %reshape.687) | copy-start | bytes 328
  710.1 27.0 %copy-start.72 = (s32[27]{0:T(128)S(1)}, s32[27]{0:T(128)}, u32[]{:S(2)}) copy-start(s32[27]{0:T(128)} %reshape.693) | copy-start | bytes 328
  713.1 27.0 %copy-start.71 = (s32[27]{0:T(128)S(1)}, s32[27]{0:T(128)}, u32[]{:S(2)}) copy-start(s32[27]{0:T(128)} %reshape.699) | copy-start | bytes 328
  716.1 27.0 %copy-start.70 = (s32[27]{0:T(128)S(1)}, s32[27]{0:T(128)}, u32[]{:S(2)}) copy-start(s32[27]{0:T(128)} %reshape.705) | copy-start | bytes 328
  719.1 27.0 %copy-start.69 = (s32[27]{0:T(128)S(1)}, s32[27]{0:T(128)}, u32[]{:S(2)}) copy-start(s32[27]{0:T(128)} %reshape.711) | copy-start | bytes 328
  722.1 27.0 %copy-start.68 = (s32[27]{0:T(128)S(1)}, s32[27]{0:T(128)}, u32[]{:S(2)}) copy-start(s32[27]{0:T(128)} %reshape.717) | copy-start | bytes 328
  725.0 27.0 %copy-start.67 = (s32[27]{0:T(128)S(1)}, s32[27]{0:T(128)}, u32[]{:S(2)}) copy-start(s32[27]{0:T(128)} %reshape.723) | copy-start | bytes 328
  728.0 27.0 %copy-start.66 = (s32[27]{0:T(128)S(1)}, s32[27]{0:T(128)}, u32[]{:S(2)}) copy-start(s32[27]{0:T(128)} %reshape.729) | copy-start | bytes 328
  731.2 26.8 %copy-start.65 = (s32[27]{0:T(128)S(1)}, s32[27]{0:T(128)}, u32[]{:S(2)}) copy-start(s32[27]{0:T(128)} %reshape.735) | copy-start | bytes 328
  829.2 1299.4 %reduce-scatter.5.cloned.1.call-start = ((), (), s32[]{:S(2)}) async-start(), calls=%async_computation.5 | async-start | bytes 8454144 | tf_op jit(solution)/shard_map/reduce_scatter | solution.py:93
  876.1 606.2 %copy-start.212 = (f32[27,512]{1,0:T(8,128)S(1)}, f32[27,512]{1,0:T(8,128)}, u32[]{:S(2)}) copy-start(f32[27,512]{1,0:T(8,128)} %param.10) | copy-start | bytes 165892
  876.1 606.2 %copy-start.220 = (f32[27,512]{1,0:T(8,128)S(1)}, f32[27,512]{1,0:T(8,128)}, u32[]{:S(2)}) copy-start(f32[27,512]{1,0:T(8,128)} %param.11) | copy-start | bytes 165892
  876.1 606.2 %copy-start.221 = (f32[27,512]{1,0:T(8,128)S(1)}, f32[27,512]{1,0:T(8,128)}, u32[]{:S(2)}) copy-start(f32[27,512]{1,0:T(8,128)} %param.12) | copy-start | bytes 165892
  876.1 1252.5 %copy-start.213 = (f32[27,512]{1,0:T(8,128)S(1)}, f32[27,512]{1,0:T(8,128)}, u32[]{:S(2)}) copy-start(f32[27,512]{1,0:T(8,128)} %param.13) | copy-start | bytes 165892
  876.1 1252.5 %copy-start.222 = (f32[27,512]{1,0:T(8,128)S(1)}, f32[27,512]{1,0:T(8,128)}, u32[]{:S(2)}) copy-start(f32[27,512]{1,0:T(8,128)} %param.14) | copy-start | bytes 165892
  876.1 1252.5 %copy-start.223 = (f32[27,512]{1,0:T(8,128)S(1)}, f32[27,512]{1,0:T(8,128)}, u32[]{:S(2)}) copy-start(f32[27,512]{1,0:T(8,128)} %param.15) | copy-start | bytes 165892
  (182 other events, 826.7 us)
Sparse Core Ops, SparseCore 0:
  11.4 70.2 all-gather.2
  85.2 65.8 all-gather.4
  829.3 652.9 reduce-scatter.2
  1484.6 643.9 reduce-scatter.4
where the time goes:
time: 2160 us; the launch traced here: 2140 us
  waiting for transfers between devices  1250 us (58%)
  local copies, waits for them, and re-layouts  707 us (33%)
  other arithmetic  94.7 us (4%)
  matrix products  67.9 us (3%)
    reduce_scatter x1, waiting for transfers between devices, body(): summed2 = lax.psum_scatter(grad2, 'dp', scatter_dimension=1, tiled=True)  645 us
    reduce_scatter x1, waiting for transfers between devices, body(): summed1 = lax.psum_scatter(grad1, 'dp', scatter_dimension=1, tiled=True)  605 us
    slice x27, local copies, waits for them, and re-layouts, window_strided(): piece = padded[:, di:di + span:2, dj:dj + span:2, dl:dl + span:2, :]  291 us
    scatter-add x27, other arithmetic, body(): grad_pad = grad_pad.at[:, di:di + span:2, dj:dj + span:2, dl:dl + span:2,...  80.8 us
    unnamed x508, local copies, waits for them, and re-layouts  48 us
    slice x28, local copies, waits for them, and re-layouts, window_same(): piece = padded[:, di:di + edge, dj:dj + edge, dl:dl + edge, :]  44.1 us
  transfers between devices with their start and end apart: 4, of which 2 were waited for; matrix products, arithmetic and copies ran while one was open for 26% of the time, Pallas kernels for 0%

commit v1 on v0

v1 whole, which is shorter than its diff:
```python
import functools
import itertools

import jax
import jax.numpy as jnp
import numpy as np
from jax import lax
from jax.experimental import pallas as pl
from jax.experimental.pallas import tpu as pltpu
from jax.sharding import PartitionSpec as P

C = 256
HALF = 128
EDGE = 6
OUTER = 3
TAPS = 27
SAMP = 4
ROWS = 32
ACT_ROWS = EDGE * EDGE * ROWS
PAD_ROWS = 64 * ROWS
OUT_ROWS = 16
PRE_ROWS = 9 * OUT_ROWS
VMEM_LIMIT = 56 * 1024 * 1024
BF = jnp.bfloat16
F32 = jnp.float32

VM = pl.BlockSpec(memory_space=pltpu.VMEM)


def dot(a, b):
    return jnp.dot(a, b, preferred_element_type=F32)


def dot_t(a, b):
    return lax.dot_general(a, b, (((1,), (1,)), ((), ())), preferred_element_type=F32)


def sigmoid(v):
    return 1.0 / (1.0 + jnp.exp(-v))


def load(ref, start, count, stride=1):
    return jnp.concatenate(
        [ref[half, pl.ds(start, count, stride=stride), :] for half in range(2)], axis=1
    )


def store(ref, start, count, value, stride=1):
    for half in range(2):
        ref[half, pl.ds(start, count, stride=stride), :] = value[
            :, half * HALF : (half + 1) * HALF
        ]


def one_hot(order_row):
    return (lax.broadcasted_iota(jnp.int32, (C, C), 0) == order_row).astype(BF)


def prep_kernel(latent, out_grad, order, x3, skip, cot, xs, og):
    xs[...] = jnp.zeros_like(xs)
    og[...] = jnp.zeros_like(og)
    for s in range(SAMP):
        for i in range(EDGE):
            for j in range(EDGE):
                base = 8 + ((i + 1) * 8 + j + 1) * ROWS + s * 8 + 1
                store(xs, base, EDGE, latent[s, i, j].astype(F32))
        for qi in range(OUTER):
            for qj in range(OUTER):
                base = (qi * 3 + qj) * OUT_ROWS + s * 4
                og[base : base + OUTER, :] = out_grad[s, qi, qj].astype(F32)
    cot[...] = og[...]
    for qi in range(OUTER):
        for qj in range(OUTER):
            base = 8 + ((2 * qi + 1) * 8 + 2 * qj + 1) * ROWS + 1
            skip[pl.ds((qi * 3 + qj) * OUT_ROWS, OUT_ROWS), :] = load(xs, base, OUT_ROWS, 2)
    perm = one_hot(order[...])
    for dl in range(3):
        for i in range(8):
            rows = load(xs, 7 + dl + i * 256, 256).astype(BF)
            x3[dl, i] = dot(rows, perm).astype(BF).reshape(8, ROWS, C)


def prep(latent, out_grad, order):
    return pl.pallas_call(
        prep_kernel,
        out_shape=(
            jax.ShapeDtypeStruct((3, 8, 8, ROWS, C), BF),
            jax.ShapeDtypeStruct((PRE_ROWS, C), F32),
            jax.ShapeDtypeStruct((PRE_ROWS, C), F32),
        ),
        in_specs=[VM] * 3,
        out_specs=(VM, VM, VM),
        scratch_shapes=[
            pltpu.VMEM((2, PAD_ROWS + 16, HALF), F32),
            pltpu.VMEM((PRE_ROWS, C), F32),
        ],
        compiler_params=pltpu.CompilerParams(vmem_limit_bytes=VMEM_LIMIT),
        cost_estimate=pl.CostEstimate(
            flops=2 * 3 * PAD_ROWS * C * C, bytes_accessed=8_000_000, transcendentals=0
        ),
        name="prep",
    )(latent, out_grad, order)


def swap_halves(value, core):
    swapped = jnp.concatenate([value[:, HALF:], value[:, :HALF]], axis=1)
    return jnp.where(core == 1, swapped, value)


def main_kernel(
    core_ref, x3, skip, cot, mine, recv, block_out, keep, send,
    act, hs, hsel, y, gh, gat, bo,
):
    core = core_ref[0]

    def weight(t):
        return jnp.concatenate(
            [mine[:, t].reshape(HALF, C), recv[:, t].reshape(HALF, C)], axis=0
        )

    def store_grad(t, grad_t):
        eye = (
            lax.broadcasted_iota(jnp.int32, (C, C), 0)
            == lax.broadcasted_iota(jnp.int32, (C, C), 1)
        ).astype(BF)
        grad = dot_t(eye, grad_t.astype(BF)).astype(BF)
        keep[:, t] = grad[:HALF].reshape(4, ROWS, C)
        send[:, t] = grad[HALF:].reshape(4, ROWS, C)

    act[...] = jnp.zeros_like(act)

    def first_step(n, carry):
        di, dj = n // 3, n % 3
        total = None
        for dl in range(3):
            window = x3[dl, pl.ds(di, EDGE), pl.ds(dj, EDGE)].reshape(ACT_ROWS, C)
            term = dot(window, weight(n * 3 + dl))
            total = term if total is None else total + term
        act[...] += total
        return carry

    lax.fori_loop(0, 9, first_step, 0)

    hsel[:, 0] = jnp.zeros_like(hsel[:, 0])
    hsel[:, :, 0] = jnp.zeros_like(hsel[:, :, 0])
    store(hs, ACT_ROWS, 8, jnp.zeros((8, C), F32))
    cell = lax.broadcasted_iota(jnp.int32, (EDGE * ROWS, C), 0) % 8
    inside = (cell >= 1) & (cell <= EDGE)
    for i in range(EDGE):
        part = pl.ds(i * EDGE * ROWS, EDGE * ROWS)
        value = swap_halves(act[part, :], core)
        act[part, :] = value
        hidden = jnp.where(inside, value * sigmoid(value), 0.0)
        store(hs, i * EDGE * ROWS, EDGE * ROWS, hidden.astype(BF).astype(F32))
    for dl in range(3):
        for i in range(EDGE):
            rows = load(hs, i * EDGE * ROWS + dl, EDGE * OUT_ROWS, 2)
            hsel[dl, i + 1, 1:] = rows.astype(BF).reshape(EDGE, OUT_ROWS, C)

    def strided_window(dl, di, dj):
        blocks = [
            hsel[dl, 2 * qi + di, 2 * qj + dj] for qi in range(OUTER) for qj in range(OUTER)
        ]
        return jnp.concatenate(blocks, axis=0)

    def second_step(n, total):
        di, dj = n // 3, n % 3
        for dl in range(3):
            total = total + dot(strided_window(dl, di, dj), weight(TAPS + n * 3 + dl))
        return total

    pre = lax.fori_loop(0, 9, second_step, skip[...])
    sigma = sigmoid(pre)
    bo[...] = pre * sigma
    for s in range(SAMP):
        for qi in range(OUTER):
            for qj in range(OUTER):
                base = (qi * 3 + qj) * OUT_ROWS + s * 4
                block_out[s, qi, qj] = bo[base : base + OUTER, :].astype(BF)
    grad_pre32 = (cot[...] * (sigma * (1.0 + pre * (1.0 - sigma)))).astype(BF).astype(F32)
    grad_pre = grad_pre32.astype(BF)
    grad_pre_t = grad_pre32.T.astype(BF)

    y[...] = jnp.zeros_like(y)

    def back_step(n, carry):
        di, dj = n // 3, n % 3
        for dl in range(3):
            t = TAPS + n * 3 + dl
            store_grad(t, dot(grad_pre_t, strided_window(dl, di, dj)))
            term = dot_t(grad_pre, weight(t)).reshape(9, OUT_ROWS, C)
            for qi in range(OUTER):
                for qj in range(OUTER):
                    y[dl, 2 * qi + di, 2 * qj + dj] += term[qi * 3 + qj]
        return carry

    lax.fori_loop(0, 9, back_step, 0)

    store(gh, ACT_ROWS, 8, jnp.zeros((8, C), F32))
    count = EDGE * OUT_ROWS
    for i in range(EDGE):
        base = i * EDGE * ROWS
        store(gh, base, count, y[0, i + 1, 1:].reshape(count, C), 2)
        store(gh, base + 1, count, y[1, i + 1, 1:].reshape(count, C), 2)
    for i in range(EDGE):
        base = i * EDGE * ROWS + 2
        total = load(gh, base, count, 2) + y[2, i + 1, 1:].reshape(count, C)
        store(gh, base, count, total, 2)
    for i in range(EDGE):
        part = pl.ds(i * EDGE * ROWS, EDGE * ROWS)
        value = act[part, :]
        sigma = sigmoid(value)
        grad = load(gh, i * EDGE * ROWS, EDGE * ROWS) * (sigma * (1.0 + value * (1.0 - sigma)))
        grad = swap_halves(jnp.where(inside, grad, 0.0), core)
        store(gh, i * EDGE * ROWS, EDGE * ROWS, grad.astype(BF).astype(F32))
    for n in range(ACT_ROWS // HALF):
        gat[:, n * HALF : (n + 1) * HALF] = load(gh, n * HALF, HALF).T.astype(BF)

    def first_back(n, carry):
        di, dj = n // 3, n % 3
        for dl in range(3):
            window = x3[dl, pl.ds(di, EDGE), pl.ds(dj, EDGE)].reshape(ACT_ROWS, C)
            store_grad(n * 3 + dl, dot(gat[...], window))
        return carry

    lax.fori_loop(0, 9, first_back, 0)


def block(core, x3, skip, cot, mine, recv):
    grads = jax.ShapeDtypeStruct((4, 2 * TAPS, ROWS, C), BF)
    return pl.pallas_call(
        main_kernel,
        out_shape=(
            jax.ShapeDtypeStruct((SAMP, OUTER, OUTER, OUTER, C), BF),
            grads,
            grads,
        ),
        in_specs=[pl.BlockSpec(memory_space=pltpu.SMEM)] + [VM] * 5,
        out_specs=(VM, VM, VM),
        scratch_shapes=[
            pltpu.VMEM((ACT_ROWS, C), F32),
            pltpu.VMEM((2, ACT_ROWS + 8, HALF), F32),
            pltpu.VMEM((3, 7, 7, OUT_ROWS, C), BF),
            pltpu.VMEM((3, 7, 7, OUT_ROWS, C), F32),
            pltpu.VMEM((2, ACT_ROWS + 8, HALF), F32),
            pltpu.VMEM((C, ACT_ROWS), BF),
            pltpu.VMEM((PRE_ROWS, C), F32),
        ],
        compiler_params=pltpu.CompilerParams(vmem_limit_bytes=VMEM_LIMIT),
        cost_estimate=pl.CostEstimate(
            flops=8_000_000_000, bytes_accessed=18_000_000, transcendentals=1_000_000
        ),
        name="block",
    )(core, x3, skip, cot, mine, recv)


def place(x, y, z, c):
    return ((x * 4 + y) * 4 + z) * 2 + c


def channel_orders():
    orders = []
    for c in range(2):
        order = []
        for a, b, d in itertools.product(range(4), repeat=3):
            x, y, z = (b, d, a) if c == 0 else (a, b, d)
            order += [2 * place(x, y, z, c), 2 * place(x, y, z, c) + 1]
        orders.append(order)
    zero, one = orders
    return np.array([zero + one, one + zero], np.int32).reshape(2, 1, C)


ORDERS = channel_orders()


def pack_kernel(first, second, order, out, flat):
    perm = one_hot(order[...])
    for i in range(2):
        lanes = slice(i * C, (i + 1) * C)
        flat[:TAPS, lanes] = dot(first[:, lanes].astype(BF), perm)
        flat[TAPS:, lanes] = second[:, lanes].astype(BF).astype(F32)
    shard = flat[...].astype(BF)
    for n in range(16):
        out[n] = shard


def pack(first, second, order):
    return pl.pallas_call(
        pack_kernel,
        out_shape=jax.ShapeDtypeStruct((16, 2 * TAPS, 2 * C), BF),
        in_specs=[VM] * 3,
        out_specs=VM,
        scratch_shapes=[pltpu.VMEM((2 * TAPS, 2 * C), F32)],
        compiler_params=pltpu.CompilerParams(vmem_limit_bytes=VMEM_LIMIT),
        name="pack",
    )(first, second, order)


def spread_kernel(shards, out, wide):
    for m in range(16):
        rows = shards[m].astype(F32)
        for i in range(2):
            store(wide, 2 * m + i, 2 * TAPS, rows[:, i * C : (i + 1) * C], ROWS)

    def step(t, carry):
        value = load(wide, pl.multiple_of(t * ROWS, ROWS), ROWS).astype(BF)
        for n in range(4):
            out[n, t] = value
        return carry

    lax.fori_loop(0, 2 * TAPS, step, 0)


def spread(shards):
    return pl.pallas_call(
        spread_kernel,
        out_shape=jax.ShapeDtypeStruct((4, 2 * TAPS, ROWS, C), BF),
        in_specs=[VM],
        out_specs=VM,
        scratch_shapes=[pltpu.VMEM((2, 2 * TAPS * ROWS, HALF), F32)],
        compiler_params=pltpu.CompilerParams(vmem_limit_bytes=VMEM_LIMIT),
        name="spread",
    )(shards)


def pair_kernel(one, two, out):
    def step(t, carry):
        for n in range(4):
            out[n, t] = (one[n, t].astype(F32) + two[n, t].astype(F32)).astype(BF)
        return carry

    lax.fori_loop(0, 2 * TAPS, step, 0)


def pair_sum(one, two):
    return pl.pallas_call(
        pair_kernel,
        out_shape=jax.ShapeDtypeStruct(one.shape, BF),
        in_specs=[VM] * 2,
        out_specs=VM,
        compiler_params=pltpu.CompilerParams(vmem_limit_bytes=VMEM_LIMIT),
        name="pair_sum",
    )(one, two)


def collect_kernel(parts, out, wide):
    def step(t, carry):
        total = parts[0, t].astype(F32)
        for n in range(1, 4):
            total = total + parts[n, t].astype(F32)
        store(wide, pl.multiple_of(t * ROWS, ROWS), ROWS, total)
        return carry

    lax.fori_loop(0, 2 * TAPS, step, 0)
    for m in range(16):
        for i in range(2):
            rows = load(wide, 2 * m + i, 2 * TAPS, ROWS)
            out[m, :, i * C : (i + 1) * C] = rows.astype(BF)


def collect(parts):
    return pl.pallas_call(
        collect_kernel,
        out_shape=jax.ShapeDtypeStruct((16, 2 * TAPS, 2 * C), BF),
        in_specs=[VM],
        out_specs=VM,
        scratch_shapes=[pltpu.VMEM((2, 2 * TAPS * ROWS, HALF), F32)],
        compiler_params=pltpu.CompilerParams(vmem_limit_bytes=VMEM_LIMIT),
        name="collect",
    )(parts)


def adam_update(weight, first, second, grad):
    first_new = 0.9 * first + 0.1 * grad
    second_new = 0.999 * second + 0.001 * grad * grad
    fix_first = 1.0 - 0.9**10
    fix_second = 1.0 - 0.999**10
    weight_new = weight - 0.05 * (first_new / fix_first) / (
        jnp.sqrt(second_new / fix_second) + 1e-08
    )
    return (weight_new, first_new, second_new)


def adam_kernel(scale, parts, order, k1, m1, v1, k2, m2, v2, k1n, m1n, v1n, k2n, m2n, v2n):
    total = parts[0].astype(F32)
    for n in range(1, 16):
        total = total + parts[n].astype(F32)
    total = total * scale
    back = one_hot(order[...]).astype(F32)
    for i in range(2):
        lanes = slice(i * C, (i + 1) * C)
        grad = lax.dot_general(
            total[:TAPS, lanes],
            back,
            (((1,), (1,)), ((), ())),
            precision=lax.Precision.HIGHEST,
            preferred_element_type=F32,
        )
        k1n[:, lanes], m1n[:, lanes], v1n[:, lanes] = adam_update(
            k1[:, lanes], m1[:, lanes], v1[:, lanes], grad
        )
    k2n[...], m2n[...], v2n[...] = adam_update(k2[...], m2[...], v2[...], total[TAPS:])


def adam(scale, parts, order, *state):
    return pl.pallas_call(
        functools.partial(adam_kernel, scale),
        out_shape=(jax.ShapeDtypeStruct((TAPS, 2 * C), F32),) * 6,
        in_specs=[VM] * 8,
        out_specs=(VM,) * 6,
        compiler_params=pltpu.CompilerParams(vmem_limit_bytes=VMEM_LIMIT),
        name="adam",
    )(parts, order, *state)


def lines(c, axes):
    rest = [a for a in "xyz" if a not in axes]
    groups = []
    for fixed in itertools.product(range(4), repeat=len(rest)):
        group = []
        for moving in itertools.product(range(4), repeat=len(axes)):
            at = dict(zip(rest, fixed)) | dict(zip(axes, moving))
            group.append(place(at["x"], at["y"], at["z"], c))
        groups.append(group)
    return groups


PLANES = lines(0, "xy") + lines(1, "yz")
LINES = lines(0, "z") + lines(1, "x")
PARTNERS = [(n, n ^ 1) for n in range(128)]


def exchange(value, groups):
    return lax.all_to_all(value, "dp", 0, 0, axis_index_groups=groups, tiled=True)


def body(latent, out_grad, k1, m1, v1, k2, m2, v2):
    total_samples = latent.shape[0] * lax.axis_size("dp")
    core = lax.axis_index("dp") % 2
    orders = jnp.asarray(ORDERS)
    fixed = orders[0]
    own = lax.dynamic_index_in_dim(orders, core, keepdims=False)
    shards = exchange(pack(k1, k2, fixed), PLANES)
    mine = exchange(spread(shards), LINES)
    recv = lax.ppermute(mine, "dp", PARTNERS)
    x3, skip, cot = prep(latent, out_grad, own)
    block_out, keep, send = block(core.reshape(1), x3, skip, cot, mine, recv)
    got = lax.ppermute(send, "dp", PARTNERS)
    parts = exchange(pair_sum(keep, got), LINES)
    parts = exchange(collect(parts), PLANES)
    return (block_out, *adam(1.0 / total_samples, parts, fixed, k1, m1, v1, k2, m2, v2))


def solution(mesh):
    wide = P("dp", None, None, None, None)
    flat = P(None, "dp")
    return jax.shard_map(
        body,
        mesh=mesh,
        in_specs=(wide, wide) + (flat,) * 6,
        out_specs=(wide,) + (flat,) * 6,
        check_vma=False,
    )
```

time: 2160 us -> 177 us (0.08)
  the two profiles are of different devices: /device:TPU:0 before, /device:TPU:1 now
where the time goes in v1:
time: 177 us; the launch traced here: 176 us
  blocking collectives  80.5 us (45%)
  Pallas kernels  62.9 us (36%)
  waiting for transfers between devices  20.6 us (12%)
  local copies, waits for them, and re-layouts  7.6 us (4%)
  starting transfers between devices  3.84 us (2%)
    all_to_all x3, blocking collectives, exchange(): lax.all_to_all(value, 'dp', 0, 0, axis_index_groups=groups, tiled=True)  80.5 us
    pallas_call x1, Pallas kernels, block(): pl.pallas_call(main_kernel, out_shape=(jax.ShapeDtypeStruct((SAMP, OUTER,...  38.3 us
    all_to_all x1, waiting for transfers between devices, exchange(): lax.all_to_all(value, 'dp', 0, 0, axis_index_groups=groups, tiled=True)  14.4 us
    unnamed x13, local copies, waits for them, and re-layouts  7.04 us
    ppermute x1, waiting for transfers between devices, body(): got = lax.ppermute(send, 'dp', PARTNERS)  6.23 us
    pallas_call x1, Pallas kernels, pair_sum(): pl.pallas_call(pair_kernel, out_shape=jax.ShapeDtypeStruct(one.shape, BF)...  5.87 us
    pallas_call x1, Pallas kernels, spread(): pl.pallas_call(spread_kernel, out_shape=jax.ShapeDtypeStruct((4, 2 * TAPS...  5.22 us
    pallas_call x1, Pallas kernels, collect(): pl.pallas_call(collect_kernel, out_shape=jax.ShapeDtypeStruct((16, 2 * TA...  4.95 us
  transfers between devices with their start and end apart: 3, of which 2 were waited for; matrix products, arithmetic and copies ran while one was open for 3% of the time, Pallas kernels for 2%

profile of v1, /device:TPU:1, one launch (start us, length us, event | category | flops | bytes accessed | tf_op | source)
XLA Modules:
  0.0 176.1 jit_solution(15980365735492004341)
XLA Ops:
  0.6 2.0 %pack.1 = bf16[16,54,512]{2,1,0:T(8,128)(2,1)} custom-call(f32[27,512]{1,0:T(8,128)} %k1.1, f32[27,512]{1,0:T(8,128)} %k2.1, s32[1,256]{1,0:T(1,128)} %constant.27.order), custom_call_target="tpu_custom_call" | custom-call | tf_op jit(solution)/shard_map/pack/pallas_call | solution.py:288
  2.6 24.4 %all_to_all.20.shards = bf16[16,54,512]{2,1,0:T(8,128)(2,1)} all-to-all(bf16[16,54,512]{2,1,0:T(8,128)(2,1)} %pack.1), channel_id=1, replica_groups={{0,8,16,24,32,40,48,56,64,72,80,88,96,104,112,120},{2,10,18,26,34,42,50..., dimensions={0} | all-to-all | bytes 1769472 | tf_op jit(solution)/shard_map/all_to_all | solution.py:434
  27.0 5.2 %spread.1 = bf16[4,54,32,256]{3,2,1,0:T(8,128)(2,1)} custom-call(bf16[16,54,512]{2,1,0:T(8,128)(2,1)} %all_to_all.20.shards), custom_call_target="tpu_custom_call" | custom-call | tf_op jit(solution)/shard_map/spread/pallas_call | solution.py:315
  32.3 0.0 copy-start.4
  32.3 27.2 %all_to_all.21.mine = bf16[4,54,32,256]{3,2,1,0:T(8,128)(2,1)S(1)} all-to-all(bf16[4,54,32,256]{3,2,1,0:T(8,128)(2,1)} %spread.1), channel_id=1, replica_groups={{0,2,4,6},{8,10,12,14},{16,18,20,22},{24,26,28,30},{32,34,36,38},{40,42..., dimensions={0} | all-to-all | bytes 7077888 | tf_op jit(solution)/shard_map/all_to_all | solution.py:434
  59.5 0.0 copy-start.1
  59.5 0.0 collective-permute-start
  59.5 1.8 %copy.17.out_grad = bf16[4,3,3,3,256]{4,3,2,1,0:T(4,128)(2,1)} copy(bf16[4,3,3,3,256]{4,0,3,2,1:T(4,128)(2,1)} %param.10) | data formatting | bytes 110592 | tf_op args[1]
  61.3 1.9 %copy.16.latent = bf16[4,6,6,6,256]{4,3,2,1,0:T(8,128)(2,1)} copy(bf16[4,6,6,6,256]{4,0,3,2,1:T(4,128)(2,1)} %param.9) | data formatting | bytes 884736 | tf_op args[0]
  63.2 0.0 copy-done.4
  63.2 0.6 dynamic-slice_bitcast_fusion.order
  63.7 3.9 %prep.1 = (bf16[3,8,8,32,256]{4,3,2,1,0:T(8,128)(2,1)}, f32[144,256]{1,0:T(8,128)}, f32[144,256]{1,0:T(8,128)}) custom-call(bf16[4,6,6,6,256]{4,3,2,1,0:T(8,128)(2,1)} %copy.16.latent, bf16[4,3,3,3,256]{4,3,2,1,0:T(4,128)(2,1)} %copy.17.out_grad, s32[1,256]{1,0:T(1,128)} %dynamic-slice_bitcast_fusion.order), custom_call_target="tpu_custom_call" | custom-call | flops 805306368 | bytes 8000000 | tf_op jit(solution)/shard_map/prep/pallas_call | solution.py:84
  67.6 0.0 collective-permute-done.recv
  67.6 0.0 copy-done.1
  67.6 38.3 %block.1 = (bf16[4,3,3,3,256]{4,3,2,1,0:T(4,128)(2,1)}, bf16[4,54,32,256]{3,2,1,0:T(8,128)(2,1)}, bf16[4,54,32,256]{3,2,1,0:T(8,128)(2,1)}) custom-call(s32[1]{0:T(128)} %bitcast.core_ref, bf16[3,8,8,32,256]{4,3,2,1,0:T(8,128)(2,1)} %get-tuple-element.19.x3, f32[144,256]{1,0:T(8,128)} %get-tuple-element.20.skip, f32[144,256]{1,0:T(8,128)} %get-tuple-element.21.cot, ...), custom_call_target="tpu_custom_call" | custom-call | flops 8000000000 | bytes 18000000 | tf_op jit(solution)/shard_map/block/pallas_call | solution.py:231
  106.0 0.2 collective-permute-start.1
  106.2 6.2 %collective-permute-done.1.two = bf16[4,54,32,256]{3,2,1,0:T(8,128)(2,1)S(1)} collective-permute-done((bf16[4,54,32,256]{3,2,1,0:T(8,128)(2,1)}, bf16[4,54,32,256]{3,2,1,0:T(8,128)(2,1)S(1)}, u32[]{:S(2)}, u32[]{:S(2)}) %collective-permute-start.1) | collective-permute-done | bytes 3538976 | tf_op jit(solution)/shard_map/ppermute | solution.py:448
  112.4 0.0 copy-start.2
  112.4 1.8 %copy-done.2 = bf16[4,54,32,256]{3,2,1,0:T(8,128)(2,1)} copy-done((bf16[4,54,32,256]{3,2,1,0:T(8,128)(2,1)}, bf16[4,54,32,256]{3,2,1,0:T(8,128)(2,1)S(1)}, u32[]{:S(2)}) %copy-start.2) | copy-done | bytes 3538968
  114.2 5.9 %pair_sum.1 = bf16[4,54,32,256]{3,2,1,0:T(8,128)(2,1)} custom-call(bf16[4,54,32,256]{3,2,1,0:T(8,128)(2,1)} %get-tuple-element.23.one, bf16[4,54,32,256]{3,2,1,0:T(8,128)(2,1)} %copy-done.2), custom_call_target="tpu_custom_call" | custom-call | tf_op jit(solution)/shard_map/pair_sum/pallas_call | solution.py:336
  120.1 28.9 %all_to_all.22.parts = bf16[4,54,32,256]{3,2,1,0:T(8,128)(2,1)} all-to-all(bf16[4,54,32,256]{3,2,1,0:T(8,128)(2,1)} %pair_sum.1), channel_id=1, replica_groups={{0,2,4,6},{8,10,12,14},{16,18,20,22},{24,26,28,30},{32,34,36,38},{40,42..., dimensions={0} | all-to-all | bytes 7077888 | tf_op jit(solution)/shard_map/all_to_all | solution.py:434
  148.9 0.0 copy-start.3
  148.9 5.0 %collect.1 = bf16[16,54,512]{2,1,0:T(8,128)(2,1)} custom-call(bf16[4,54,32,256]{3,2,1,0:T(8,128)(2,1)} %all_to_all.22.parts), custom_call_target="tpu_custom_call" | custom-call | tf_op jit(solution)/shard_map/collect/pallas_call | solution.py:362
  153.9 3.6 %all-to-all-start.3 = ((bf16[16,54,512]{2,1,0:T(8,128)(2,1)}), bf16[16,54,512]{2,1,0:T(8,128)(2,1)S(1)}, u32[]{:S(2)}, u32[]{:S(2)}) async-start(bf16[16,54,512]{2,1,0:T(8,128)(2,1)} %collect.1), calls=%async_computation.3 | async-start | bytes 1835008 | tf_op jit(solution)/shard_map/all_to_all | solution.py:434
  157.5 0.0 copy-done.3
  157.5 0.6 copy.18
  158.2 14.4 %all-to-all-done.3.parts = bf16[16,54,512]{2,1,0:T(8,128)(2,1)S(1)} async-done(((bf16[16,54,512]{2,1,0:T(8,128)(2,1)}), bf16[16,54,512]{2,1,0:T(8,128)(2,1)S(1)}, u32[]{:S(2)}, u32[]{:S(2)}) %all-to-all-start.3) | async-done | bytes 884768 | tf_op jit(solution)/shard_map/all_to_all | solution.py:434
  172.6 0.0 copy-start
  172.6 0.9 copy-done
  173.5 2.6 %adam.1 = (f32[27,512]{1,0:T(8,128)}, f32[27,512]{1,0:T(8,128)}, f32[27,512]{1,0:T(8,128)}, f32[27,512]{1,0:T(8,128)}, f32[27,512]{1,0:T(8,128)}, /*index=5*/f32[27,512]{1,0:T(8,128)}) custom-call(bf16[16,54,512]{2,1,0:T(8,128)(2,1)} %copy-done, s32[1,256]{1,0:T(1,128)} %constant.27.order, f32[27,512]{1,0:T(8,128)} %k1.1, f32[27,512]{1,0:T(8,128)} %m1.1, ...), custom_call_target="tpu_custom_call" | custom-call | tf_op jit(solution)/shard_map/adam/pallas_call | solution.py:406
Async XLA Ops:
  32.3 30.9 %copy-start.4 = (s32[2,1,256]{2,1,0:T(1,128)S(1)}, s32[2,1,256]{2,1,0:T(1,128)}, u32[]{:S(2)}) copy-start(s32[2,1,256]{2,1,0:T(1,128)} %constant.23.clone) | copy-start | bytes 6148
  59.5 8.1 %copy-start.1 = (bf16[4,54,32,256]{3,2,1,0:T(8,128)(2,1)}, bf16[4,54,32,256]{3,2,1,0:T(8,128)(2,1)S(1)}, u32[]{:S(2)}) copy-start(bf16[4,54,32,256]{3,2,1,0:T(8,128)(2,1)S(1)} %all_to_all.21.mine) | copy-start | bytes 10616836
  59.5 8.1 %collective-permute-start = (bf16[4,54,32,256]{3,2,1,0:T(8,128)(2,1)S(1)}, bf16[4,54,32,256]{3,2,1,0:T(8,128)(2,1)}, u32[]{:S(2)}, u32[]{:S(2)}) collective-permute-start(bf16[4,54,32,256]{3,2,1,0:T(8,128)(2,1)S(1)} %all_to_all.21.mine), channel_id=1, source_target_pairs={{0,1},{1,0},{2,3},{3,2},{4,5},{5,4},{6,7},{7,6},{8,9},{9,8},{10,11... | collective-permute-start | bytes 10616840 | tf_op jit(solution)/shard_map/ppermute | solution.py:445
  106.0 6.4 %collective-permute-start.1 = (bf16[4,54,32,256]{3,2,1,0:T(8,128)(2,1)}, bf16[4,54,32,256]{3,2,1,0:T(8,128)(2,1)S(1)}, u32[]{:S(2)}, u32[]{:S(2)}) collective-permute-start(bf16[4,54,32,256]{3,2,1,0:T(8,128)(2,1)} %get-tuple-element.24), channel_id=1, source_target_pairs={{0,1},{1,0},{2,3},{3,2},{4,5},{5,4},{6,7},{7,6},{8,9},{9,8},{10,11... | collective-permute-start | bytes 10616840 | tf_op jit(solution)/shard_map/ppermute | solution.py:448
  112.4 1.8 %copy-start.2 = (bf16[4,54,32,256]{3,2,1,0:T(8,128)(2,1)}, bf16[4,54,32,256]{3,2,1,0:T(8,128)(2,1)S(1)}, u32[]{:S(2)}) copy-start(bf16[4,54,32,256]{3,2,1,0:T(8,128)(2,1)S(1)} %collective-permute-done.1.two) | copy-start | bytes 10616836
  148.9 8.6 %copy-start.3 = (bf16[4,3,3,3,256]{4,3,2,1,0:T(4,128)(2,1)S(1)}, bf16[4,3,3,3,256]{4,3,2,1,0:T(4,128)(2,1)}, u32[]{:S(2)}) copy-start(bf16[4,3,3,3,256]{4,3,2,1,0:T(4,128)(2,1)} %get-tuple-element.31) | copy-start | bytes 165892
  153.9 18.7 %all-to-all-start.3 = ((bf16[16,54,512]{2,1,0:T(8,128)(2,1)}), bf16[16,54,512]{2,1,0:T(8,128)(2,1)S(1)}, u32[]{:S(2)}, u32[]{:S(2)}) async-start(bf16[16,54,512]{2,1,0:T(8,128)(2,1)} %collect.1), calls=%async_computation.3 | async-start | bytes 1835008 | tf_op jit(solution)/shard_map/all_to_all | solution.py:434
  172.6 0.9 copy-start

commit v2 on v1

v2 whole, which is shorter than its diff:
```python
import functools
import itertools

import jax
import jax.numpy as jnp
import numpy as np
from jax import lax
from jax.experimental import pallas as pl
from jax.experimental.pallas import tpu as pltpu
from jax.sharding import PartitionSpec as P

C = 256
HALF = 128
EDGE = 6
OUTER = 3
TAPS = 27
SAMP = 4
ROWS = 32
ACT_ROWS = EDGE * EDGE * ROWS
PAD_ROWS = 64 * ROWS
OUT_ROWS = 16
PRE_ROWS = 9 * OUT_ROWS
MIB = 1024 * 1024
BF = jnp.bfloat16
F32 = jnp.float32

VM = pl.BlockSpec(memory_space=pltpu.VMEM)
SM = pl.BlockSpec(memory_space=pltpu.SMEM)
ANY = pl.BlockSpec(memory_space=pl.ANY)


def shape(dims, dtype):
    return jax.ShapeDtypeStruct(dims, dtype)


def call(kernel, name, out_shape, in_specs, scratch, mib, flops, moved):
    single = not isinstance(out_shape, tuple)
    return pl.pallas_call(
        kernel,
        out_shape=out_shape,
        in_specs=in_specs,
        out_specs=VM if single else (VM,) * len(out_shape),
        scratch_shapes=scratch,
        compiler_params=pltpu.CompilerParams(vmem_limit_bytes=mib * MIB),
        cost_estimate=pl.CostEstimate(flops=flops, bytes_accessed=moved, transcendentals=0),
        name=name,
    )


def dot(a, b):
    return jnp.dot(a, b, preferred_element_type=F32)


def dot_t(a, b):
    return lax.dot_general(a, b, (((1,), (1,)), ((), ())), preferred_element_type=F32)


def sigmoid(v):
    return 1.0 / (1.0 + jnp.exp(-v))


def load(ref, start, count, stride=1):
    return jnp.concatenate(
        [ref[half, pl.ds(start, count, stride=stride), :] for half in range(2)], axis=1
    )


def store(ref, start, count, value, stride=1):
    for half in range(2):
        ref[half, pl.ds(start, count, stride=stride), :] = value[
            :, half * HALF : (half + 1) * HALF
        ]


def one_hot(order_row):
    return (lax.broadcasted_iota(jnp.int32, (C, C), 0) == order_row).astype(BF)


def fill_cells(source, xs):
    for i in range(EDGE):
        for j in range(EDGE):
            value = source[i, j].astype(F32)
            base = 8 + ((i + 1) * 8 + j + 1) * ROWS + 1
            for l in range(EDGE):
                store(xs, base + l, SAMP, value[l], 8)


def prep_kernel(latent, other, out_grad, order, x3a, x3b, x3o, skip, cot, xs, og):
    perm = one_hot(order[...])
    xs[...] = jnp.zeros_like(xs)
    og[...] = jnp.zeros_like(og)
    fill_cells(latent, xs)
    for qi in range(OUTER):
        for qj in range(OUTER):
            q = (qi * 3 + qj) * OUT_ROWS
            value = out_grad[qi, qj].astype(F32)
            for ql in range(OUTER):
                store(og, q + ql, SAMP, value[ql], 4)
            base = 8 + ((2 * qi + 1) * 8 + 2 * qj + 1) * ROWS + 1
            skip[q : q + OUT_ROWS, :] = load(xs, base, OUT_ROWS, 2)
    cot[...] = load(og, 0, PRE_ROWS)
    for i in range(8):
        for dl in range(3):
            rows = dot(load(xs, 7 + dl + i * 256, 256).astype(BF), perm).astype(BF)
            x3a[dl, i] = rows[:, :HALF].reshape(8, ROWS, HALF)
            x3b[dl, i] = rows[:, HALF:].reshape(8, ROWS, HALF)
    fill_cells(other, xs)
    for i in range(8):
        for dl in range(3):
            rows = dot(load(xs, 7 + dl + i * 256, 256).astype(BF), perm[:, :HALF])
            x3o[dl, i] = rows.astype(BF).reshape(8, ROWS, HALF)


def prep(latent, other, out_grad, order):
    wide = shape((3, 8, 8, ROWS, HALF), BF)
    pre = shape((PRE_ROWS, C), F32)
    return call(
        prep_kernel, "prep", (wide, wide, wide, pre, pre), [VM] * 4,
        [pltpu.VMEM((2, PAD_ROWS + 16, HALF), F32), pltpu.VMEM((2, PRE_ROWS, HALF), F32)],
        20, 2_000_000_000, 8_000_000,
    )(latent, other, out_grad, order)


def swap_halves(value, core):
    swapped = jnp.concatenate([value[:, HALF:], value[:, :HALF]], axis=1)
    return jnp.where(core == 1, swapped, value)


def cell_mask():
    cell = lax.broadcasted_iota(jnp.int32, (EDGE * ROWS, C), 0) % 8
    return (cell >= 1) & (cell <= EDGE)


def fetch_weights(mine, recv, first, weights, sems):
    copies = []
    for di in range(3):
        for half, source in enumerate((mine, recv)):
            copies.append(
                pltpu.make_async_copy(
                    source.at[:, pl.ds(first + 9 * di, 9)],
                    weights.at[half, :, pl.ds(9 * di, 9)],
                    sems.at[2 * di + half],
                )
            )
            copies[-1].start()
    return copies


def weight(weights, t):
    return jnp.concatenate([weights[half, :, t].reshape(HALF, C) for half in range(2)], axis=0)


WEIGHTS = [pltpu.VMEM((2, 4, TAPS, ROWS, C), BF), pltpu.SemaphoreType.DMA((6,))]


def conv1_kernel(core_ref, x3a, x3b, mine, recv, act, hsel, hsend, weights, sems, hs):
    core = core_ref[0]
    copies = fetch_weights(mine, recv, 0, weights, sems)
    for di in range(3):
        copies[2 * di].wait()
        copies[2 * di + 1].wait()

        def step(dj, carry):
            total = None
            for dl in range(3):
                window = jnp.concatenate(
                    [
                        half[dl, pl.ds(di, EDGE), pl.ds(dj, EDGE)].reshape(ACT_ROWS, HALF)
                        for half in (x3a, x3b)
                    ],
                    axis=1,
                )
                term = dot(window, weight(weights, di * 9 + dj * 3 + dl))
                total = term if total is None else total + term
            if di == 0:
                act[...] = jnp.where(dj == 0, 0.0, act[...]) + total
            else:
                act[...] += total
            return carry

        lax.fori_loop(0, 3, step, 0)

    hsel[:, 0] = jnp.zeros_like(hsel[:, 0])
    hsel[:, :, 0] = jnp.zeros_like(hsel[:, :, 0])
    hsend[:, 0] = jnp.zeros_like(hsend[:, 0])
    hsend[:, :, 0] = jnp.zeros_like(hsend[:, :, 0])
    store(hs, ACT_ROWS, 8, jnp.zeros((8, C), F32))
    inside = cell_mask()
    for i in range(EDGE):
        part = pl.ds(i * EDGE * ROWS, EDGE * ROWS)
        value = swap_halves(act[part, :], core)
        act[part, :] = value
        hidden = jnp.where(inside, value * sigmoid(value), 0.0)
        store(hs, i * EDGE * ROWS, EDGE * ROWS, hidden.astype(BF).astype(F32))
    for dl in range(3):
        for i in range(EDGE):
            rows = load(hs, i * EDGE * ROWS + dl, EDGE * OUT_ROWS, 2)
            rows = rows.astype(BF).reshape(EDGE, OUT_ROWS, C)
            hsel[dl, i + 1, 1:] = rows
            hsend[dl, i + 1, 1:] = rows[..., HALF:]


def conv1(core, x3a, x3b, mine, recv):
    return call(
        conv1_kernel, "conv1",
        (
            shape((ACT_ROWS, C), F32),
            shape((3, 7, 7, OUT_ROWS, C), BF),
            shape((3, 7, 7, OUT_ROWS, HALF), BF),
        ),
        [SM, VM, VM, ANY, ANY],
        WEIGHTS + [pltpu.VMEM((2, ACT_ROWS + 8, HALF), F32)],
        24, 4_000_000_000, 10_000_000,
    )(core, x3a, x3b, mine, recv)


def strided_window(hsel, dl, di, dj, lanes=slice(None)):
    blocks = [
        hsel[dl, 2 * qi + di, 2 * qj + dj, :, lanes] for qi in range(OUTER) for qj in range(OUTER)
    ]
    return jnp.concatenate(blocks, axis=0)


def conv2_kernel(skip, cot, hsel, mine, recv, block_out, grad_pre, grad_pre_t, weights, sems, bo):
    copies = fetch_weights(mine, recv, TAPS, weights, sems)
    pre = skip[...]
    for di in range(3):
        copies[2 * di].wait()
        copies[2 * di + 1].wait()
        for dj in range(3):
            for dl in range(3):
                pre = pre + dot(
                    strided_window(hsel, dl, di, dj), weight(weights, di * 9 + dj * 3 + dl)
                )
    sigma = sigmoid(pre)
    store(bo, 0, PRE_ROWS, pre * sigma)
    for qi in range(OUTER):
        for qj in range(OUTER):
            for ql in range(OUTER):
                base = (qi * 3 + qj) * OUT_ROWS + ql
                block_out[qi, qj, ql] = load(bo, base, SAMP, 4).astype(BF)
    grad = (cot[...] * (sigma * (1.0 + pre * (1.0 - sigma)))).astype(BF)
    grad_pre[...] = grad
    grad_pre_t[...] = grad.astype(F32).T.astype(BF)


def conv2(skip, cot, hsel, mine, recv):
    return call(
        conv2_kernel, "conv2",
        (
            shape((OUTER, OUTER, OUTER, SAMP, C), BF),
            shape((PRE_ROWS, C), BF),
            shape((C, PRE_ROWS), BF),
        ),
        [VM, VM, VM, ANY, ANY],
        WEIGHTS + [pltpu.VMEM((2, PRE_ROWS, HALF), F32)],
        16, 1_500_000_000, 6_000_000,
    )(skip, cot, hsel, mine, recv)


def back_kernel(core_ref, act, grad_pre, mine, recv, gat, weights, sems, y, gh):
    core = core_ref[0]
    copies = fetch_weights(mine, recv, TAPS, weights, sems)
    y[...] = jnp.zeros_like(y)
    grad = grad_pre[...]
    for di in range(3):
        copies[2 * di].wait()
        copies[2 * di + 1].wait()
        for dj in range(3):
            for dl in range(3):
                term = dot_t(grad, weight(weights, di * 9 + dj * 3 + dl))
                term = term.reshape(9, OUT_ROWS, C)
                for qi in range(OUTER):
                    for qj in range(OUTER):
                        y[dl, 2 * qi + di, 2 * qj + dj] += term[qi * 3 + qj]
    store(gh, ACT_ROWS, 8, jnp.zeros((8, C), F32))
    count = EDGE * OUT_ROWS
    for i in range(EDGE):
        base = i * EDGE * ROWS
        store(gh, base, count, y[0, i + 1, 1:].reshape(count, C), 2)
        store(gh, base + 1, count, y[1, i + 1, 1:].reshape(count, C), 2)
    for i in range(EDGE):
        base = i * EDGE * ROWS + 2
        total = load(gh, base, count, 2) + y[2, i + 1, 1:].reshape(count, C)
        store(gh, base, count, total, 2)
    inside = cell_mask()
    for i in range(EDGE):
        value = act[pl.ds(i * EDGE * ROWS, EDGE * ROWS), :]
        sigma = sigmoid(value)
        part = load(gh, i * EDGE * ROWS, EDGE * ROWS) * (sigma * (1.0 + value * (1.0 - sigma)))
        part = swap_halves(jnp.where(inside, part, 0.0), core)
        store(gh, i * EDGE * ROWS, EDGE * ROWS, part)
    for n in range(ACT_ROWS // HALF):
        gat[:, n * HALF : (n + 1) * HALF] = load(gh, n * HALF, HALF).T.astype(BF)


def back(core, act, grad_pre, mine, recv):
    return call(
        back_kernel, "back", shape((C, ACT_ROWS), BF),
        [SM, VM, VM, ANY, ANY],
        WEIGHTS
        + [
            pltpu.VMEM((3, 7, 7, OUT_ROWS, C), F32),
            pltpu.VMEM((2, ACT_ROWS + 8, HALF), F32),
        ],
        18, 1_500_000_000, 8_000_000,
    )(core, act, grad_pre, mine, recv)


def grad_loop(out, lefts, windows):
    eye = (
        lax.broadcasted_iota(jnp.int32, (C, C), 0) == lax.broadcasted_iota(jnp.int32, (C, C), 1)
    ).astype(BF)

    def product(taps):
        total = None
        for left, window in zip(lefts, windows):
            right = jnp.concatenate([window(t // 9, t // 3 % 3, t % 3) for t in taps], axis=1)
            term = dot(left[...], right)
            total = term if total is None else total + term
        width = HALF * len(taps)
        turned = dot_t(eye[:width, :width], total.astype(BF)).astype(BF)
        for n, t in enumerate(taps):
            out[:, t] = turned[n * HALF : (n + 1) * HALF].reshape(4, ROWS, C)

    def step(n, carry):
        product((2 * n, 2 * n + 1))
        return carry

    lax.fori_loop(0, TAPS // 2, step, 0)
    product((TAPS - 1,))


def grad2_kernel(grad_t, grad_t_other, hsel, hsel_other, out):
    grad_loop(
        out,
        (grad_t, grad_t_other),
        (
            lambda di, dj, dl: strided_window(hsel, dl, di, dj, slice(0, HALF)),
            lambda di, dj, dl: strided_window(hsel_other, dl, di, dj),
        ),
    )


def grad2(grad_t, grad_t_other, hsel, hsel_other):
    return call(
        grad2_kernel, "grad2", shape((4, TAPS, ROWS, C), BF), [VM] * 4, [],
        8, 1_000_000_000, 4_000_000,
    )(grad_t, grad_t_other, hsel, hsel_other)


def same_window(x3):
    def window(di, dj, dl):
        return x3[dl, pl.ds(di, EDGE), pl.ds(dj, EDGE)].reshape(ACT_ROWS, HALF)

    return window


def grad1_kernel(gat, gat_other, x3a, x3o, out):
    grad_loop(out, (gat, gat_other), (same_window(x3a), same_window(x3o)))


def grad1(gat, gat_other, x3a, x3o):
    return call(
        grad1_kernel, "grad1", shape((4, TAPS, ROWS, C), BF), [VM] * 4, [],
        12, 4_000_000_000, 7_000_000,
    )(gat, gat_other, x3a, x3o)


def pack_kernel(first, second, order, out, flat):
    perm = one_hot(order[...])
    for i in range(2):
        lanes = slice(i * C, (i + 1) * C)
        flat[:TAPS, lanes] = dot(first[:, lanes].astype(BF), perm)
        flat[TAPS:, lanes] = second[:, lanes].astype(BF).astype(F32)
    shard = flat[...].astype(BF)
    for n in range(16):
        out[n] = shard


def pack(first, second, order):
    return call(
        pack_kernel, "pack", shape((16, 2 * TAPS, 2 * C), BF), [VM] * 3,
        [pltpu.VMEM((2 * TAPS, 2 * C), F32)], 4, 10_000_000, 1_000_000,
    )(first, second, order)


def spread_kernel(shards, out, wide):
    for m in range(16):
        rows = shards[m].astype(F32)
        for i in range(2):
            store(wide, 2 * m + i, 2 * TAPS, rows[:, i * C : (i + 1) * C], ROWS)

    def step(t, carry):
        value = load(wide, pl.multiple_of(t * ROWS, ROWS), ROWS).astype(BF)
        for n in range(4):
            out[n, t] = value
        return carry

    lax.fori_loop(0, 2 * TAPS, step, 0)


def spread(shards):
    return call(
        spread_kernel, "spread", shape((4, 2 * TAPS, ROWS, C), BF), [VM],
        [pltpu.VMEM((2, 2 * TAPS * ROWS, HALF), F32)], 10, 1_000_000, 5_000_000,
    )(shards)


def collect_kernel(parts, out, wide):
    def step(t, carry):
        total = parts[0, t].astype(F32)
        for n in range(1, 4):
            total = total + parts[n, t].astype(F32)
        store(wide, pl.multiple_of(t * ROWS, ROWS), ROWS, total)
        return carry

    lax.fori_loop(0, TAPS, step, 0)
    for m in range(16):
        for i in range(2):
            rows = load(wide, 2 * m + i, TAPS, ROWS)
            out[m, :, i * C : (i + 1) * C] = rows.astype(BF)


def collect(parts):
    return call(
        collect_kernel, "collect", shape((16, TAPS, 2 * C), BF), [VM],
        [pltpu.VMEM((2, TAPS * ROWS, HALF), F32)], 6, 1_000_000, 3_000_000,
    )(parts)


def adam_update(weight, first, second, grad):
    first_new = 0.9 * first + 0.1 * grad
    second_new = 0.999 * second + 0.001 * grad * grad
    fix_first = 1.0 - 0.9**10
    fix_second = 1.0 - 0.999**10
    weight_new = weight - 0.05 * (first_new / fix_first) / (
        jnp.sqrt(second_new / fix_second) + 1e-08
    )
    return (weight_new, first_new, second_new)


def adam_kernel(scale, turn_back, parts, order, k, m, v, kn, mn, vn):
    total = parts[0].astype(F32)
    for n in range(1, 16):
        total = total + parts[n].astype(F32)
    total = total * scale
    back = one_hot(order[...]).astype(F32)
    for i in range(2):
        lanes = slice(i * C, (i + 1) * C)
        grad = total[:, lanes]
        if turn_back:
            grad = lax.dot_general(
                grad,
                back,
                (((1,), (1,)), ((), ())),
                precision=lax.Precision.HIGHEST,
                preferred_element_type=F32,
            )
        kn[:, lanes], mn[:, lanes], vn[:, lanes] = adam_update(
            k[:, lanes], m[:, lanes], v[:, lanes], grad
        )


def adam(scale, turn_back, parts, order, *state):
    return call(
        functools.partial(adam_kernel, scale, turn_back), "adam",
        (shape((TAPS, 2 * C), F32),) * 3, [VM] * 5, [], 6, 10_000_000, 1_000_000,
    )(parts, order, *state)


def place(x, y, z, c):
    return ((x * 4 + y) * 4 + z) * 2 + c


def channel_orders():
    orders = []
    for c in range(2):
        order = []
        for a, b, d in itertools.product(range(4), repeat=3):
            x, y, z = (b, d, a) if c == 0 else (a, b, d)
            order += [2 * place(x, y, z, c), 2 * place(x, y, z, c) + 1]
        orders.append(order)
    zero, one = orders
    return np.array([zero + one, one + zero], np.int32).reshape(2, 1, C)


def lines(c, axes):
    rest = [a for a in "xyz" if a not in axes]
    groups = []
    for fixed in itertools.product(range(4), repeat=len(rest)):
        group = []
        for moving in itertools.product(range(4), repeat=len(axes)):
            at = dict(zip(rest, fixed)) | dict(zip(axes, moving))
            group.append(place(at["x"], at["y"], at["z"], c))
        groups.append(group)
    return groups


ORDERS = channel_orders()
PLANES = lines(0, "xy") + lines(1, "yz")
LINES = lines(0, "z") + lines(1, "x")
PARTNERS = [(n, n ^ 1) for n in range(128)]


def exchange(value, groups):
    return lax.all_to_all(value, "dp", 0, 0, axis_index_groups=groups, tiled=True)


def swap(value):
    return lax.ppermute(value, "dp", PARTNERS)


def body(latent, out_grad, k1, m1, v1, k2, m2, v2):
    scale = 1.0 / (latent.shape[0] * lax.axis_size("dp"))
    core = lax.axis_index("dp") % 2
    orders = jnp.asarray(ORDERS)
    fixed = orders[0]
    own = jnp.where(core == 0, orders[0], orders[1])
    core = core.reshape(1)

    shards = pack(k1, k2, fixed)
    latent = latent.transpose(1, 2, 3, 0, 4)
    cells = prep(latent, swap(latent), out_grad.transpose(1, 2, 3, 0, 4), own)
    shards, cells = lax.optimization_barrier((exchange(shards, PLANES), cells))
    x3a, x3b, x3o, skip, cot = cells
    mine = exchange(spread(shards), LINES)
    recv = swap(mine)

    act, hsel, hsend = conv1(core, x3a, x3b, mine, recv)
    hsel_other = swap(hsend)
    block_out, grad_pre, grad_pre_t = conv2(skip, cot, hsel, mine, recv)
    grad_pre_t_other = swap(grad_pre_t)
    gat = back(core, act, grad_pre, mine, recv)
    gat_other = swap(gat)
    parts2 = exchange(grad2(grad_pre_t, grad_pre_t_other, hsel, hsel_other), LINES)
    parts1 = exchange(grad1(gat, gat_other, x3a, x3o), LINES)
    new_two = adam(scale, False, exchange(collect(parts2), PLANES), fixed, k2, m2, v2)
    new_one = adam(scale, True, exchange(collect(parts1), PLANES), fixed, k1, m1, v1)
    return (block_out.transpose(3, 0, 1, 2, 4), *new_one, *new_two)


def solution(mesh):
    wide = P("dp", None, None, None, None)
    flat = P(None, "dp")
    return jax.shard_map(
        body,
        mesh=mesh,
        in_specs=(wide, wide) + (flat,) * 6,
        out_specs=(wide,) + (flat,) * 6,
        check_vma=False,
    )
```

time: 177 us -> 156 us (0.88)
  the two profiles are of different devices: /device:TPU:1 before, /device:TPU:0 now
where the time goes in v2:
time: 156 us; the launch traced here: 153 us
  waiting for transfers between devices  50 us (32%)
  Pallas kernels  38.8 us (25%)
  blocking collectives  29.6 us (19%)
  starting transfers between devices  24.9 us (16%)
  local copies, waits for them, and re-layouts  9.09 us (6%)
    all_to_all x5, waiting for transfers between devices, exchange(): lax.all_to_all(value, 'dp', 0, 0, axis_index_groups=groups, tiled=True)  39.4 us
    all_to_all x1, blocking collectives, exchange(): lax.all_to_all(value, 'dp', 0, 0, axis_index_groups=groups, tiled=True)  29.6 us
    all_to_all x5, starting transfers between devices, exchange(): lax.all_to_all(value, 'dp', 0, 0, axis_index_groups=groups, tiled=True)  21.4 us
    pallas_call x1, Pallas kernels, grad1(): call(grad1_kernel, 'grad1', shape((4, TAPS, ROWS, C), BF), [VM] * 4, [],...  10.6 us
    ppermute x5, waiting for transfers between devices, swap(): return lax.ppermute(value, 'dp', PARTNERS)  10.6 us
    unnamed x46, local copies, waits for them, and re-layouts  9.09 us
    pallas_call x1, Pallas kernels, conv1(): call(conv1_kernel, 'conv1', (shape((ACT_ROWS, C), F32), shape((3, 7, 7, O...  6.75 us
    pallas_call x1, Pallas kernels, grad2(): call(grad2_kernel, 'grad2', shape((4, TAPS, ROWS, C), BF), [VM] * 4, [],...  6.69 us
  transfers between devices with their start and end apart: 10, of which 9 were waited for; matrix products, arithmetic and copies ran while one was open for 0% of the time, Pallas kernels for 8%

profile of v2, /device:TPU:0, one launch (start us, length us, event | category | flops | bytes accessed | tf_op | source)
XLA Modules:
  0.0 153.3 jit_solution(16155490813039309973)
XLA Ops:
  0.6 0.0 copy-start.12
  0.6 0.0 copy-start.3
  0.7 0.8 copy-done.3
  1.5 0.8 copy-done.5
  2.3 0.7 copy-done.11
  3.0 1.2 pack.1
  4.2 7.1 %all-to-all-start = ((bf16[16,54,512]{2,1,0:T(8,128)(2,1)}), bf16[16,54,512]{2,1,0:T(8,128)(2,1)S(1)}, u32[]{:S(2)}, u32[]{:S(2)}) async-start(bf16[16,54,512]{2,1,0:T(8,128)(2,1)} %pack.1), calls=%async_computation | async-start | bytes 1835008 | tf_op jit(solution)/shard_map/all_to_all | solution.py:507
  11.3 0.6 collective-permute-start
  12.0 1.4 collective-permute-done.other
  13.4 2.0 %prep.1 = (bf16[3,8,8,32,128]{4,3,2,1,0:T(8,128)(2,1)S(1)}, bf16[3,8,8,32,128]{4,3,2,1,0:T(8,128)(2,1)S(1)}, bf16[3,8,8,32,128]{4,3,2,1,0:T(8,128)(2,1)S(1)}, f32[144,256]{1,0:T(8,128)S(1)}, f32[144,256]{1,0:T(8,128)S(1)}) custom-call(bf16[6,6,6,4,256]{4,3,2,1,0:T(4,128)(2,1)S(1)} %bitcast.5, bf16[6,6,6,4,256]{4,3,2,1,0:T(4,128)(2,1)S(1)} %collective-permute-done.other, ...), custom_call_target="tpu_custom_call" | custom-call | flops 2000000000 | bytes 8000000 | tf_op jit(solution)/shard_map/prep/pallas_call | solution.py:117
  15.4 1.2 copy-done.16
  16.5 1.1 copy-done.18
  17.7 1.2 copy-done.20
  18.8 4.8 %all-to-all-done.shards = bf16[16,54,512]{2,1,0:T(8,128)(2,1)S(1)} async-done(((bf16[16,54,512]{2,1,0:T(8,128)(2,1)}), bf16[16,54,512]{2,1,0:T(8,128)(2,1)S(1)}, u32[]{:S(2)}, u32[]{:S(2)}) %all-to-all-start) | async-done | bytes 884768 | tf_op jit(solution)/shard_map/all_to_all | solution.py:507
  23.6 2.2 %spread.1 = bf16[4,54,32,256]{3,2,1,0:T(8,128)(2,1)S(1)} custom-call(bf16[16,54,512]{2,1,0:T(8,128)(2,1)S(1)} %all-to-all-done.shards), custom_call_target="tpu_custom_call" | custom-call | flops 1000000 | bytes 5000000 | tf_op jit(solution)/shard_map/spread/pallas_call | solution.py:404
  25.8 29.6 %all_to_all.30.mine = bf16[4,54,32,256]{3,2,1,0:T(8,128)(2,1)S(1)} all-to-all(bf16[4,54,32,256]{3,2,1,0:T(8,128)(2,1)S(1)} %spread.1), channel_id=1, replica_groups={{0,2,4,6},{8,10,12,14},{16,18,20,22},{24,26,28,30},{32,34,36,38},{40,42..., dimensions={0} | all-to-all | bytes 7077888 | tf_op jit(solution)/shard_map/all_to_all | solution.py:507
  55.5 1.8 %collective-permute-start.1 = (bf16[4,54,32,256]{3,2,1,0:T(8,128)(2,1)S(1)}, bf16[4,54,32,256]{3,2,1,0:T(8,128)(2,1)S(1)}, u32[]{:S(2)}, u32[]{:S(2)}) collective-permute-start(bf16[4,54,32,256]{3,2,1,0:T(8,128)(2,1)S(1)} %all_to_all.30.mine), channel_id=1, source_target_pairs={{0,1},{1,0},{2,3},{3,2},{4,5},{5,4},{6,7},{7,6},{8,9},{9,8},{10,11... | collective-permute-start | bytes 10616840 | tf_op jit(solution)/shard_map/ppermute | solution.py:511
  57.2 5.8 %collective-permute-done.1.recv = bf16[4,54,32,256]{3,2,1,0:T(8,128)(2,1)S(1)} collective-permute-done((bf16[4,54,32,256]{3,2,1,0:T(8,128)(2,1)S(1)}, bf16[4,54,32,256]{3,2,1,0:T(8,128)(2,1)S(1)}, u32[]{:S(2)}, u32[]{:S(2)}) %collective-permute-start.1) | collective-permute-done | bytes 3538976 | tf_op jit(solution)/shard_map/ppermute | solution.py:511
  63.1 6.8 %conv1.1 = (f32[1152,256]{1,0:T(8,128)S(1)}, bf16[3,7,7,16,256]{4,3,2,1,0:T(8,128)(2,1)S(1)}, bf16[3,7,7,16,128]{4,3,2,1,0:T(8,128)(2,1)S(1)}) custom-call(s32[1]{0:T(128)} %bitcast.2.core_ref, bf16[3,8,8,32,128]{4,3,2,1,0:T(8,128)(2,1)S(1)} %copy-done.17, bf16[3,8,8,32,128]{4,3,2,1,0:T(8,128)(2,1)S(1)} %copy-done.19, ...), custom_call_target="tpu_custom_call" | custom-call | flops 4000000000 | bytes 10000000 | tf_op jit(solution)/shard_map/conv1/pallas_call | solution.py:204
  69.9 2.2 %conv2.1 = (bf16[3,3,3,4,256]{4,3,2,1,0:T(4,128)(2,1)}, bf16[144,256]{1,0:T(8,128)(2,1)S(1)}, bf16[256,144]{1,0:T(8,128)(2,1)S(1)}) custom-call(f32[144,256]{1,0:T(8,128)S(1)} %get-tuple-element.35.skip, f32[144,256]{1,0:T(8,128)S(1)} %get-tuple-element.36.cot, bf16[3,7,7,16,256]{4,3,2,1,0:T(8,128)(2,1)S(1)} %get-tuple-element.40.hsel, ...), custom_call_target="tpu_custom_call" | custom-call | flops 1500000000 | bytes 6000000 | tf_op jit(solution)/shard_map/conv2/pallas_call | solution.py:248
  72.1 2.6 %back.1.gat = bf16[256,1152]{1,0:T(8,128)(2,1)S(1)} custom-call(s32[1]{0:T(128)} %bitcast.2.core_ref, f32[1152,256]{1,0:T(8,128)S(1)} %get-tuple-element.42.act, bf16[144,256]{1,0:T(8,128)(2,1)S(1)} %get-tuple-element.43.grad_pre, bf16[4,54,32,256]{3,2,1,0:T(8,128)(2,1)S(1)} %all_to_all.30.mine, bf16[4,54,32,256]{3,2,1,0:T(8,128)(2,1)S(1)} %collective-permute-done.1.recv), custom_call_target="tpu_custom_call" | custom-call | flops 1500000000 | bytes 8000000 | tf_op jit(solution)/shard_map/back/pallas_call | solution.py:298
  74.7 0.4 collective-permute-start.2
  75.1 1.6 %collective-permute-done.2.gat_other = bf16[256,1152]{1,0:T(8,128)(2,1)S(1)} collective-permute-done((bf16[256,1152]{1,0:T(8,128)(2,1)S(1)}, bf16[256,1152]{1,0:T(8,128)(2,1)S(1)}, u32[]{:S(2)}, u32[]{:S(2)}) %collective-permute-start.2) | collective-permute-done | bytes 589856 | tf_op jit(solution)/shard_map/ppermute | solution.py:511
  76.8 10.6 %grad1.1 = bf16[4,27,32,256]{3,2,1,0:T(8,128)(2,1)S(1)} custom-call(bf16[256,1152]{1,0:T(8,128)(2,1)S(1)} %back.1.gat, bf16[256,1152]{1,0:T(8,128)(2,1)S(1)} %collective-permute-done.2.gat_other, bf16[3,8,8,32,128]{4,3,2,1,0:T(8,128)(2,1)S(1)} %copy-done.17, bf16[3,8,8,32,128]{4,3,2,1,0:T(8,128)(2,1)S(1)} %copy-done.21), custom_call_target="tpu_custom_call" | custom-call | flops 4000000000 | bytes 7000000 | tf_op jit(solution)/shard_map/grad1/pallas_call | solution.py:364
  87.4 1.2 copy-done.2
  88.7 3.6 %all-to-all-start.2 = ((bf16[4,27,32,256]{3,2,1,0:T(8,128)(2,1)}), bf16[4,27,32,256]{3,2,1,0:T(8,128)(2,1)S(1)}, u32[]{:S(2)}, u32[]{:S(2)}) async-start(bf16[4,27,32,256]{3,2,1,0:T(8,128)(2,1)} %copy-done.2), calls=%async_computation.2 | async-start | bytes 3538944 | tf_op jit(solution)/shard_map/all_to_all | solution.py:507
  92.2 0.4 collective-permute-start.4
  92.7 0.2 collective-permute-start.3
  92.8 1.7 %collective-permute-done.3.grad_t_other = bf16[256,144]{1,0:T(8,128)(2,1)S(1)} collective-permute-done((bf16[256,144]{1,0:T(8,128)(2,1)S(1)}, bf16[256,144]{1,0:T(8,128)(2,1)S(1)}, u32[]{:S(2)}, u32[]{:S(2)}) %collective-permute-start.3) | collective-permute-done | bytes 73760 | tf_op jit(solution)/shard_map/ppermute | solution.py:511
  94.5 0.0 collective-permute-done.4.hsel_other
  94.6 6.7 %grad2.1 = bf16[4,27,32,256]{3,2,1,0:T(8,128)(2,1)S(1)} custom-call(bf16[256,144]{1,0:T(8,128)(2,1)S(1)} %get-tuple-element.48.grad_t, bf16[256,144]{1,0:T(8,128)(2,1)S(1)} %collective-permute-done.3.grad_t_other, bf16[3,7,7,16,256]{4,3,2,1,0:T(8,128)(2,1)S(1)} %get-tuple-element.40.hsel, bf16[3,7,7,16,128]{4,3,2,1,0:T(8,128)(2,1)S(1)} %collective-permute-done.4.hsel_other), custom_call_target="tpu_custom_call" | custom-call | flops 1000000000 | bytes 4000000 | tf_op jit(solution)/shard_map/grad2/pallas_call | solution.py:346
  101.3 1.2 copy-done
  102.5 4.5 %all-to-all-done.2.parts = bf16[4,27,32,256]{3,2,1,0:T(8,128)(2,1)S(1)} async-done(((bf16[4,27,32,256]{3,2,1,0:T(8,128)(2,1)}), bf16[4,27,32,256]{3,2,1,0:T(8,128)(2,1)S(1)}, u32[]{:S(2)}, u32[]{:S(2)}) %all-to-all-start.2) | async-done | bytes 1769504 | tf_op jit(solution)/shard_map/all_to_all | solution.py:507
  107.0 3.6 %all-to-all-start.4 = ((bf16[4,27,32,256]{3,2,1,0:T(8,128)(2,1)}), bf16[4,27,32,256]{3,2,1,0:T(8,128)(2,1)S(1)}, u32[]{:S(2)}, u32[]{:S(2)}) async-start(bf16[4,27,32,256]{3,2,1,0:T(8,128)(2,1)} %copy-done), calls=%async_computation.4 | async-start | bytes 3538944 | tf_op jit(solution)/shard_map/all_to_all | solution.py:507
  110.5 0.8 collect.2
  111.4 0.8 copy-done.1
  112.2 13.1 %all-to-all-done.4.parts = bf16[4,27,32,256]{3,2,1,0:T(8,128)(2,1)S(1)} async-done(((bf16[4,27,32,256]{3,2,1,0:T(8,128)(2,1)}), bf16[4,27,32,256]{3,2,1,0:T(8,128)(2,1)S(1)}, u32[]{:S(2)}, u32[]{:S(2)}) %all-to-all-start.4) | async-done | bytes 1769504 | tf_op jit(solution)/shard_map/all_to_all | solution.py:507
  125.3 3.6 %all-to-all-start.3 = ((bf16[16,27,512]{2,1,0:T(8,128)(2,1)}), bf16[16,27,512]{2,1,0:T(8,128)(2,1)S(1)}, u32[]{:S(2)}, u32[]{:S(2)}) async-start(bf16[16,27,512]{2,1,0:T(8,128)(2,1)} %copy-done.1), calls=%async_computation.3 | async-start | bytes 1048576 | tf_op jit(solution)/shard_map/all_to_all | solution.py:507
  128.8 0.0 copy-start.4
  128.9 0.0 copy-start.7
  128.9 0.0 copy-start.8
  128.9 0.0 copy-start.6
  128.9 1.7 %collect.3 = bf16[16,27,512]{2,1,0:T(8,128)(2,1)} custom-call(bf16[4,27,32,256]{3,2,1,0:T(8,128)(2,1)S(1)} %all-to-all-done.4.parts), custom_call_target="tpu_custom_call" | custom-call | flops 1000000 | bytes 3000000 | tf_op jit(solution)/shard_map/collect/pallas_call | solution.py:426
  130.6 8.3 %all-to-all-done.3.parts = bf16[16,27,512]{2,1,0:T(8,128)(2,1)S(1)} async-done(((bf16[16,27,512]{2,1,0:T(8,128)(2,1)}), bf16[16,27,512]{2,1,0:T(8,128)(2,1)S(1)}, u32[]{:S(2)}, u32[]{:S(2)}) %all-to-all-start.3) | async-done | bytes 442400 | tf_op jit(solution)/shard_map/all_to_all | solution.py:507
  138.9 3.6 %all-to-all-start.5 = ((bf16[16,27,512]{2,1,0:T(8,128)(2,1)}), bf16[16,27,512]{2,1,0:T(8,128)(2,1)S(1)}, u32[]{:S(2)}, u32[]{:S(2)}) async-start(bf16[16,27,512]{2,1,0:T(8,128)(2,1)} %collect.3), calls=%async_computation.5 | async-start | bytes 1048576 | tf_op jit(solution)/shard_map/all_to_all | solution.py:507
  142.5 1.3 adam.2
  143.8 8.8 %all-to-all-done.5.parts = bf16[16,27,512]{2,1,0:T(8,128)(2,1)S(1)} async-done(((bf16[16,27,512]{2,1,0:T(8,128)(2,1)}), bf16[16,27,512]{2,1,0:T(8,128)(2,1)S(1)}, u32[]{:S(2)}, u32[]{:S(2)}) %all-to-all-start.5) | async-done | bytes 442400 | tf_op jit(solution)/shard_map/all_to_all | solution.py:507
  152.6 0.8 adam.3
  (32 shorter events, 0.1 us)
Async XLA Ops:
  0.6 11.3 %copy-start.12 = (s32[1,256]{1,0:T(1,128)S(1)}, s32[1,256]{1,0:T(1,128)}, u32[]{:S(2)}) copy-start(s32[1,256]{1,0:T(1,128)} %constant.24.order) | copy-start | bytes 3076
  0.6 0.8 copy-start.3
  1.5 0.8 copy-start.5
  2.3 0.7 copy-start.11
  3.0 8.3 %copy-start.14 = (bf16[4,6,6,6,256]{4,0,3,2,1:T(4,128)(2,1)S(1)}, bf16[4,6,6,6,256]{4,0,3,2,1:T(4,128)(2,1)}, u32[]{:S(2)}) copy-start(bf16[4,6,6,6,256]{4,0,3,2,1:T(4,128)(2,1)} %param.9) | copy-start | bytes 1327108
  3.0 9.0 %copy-start.22 = (s32[1,256]{1,0:T(1,128)S(1)}, s32[1,256]{1,0:T(1,128)}, u32[]{:S(2)}) copy-start(s32[1,256]{1,0:T(1,128)} %constant.26) | copy-start | bytes 3076
  3.0 10.4 %copy-start.15 = (bf16[4,3,3,3,256]{4,0,3,2,1:T(4,128)(2,1)S(1)}, bf16[4,3,3,3,256]{4,0,3,2,1:T(4,128)(2,1)}, u32[]{:S(2)}) copy-start(bf16[4,3,3,3,256]{4,0,3,2,1:T(4,128)(2,1)} %param.10) | copy-start | bytes 165892
  4.2 19.4 %all-to-all-start = ((bf16[16,54,512]{2,1,0:T(8,128)(2,1)}), bf16[16,54,512]{2,1,0:T(8,128)(2,1)S(1)}, u32[]{:S(2)}, u32[]{:S(2)}) async-start(bf16[16,54,512]{2,1,0:T(8,128)(2,1)} %pack.1), calls=%async_computation | async-start | bytes 1835008 | tf_op jit(solution)/shard_map/all_to_all | solution.py:507
  11.3 2.1 %collective-permute-start = (bf16[6,6,6,4,256]{4,3,2,1,0:T(4,128)(2,1)S(1)}, bf16[6,6,6,4,256]{4,3,2,1,0:T(4,128)(2,1)S(1)}, u32[]{:S(2)}, u32[]{:S(2)}) collective-permute-start(bf16[6,6,6,4,256]{4,3,2,1,0:T(4,128)(2,1)S(1)} %bitcast.4), channel_id=1, source_target_pairs={{0,1},{1,0},{2,3},{3,2},{4,5},{5,4},{6,7},{7,6},{8,9},{9,8},{10,11... | collective-permute-start | bytes 1327112 | tf_op jit(solution)/shard_map/ppermute | solution.py:511
  15.4 1.2 copy-start.16
  16.5 1.1 copy-start.18
  17.7 1.2 copy-start.20
  25.8 37.3 %copy-start.17 = (bf16[3,8,8,32,128]{4,3,2,1,0:T(8,128)(2,1)S(1)}, bf16[3,8,8,32,128]{4,3,2,1,0:T(8,128)(2,1)}, u32[]{:S(2)}) copy-start(bf16[3,8,8,32,128]{4,3,2,1,0:T(8,128)(2,1)} %copy-done.16) | copy-start | bytes 4718596
  25.8 37.3 %copy-start.19 = (bf16[3,8,8,32,128]{4,3,2,1,0:T(8,128)(2,1)S(1)}, bf16[3,8,8,32,128]{4,3,2,1,0:T(8,128)(2,1)}, u32[]{:S(2)}) copy-start(bf16[3,8,8,32,128]{4,3,2,1,0:T(8,128)(2,1)} %copy-done.18) | copy-start | bytes 4718596
  55.5 7.6 %collective-permute-start.1 = (bf16[4,54,32,256]{3,2,1,0:T(8,128)(2,1)S(1)}, bf16[4,54,32,256]{3,2,1,0:T(8,128)(2,1)S(1)}, u32[]{:S(2)}, u32[]{:S(2)}) collective-permute-start(bf16[4,54,32,256]{3,2,1,0:T(8,128)(2,1)S(1)} %all_to_all.30.mine), channel_id=1, source_target_pairs={{0,1},{1,0},{2,3},{3,2},{4,5},{5,4},{6,7},{7,6},{8,9},{9,8},{10,11... | collective-permute-start | bytes 10616840 | tf_op jit(solution)/shard_map/ppermute | solution.py:511
  69.9 4.8 %copy-start.13 = (bf16[3,7,7,16,128]{4,3,2,1,0:T(8,128)(2,1)}, bf16[3,7,7,16,128]{4,3,2,1,0:T(8,128)(2,1)S(1)}, u32[]{:S(2)}) copy-start(bf16[3,7,7,16,128]{4,3,2,1,0:T(8,128)(2,1)S(1)} %get-tuple-element.49) | copy-start | bytes 1806340
  72.1 4.7 %copy-start.21 = (bf16[3,8,8,32,128]{4,3,2,1,0:T(8,128)(2,1)S(1)}, bf16[3,8,8,32,128]{4,3,2,1,0:T(8,128)(2,1)}, u32[]{:S(2)}) copy-start(bf16[3,8,8,32,128]{4,3,2,1,0:T(8,128)(2,1)} %copy-done.20) | copy-start | bytes 4718596
  74.7 2.1 %collective-permute-start.2 = (bf16[256,1152]{1,0:T(8,128)(2,1)S(1)}, bf16[256,1152]{1,0:T(8,128)(2,1)S(1)}, u32[]{:S(2)}, u32[]{:S(2)}) collective-permute-start(bf16[256,1152]{1,0:T(8,128)(2,1)S(1)} %back.1.gat), channel_id=1, source_target_pairs={{0,1},{1,0},{2,3},{3,2},{4,5},{5,4},{6,7},{7,6},{8,9},{9,8},{10,11... | collective-permute-start | bytes 1769480 | tf_op jit(solution)/shard_map/ppermute | solution.py:511
  87.4 1.2 copy-start.2
  88.7 18.3 %all-to-all-start.2 = ((bf16[4,27,32,256]{3,2,1,0:T(8,128)(2,1)}), bf16[4,27,32,256]{3,2,1,0:T(8,128)(2,1)S(1)}, u32[]{:S(2)}, u32[]{:S(2)}) async-start(bf16[4,27,32,256]{3,2,1,0:T(8,128)(2,1)} %copy-done.2), calls=%async_computation.2 | async-start | bytes 3538944 | tf_op jit(solution)/shard_map/all_to_all | solution.py:507
  92.2 2.3 %collective-permute-start.4 = (bf16[3,7,7,16,128]{4,3,2,1,0:T(8,128)(2,1)}, bf16[3,7,7,16,128]{4,3,2,1,0:T(8,128)(2,1)S(1)}, u32[]{:S(2)}, u32[]{:S(2)}) collective-permute-start(bf16[3,7,7,16,128]{4,3,2,1,0:T(8,128)(2,1)} %copy-done.13), channel_id=1, source_target_pairs={{0,1},{1,0},{2,3},{3,2},{4,5},{5,4},{6,7},{7,6},{8,9},{9,8},{10,11... | collective-permute-start | bytes 1806344 | tf_op jit(solution)/shard_map/ppermute | solution.py:511
  92.7 1.9 %collective-permute-start.3 = (bf16[256,144]{1,0:T(8,128)(2,1)S(1)}, bf16[256,144]{1,0:T(8,128)(2,1)S(1)}, u32[]{:S(2)}, u32[]{:S(2)}) collective-permute-start(bf16[256,144]{1,0:T(8,128)(2,1)S(1)} %get-tuple-element.48.grad_t), channel_id=1, source_target_pairs={{0,1},{1,0},{2,3},{3,2},{4,5},{5,4},{6,7},{7,6},{8,9},{9,8},{10,11... | collective-permute-start | bytes 221192 | tf_op jit(solution)/shard_map/ppermute | solution.py:511
  101.3 1.2 copy-start
  107.0 18.3 %all-to-all-start.4 = ((bf16[4,27,32,256]{3,2,1,0:T(8,128)(2,1)}), bf16[4,27,32,256]{3,2,1,0:T(8,128)(2,1)S(1)}, u32[]{:S(2)}, u32[]{:S(2)}) async-start(bf16[4,27,32,256]{3,2,1,0:T(8,128)(2,1)} %copy-done), calls=%async_computation.4 | async-start | bytes 3538944 | tf_op jit(solution)/shard_map/all_to_all | solution.py:507
  111.4 0.8 copy-start.1
  125.3 13.6 %all-to-all-start.3 = ((bf16[16,27,512]{2,1,0:T(8,128)(2,1)}), bf16[16,27,512]{2,1,0:T(8,128)(2,1)S(1)}, u32[]{:S(2)}, u32[]{:S(2)}) async-start(bf16[16,27,512]{2,1,0:T(8,128)(2,1)} %copy-done.1), calls=%async_computation.3 | async-start | bytes 1048576 | tf_op jit(solution)/shard_map/all_to_all | solution.py:507
  128.8 13.6 %copy-start.4 = (f32[27,512]{1,0:T(8,128)S(1)}, f32[27,512]{1,0:T(8,128)}, u32[]{:S(2)}) copy-start(f32[27,512]{1,0:T(8,128)} %k.2) | copy-start | bytes 165892
  128.9 13.6 %copy-start.7 = (f32[27,512]{1,0:T(8,128)S(1)}, f32[27,512]{1,0:T(8,128)}, u32[]{:S(2)}) copy-start(f32[27,512]{1,0:T(8,128)} %m.2) | copy-start | bytes 165892
  128.9 13.6 %copy-start.8 = (f32[27,512]{1,0:T(8,128)S(1)}, f32[27,512]{1,0:T(8,128)}, u32[]{:S(2)}) copy-start(f32[27,512]{1,0:T(8,128)} %v.2) | copy-start | bytes 165892
  128.9 23.7 %copy-start.6 = (f32[27,512]{1,0:T(8,128)S(1)}, f32[27,512]{1,0:T(8,128)}, u32[]{:S(2)}) copy-start(f32[27,512]{1,0:T(8,128)} %k.3) | copy-start | bytes 165892
  128.9 23.7 %copy-start.9 = (f32[27,512]{1,0:T(8,128)S(1)}, f32[27,512]{1,0:T(8,128)}, u32[]{:S(2)}) copy-start(f32[27,512]{1,0:T(8,128)} %m.3) | copy-start | bytes 165892
  128.9 23.6 %copy-start.10 = (f32[27,512]{1,0:T(8,128)S(1)}, f32[27,512]{1,0:T(8,128)}, u32[]{:S(2)}) copy-start(f32[27,512]{1,0:T(8,128)} %v.3) | copy-start | bytes 165892
  138.9 13.6 %all-to-all-start.5 = ((bf16[16,27,512]{2,1,0:T(8,128)(2,1)}), bf16[16,27,512]{2,1,0:T(8,128)(2,1)S(1)}, u32[]{:S(2)}, u32[]{:S(2)}) async-start(bf16[16,27,512]{2,1,0:T(8,128)(2,1)} %collect.3), calls=%async_computation.5 | async-start | bytes 1048576 | tf_op jit(solution)/shard_map/all_to_all | solution.py:507

commit v3 on v2

--- a/solution.py
+++ b/solution.py
@@ -23,6 +23,9 @@
 MIB = 1024 * 1024
 BF = jnp.bfloat16
 F32 = jnp.float32
+
+MEMBERS = 8
+BLOCK = 16
 
 VM = pl.BlockSpec(memory_space=pltpu.VMEM)
 SM = pl.BlockSpec(memory_space=pltpu.SMEM)
@@ -131,54 +134,57 @@
     return (cell >= 1) & (cell <= EDGE)
 
 
-def fetch_weights(mine, recv, first, weights, sems):
+def fetch_weights(source, first, weights, sems):
     copies = []
     for di in range(3):
-        for half, source in enumerate((mine, recv)):
-            copies.append(
-                pltpu.make_async_copy(
-                    source.at[:, pl.ds(first + 9 * di, 9)],
-                    weights.at[half, :, pl.ds(9 * di, 9)],
-                    sems.at[2 * di + half],
-                )
+        copies.append(
+            pltpu.make_async_copy(
+                source.at[:, pl.ds(first + 9 * di, 9)],
+                weights.at[:, pl.ds(9 * di, 9)],
+                sems.at[di],
             )
-            copies[-1].start()
+        )
+        copies[-1].start()
     return copies
 
 
-def weight(weights, t):
-    return jnp.concatenate([weights[half, :, t].reshape(HALF, C) for half in range(2)], axis=0)
-
-
-WEIGHTS = [pltpu.VMEM((2, 4, TAPS, ROWS, C), BF), pltpu.SemaphoreType.DMA((6,))]
-
-
-def conv1_kernel(core_ref, x3a, x3b, mine, recv, act, hsel, hsend, weights, sems, hs):
+def half_weight(weights, t):
+    return weights[:, t].reshape(HALF, C)
+
+
+HALF_WEIGHTS = [pltpu.VMEM((MEMBERS, TAPS, BLOCK, C), BF), pltpu.SemaphoreType.DMA((3,))]
+WEIGHTS = HALF_WEIGHTS + HALF_WEIGHTS
+
+
+def half_conv(x3, weights, copies, act, start):
+    for di in range(3):
+        copies[di].wait()
+        taps = range(9 * di, 9 * di + 9)
+        windows = [
+            x3[t % 3, di : di + EDGE, t // 3 % 3 : t // 3 % 3 + EDGE].reshape(ACT_ROWS, HALF)
+            for t in taps
+        ]
+        total = dot(
+            jnp.concatenate(windows, axis=1),
+            jnp.concatenate([half_weight(weights, t) for t in taps], axis=0),
+        )
+        act[...] = (start if di == 0 else act)[...] + total if start is not None or di else total
+
+
+def conv1_own_kernel(x3a, mine, act, weights, sems):
+    half_conv(x3a, weights, fetch_weights(mine, 0, weights, sems), act, None)
+
+
+def conv1_own(x3a, mine):
+    return call(
+        conv1_own_kernel, "conv1_own", shape((ACT_ROWS, C), F32), [VM, ANY], HALF_WEIGHTS,
+        12, 2_000_000_000, 5_000_000,
+    )(x3a, mine)
+
+
+def conv1_kernel(core_ref, x3b, recv, part_act, act, hsel, hsend, weights, sems, hs):
     core = core_ref[0]
-    copies = fetch_weights(mine, recv, 0, weights, sems)
-    for di in range(3):
-        copies[2 * di].wait()
-        copies[2 * di + 1].wait()
-
-        def step(dj, carry):
-            total = None
-            for dl in range(3):
-                window = jnp.concatenate(
-                    [
-                        half[dl, pl.ds(di, EDGE), pl.ds(dj, EDGE)].reshape(ACT_ROWS, HALF)
-                        for half in (x3a, x3b)
-                    ],
-                    axis=1,
-                )
-                term = dot(window, weight(weights, di * 9 + dj * 3 + dl))
-                total = term if total is None else total + term
-            if di == 0:
-                act[...] = jnp.where(dj == 0, 0.0, act[...]) + total
-            else:
-                act[...] += total
-            return carry
-
-        lax.fori_loop(0, 3, step, 0)
+    half_conv(x3b, weights, fetch_weights(recv, 0, weights, sems), act, part_act)
 
     hsel[:, 0] = jnp.zeros_like(hsel[:, 0])
     hsel[:, :, 0] = jnp.zeros_like(hsel[:, :, 0])
@@ -200,7 +206,7 @@
             hsend[dl, i + 1, 1:] = rows[..., HALF:]
 
 
-def conv1(core, x3a, x3b, mine, recv):
+def conv1(core, x3b, recv, part_act):
     return call(
         conv1_kernel, "conv1",
         (
@@ -208,10 +214,14 @@
             shape((3, 7, 7, OUT_ROWS, C), BF),
             shape((3, 7, 7, OUT_ROWS, HALF), BF),
         ),
-        [SM, VM, VM, ANY, ANY],
-        WEIGHTS + [pltpu.VMEM((2, ACT_ROWS + 8, HALF), F32)],
-        24, 4_000_000_000, 10_000_000,
-    )(core, x3a, x3b, mine, recv)
+        [SM, VM, ANY, VM],
+        HALF_WEIGHTS + [pltpu.VMEM((2, ACT_ROWS + 8, HALF), F32)],
+        24, 2_000_000_000, 7_000_000,
+    )(core, x3b, recv, part_act)
+
+
+def weight(wa, wb, t):
+    return jnp.concatenate([half_weight(wa, t), half_weight(wb, t)], axis=0)
 
 
 def strided_window(hsel, dl, di, dj, lanes=slice(None)):
@@ -221,16 +231,16 @@
     return jnp.concatenate(blocks, axis=0)
 
 
-def conv2_kernel(skip, cot, hsel, mine, recv, block_out, grad_pre, grad_pre_t, weights, sems, bo):
-    copies = fetch_weights(mine, recv, TAPS, weights, sems)
+def conv2_kernel(skip, cot, hsel, mine, recv, block_out, grad_pre, grad_pre_t, wa, sa, wb, sb, bo):
+    halves = (fetch_weights(mine, TAPS, wa, sa), fetch_weights(recv, TAPS, wb, sb))
     pre = skip[...]
     for di in range(3):
-        copies[2 * di].wait()
-        copies[2 * di + 1].wait()
+        for copies in halves:
+            copies[di].wait()
         for dj in range(3):
             for dl in range(3):
                 pre = pre + dot(
-                    strided_window(hsel, dl, di, dj), weight(weights, di * 9 + dj * 3 + dl)
+                    strided_window(hsel, dl, di, dj), weight(wa, wb, di * 9 + dj * 3 + dl)
                 )
     sigma = sigmoid(pre)
     store(bo, 0, PRE_ROWS, pre * sigma)
@@ -258,17 +268,17 @@
     )(skip, cot, hsel, mine, recv)
 
 
-def back_kernel(core_ref, act, grad_pre, mine, recv, gat, weights, sems, y, gh):
+def back_kernel(core_ref, act, grad_pre, mine, recv, gat, wa, sa, wb, sb, y, gh):
     core = core_ref[0]
-    copies = fetch_weights(mine, recv, TAPS, weights, sems)
+    halves = (fetch_weights(mine, TAPS, wa, sa), fetch_weights(recv, TAPS, wb, sb))
     y[...] = jnp.zeros_like(y)
     grad = grad_pre[...]
     for di in range(3):
-        copies[2 * di].wait()
-        copies[2 * di + 1].wait()
+        for copies in halves:
+            copies[di].wait()
         for dj in range(3):
             for dl in range(3):
-                term = dot_t(grad, weight(weights, di * 9 + dj * 3 + dl))
+                term = dot_t(grad, weight(wa, wb, di * 9 + dj * 3 + dl))
                 term = term.reshape(9, OUT_ROWS, C)
                 for qi in range(OUTER):
                     for qj in range(OUTER):
@@ -307,7 +317,7 @@
     )(core, act, grad_pre, mine, recv)
 
 
-def grad_loop(out, lefts, windows):
+def grad_loop(out, lefts, windows, unroll):
     eye = (
         lax.broadcasted_iota(jnp.int32, (C, C), 0) == lax.broadcasted_iota(jnp.int32, (C, C), 1)
     ).astype(BF)
@@ -321,14 +331,18 @@
         width = HALF * len(taps)
         turned = dot_t(eye[:width, :width], total.astype(BF)).astype(BF)
         for n, t in enumerate(taps):
-            out[:, t] = turned[n * HALF : (n + 1) * HALF].reshape(4, ROWS, C)
+            out[:, t] = turned[n * HALF : (n + 1) * HALF].reshape(MEMBERS, BLOCK, C)
 
     def step(n, carry):
-        product((2 * n, 2 * n + 1))
+        for k in range(0, unroll, 2):
+            product((unroll * n + k, unroll * n + k + 1))
         return carry
 
-    lax.fori_loop(0, TAPS // 2, step, 0)
-    product((TAPS - 1,))
+    whole = TAPS // unroll
+    if whole > 1:
+        lax.fori_loop(0, whole, step, 0)
+    for t in range(unroll * whole if whole > 1 else 0, TAPS, 2):
+        product(tuple(range(t, min(t + 2, TAPS))))
 
 
 def grad2_kernel(grad_t, grad_t_other, hsel, hsel_other, out):
@@ -339,12 +353,13 @@
             lambda di, dj, dl: strided_window(hsel, dl, di, dj, slice(0, HALF)),
             lambda di, dj, dl: strided_window(hsel_other, dl, di, dj),
         ),
+        TAPS,
     )
 
 
 def grad2(grad_t, grad_t_other, hsel, hsel_other):
     return call(
-        grad2_kernel, "grad2", shape((4, TAPS, ROWS, C), BF), [VM] * 4, [],
+        grad2_kernel, "grad2", shape((MEMBERS, TAPS, BLOCK, C), BF), [VM] * 4, [],
         8, 1_000_000_000, 4_000_000,
     )(grad_t, grad_t_other, hsel, hsel_other)
 
@@ -357,43 +372,45 @@
 
 
 def grad1_kernel(gat, gat_other, x3a, x3o, out):
-    grad_loop(out, (gat, gat_other), (same_window(x3a), same_window(x3o)))
+    grad_loop(out, (gat, gat_other), (same_window(x3a), same_window(x3o)), 2)
 
 
 def grad1(gat, gat_other, x3a, x3o):
     return call(
-        grad1_kernel, "grad1", shape((4, TAPS, ROWS, C), BF), [VM] * 4, [],
+        grad1_kernel, "grad1", shape((MEMBERS, TAPS, BLOCK, C), BF), [VM] * 4, [],
         12, 4_000_000_000, 7_000_000,
     )(gat, gat_other, x3a, x3o)
 
 
-def pack_kernel(first, second, order, out, flat):
+def pack_kernel(first, second, order, out):
     perm = one_hot(order[...])
     for i in range(2):
         lanes = slice(i * C, (i + 1) * C)
-        flat[:TAPS, lanes] = dot(first[:, lanes].astype(BF), perm)
-        flat[TAPS:, lanes] = second[:, lanes].astype(BF).astype(F32)
-    shard = flat[...].astype(BF)
-    for n in range(16):
-        out[n] = shard
+        one = dot(first[:, lanes].astype(BF), perm).astype(BF)
+        two = second[:, lanes].astype(BF)
+        for n in range(MEMBERS):
+            out[n, 0, :, lanes] = one
+            out[n, 1, :, lanes] = two
 
 
 def pack(first, second, order):
     return call(
-        pack_kernel, "pack", shape((16, 2 * TAPS, 2 * C), BF), [VM] * 3,
-        [pltpu.VMEM((2 * TAPS, 2 * C), F32)], 4, 10_000_000, 1_000_000,
+        pack_kernel, "pack", shape((MEMBERS, 2, TAPS, 2 * C), BF), [VM] * 3,
+        [], 56, 10_000_000, 1_000_000,
     )(first, second, order)
 
 
 def spread_kernel(shards, out, wide):
-    for m in range(16):
-        rows = shards[m].astype(F32)
-        for i in range(2):
-            store(wide, 2 * m + i, 2 * TAPS, rows[:, i * C : (i + 1) * C], ROWS)
+    for m in range(MEMBERS):
+        for k in range(2):
+            rows = shards[m, k].astype(F32)
+            for i in range(2):
+                start = k * TAPS * BLOCK + 2 * m + i
+                store(wide, start, TAPS, rows[:, i * C : (i + 1) * C], BLOCK)
 
     def step(t, carry):
-        value = load(wide, pl.multiple_of(t * ROWS, ROWS), ROWS).astype(BF)
-        for n in range(4):
+        value = load(wide, pl.multiple_of(t * BLOCK, BLOCK), BLOCK).astype(BF)
+        for n in range(MEMBERS):
             out[n, t] = value
         return carry
 
@@ -402,31 +419,54 @@
 
 def spread(shards):
     return call(
-        spread_kernel, "spread", shape((4, 2 * TAPS, ROWS, C), BF), [VM],
-        [pltpu.VMEM((2, 2 * TAPS * ROWS, HALF), F32)], 10, 1_000_000, 5_000_000,
+        spread_kernel, "spread", shape((MEMBERS, 2 * TAPS, BLOCK, C), BF), [VM],
+        [pltpu.VMEM((2, 2 * TAPS * BLOCK, HALF), F32)], 10, 1_000_000, 5_000_000,
     )(shards)
 
 
-def collect_kernel(parts, out, wide):
+def collect_one(parts, wide, write):
     def step(t, carry):
         total = parts[0, t].astype(F32)
-        for n in range(1, 4):
+        for n in range(1, MEMBERS):
             total = total + parts[n, t].astype(F32)
-        store(wide, pl.multiple_of(t * ROWS, ROWS), ROWS, total)
+        store(wide, pl.multiple_of(t * BLOCK, BLOCK), BLOCK, total)
         return carry
 
     lax.fori_loop(0, TAPS, step, 0)
-    for m in range(16):
+    for m in range(MEMBERS):
         for i in range(2):
-            rows = load(wide, 2 * m + i, TAPS, ROWS)
-            out[m, :, i * C : (i + 1) * C] = rows.astype(BF)
-
-
-def collect(parts):
-    return call(
-        collect_kernel, "collect", shape((16, TAPS, 2 * C), BF), [VM],
-        [pltpu.VMEM((2, TAPS * ROWS, HALF), F32)], 6, 1_000_000, 3_000_000,
+            rows = load(wide, 2 * m + i, TAPS, BLOCK).astype(BF)
+            write(m, slice(i * C, (i + 1) * C), rows)
+
+
+def collect2_kernel(parts, out, wide):
+    def write(m, lanes, rows):
+        out[m, :, lanes] = rows
+
+    collect_one(parts, wide, write)
+
+
+def collect2(parts):
+    return call(
+        collect2_kernel, "collect2", shape((MEMBERS, TAPS, 2 * C), BF), [VM],
+        [pltpu.VMEM((2, TAPS * BLOCK, HALF), F32)], 6, 1_000_000, 3_000_000,
     )(parts)
+
+
+def collect_kernel(parts, second, out, wide):
+    def write(m, lanes, rows):
+        out[m, 0, :, lanes] = rows
+
+    for m in range(MEMBERS):
+        out[m, 1] = second[m]
+    collect_one(parts, wide, write)
+
+
+def collect(parts, second):
+    return call(
+        collect_kernel, "collect", shape((MEMBERS, 2, TAPS, 2 * C), BF), [VM] * 2,
+        [pltpu.VMEM((2, TAPS * BLOCK, HALF), F32)], 8, 1_000_000, 3_000_000,
+    )(parts, second)
 
 
 def adam_update(weight, first, second, grad):
@@ -440,67 +480,75 @@
     return (weight_new, first_new, second_new)
 
 
-def adam_kernel(scale, turn_back, parts, order, k, m, v, kn, mn, vn):
-    total = parts[0].astype(F32)
-    for n in range(1, 16):
-        total = total + parts[n].astype(F32)
-    total = total * scale
+def adam_kernel(
+    scale, parts, order, k1, m1, v1, k2, m2, v2, k1n, m1n, v1n, k2n, m2n, v2n
+):
     back = one_hot(order[...]).astype(F32)
+    state = ((k1, m1, v1, k1n, m1n, v1n), (k2, m2, v2, k2n, m2n, v2n))
     for i in range(2):
         lanes = slice(i * C, (i + 1) * C)
-        grad = total[:, lanes]
-        if turn_back:
-            grad = lax.dot_general(
-                grad,
-                back,
-                (((1,), (1,)), ((), ())),
-                precision=lax.Precision.HIGHEST,
-                preferred_element_type=F32,
+        for which, (k, m, v, kn, mn, vn) in enumerate(state):
+            grad = parts[0, which, :, lanes].astype(F32)
+            for n in range(1, MEMBERS):
+                grad = grad + parts[n, which, :, lanes].astype(F32)
+            grad = grad * scale
+            if which == 0:
+                grad = lax.dot_general(
+                    grad,
+                    back,
+                    (((1,), (1,)), ((), ())),
+                    precision=lax.Precision.HIGHEST,
+                    preferred_element_type=F32,
+                )
+            kn[:, lanes], mn[:, lanes], vn[:, lanes] = adam_update(
+                k[:, lanes], m[:, lanes], v[:, lanes], grad
             )
-        kn[:, lanes], mn[:, lanes], vn[:, lanes] = adam_update(
-            k[:, lanes], m[:, lanes], v[:, lanes], grad
-        )
-
-
-def adam(scale, turn_back, parts, order, *state):
-    return call(
-        functools.partial(adam_kernel, scale, turn_back), "adam",
-        (shape((TAPS, 2 * C), F32),) * 3, [VM] * 5, [], 6, 10_000_000, 1_000_000,
+
+
+def adam(scale, parts, order, *state):
+    return call(
+        functools.partial(adam_kernel, scale), "adam",
+        (shape((TAPS, 2 * C), F32),) * 6, [VM] * 8, [], 6, 10_000_000, 1_000_000,
     )(parts, order, *state)
 
 
 def place(x, y, z, c):
     return ((x * 4 + y) * 4 + z) * 2 + c
+
+
+LINE = [[0, 1, 2, 3]]
+ONE = [[0], [1], [2], [3]]
+EVEN_PAIRS = [[0, 1], [2, 3]]
+ODD_PAIRS = [[1, 2], [3, 0]]
+FAR_PAIRS = [[0, 2], [1, 3]]
+
+
+def groups(c, xs, ys, zs):
+    return [
+        [place(x, y, z, c) for x in gx for y in gy for z in gz]
+        for gx, gy, gz in itertools.product(xs, ys, zs)
+    ]
+
+
+NEAR = groups(0, LINE, EVEN_PAIRS, ONE) + groups(1, ONE, ODD_PAIRS, LINE)
+FAR = groups(0, ONE, FAR_PAIRS, LINE) + groups(1, LINE, FAR_PAIRS, ONE)
+PARTNERS = [(n, n ^ 1) for n in range(128)]
 
 
 def channel_orders():
     orders = []
     for c in range(2):
+        near = next(group for group in NEAR if group[0] % 2 == c)
         order = []
-        for a, b, d in itertools.product(range(4), repeat=3):
-            x, y, z = (b, d, a) if c == 0 else (a, b, d)
-            order += [2 * place(x, y, z, c), 2 * place(x, y, z, c) + 1]
+        for member in near:
+            far = next(group for group in FAR if member in group)
+            order += [2 * device + i for device in far for i in range(2)]
         orders.append(order)
     zero, one = orders
     return np.array([zero + one, one + zero], np.int32).reshape(2, 1, C)
 
 
-def lines(c, axes):
-    rest = [a for a in "xyz" if a not in axes]
-    groups = []
-    for fixed in itertools.product(range(4), repeat=len(rest)):
-        group = []
-        for moving in itertools.product(range(4), repeat=len(axes)):
-            at = dict(zip(rest, fixed)) | dict(zip(axes, moving))
-            group.append(place(at["x"], at["y"], at["z"], c))
-        groups.append(group)
-    return groups
-
-
 ORDERS = channel_orders()
-PLANES = lines(0, "xy") + lines(1, "yz")
-LINES = lines(0, "z") + lines(1, "x")
-PARTNERS = [(n, n ^ 1) for n in range(128)]
 
 
 def exchange(value, groups):
@@ -522,22 +570,22 @@
     shards = pack(k1, k2, fixed)
     latent = latent.transpose(1, 2, 3, 0, 4)
     cells = prep(latent, swap(latent), out_grad.transpose(1, 2, 3, 0, 4), own)
-    shards, cells = lax.optimization_barrier((exchange(shards, PLANES), cells))
+    shards, cells = lax.optimization_barrier((exchange(shards, FAR), cells))
     x3a, x3b, x3o, skip, cot = cells
-    mine = exchange(spread(shards), LINES)
+    mine = exchange(spread(shards), NEAR)
     recv = swap(mine)
 
-    act, hsel, hsend = conv1(core, x3a, x3b, mine, recv)
+    act, hsel, hsend = conv1(core, x3b, recv, conv1_own(x3a, mine))
     hsel_other = swap(hsend)
     block_out, grad_pre, grad_pre_t = conv2(skip, cot, hsel, mine, recv)
-    grad_pre_t_other = swap(grad_pre_t)
+    second = grad2(grad_pre_t, swap(grad_pre_t), hsel, hsel_other)
+    second, grad_pre = lax.optimization_barrier((second, grad_pre))
+    parts2 = exchange(second, NEAR)
     gat = back(core, act, grad_pre, mine, recv)
-    gat_other = swap(gat)
-    parts2 = exchange(grad2(grad_pre_t, grad_pre_t_other, hsel, hsel_other), LINES)
-    parts1 = exchange(grad1(gat, gat_other, x3a, x3o), LINES)
-    new_two = adam(scale, False, exchange(collect(parts2), PLANES), fixed, k2, m2, v2)
-    new_one = adam(scale, True, exchange(collect(parts1), PLANES), fixed, k1, m1, v1)
-    return (block_out.transpose(3, 0, 1, 2, 4), *new_one, *new_two)
+    parts1 = exchange(grad1(gat, swap(gat), x3a, x3o), NEAR)
+    parts = exchange(collect(parts1, collect2(parts2)), FAR)
+    new = adam(scale, parts, fixed, k1, m1, v1, k2, m2, v2)
+    return (block_out.transpose(3, 0, 1, 2, 4), *new)
 
 
 def solution(mesh):

time: 156 us -> 139 us (0.89); the launches traced: 153 us -> 138 us
  waiting for transfers between devices: 50 us -> 22.9 us
  blocking collectives: 29.6 us -> 42.8 us
  starting transfers between devices: 24.9 us -> 19.3 us
  local copies, waits for them, and re-layouts: 9.09 us -> 13.2 us
    all_to_all x5 -> x3, waiting for transfers between devices: 39.4 us -> 18.5 us  [exchange(): lax.all_to_all(value, 'dp', 0, 0, axis_index_groups=groups, tiled=True)]
    all_to_all x1 -> x2, blocking collectives: 29.6 us -> 42.8 us  [exchange(): lax.all_to_all(value, 'dp', 0, 0, axis_index_groups=groups, tiled=True)]
    ppermute x5, waiting for transfers between devices: 10.6 us -> 4.47 us  [swap(): return lax.ppermute(value, 'dp', PARTNERS)]
    all_to_all x5 -> x3, starting transfers between devices: 21.4 us -> 17.6 us  [exchange(): lax.all_to_all(value, 'dp', 0, 0, axis_index_groups=groups, tiled=True)]
    pallas_call x0 -> x2, local copies, waits for them, and re-layouts: none -> 2.75 us  [the longest x1 2.29 us: pack(): call(pack_kernel, 'pack', shape((MEMBERS, 2, TAPS, 2 * C), BF), [VM] * 3,...]
    pallas_call x8, Pallas kernels: 25.2 us -> 27.3 us  [the longest x1 11.9 us: grad1(): call(grad1_kernel, 'grad1', shape((MEMBERS, TAPS, BLOCK, C), BF), [VM] *...]
    pallas_call x1, Pallas kernels: 6.75 us -> 4.74 us  [conv1(): call(conv1_kernel, 'conv1', (shape((ACT_ROWS, C), F32), shape((3, 7, 7, O...]
    ppermute x5, starting transfers between devices: 3.47 us -> 1.72 us  [swap(): return lax.ppermute(value, 'dp', PARTNERS)]
  transfers between devices with their start and end apart: 10 -> 8, of which waited for: 9 -> 5; matrix products, arithmetic and copies ran while one was open for 0% -> 2% of each run, Pallas kernels for 8% -> 19%
where the time goes in v3:
time: 139 us; the launch traced here: 138 us
  blocking collectives  42.8 us (31%)
  Pallas kernels  38.8 us (28%)
  waiting for transfers between devices  22.9 us (16%)
  starting transfers between devices  19.3 us (14%)
  local copies, waits for them, and re-layouts  13.2 us (9%)
    all_to_all x2, blocking collectives, exchange(): lax.all_to_all(value, 'dp', 0, 0, axis_index_groups=groups, tiled=True)  42.8 us
    all_to_all x3, waiting for transfers between devices, exchange(): lax.all_to_all(value, 'dp', 0, 0, axis_index_groups=groups, tiled=True)  18.5 us
    all_to_all x3, starting transfers between devices, exchange(): lax.all_to_all(value, 'dp', 0, 0, axis_index_groups=groups, tiled=True)  17.6 us
    pallas_call x1, Pallas kernels, grad1(): call(grad1_kernel, 'grad1', shape((MEMBERS, TAPS, BLOCK, C), BF), [VM] *...  11.9 us
    unnamed x56, local copies, waits for them, and re-layouts  10.3 us
    pallas_call x1, Pallas kernels, conv1(): call(conv1_kernel, 'conv1', (shape((ACT_ROWS, C), F32), shape((3, 7, 7, O...  4.74 us
    pallas_call x1, Pallas kernels, grad2(): call(grad2_kernel, 'grad2', shape((MEMBERS, TAPS, BLOCK, C), BF), [VM] *...  4.56 us
    ppermute x5, waiting for transfers between devices, swap(): return lax.ppermute(value, 'dp', PARTNERS)  4.47 us
  transfers between devices with their start and end apart: 8, of which 5 were waited for; matrix products, arithmetic and copies ran while one was open for 2% of the time, Pallas kernels for 19%

profile of v3, /device:TPU:0, one launch (start us, length us, event | category | flops | bytes accessed | tf_op | source)
XLA Modules:
  0.0 138.1 jit_solution(11180978174798653397)
XLA Ops:
  0.6 0.0 copy-start.17
  0.6 0.0 copy-start.27
  0.7 0.1 collective-permute-start
  0.8 1.9 %pack.1 = bf16[8,2,27,512]{3,2,1,0:T(8,128)(2,1)} custom-call(f32[27,512]{1,0:T(8,128)} %k1.1, f32[27,512]{1,0:T(8,128)} %k2.1, s32[1,256]{1,0:T(1,128)} %constant.24.order), custom_call_target="tpu_custom_call" | custom-call | flops 10000000 | bytes 1000000 | tf_op jit(solution)/shard_map/pack/pallas_call | solution.py:397
  2.6 2.3 %copy.16 = bf16[8,2,27,512]{3,1,2,0:T(2,128)(2,1)} copy(bf16[8,2,27,512]{3,2,1,0:T(8,128)(2,1)} %pack.1) | data formatting | bytes 884736 | tf_op jit(solution)/shard_map/pack/pallas_call | solution.py:397
  4.9 8.0 %all-to-all-start = ((bf16[8,2,27,512]{3,1,2,0:T(2,128)(2,1)}), bf16[8,2,27,512]{3,1,2,0:T(2,128)(2,1)S(1)}, u32[]{:S(2)}, u32[]{:S(2)}) async-start(bf16[8,2,27,512]{3,1,2,0:T(2,128)(2,1)} %copy.16), calls=%async_computation | async-start | bytes 884736 | tf_op jit(solution)/shard_map/all_to_all | solution.py:555
  13.0 2.0 %prep.1 = (bf16[3,8,8,32,128]{4,3,2,1,0:T(8,128)(2,1)S(1)}, bf16[3,8,8,32,128]{4,3,2,1,0:T(8,128)(2,1)S(1)}, bf16[3,8,8,32,128]{4,3,2,1,0:T(8,128)(2,1)S(1)}, f32[144,256]{1,0:T(8,128)S(1)}, f32[144,256]{1,0:T(8,128)S(1)}) custom-call(bf16[6,6,6,4,256]{4,3,2,1,0:T(4,128)(2,1)S(1)} %bitcast.5, bf16[6,6,6,4,256]{4,3,2,1,0:T(4,128)(2,1)S(1)} %collective-permute-done.other, ...), custom_call_target="tpu_custom_call" | custom-call | flops 2000000000 | bytes 8000000 | tf_op jit(solution)/shard_map/prep/pallas_call | solution.py:120
  15.0 0.6 copy-done.7
  15.7 0.7 copy-done.9
  16.3 1.2 copy-done.20
  17.5 1.2 copy-done.22
  18.7 1.2 copy-done.25
  19.9 4.1 %all-to-all-done = bf16[8,2,27,512]{3,1,2,0:T(2,128)(2,1)S(1)} async-done(((bf16[8,2,27,512]{3,1,2,0:T(2,128)(2,1)}), bf16[8,2,27,512]{3,1,2,0:T(2,128)(2,1)S(1)}, u32[]{:S(2)}, u32[]{:S(2)}) %all-to-all-start) | async-done | bytes 442400 | tf_op jit(solution)/shard_map/all_to_all | solution.py:555
  24.0 0.1 copy.17.shards
  24.1 0.8 spread.1
  24.9 28.9 %all_to_all.25.mine = bf16[8,54,16,256]{3,2,1,0:T(8,128)(2,1)S(1)} all-to-all(bf16[8,54,16,256]{3,2,1,0:T(8,128)(2,1)S(1)} %spread.1), channel_id=1, replica_groups={{0,8,32,40,64,72,96,104},{2,10,34,42,66,74,98,106},{4,12,36,44,68,76,10..., dimensions={0} | all-to-all | bytes 7077888 | tf_op jit(solution)/shard_map/all_to_all | solution.py:555
  53.9 0.0 collective-permute-start.1
  53.9 4.4 %conv1_own.1.part_act = f32[1152,256]{1,0:T(8,128)S(1)} custom-call(bf16[3,8,8,32,128]{4,3,2,1,0:T(8,128)(2,1)S(1)} %copy-done.23, bf16[8,54,16,256]{3,2,1,0:T(8,128)(2,1)S(1)} %all_to_all.25.mine), custom_call_target="tpu_custom_call" | custom-call | flops 2000000000 | bytes 5000000 | tf_op jit(solution)/shard_map/conv1_own/pallas_call | solution.py:179
  58.3 1.9 %collective-permute-done.1.recv = bf16[8,54,16,256]{3,2,1,0:T(8,128)(2,1)S(1)} collective-permute-done((bf16[8,54,16,256]{3,2,1,0:T(8,128)(2,1)S(1)}, bf16[8,54,16,256]{3,2,1,0:T(8,128)(2,1)S(1)}, u32[]{:S(2)}, u32[]{:S(2)}) %collective-permute-start.1) | collective-permute-done | bytes 3538976 | tf_op jit(solution)/shard_map/ppermute | solution.py:559
  60.1 4.7 %conv1.1 = (f32[1152,256]{1,0:T(8,128)S(1)}, bf16[3,7,7,16,256]{4,3,2,1,0:T(8,128)(2,1)S(1)}, bf16[3,7,7,16,128]{4,3,2,1,0:T(8,128)(2,1)S(1)}) custom-call(s32[1]{0:T(128)} %bitcast.2.core_ref, bf16[3,8,8,32,128]{4,3,2,1,0:T(8,128)(2,1)S(1)} %copy-done.21, bf16[8,54,16,256]{3,2,1,0:T(8,128)(2,1)S(1)} %collective-permute-done.1.recv, ...), custom_call_target="tpu_custom_call" | custom-call | flops 2000000000 | bytes 7000000 | tf_op jit(solution)/shard_map/conv1/pallas_call | solution.py:210
  64.9 0.2 collective-permute-start.3
  65.1 2.2 %conv2.1 = (bf16[3,3,3,4,256]{4,3,2,1,0:T(4,128)(2,1)}, bf16[144,256]{1,0:T(8,128)(2,1)S(1)}, bf16[256,144]{1,0:T(8,128)(2,1)S(1)}) custom-call(f32[144,256]{1,0:T(8,128)S(1)} %copy-done.8, f32[144,256]{1,0:T(8,128)S(1)} %copy-done.10, bf16[3,7,7,16,256]{4,3,2,1,0:T(8,128)(2,1)S(1)} %get-tuple-element.42.hsel, bf16[8,54,16,256]{3,2,1,0:T(8,128)(2,1)S(1)} %all_to_all.25.mine, ...), custom_call_target="tpu_custom_call" | custom-call | flops 1500000000 | bytes 6000000 | tf_op jit(solution)/shard_map/conv2/pallas_call | solution.py:258
  67.3 0.6 collective-permute-start.2
  68.0 1.0 collective-permute-done.2.grad_t_other
  69.0 4.6 %grad2.1 = bf16[8,27,16,256]{3,2,1,0:T(8,128)(2,1)S(1)} custom-call(bf16[256,144]{1,0:T(8,128)(2,1)S(1)} %get-tuple-element.45.grad_t, bf16[256,144]{1,0:T(8,128)(2,1)S(1)} %collective-permute-done.2.grad_t_other, bf16[3,7,7,16,256]{4,3,2,1,0:T(8,128)(2,1)S(1)} %get-tuple-element.42.hsel, bf16[3,7,7,16,128]{4,3,2,1,0:T(8,128)(2,1)S(1)} %collective-permute-done.3.hsel_other), custom_call_target="tpu_custom_call" | custom-call | flops 1000000000 | bytes 4000000 | tf_op jit(solution)/shard_map/grad2/pallas_call | solution.py:361
  73.5 1.2 copy-done.2
  74.8 4.3 %all-to-all-start.3 = ((bf16[8,27,16,256]{3,2,1,0:T(8,128)(2,1)}), bf16[8,27,16,256]{3,2,1,0:T(8,128)(2,1)}, u32[]{:S(2)}, u32[]{:S(2)}) async-start(bf16[8,27,16,256]{3,2,1,0:T(8,128)(2,1)} %copy-done.2), calls=%async_computation.3 | async-start | bytes 3538944 | tf_op jit(solution)/shard_map/all_to_all | solution.py:555
  79.1 2.0 %copy-done.1 = bf16[8,54,16,256]{3,2,1,0:T(8,128)(2,1)S(1)} copy-done((bf16[8,54,16,256]{3,2,1,0:T(8,128)(2,1)S(1)}, bf16[8,54,16,256]{3,2,1,0:T(8,128)(2,1)}, u32[]{:S(2)}) %copy-start.1) | copy-done | bytes 3538968
  81.1 1.3 copy-done.4
  82.3 0.9 copy-done.12
  83.2 2.5 %back.1.gat = bf16[256,1152]{1,0:T(8,128)(2,1)S(1)} custom-call(s32[1]{0:T(128)} %bitcast.2.core_ref, f32[1152,256]{1,0:T(8,128)S(1)} %copy-done.4, bf16[144,256]{1,0:T(8,128)(2,1)S(1)} %copy-done.12, bf16[8,54,16,256]{3,2,1,0:T(8,128)(2,1)S(1)} %all_to_all.25.mine, bf16[8,54,16,256]{3,2,1,0:T(8,128)(2,1)S(1)} %copy-done.1), custom_call_target="tpu_custom_call" | custom-call | flops 1500000000 | bytes 8000000 | tf_op jit(solution)/shard_map/back/pallas_call | solution.py:308
  85.8 0.8 collective-permute-start.4
  86.5 1.6 %collective-permute-done.4.gat_other = bf16[256,1152]{1,0:T(8,128)(2,1)S(1)} collective-permute-done((bf16[256,1152]{1,0:T(8,128)(2,1)S(1)}, bf16[256,1152]{1,0:T(8,128)(2,1)S(1)}, u32[]{:S(2)}, u32[]{:S(2)}) %collective-permute-start.4) | collective-permute-done | bytes 589856 | tf_op jit(solution)/shard_map/ppermute | solution.py:559
  88.2 11.9 %grad1.1 = bf16[8,27,16,256]{3,2,1,0:T(8,128)(2,1)} custom-call(bf16[256,1152]{1,0:T(8,128)(2,1)S(1)} %back.1.gat, bf16[256,1152]{1,0:T(8,128)(2,1)S(1)} %collective-permute-done.4.gat_other, bf16[3,8,8,32,128]{4,3,2,1,0:T(8,128)(2,1)S(1)} %copy-done.24, bf16[3,8,8,32,128]{4,3,2,1,0:T(8,128)(2,1)S(1)} %copy-done.26), custom_call_target="tpu_custom_call" | custom-call | flops 4000000000 | bytes 7000000 | tf_op jit(solution)/shard_map/grad1/pallas_call | solution.py:379
  100.1 5.3 %all-to-all-start.2 = ((bf16[8,27,16,256]{3,2,1,0:T(8,128)(2,1)}), bf16[8,27,16,256]{3,2,1,0:T(8,128)(2,1)S(1)}, u32[]{:S(2)}, u32[]{:S(2)}) async-start(bf16[8,27,16,256]{3,2,1,0:T(8,128)(2,1)} %grad1.1), calls=%async_computation.2 | async-start | bytes 3538944 | tf_op jit(solution)/shard_map/all_to_all | solution.py:555
  105.3 2.0 %collect2.1.second = bf16[8,27,512]{2,1,0:T(8,128)(2,1)S(1)} custom-call(bf16[8,27,16,256]{3,2,1,0:T(8,128)(2,1)} %all-to-all-done.3.parts), custom_call_target="tpu_custom_call" | custom-call | flops 1000000 | bytes 3000000 | tf_op jit(solution)/shard_map/collect2/pallas_call | solution.py:450
  107.3 14.3 %all-to-all-done.2.parts = bf16[8,27,16,256]{3,2,1,0:T(8,128)(2,1)S(1)} async-done(((bf16[8,27,16,256]{3,2,1,0:T(8,128)(2,1)}), bf16[8,27,16,256]{3,2,1,0:T(8,128)(2,1)S(1)}, u32[]{:S(2)}, u32[]{:S(2)}) %all-to-all-start.2) | async-done | bytes 1769504 | tf_op jit(solution)/shard_map/all_to_all | solution.py:555
  121.6 0.5 collect.1
  122.2 0.0 copy-start.5
  122.2 0.0 copy-start.6
  122.2 0.0 copy-start.13
  122.2 0.0 copy-start.14
  122.2 0.0 copy-start.15
  122.2 0.0 copy-start.16
  122.2 0.5 copy.18
  122.7 13.9 %all_to_all.26 = bf16[8,2,27,512]{3,1,2,0:T(2,128)(2,1)S(1)} all-to-all(bf16[8,2,27,512]{3,1,2,0:T(2,128)(2,1)S(1)} %copy.18), channel_id=1, replica_groups={{0,2,4,6,16,18,20,22},{8,10,12,14,24,26,28,30},{32,34,36,38,48,50,52,54..., dimensions={0} | all-to-all | bytes 884736 | tf_op jit(solution)/shard_map/all_to_all | solution.py:555
  136.6 0.1 copy.19.parts
  136.7 1.3 adam.1
  (43 shorter events, 0.1 us)
Async XLA Ops:
  0.6 12.3 %copy-start.17 = (s32[1,256]{1,0:T(1,128)S(1)}, s32[1,256]{1,0:T(1,128)}, u32[]{:S(2)}) copy-start(s32[1,256]{1,0:T(1,128)} %constant.24.order) | copy-start | bytes 3076
  0.6 12.3 %copy-start.27 = (s32[1,256]{1,0:T(1,128)S(1)}, s32[1,256]{1,0:T(1,128)}, u32[]{:S(2)}) copy-start(s32[1,256]{1,0:T(1,128)} %constant.26) | copy-start | bytes 3076
  0.7 12.3 %copy-start.18 = (bf16[4,6,6,6,256]{4,0,3,2,1:T(4,128)(2,1)S(1)}, bf16[4,6,6,6,256]{4,0,3,2,1:T(4,128)(2,1)}, u32[]{:S(2)}) copy-start(bf16[4,6,6,6,256]{4,0,3,2,1:T(4,128)(2,1)} %param.9) | copy-start | bytes 1327108
  0.7 12.3 %copy-start.19 = (bf16[4,3,3,3,256]{4,0,3,2,1:T(4,128)(2,1)S(1)}, bf16[4,3,3,3,256]{4,0,3,2,1:T(4,128)(2,1)}, u32[]{:S(2)}) copy-start(bf16[4,3,3,3,256]{4,0,3,2,1:T(4,128)(2,1)} %param.10) | copy-start | bytes 165892
  0.7 12.3 %collective-permute-start = (bf16[6,6,6,4,256]{4,3,2,1,0:T(4,128)(2,1)}, bf16[6,6,6,4,256]{4,3,2,1,0:T(4,128)(2,1)S(1)}, u32[]{:S(2)}, u32[]{:S(2)}) collective-permute-start(bf16[6,6,6,4,256]{4,3,2,1,0:T(4,128)(2,1)} %bitcast.4), channel_id=1, source_target_pairs={{0,1},{1,0},{2,3},{3,2},{4,5},{5,4},{6,7},{7,6},{8,9},{9,8},{10,11... | collective-permute-start | bytes 1327112 | tf_op jit(solution)/shard_map/ppermute | solution.py:559
  4.9 19.1 %all-to-all-start = ((bf16[8,2,27,512]{3,1,2,0:T(2,128)(2,1)}), bf16[8,2,27,512]{3,1,2,0:T(2,128)(2,1)S(1)}, u32[]{:S(2)}, u32[]{:S(2)}) async-start(bf16[8,2,27,512]{3,1,2,0:T(2,128)(2,1)} %copy.16), calls=%async_computation | async-start | bytes 884736 | tf_op jit(solution)/shard_map/all_to_all | solution.py:555
  15.0 0.6 copy-start.7
  15.7 0.7 copy-start.9
  16.3 1.2 copy-start.20
  17.5 1.2 copy-start.22
  18.7 1.2 copy-start.25
  24.9 29.0 %copy-start.23 = (bf16[3,8,8,32,128]{4,3,2,1,0:T(8,128)(2,1)S(1)}, bf16[3,8,8,32,128]{4,3,2,1,0:T(8,128)(2,1)}, u32[]{:S(2)}) copy-start(bf16[3,8,8,32,128]{4,3,2,1,0:T(8,128)(2,1)} %copy-done.22) | copy-start | bytes 4718596
  53.9 6.2 %copy-start.21 = (bf16[3,8,8,32,128]{4,3,2,1,0:T(8,128)(2,1)S(1)}, bf16[3,8,8,32,128]{4,3,2,1,0:T(8,128)(2,1)}, u32[]{:S(2)}) copy-start(bf16[3,8,8,32,128]{4,3,2,1,0:T(8,128)(2,1)} %copy-done.20) | copy-start | bytes 4718596
  53.9 6.2 %collective-permute-start.1 = (bf16[8,54,16,256]{3,2,1,0:T(8,128)(2,1)S(1)}, bf16[8,54,16,256]{3,2,1,0:T(8,128)(2,1)S(1)}, u32[]{:S(2)}, u32[]{:S(2)}) collective-permute-start(bf16[8,54,16,256]{3,2,1,0:T(8,128)(2,1)S(1)} %all_to_all.25.mine), channel_id=1, source_target_pairs={{0,1},{1,0},{2,3},{3,2},{4,5},{5,4},{6,7},{7,6},{8,9},{9,8},{10,11... | collective-permute-start | bytes 10616840 | tf_op jit(solution)/shard_map/ppermute | solution.py:559
  60.1 5.0 %copy-start = (bf16[8,54,16,256]{3,2,1,0:T(8,128)(2,1)}, bf16[8,54,16,256]{3,2,1,0:T(8,128)(2,1)S(1)}, u32[]{:S(2)}) copy-start(bf16[8,54,16,256]{3,2,1,0:T(8,128)(2,1)S(1)} %collective-permute-done.1.recv) | copy-start | bytes 10616836
  60.1 5.0 %copy-start.8 = (f32[144,256]{1,0:T(8,128)S(1)}, f32[144,256]{1,0:T(8,128)}, u32[]{:S(2)}) copy-start(f32[144,256]{1,0:T(8,128)} %copy-done.7) | copy-start | bytes 442372
  60.1 5.0 %copy-start.10 = (f32[144,256]{1,0:T(8,128)S(1)}, f32[144,256]{1,0:T(8,128)}, u32[]{:S(2)}) copy-start(f32[144,256]{1,0:T(8,128)} %copy-done.9) | copy-start | bytes 442372
  64.9 2.4 %copy-start.3 = (f32[1152,256]{1,0:T(8,128)}, f32[1152,256]{1,0:T(8,128)S(1)}, u32[]{:S(2)}) copy-start(f32[1152,256]{1,0:T(8,128)S(1)} %get-tuple-element.44.act) | copy-start | bytes 3538948
  64.9 4.1 %collective-permute-start.3 = (bf16[3,7,7,16,128]{4,3,2,1,0:T(8,128)(2,1)S(1)}, bf16[3,7,7,16,128]{4,3,2,1,0:T(8,128)(2,1)S(1)}, u32[]{:S(2)}, u32[]{:S(2)}) collective-permute-start(bf16[3,7,7,16,128]{4,3,2,1,0:T(8,128)(2,1)S(1)} %get-tuple-element.46), channel_id=1, source_target_pairs={{0,1},{1,0},{2,3},{3,2},{4,5},{5,4},{6,7},{7,6},{8,9},{9,8},{10,11... | collective-permute-start | bytes 1806344 | tf_op jit(solution)/shard_map/ppermute | solution.py:559
  67.3 6.2 %copy-start.11 = (bf16[144,256]{1,0:T(8,128)(2,1)}, bf16[144,256]{1,0:T(8,128)(2,1)S(1)}, u32[]{:S(2)}) copy-start(bf16[144,256]{1,0:T(8,128)(2,1)S(1)} %get-tuple-element.48.grad_pre) | copy-start | bytes 221188
  67.3 1.6 %collective-permute-start.2 = (bf16[256,144]{1,0:T(8,128)(2,1)S(1)}, bf16[256,144]{1,0:T(8,128)(2,1)S(1)}, u32[]{:S(2)}, u32[]{:S(2)}) collective-permute-start(bf16[256,144]{1,0:T(8,128)(2,1)S(1)} %get-tuple-element.45.grad_t), channel_id=1, source_target_pairs={{0,1},{1,0},{2,3},{3,2},{4,5},{5,4},{6,7},{7,6},{8,9},{9,8},{10,11... | collective-permute-start | bytes 221192 | tf_op jit(solution)/shard_map/ppermute | solution.py:559
  73.5 1.2 copy-start.2
  74.8 25.3 %all-to-all-start.3 = ((bf16[8,27,16,256]{3,2,1,0:T(8,128)(2,1)}), bf16[8,27,16,256]{3,2,1,0:T(8,128)(2,1)}, u32[]{:S(2)}, u32[]{:S(2)}) async-start(bf16[8,27,16,256]{3,2,1,0:T(8,128)(2,1)} %copy-done.2), calls=%async_computation.3 | async-start | bytes 3538944 | tf_op jit(solution)/shard_map/all_to_all | solution.py:555
  79.1 2.0 %copy-start.1 = (bf16[8,54,16,256]{3,2,1,0:T(8,128)(2,1)S(1)}, bf16[8,54,16,256]{3,2,1,0:T(8,128)(2,1)}, u32[]{:S(2)}) copy-start(bf16[8,54,16,256]{3,2,1,0:T(8,128)(2,1)} %copy-done) | copy-start | bytes 10616836
  81.1 1.3 copy-start.4
  82.3 0.9 copy-start.12
  83.2 4.9 %copy-start.24 = (bf16[3,8,8,32,128]{4,3,2,1,0:T(8,128)(2,1)S(1)}, bf16[3,8,8,32,128]{4,3,2,1,0:T(8,128)(2,1)}, u32[]{:S(2)}) copy-start(bf16[3,8,8,32,128]{4,3,2,1,0:T(8,128)(2,1)} %copy-done.22) | copy-start | bytes 4718596
  83.2 4.9 %copy-start.26 = (bf16[3,8,8,32,128]{4,3,2,1,0:T(8,128)(2,1)S(1)}, bf16[3,8,8,32,128]{4,3,2,1,0:T(8,128)(2,1)}, u32[]{:S(2)}) copy-start(bf16[3,8,8,32,128]{4,3,2,1,0:T(8,128)(2,1)} %copy-done.25) | copy-start | bytes 4718596
  85.8 2.4 %collective-permute-start.4 = (bf16[256,1152]{1,0:T(8,128)(2,1)S(1)}, bf16[256,1152]{1,0:T(8,128)(2,1)S(1)}, u32[]{:S(2)}, u32[]{:S(2)}) collective-permute-start(bf16[256,1152]{1,0:T(8,128)(2,1)S(1)} %back.1.gat), channel_id=1, source_target_pairs={{0,1},{1,0},{2,3},{3,2},{4,5},{5,4},{6,7},{7,6},{8,9},{9,8},{10,11... | collective-permute-start | bytes 1769480 | tf_op jit(solution)/shard_map/ppermute | solution.py:559
  100.1 21.6 %all-to-all-start.2 = ((bf16[8,27,16,256]{3,2,1,0:T(8,128)(2,1)}), bf16[8,27,16,256]{3,2,1,0:T(8,128)(2,1)S(1)}, u32[]{:S(2)}, u32[]{:S(2)}) async-start(bf16[8,27,16,256]{3,2,1,0:T(8,128)(2,1)} %grad1.1), calls=%async_computation.2 | async-start | bytes 3538944 | tf_op jit(solution)/shard_map/all_to_all | solution.py:555
  122.2 14.5 %copy-start.5 = (f32[27,512]{1,0:T(8,128)S(1)}, f32[27,512]{1,0:T(8,128)}, u32[]{:S(2)}) copy-start(f32[27,512]{1,0:T(8,128)} %k1.1) | copy-start | bytes 165892
  122.2 14.5 %copy-start.6 = (f32[27,512]{1,0:T(8,128)S(1)}, f32[27,512]{1,0:T(8,128)}, u32[]{:S(2)}) copy-start(f32[27,512]{1,0:T(8,128)} %k2.1) | copy-start | bytes 165892
  122.2 14.5 %copy-start.13 = (f32[27,512]{1,0:T(8,128)S(1)}, f32[27,512]{1,0:T(8,128)}, u32[]{:S(2)}) copy-start(f32[27,512]{1,0:T(8,128)} %m1.1) | copy-start | bytes 165892
  122.2 14.5 %copy-start.14 = (f32[27,512]{1,0:T(8,128)S(1)}, f32[27,512]{1,0:T(8,128)}, u32[]{:S(2)}) copy-start(f32[27,512]{1,0:T(8,128)} %v1.1) | copy-start | bytes 165892
  122.2 14.5 %copy-start.15 = (f32[27,512]{1,0:T(8,128)S(1)}, f32[27,512]{1,0:T(8,128)}, u32[]{:S(2)}) copy-start(f32[27,512]{1,0:T(8,128)} %m2.1) | copy-start | bytes 165892
  122.2 14.5 %copy-start.16 = (f32[27,512]{1,0:T(8,128)S(1)}, f32[27,512]{1,0:T(8,128)}, u32[]{:S(2)}) copy-start(f32[27,512]{1,0:T(8,128)} %v2.1) | copy-start | bytes 165892

commit v4 on v3

--- a/solution.py
+++ b/solution.py
@@ -25,24 +25,25 @@
 F32 = jnp.float32
 
 MEMBERS = 8
+GROUP = 6
 BLOCK = 16
 
 VM = pl.BlockSpec(memory_space=pltpu.VMEM)
 SM = pl.BlockSpec(memory_space=pltpu.SMEM)
-ANY = pl.BlockSpec(memory_space=pl.ANY)
+HB = pl.BlockSpec(memory_space=pltpu.HBM)
 
 
 def shape(dims, dtype):
     return jax.ShapeDtypeStruct(dims, dtype)
 
 
-def call(kernel, name, out_shape, in_specs, scratch, mib, flops, moved):
+def call(kernel, name, out_shape, in_specs, scratch, mib, flops, moved, out_spec=VM):
     single = not isinstance(out_shape, tuple)
     return pl.pallas_call(
         kernel,
         out_shape=out_shape,
         in_specs=in_specs,
-        out_specs=VM if single else (VM,) * len(out_shape),
+        out_specs=out_spec if single else (out_spec,) * len(out_shape),
         scratch_shapes=scratch,
         compiler_params=pltpu.CompilerParams(vmem_limit_bytes=mib * MIB),
         cost_estimate=pl.CostEstimate(flops=flops, bytes_accessed=moved, transcendentals=0),
@@ -120,7 +121,7 @@
     return call(
         prep_kernel, "prep", (wide, wide, wide, pre, pre), [VM] * 4,
         [pltpu.VMEM((2, PAD_ROWS + 16, HALF), F32), pltpu.VMEM((2, PRE_ROWS, HALF), F32)],
-        20, 2_000_000_000, 8_000_000,
+        56, 2_000_000_000, 8_000_000,
     )(latent, other, out_grad, order)
 
 
@@ -157,18 +158,20 @@
 
 
 def half_conv(x3, weights, copies, act, start):
-    for di in range(3):
-        copies[di].wait()
-        taps = range(9 * di, 9 * di + 9)
+    for first in range(0, TAPS, GROUP):
+        taps = range(first, min(first + GROUP, TAPS))
+        for di in range(3):
+            if first <= 9 * di < first + GROUP or (first, di) == (0, 0):
+                copies[di].wait()
         windows = [
-            x3[t % 3, di : di + EDGE, t // 3 % 3 : t // 3 % 3 + EDGE].reshape(ACT_ROWS, HALF)
-            for t in taps
+            x3[t % 3, t // 9 : t // 9 + EDGE, t // 3 % 3 : t // 3 % 3 + EDGE] for t in taps
         ]
         total = dot(
-            jnp.concatenate(windows, axis=1),
+            jnp.concatenate([window.reshape(ACT_ROWS, HALF) for window in windows], axis=1),
             jnp.concatenate([half_weight(weights, t) for t in taps], axis=0),
         )
-        act[...] = (start if di == 0 else act)[...] + total if start is not None or di else total
+        before = act if first else start
+        act[...] = total if before is None else before[...] + total
 
 
 def conv1_own_kernel(x3a, mine, act, weights, sems):
@@ -177,7 +180,7 @@
 
 def conv1_own(x3a, mine):
     return call(
-        conv1_own_kernel, "conv1_own", shape((ACT_ROWS, C), F32), [VM, ANY], HALF_WEIGHTS,
+        conv1_own_kernel, "conv1_own", shape((ACT_ROWS, C), F32), [VM, HB], HALF_WEIGHTS,
         12, 2_000_000_000, 5_000_000,
     )(x3a, mine)
 
@@ -214,7 +217,7 @@
             shape((3, 7, 7, OUT_ROWS, C), BF),
             shape((3, 7, 7, OUT_ROWS, HALF), BF),
         ),
-        [SM, VM, ANY, VM],
+        [SM, VM, HB, VM],
         HALF_WEIGHTS + [pltpu.VMEM((2, ACT_ROWS + 8, HALF), F32)],
         24, 2_000_000_000, 7_000_000,
     )(core, x3b, recv, part_act)
@@ -262,16 +265,23 @@
             shape((PRE_ROWS, C), BF),
             shape((C, PRE_ROWS), BF),
         ),
-        [VM, VM, VM, ANY, ANY],
+        [VM, VM, VM, HB, HB],
         WEIGHTS + [pltpu.VMEM((2, PRE_ROWS, HALF), F32)],
         16, 1_500_000_000, 6_000_000,
     )(skip, cot, hsel, mine, recv)
 
 
-def back_kernel(core_ref, act, grad_pre, mine, recv, gat, wa, sa, wb, sb, y, gh):
+def back_kernel(
+    core_ref, act_far, grad_far, mine, recv, gat, wa, sa, wb, sb, y, gh, act, grad_pre, sems
+):
     core = core_ref[0]
+    fetch_grad = pltpu.make_async_copy(grad_far, grad_pre, sems.at[0])
+    fetch_act = pltpu.make_async_copy(act_far, act, sems.at[1])
+    fetch_grad.start()
     halves = (fetch_weights(mine, TAPS, wa, sa), fetch_weights(recv, TAPS, wb, sb))
+    fetch_act.start()
     y[...] = jnp.zeros_like(y)
+    fetch_grad.wait()
     grad = grad_pre[...]
     for di in range(3):
         for copies in halves:
@@ -294,6 +304,7 @@
         total = load(gh, base, count, 2) + y[2, i + 1, 1:].reshape(count, C)
         store(gh, base, count, total, 2)
     inside = cell_mask()
+    fetch_act.wait()
     for i in range(EDGE):
         value = act[pl.ds(i * EDGE * ROWS, EDGE * ROWS), :]
         sigma = sigmoid(value)
@@ -307,60 +318,78 @@
 def back(core, act, grad_pre, mine, recv):
     return call(
         back_kernel, "back", shape((C, ACT_ROWS), BF),
-        [SM, VM, VM, ANY, ANY],
+        [SM, HB, HB, HB, HB],
         WEIGHTS
         + [
             pltpu.VMEM((3, 7, 7, OUT_ROWS, C), F32),
             pltpu.VMEM((2, ACT_ROWS + 8, HALF), F32),
+            pltpu.VMEM((ACT_ROWS, C), F32),
+            pltpu.VMEM((PRE_ROWS, C), BF),
+            pltpu.SemaphoreType.DMA((2,)),
         ],
-        18, 1_500_000_000, 8_000_000,
+        20, 1_500_000_000, 8_000_000,
     )(core, act, grad_pre, mine, recv)
 
 
-def grad_loop(out, lefts, windows, unroll):
+def grad_loop(far_out, out, sems, left, windows):
     eye = (
         lax.broadcasted_iota(jnp.int32, (C, C), 0) == lax.broadcasted_iota(jnp.int32, (C, C), 1)
     ).astype(BF)
 
+    def send(n, count):
+        part = pl.ds(GROUP * n, count)
+        return pltpu.make_async_copy(out.at[:, part], far_out.at[:, part], sems.at[n])
+
     def product(taps):
-        total = None
-        for left, window in zip(lefts, windows):
-            right = jnp.concatenate([window(t // 9, t // 3 % 3, t % 3) for t in taps], axis=1)
-            term = dot(left[...], right)
-            total = term if total is None else total + term
-        width = HALF * len(taps)
-        turned = dot_t(eye[:width, :width], total.astype(BF)).astype(BF)
-        for n, t in enumerate(taps):
-            out[:, t] = turned[n * HALF : (n + 1) * HALF].reshape(MEMBERS, BLOCK, C)
+        right = [
+            jnp.concatenate([window(t // 9, t // 3 % 3, t % 3) for t in taps], axis=1)
+            for window in windows
+        ]
+        total = dot(left[...], jnp.concatenate(right, axis=0)).astype(BF)
+        for n in range(0, len(taps), 2):
+            two = taps[n : n + 2]
+            width = HALF * len(two)
+            turned = dot_t(eye[:width, :width], total[:, n * HALF : n * HALF + width]).astype(BF)
+            for m, t in enumerate(two):
+                out[:, t] = turned[m * HALF : (m + 1) * HALF].reshape(MEMBERS, BLOCK, C)
 
     def step(n, carry):
-        for k in range(0, unroll, 2):
-            product((unroll * n + k, unroll * n + k + 1))
+        product([GROUP * n + k for k in range(GROUP)])
+        send(n, GROUP).start()
         return carry
 
-    whole = TAPS // unroll
-    if whole > 1:
-        lax.fori_loop(0, whole, step, 0)
-    for t in range(unroll * whole if whole > 1 else 0, TAPS, 2):
-        product(tuple(range(t, min(t + 2, TAPS))))
-
-
-def grad2_kernel(grad_t, grad_t_other, hsel, hsel_other, out):
+    whole = TAPS // GROUP
+    lax.fori_loop(0, whole, step, 0)
+    product(list(range(GROUP * whole, TAPS)))
+    send(whole, TAPS - GROUP * whole).start()
+    for n in range(whole):
+        send(n, GROUP).wait()
+    send(whole, TAPS - GROUP * whole).wait()
+
+
+GRAD = (MEMBERS, TAPS, BLOCK, C)
+STAGING = [pltpu.VMEM(GRAD, BF), pltpu.SemaphoreType.DMA((-(-TAPS // GROUP),))]
+
+
+def grad2_kernel(grad_t, grad_t_other, hsel, hsel_other, far_out, out, sems, left):
+    left[:, :PRE_ROWS] = grad_t[...]
+    left[:, PRE_ROWS:] = grad_t_other[...]
     grad_loop(
+        far_out,
         out,
-        (grad_t, grad_t_other),
+        sems,
+        left,
         (
             lambda di, dj, dl: strided_window(hsel, dl, di, dj, slice(0, HALF)),
             lambda di, dj, dl: strided_window(hsel_other, dl, di, dj),
         ),
-        TAPS,
     )
 
 
 def grad2(grad_t, grad_t_other, hsel, hsel_other):
     return call(
-        grad2_kernel, "grad2", shape((MEMBERS, TAPS, BLOCK, C), BF), [VM] * 4, [],
-        8, 1_000_000_000, 4_000_000,
+        grad2_kernel, "grad2", shape(GRAD, BF), [VM] * 4,
+        STAGING + [pltpu.VMEM((C, 2 * PRE_ROWS), BF)], 12, 1_000_000_000, 4_000_000, HB,
     )(grad_t, grad_t_other, hsel, hsel_other)
 
 
@@ -371,14 +400,16 @@
     return window
 
 
-def grad1_kernel(gat, gat_other, x3a, x3o, out):
-    grad_loop(out, (gat, gat_other), (same_window(x3a), same_window(x3o)), 2)
+def grad1_kernel(gat, gat_other, x3a, x3o, far_out, out, sems, left):
+    left[:, :ACT_ROWS] = gat[...]
+    left[:, ACT_ROWS:] = gat_other[...]
+    grad_loop(far_out, out, sems, left, (same_window(x3a), same_window(x3o)))
 
 
 def grad1(gat, gat_other, x3a, x3o):
     return call(
-        grad1_kernel, "grad1", shape((MEMBERS, TAPS, BLOCK, C), BF), [VM] * 4, [],
-        12, 4_000_000_000, 7_000_000,
+        grad1_kernel, "grad1", shape(GRAD, BF), [VM] * 4,
+        STAGING + [pltpu.VMEM((C, 2 * ACT_ROWS), BF)], 16, 4_000_000_000, 7_000_000, HB,
     )(gat, gat_other, x3a, x3o)
 
 
@@ -386,27 +417,24 @@
     perm = one_hot(order[...])
     for i in range(2):
         lanes = slice(i * C, (i + 1) * C)
-        one = dot(first[:, lanes].astype(BF), perm).astype(BF)
-        two = second[:, lanes].astype(BF)
+        one = dot(first[:, lanes].astype(BF), perm)
+        both = jnp.concatenate([one, second[:, lanes]], axis=0).astype(BF)
         for n in range(MEMBERS):
-            out[n, 0, :, lanes] = one
-            out[n, 1, :, lanes] = two
+            out[n, :, lanes] = both
 
 
 def pack(first, second, order):
     return call(
-        pack_kernel, "pack", shape((MEMBERS, 2, TAPS, 2 * C), BF), [VM] * 3,
+        pack_kernel, "pack", shape((MEMBERS, 2 * TAPS, 2 * C), BF), [VM] * 3,
         [], 56, 10_000_000, 1_000_000,
     )(first, second, order)
 
 
 def spread_kernel(shards, out, wide):
     for m in range(MEMBERS):
-        for k in range(2):
-            rows = shards[m, k].astype(F32)
-            for i in range(2):
-                start = k * TAPS * BLOCK + 2 * m + i
-                store(wide, start, TAPS, rows[:, i * C : (i + 1) * C], BLOCK)
+        rows = shards[m].astype(F32)
+        for i in range(2):
+            store(wide, 2 * m + i, 2 * TAPS, rows[:, i * C : (i + 1) * C], BLOCK)
 
     def step(t, carry):
         value = load(wide, pl.multiple_of(t * BLOCK, BLOCK), BLOCK).astype(BF)
@@ -424,7 +452,7 @@
     )(shards)
 
 
-def collect_one(parts, wide, write):
+def add_parts(parts, wide):
     def step(t, carry):
         total = parts[0, t].astype(F32)
         for n in range(1, MEMBERS):
@@ -433,39 +461,28 @@
         return carry
 
     lax.fori_loop(0, TAPS, step, 0)
+
+
+def collect2(parts):
+    return call(
+        add_parts, "collect2", shape((2, TAPS * BLOCK, HALF), F32), [VM], [],
+        6, 1_000_000, 3_000_000,
+    )(parts)
+
+
+def collect_kernel(parts, second, out, wide):
+    wide[:, TAPS * BLOCK :] = second[...]
+    add_parts(parts, wide)
     for m in range(MEMBERS):
         for i in range(2):
-            rows = load(wide, 2 * m + i, TAPS, BLOCK).astype(BF)
-            write(m, slice(i * C, (i + 1) * C), rows)
-
-
-def collect2_kernel(parts, out, wide):
-    def write(m, lanes, rows):
-        out[m, :, lanes] = rows
-
-    collect_one(parts, wide, write)
-
-
-def collect2(parts):
-    return call(
-        collect2_kernel, "collect2", shape((MEMBERS, TAPS, 2 * C), BF), [VM],
-        [pltpu.VMEM((2, TAPS * BLOCK, HALF), F32)], 6, 1_000_000, 3_000_000,
-    )(parts)
-
-
-def collect_kernel(parts, second, out, wide):
-    def write(m, lanes, rows):
-        out[m, 0, :, lanes] = rows
-
-    for m in range(MEMBERS):
-        out[m, 1] = second[m]
-    collect_one(parts, wide, write)
+            rows = load(wide, 2 * m + i, 2 * TAPS, BLOCK)
+            out[m, :, i * C : (i + 1) * C] = rows.astype(BF)
 
 
 def collect(parts, second):
     return call(
-        collect_kernel, "collect", shape((MEMBERS, 2, TAPS, 2 * C), BF), [VM] * 2,
-        [pltpu.VMEM((2, TAPS * BLOCK, HALF), F32)], 8, 1_000_000, 3_000_000,
+        collect_kernel, "collect", shape((MEMBERS, 2 * TAPS, 2 * C), BF), [VM] * 2,
+        [pltpu.VMEM((2, 2 * TAPS * BLOCK, HALF), F32)], 8, 1_000_000, 3_000_000,
     )(parts, second)
 
 
@@ -484,25 +501,25 @@
     scale, parts, order, k1, m1, v1, k2, m2, v2, k1n, m1n, v1n, k2n, m2n, v2n
 ):
     back = one_hot(order[...]).astype(F32)
-    state = ((k1, m1, v1, k1n, m1n, v1n), (k2, m2, v2, k2n, m2n, v2n))
     for i in range(2):
         lanes = slice(i * C, (i + 1) * C)
-        for which, (k, m, v, kn, mn, vn) in enumerate(state):
-            grad = parts[0, which, :, lanes].astype(F32)
-            for n in range(1, MEMBERS):
-                grad = grad + parts[n, which, :, lanes].astype(F32)
-            grad = grad * scale
-            if which == 0:
-                grad = lax.dot_general(
-                    grad,
-                    back,
-                    (((1,), (1,)), ((), ())),
-                    precision=lax.Precision.HIGHEST,
-                    preferred_element_type=F32,
-                )
-            kn[:, lanes], mn[:, lanes], vn[:, lanes] = adam_update(
-                k[:, lanes], m[:, lanes], v[:, lanes], grad
-            )
+        total = parts[0, :, lanes].astype(F32)
+        for n in range(1, MEMBERS):
+            total = total + parts[n, :, lanes].astype(F32)
+        total = total * scale
+        grad = lax.dot_general(
+            total[:TAPS],
+            back,
+            (((1,), (1,)), ((), ())),
+            precision=lax.Precision.HIGHEST,
+            preferred_element_type=F32,
+        )
+        k1n[:, lanes], m1n[:, lanes], v1n[:, lanes] = adam_update(
+            k1[:, lanes], m1[:, lanes], v1[:, lanes], grad
+        )
+        k2n[:, lanes], m2n[:, lanes], v2n[:, lanes] = adam_update(
+            k2[:, lanes], m2[:, lanes], v2[:, lanes], total[TAPS:]
+        )
 
 
 def adam(scale, parts, order, *state):

time: 139 us -> 131 us (0.942)
  local copies, waits for them, and re-layouts: 13.2 us -> 6.25 us
  Pallas kernels: 38.8 us -> 35.8 us
    pallas_call x7, Pallas kernels: 27.7 us -> 22.3 us  [the longest x1 7.46 us: grad1(): call(grad1_kernel, 'grad1', shape(GRAD, BF), [VM] * 4, STAGING + [pltpu.V...]
    unnamed x56 -> x42, local copies, waits for them, and re-layouts: 10.3 us -> 6.25 us
    pallas_call x2 -> x0, local copies, waits for them, and re-layouts: 2.75 us -> none  [the longest x1 2.29 us: pack(): call(pack_kernel, 'pack', shape((MEMBERS, 2, TAPS, 2 * C), BF), [VM] * 3,...]
    pallas_call x1, Pallas kernels: 1.99 us -> 4.6 us  [prep(): call(prep_kernel, 'prep', (wide, wide, wide, pre, pre), [VM] * 4, [pltpu....]
  transfers between devices with their start and end apart: 8 -> 8, of which waited for: 5 -> 5; matrix products, arithmetic and copies ran while one was open for 2% -> 1% of each run, Pallas kernels for 19% -> 19%
where the time goes in v4:
time: 131 us; the launch traced here: 130 us
  blocking collectives  42.9 us (33%)
  Pallas kernels  35.8 us (27%)
  waiting for transfers between devices  23.6 us (18%)
  starting transfers between devices  19.2 us (15%)
  local copies, waits for them, and re-layouts  6.25 us (5%)
    all_to_all x2, blocking collectives, exchange(): lax.all_to_all(value, 'dp', 0, 0, axis_index_groups=groups, tiled=True)  42.9 us
    all_to_all x3, waiting for transfers between devices, exchange(): lax.all_to_all(value, 'dp', 0, 0, axis_index_groups=groups, tiled=True)  19 us
    all_to_all x3, starting transfers between devices, exchange(): lax.all_to_all(value, 'dp', 0, 0, axis_index_groups=groups, tiled=True)  17.8 us
    pallas_call x1, Pallas kernels, grad1(): call(grad1_kernel, 'grad1', shape(GRAD, BF), [VM] * 4, STAGING + [pltpu.V...  7.46 us
    unnamed x42, local copies, waits for them, and re-layouts  6.25 us
    ppermute x5, waiting for transfers between devices, swap(): return lax.ppermute(value, 'dp', PARTNERS)  4.62 us
    pallas_call x1, Pallas kernels, prep(): call(prep_kernel, 'prep', (wide, wide, wide, pre, pre), [VM] * 4, [pltpu....  4.6 us
    pallas_call x1, Pallas kernels, conv1(): call(conv1_kernel, 'conv1', (shape((ACT_ROWS, C), F32), shape((3, 7, 7, O...  4.56 us
  transfers between devices with their start and end apart: 8, of which 5 were waited for; matrix products, arithmetic and copies ran while one was open for 1% of the time, Pallas kernels for 19%

profile of v4, /device:TPU:0, one launch (start us, length us, event | category | flops | bytes accessed | tf_op | source)
XLA Modules:
  0.0 129.9 jit_solution(14881375388374046634)
XLA Ops:
  0.6 0.1 collective-permute-start
  0.7 1.8 %pack.1 = bf16[8,54,512]{2,1,0:T(8,128)(2,1)} custom-call(f32[27,512]{1,0:T(8,128)} %k1.1, f32[27,512]{1,0:T(8,128)} %k2.1, s32[1,256]{1,0:T(1,128)} %constant.24.order), custom_call_target="tpu_custom_call" | custom-call | flops 10000000 | bytes 1000000 | tf_op jit(solution)/shard_map/pack/pallas_call | solution.py:427
  2.5 8.0 %all-to-all-start = ((bf16[8,54,512]{2,1,0:T(8,128)(2,1)}), bf16[8,54,512]{2,1,0:T(8,128)(2,1)S(1)}, u32[]{:S(2)}, u32[]{:S(2)}) async-start(bf16[8,54,512]{2,1,0:T(8,128)(2,1)} %pack.1), calls=%async_computation | async-start | bytes 917504 | tf_op jit(solution)/shard_map/all_to_all | solution.py:572
  10.6 1.2 broadcast_select_fusion.order
  11.8 0.0 collective-permute-done.other
  11.8 0.8 copy-done.20
  12.6 4.6 %prep.1 = (bf16[3,8,8,32,128]{4,3,2,1,0:T(8,128)(2,1)}, bf16[3,8,8,32,128]{4,3,2,1,0:T(8,128)(2,1)}, bf16[3,8,8,32,128]{4,3,2,1,0:T(8,128)(2,1)}, f32[144,256]{1,0:T(8,128)}, f32[144,256]{1,0:T(8,128)}) custom-call(bf16[6,6,6,4,256]{4,3,2,1,0:T(4,128)(2,1)} %bitcast.5, bf16[6,6,6,4,256]{4,3,2,1,0:T(4,128)(2,1)} %copy-done.20, ...), custom_call_target="tpu_custom_call" | custom-call | flops 2000000000 | bytes 8000000 | tf_op jit(solution)/shard_map/prep/pallas_call | solution.py:121
  17.2 4.6 %all-to-all-done.shards = bf16[8,54,512]{2,1,0:T(8,128)(2,1)S(1)} async-done(((bf16[8,54,512]{2,1,0:T(8,128)(2,1)}), bf16[8,54,512]{2,1,0:T(8,128)(2,1)S(1)}, u32[]{:S(2)}, u32[]{:S(2)}) %all-to-all-start) | async-done | bytes 442400 | tf_op jit(solution)/shard_map/all_to_all | solution.py:572
  21.8 0.8 spread.1
  22.7 0.0 copy-start.17
  22.7 28.9 %all_to_all.25.mine = bf16[8,54,16,256]{3,2,1,0:T(8,128)(2,1)S(1)} all-to-all(bf16[8,54,16,256]{3,2,1,0:T(8,128)(2,1)S(1)} %spread.1), channel_id=1, replica_groups={{0,8,32,40,64,72,96,104},{2,10,34,42,66,74,98,106},{4,12,36,44,68,76,10..., dimensions={0} | all-to-all | bytes 7077888 | tf_op jit(solution)/shard_map/all_to_all | solution.py:572
  51.6 0.0 collective-permute-start.1
  51.6 4.2 %conv1_own.1.part_act = f32[1152,256]{1,0:T(8,128)S(1)} custom-call(bf16[3,8,8,32,128]{4,3,2,1,0:T(8,128)(2,1)S(1)} %copy-done.17, bf16[8,54,16,256]{3,2,1,0:T(8,128)(2,1)S(1)} %all_to_all.25.mine), custom_call_target="tpu_custom_call" | custom-call | flops 2000000000 | bytes 5000000 | tf_op jit(solution)/shard_map/conv1_own/pallas_call | solution.py:182
  55.9 2.0 %collective-permute-done.1.recv = bf16[8,54,16,256]{3,2,1,0:T(8,128)(2,1)S(1)} collective-permute-done((bf16[8,54,16,256]{3,2,1,0:T(8,128)(2,1)S(1)}, bf16[8,54,16,256]{3,2,1,0:T(8,128)(2,1)S(1)}, u32[]{:S(2)}, u32[]{:S(2)}) %collective-permute-start.1) | collective-permute-done | bytes 3538976 | tf_op jit(solution)/shard_map/ppermute | solution.py:576
  57.9 4.6 %conv1.1 = (f32[1152,256]{1,0:T(8,128)S(1)}, bf16[3,7,7,16,256]{4,3,2,1,0:T(8,128)(2,1)S(1)}, bf16[3,7,7,16,128]{4,3,2,1,0:T(8,128)(2,1)S(1)}) custom-call(s32[1]{0:T(128)} %bitcast.2.core_ref, bf16[3,8,8,32,128]{4,3,2,1,0:T(8,128)(2,1)S(1)} %copy-done.16, bf16[8,54,16,256]{3,2,1,0:T(8,128)(2,1)S(1)} %collective-permute-done.1.recv, ...), custom_call_target="tpu_custom_call" | custom-call | flops 2000000000 | bytes 7000000 | tf_op jit(solution)/shard_map/conv1/pallas_call | solution.py:213
  62.5 0.2 collective-permute-start.3
  62.7 0.0 copy-done.8
  62.7 2.2 %conv2.1 = (bf16[3,3,3,4,256]{4,3,2,1,0:T(4,128)(2,1)}, bf16[144,256]{1,0:T(8,128)(2,1)S(1)}, bf16[256,144]{1,0:T(8,128)(2,1)S(1)}) custom-call(f32[144,256]{1,0:T(8,128)S(1)} %copy-done.7, f32[144,256]{1,0:T(8,128)S(1)} %copy-done.8, bf16[3,7,7,16,256]{4,3,2,1,0:T(8,128)(2,1)S(1)} %get-tuple-element.42.hsel, bf16[8,54,16,256]{3,2,1,0:T(8,128)(2,1)S(1)} %all_to_all.25.mine, ...), custom_call_target="tpu_custom_call" | custom-call | flops 1500000000 | bytes 6000000 | tf_op jit(solution)/shard_map/conv2/pallas_call | solution.py:261
  64.9 0.0 copy-done.3
  64.9 0.0 copy-start.9
  64.9 0.5 collective-permute-start.2
  65.3 1.0 collective-permute-done.2.grad_t_other
  66.3 0.0 collective-permute-done.3.hsel_other
  66.3 3.3 %grad2.1 = bf16[8,27,16,256]{3,2,1,0:T(8,128)(2,1)S(1)} custom-call(bf16[256,144]{1,0:T(8,128)(2,1)S(1)} %get-tuple-element.45.grad_t, bf16[256,144]{1,0:T(8,128)(2,1)S(1)} %collective-permute-done.2.grad_t_other, bf16[3,7,7,16,256]{4,3,2,1,0:T(8,128)(2,1)S(1)} %get-tuple-element.42.hsel, bf16[3,7,7,16,128]{4,3,2,1,0:T(8,128)(2,1)S(1)} %collective-permute-done.3.hsel_other), custom_call_target="tpu_custom_call" | custom-call | flops 1000000000 | bytes 4000000 | tf_op jit(solution)/shard_map/grad2/pallas_call | solution.py:390
  69.7 1.2 copy-done.2
  70.9 4.5 %all-to-all-start.3 = ((bf16[8,27,16,256]{3,2,1,0:T(8,128)(2,1)}), bf16[8,27,16,256]{3,2,1,0:T(8,128)(2,1)}, u32[]{:S(2)}, u32[]{:S(2)}) async-start(bf16[8,27,16,256]{3,2,1,0:T(8,128)(2,1)} %copy-done.2), calls=%async_computation.3 | async-start | bytes 3538944 | tf_op jit(solution)/shard_map/all_to_all | solution.py:572
  75.4 0.0 copy-start.1
  75.4 2.0 %copy-done.1 = bf16[8,54,16,256]{3,2,1,0:T(8,128)(2,1)S(1)} copy-done((bf16[8,54,16,256]{3,2,1,0:T(8,128)(2,1)S(1)}, bf16[8,54,16,256]{3,2,1,0:T(8,128)(2,1)}, u32[]{:S(2)}) %copy-start.1) | copy-done | bytes 3538968
  77.4 1.3 copy-done.4
  78.7 0.9 copy-done.10
  79.6 3.0 %back.1.gat = bf16[256,1152]{1,0:T(8,128)(2,1)S(1)} custom-call(s32[1]{0:T(128)} %bitcast.2.core_ref, f32[1152,256]{1,0:T(8,128)S(1)} %copy-done.4, bf16[144,256]{1,0:T(8,128)(2,1)S(1)} %copy-done.10, bf16[8,54,16,256]{3,2,1,0:T(8,128)(2,1)S(1)} %all_to_all.25.mine, bf16[8,54,16,256]{3,2,1,0:T(8,128)(2,1)S(1)} %copy-done.1), custom_call_target="tpu_custom_call" | custom-call | flops 1500000000 | bytes 8000000 | tf_op jit(solution)/shard_map/back/pallas_call | solution.py:319
  82.6 0.6 collective-permute-start.4
  83.2 1.6 %collective-permute-done.4.gat_other = bf16[256,1152]{1,0:T(8,128)(2,1)S(1)} collective-permute-done((bf16[256,1152]{1,0:T(8,128)(2,1)S(1)}, bf16[256,1152]{1,0:T(8,128)(2,1)S(1)}, u32[]{:S(2)}, u32[]{:S(2)}) %collective-permute-start.4) | collective-permute-done | bytes 589856 | tf_op jit(solution)/shard_map/ppermute | solution.py:576
  84.9 7.5 %grad1.1 = bf16[8,27,16,256]{3,2,1,0:T(8,128)(2,1)} custom-call(bf16[256,1152]{1,0:T(8,128)(2,1)S(1)} %back.1.gat, bf16[256,1152]{1,0:T(8,128)(2,1)S(1)} %collective-permute-done.4.gat_other, bf16[3,8,8,32,128]{4,3,2,1,0:T(8,128)(2,1)S(1)} %copy-done.18, bf16[3,8,8,32,128]{4,3,2,1,0:T(8,128)(2,1)S(1)} %copy-done.19), custom_call_target="tpu_custom_call" | custom-call | flops 4000000000 | bytes 7000000 | tf_op jit(solution)/shard_map/grad1/pallas_call | solution.py:410
  92.3 0.0 all-to-all-done.3.parts
  92.3 5.3 %all-to-all-start.2 = ((bf16[8,27,16,256]{3,2,1,0:T(8,128)(2,1)}), bf16[8,27,16,256]{3,2,1,0:T(8,128)(2,1)S(1)}, u32[]{:S(2)}, u32[]{:S(2)}) async-start(bf16[8,27,16,256]{3,2,1,0:T(8,128)(2,1)} %grad1.1), calls=%async_computation.2 | async-start | bytes 3538944 | tf_op jit(solution)/shard_map/all_to_all | solution.py:572
  97.6 1.8 %collect2.1.second = f32[2,432,128]{2,1,0:T(8,128)S(1)} custom-call(bf16[8,27,16,256]{3,2,1,0:T(8,128)(2,1)} %all-to-all-done.3.parts), custom_call_target="tpu_custom_call" | custom-call | flops 1000000 | bytes 3000000 | tf_op jit(solution)/shard_map/collect2/pallas_call | solution.py:467
  99.5 0.0 copy-start.5
  99.5 0.0 copy-start.6
  99.5 0.0 copy-start.11
  99.5 0.0 copy-start.12
  99.5 0.0 copy-start.13
  99.5 0.0 copy-start.14
  99.6 0.0 copy-start.15
  99.6 14.4 %all-to-all-done.2.parts = bf16[8,27,16,256]{3,2,1,0:T(8,128)(2,1)S(1)} async-done(((bf16[8,27,16,256]{3,2,1,0:T(8,128)(2,1)}), bf16[8,27,16,256]{3,2,1,0:T(8,128)(2,1)S(1)}, u32[]{:S(2)}, u32[]{:S(2)}) %all-to-all-start.2) | async-done | bytes 1769504 | tf_op jit(solution)/shard_map/all_to_all | solution.py:572
  113.9 0.7 collect.1
  114.6 14.0 %all_to_all.26.parts = bf16[8,54,512]{2,1,0:T(8,128)(2,1)S(1)} all-to-all(bf16[8,54,512]{2,1,0:T(8,128)(2,1)S(1)} %collect.1), channel_id=1, replica_groups={{0,2,4,6,16,18,20,22},{8,10,12,14,24,26,28,30},{32,34,36,38,48,50,52,54..., dimensions={0} | all-to-all | bytes 884736 | tf_op jit(solution)/shard_map/all_to_all | solution.py:572
  128.6 1.3 adam.1
  (25 shorter events, 0.0 us)
Async XLA Ops:
  0.6 11.2 %collective-permute-start = (bf16[6,6,6,4,256]{4,3,2,1,0:T(4,128)(2,1)}, bf16[6,6,6,4,256]{4,3,2,1,0:T(4,128)(2,1)S(1)}, u32[]{:S(2)}, u32[]{:S(2)}) collective-permute-start(bf16[6,6,6,4,256]{4,3,2,1,0:T(4,128)(2,1)} %bitcast.4), channel_id=1, source_target_pairs={{0,1},{1,0},{2,3},{3,2},{4,5},{5,4},{6,7},{7,6},{8,9},{9,8},{10,11... | collective-permute-start | bytes 1327112 | tf_op jit(solution)/shard_map/ppermute | solution.py:576
  2.5 19.3 %all-to-all-start = ((bf16[8,54,512]{2,1,0:T(8,128)(2,1)}), bf16[8,54,512]{2,1,0:T(8,128)(2,1)S(1)}, u32[]{:S(2)}, u32[]{:S(2)}) async-start(bf16[8,54,512]{2,1,0:T(8,128)(2,1)} %pack.1), calls=%async_computation | async-start | bytes 917504 | tf_op jit(solution)/shard_map/all_to_all | solution.py:572
  11.8 0.8 copy-start.20
  22.7 29.0 %copy-start.17 = (bf16[3,8,8,32,128]{4,3,2,1,0:T(8,128)(2,1)S(1)}, bf16[3,8,8,32,128]{4,3,2,1,0:T(8,128)(2,1)}, u32[]{:S(2)}) copy-start(bf16[3,8,8,32,128]{4,3,2,1,0:T(8,128)(2,1)} %get-tuple-element.41.x3a) | copy-start | bytes 4718596
  51.6 6.2 %copy-start.16 = (bf16[3,8,8,32,128]{4,3,2,1,0:T(8,128)(2,1)S(1)}, bf16[3,8,8,32,128]{4,3,2,1,0:T(8,128)(2,1)}, u32[]{:S(2)}) copy-start(bf16[3,8,8,32,128]{4,3,2,1,0:T(8,128)(2,1)} %get-tuple-element.39.x3b) | copy-start | bytes 4718596
  51.6 6.2 %collective-permute-start.1 = (bf16[8,54,16,256]{3,2,1,0:T(8,128)(2,1)S(1)}, bf16[8,54,16,256]{3,2,1,0:T(8,128)(2,1)S(1)}, u32[]{:S(2)}, u32[]{:S(2)}) collective-permute-start(bf16[8,54,16,256]{3,2,1,0:T(8,128)(2,1)S(1)} %all_to_all.25.mine), channel_id=1, source_target_pairs={{0,1},{1,0},{2,3},{3,2},{4,5},{5,4},{6,7},{7,6},{8,9},{9,8},{10,11... | collective-permute-start | bytes 10616840 | tf_op jit(solution)/shard_map/ppermute | solution.py:576
  57.9 4.8 %copy-start = (bf16[8,54,16,256]{3,2,1,0:T(8,128)(2,1)}, bf16[8,54,16,256]{3,2,1,0:T(8,128)(2,1)S(1)}, u32[]{:S(2)}) copy-start(bf16[8,54,16,256]{3,2,1,0:T(8,128)(2,1)S(1)} %collective-permute-done.1.recv) | copy-start | bytes 10616836
  57.9 4.8 %copy-start.7 = (f32[144,256]{1,0:T(8,128)S(1)}, f32[144,256]{1,0:T(8,128)}, u32[]{:S(2)}) copy-start(f32[144,256]{1,0:T(8,128)} %get-tuple-element.37.skip) | copy-start | bytes 442372
  57.9 4.8 %copy-start.8 = (f32[144,256]{1,0:T(8,128)S(1)}, f32[144,256]{1,0:T(8,128)}, u32[]{:S(2)}) copy-start(f32[144,256]{1,0:T(8,128)} %get-tuple-element.38.cot) | copy-start | bytes 442372
  62.4 2.4 %copy-start.3 = (f32[1152,256]{1,0:T(8,128)}, f32[1152,256]{1,0:T(8,128)S(1)}, u32[]{:S(2)}) copy-start(f32[1152,256]{1,0:T(8,128)S(1)} %get-tuple-element.44.act_far) | copy-start | bytes 3538948
  62.5 3.9 %collective-permute-start.3 = (bf16[3,7,7,16,128]{4,3,2,1,0:T(8,128)(2,1)S(1)}, bf16[3,7,7,16,128]{4,3,2,1,0:T(8,128)(2,1)S(1)}, u32[]{:S(2)}, u32[]{:S(2)}) collective-permute-start(bf16[3,7,7,16,128]{4,3,2,1,0:T(8,128)(2,1)S(1)} %get-tuple-element.46), channel_id=1, source_target_pairs={{0,1},{1,0},{2,3},{3,2},{4,5},{5,4},{6,7},{7,6},{8,9},{9,8},{10,11... | collective-permute-start | bytes 1806344 | tf_op jit(solution)/shard_map/ppermute | solution.py:576
  64.9 4.8 %copy-start.9 = (bf16[144,256]{1,0:T(8,128)(2,1)}, bf16[144,256]{1,0:T(8,128)(2,1)S(1)}, u32[]{:S(2)}) copy-start(bf16[144,256]{1,0:T(8,128)(2,1)S(1)} %get-tuple-element.48.grad_far) | copy-start | bytes 221188
  64.9 1.4 %collective-permute-start.2 = (bf16[256,144]{1,0:T(8,128)(2,1)S(1)}, bf16[256,144]{1,0:T(8,128)(2,1)S(1)}, u32[]{:S(2)}, u32[]{:S(2)}) collective-permute-start(bf16[256,144]{1,0:T(8,128)(2,1)S(1)} %get-tuple-element.45.grad_t), channel_id=1, source_target_pairs={{0,1},{1,0},{2,3},{3,2},{4,5},{5,4},{6,7},{7,6},{8,9},{9,8},{10,11... | collective-permute-start | bytes 221192 | tf_op jit(solution)/shard_map/ppermute | solution.py:576
  69.7 1.2 copy-start.2
  70.9 21.4 %all-to-all-start.3 = ((bf16[8,27,16,256]{3,2,1,0:T(8,128)(2,1)}), bf16[8,27,16,256]{3,2,1,0:T(8,128)(2,1)}, u32[]{:S(2)}, u32[]{:S(2)}) async-start(bf16[8,27,16,256]{3,2,1,0:T(8,128)(2,1)} %copy-done.2), calls=%async_computation.3 | async-start | bytes 3538944 | tf_op jit(solution)/shard_map/all_to_all | solution.py:572
  75.4 2.0 %copy-start.1 = (bf16[8,54,16,256]{3,2,1,0:T(8,128)(2,1)S(1)}, bf16[8,54,16,256]{3,2,1,0:T(8,128)(2,1)}, u32[]{:S(2)}) copy-start(bf16[8,54,16,256]{3,2,1,0:T(8,128)(2,1)} %copy-done) | copy-start | bytes 10616836
  77.4 1.3 copy-start.4
  78.7 0.9 copy-start.10
  79.6 5.3 %copy-start.18 = (bf16[3,8,8,32,128]{4,3,2,1,0:T(8,128)(2,1)S(1)}, bf16[3,8,8,32,128]{4,3,2,1,0:T(8,128)(2,1)}, u32[]{:S(2)}) copy-start(bf16[3,8,8,32,128]{4,3,2,1,0:T(8,128)(2,1)} %get-tuple-element.41.x3a) | copy-start | bytes 4718596
  79.6 5.3 %copy-start.19 = (bf16[3,8,8,32,128]{4,3,2,1,0:T(8,128)(2,1)S(1)}, bf16[3,8,8,32,128]{4,3,2,1,0:T(8,128)(2,1)}, u32[]{:S(2)}) copy-start(bf16[3,8,8,32,128]{4,3,2,1,0:T(8,128)(2,1)} %get-tuple-element.49.x3o) | copy-start | bytes 4718596
  82.6 2.2 %collective-permute-start.4 = (bf16[256,1152]{1,0:T(8,128)(2,1)S(1)}, bf16[256,1152]{1,0:T(8,128)(2,1)S(1)}, u32[]{:S(2)}, u32[]{:S(2)}) collective-permute-start(bf16[256,1152]{1,0:T(8,128)(2,1)S(1)} %back.1.gat), channel_id=1, source_target_pairs={{0,1},{1,0},{2,3},{3,2},{4,5},{5,4},{6,7},{7,6},{8,9},{9,8},{10,11... | collective-permute-start | bytes 1769480 | tf_op jit(solution)/shard_map/ppermute | solution.py:576
  92.3 21.6 %all-to-all-start.2 = ((bf16[8,27,16,256]{3,2,1,0:T(8,128)(2,1)}), bf16[8,27,16,256]{3,2,1,0:T(8,128)(2,1)S(1)}, u32[]{:S(2)}, u32[]{:S(2)}) async-start(bf16[8,27,16,256]{3,2,1,0:T(8,128)(2,1)} %grad1.1), calls=%async_computation.2 | async-start | bytes 3538944 | tf_op jit(solution)/shard_map/all_to_all | solution.py:572
  99.5 29.1 %copy-start.5 = (f32[27,512]{1,0:T(8,128)S(1)}, f32[27,512]{1,0:T(8,128)}, u32[]{:S(2)}) copy-start(f32[27,512]{1,0:T(8,128)} %k1.1) | copy-start | bytes 165892
  99.5 29.1 %copy-start.6 = (f32[27,512]{1,0:T(8,128)S(1)}, f32[27,512]{1,0:T(8,128)}, u32[]{:S(2)}) copy-start(f32[27,512]{1,0:T(8,128)} %k2.1) | copy-start | bytes 165892
  99.5 29.1 %copy-start.11 = (f32[27,512]{1,0:T(8,128)S(1)}, f32[27,512]{1,0:T(8,128)}, u32[]{:S(2)}) copy-start(f32[27,512]{1,0:T(8,128)} %m1.1) | copy-start | bytes 165892
  99.5 29.1 %copy-start.12 = (f32[27,512]{1,0:T(8,128)S(1)}, f32[27,512]{1,0:T(8,128)}, u32[]{:S(2)}) copy-start(f32[27,512]{1,0:T(8,128)} %v1.1) | copy-start | bytes 165892
  99.5 29.1 %copy-start.13 = (f32[27,512]{1,0:T(8,128)S(1)}, f32[27,512]{1,0:T(8,128)}, u32[]{:S(2)}) copy-start(f32[27,512]{1,0:T(8,128)} %m2.1) | copy-start | bytes 165892
  99.5 29.1 %copy-start.14 = (f32[27,512]{1,0:T(8,128)S(1)}, f32[27,512]{1,0:T(8,128)}, u32[]{:S(2)}) copy-start(f32[27,512]{1,0:T(8,128)} %v2.1) | copy-start | bytes 165892
  99.6 29.1 %copy-start.15 = (s32[1,256]{1,0:T(1,128)S(1)}, s32[1,256]{1,0:T(1,128)}, u32[]{:S(2)}) copy-start(s32[1,256]{1,0:T(1,128)} %constant.24.order) | copy-start | bytes 3076

commit v5 on v4

v5 whole, which is shorter than its diff:
```python
import functools
import itertools

import jax
import jax.numpy as jnp
import numpy as np
from jax import lax
from jax.experimental import pallas as pl
from jax.experimental.pallas import tpu as pltpu
from jax.sharding import PartitionSpec as P

C = 256
HALF = 128
EDGE = 6
OUTER = 3
TAPS = 27
SAMP = 4
ROWS = 32
ACT_ROWS = EDGE * EDGE * ROWS
PAD_ROWS = 64 * ROWS
OUT_ROWS = 16
PRE_ROWS = 9 * OUT_ROWS
MIB = 1024 * 1024
BF = jnp.bfloat16
F32 = jnp.float32

GROUP = 6
BLOCK = 32
QUARTER = (TAPS, BLOCK, C)

VM = pl.BlockSpec(memory_space=pltpu.VMEM)
SM = pl.BlockSpec(memory_space=pltpu.SMEM)
HB = pl.BlockSpec(memory_space=pltpu.HBM)


def shape(dims, dtype):
    return jax.ShapeDtypeStruct(dims, dtype)


def call(kernel, name, out_shape, in_specs, scratch, mib, flops, moved, out_spec=VM):
    single = not isinstance(out_shape, tuple)
    return pl.pallas_call(
        kernel,
        out_shape=out_shape,
        in_specs=in_specs,
        out_specs=out_spec if single else (out_spec,) * len(out_shape),
        scratch_shapes=scratch,
        compiler_params=pltpu.CompilerParams(vmem_limit_bytes=mib * MIB),
        cost_estimate=pl.CostEstimate(flops=flops, bytes_accessed=moved, transcendentals=0),
        name=name,
    )


def dot(a, b):
    return jnp.dot(a, b, preferred_element_type=F32)


def dot_t(a, b):
    return lax.dot_general(a, b, (((1,), (1,)), ((), ())), preferred_element_type=F32)


def sigmoid(v):
    return 1.0 / (1.0 + jnp.exp(-v))


def load(ref, start, count, stride=1):
    return jnp.concatenate(
        [ref[half, pl.ds(start, count, stride=stride), :] for half in range(2)], axis=1
    )


def store(ref, start, count, value, stride=1):
    for half in range(2):
        ref[half, pl.ds(start, count, stride=stride), :] = value[
            :, half * HALF : (half + 1) * HALF
        ]


def one_hot(order_row):
    return (lax.broadcasted_iota(jnp.int32, (C, C), 0) == order_row).astype(BF)


def fill_cells(source, xs):
    for i in range(EDGE):
        for j in range(EDGE):
            value = source[i, j].astype(F32)
            base = 8 + ((i + 1) * 8 + j + 1) * ROWS + 1
            for l in range(EDGE):
                store(xs, base + l, SAMP, value[l], 8)


def prep_kernel(meta, latent, other, out_grad, orders, x3a, x3b, x3o, skip, cot, xs, og):
    perm = one_hot(orders[meta[0]])
    xs[...] = jnp.zeros_like(xs)
    og[...] = jnp.zeros_like(og)
    fill_cells(latent, xs)
    for qi in range(OUTER):
        for qj in range(OUTER):
            q = (qi * 3 + qj) * OUT_ROWS
            value = out_grad[qi, qj].astype(F32)
            for ql in range(OUTER):
                store(og, q + ql, SAMP, value[ql], 4)
            base = 8 + ((2 * qi + 1) * 8 + 2 * qj + 1) * ROWS + 1
            skip[q : q + OUT_ROWS, :] = load(xs, base, OUT_ROWS, 2)
    cot[...] = load(og, 0, PRE_ROWS)
    for i in range(8):
        for dl in range(3):
            rows = dot(load(xs, 7 + dl + i * 256, 256).astype(BF), perm).astype(BF)
            x3a[dl, i] = rows[:, :HALF].reshape(8, ROWS, HALF)
            x3b[dl, i] = rows[:, HALF:].reshape(8, ROWS, HALF)
    fill_cells(other, xs)
    for i in range(8):
        for dl in range(3):
            rows = dot(load(xs, 7 + dl + i * 256, 256).astype(BF), perm[:, :HALF])
            x3o[dl, i] = rows.astype(BF).reshape(8, ROWS, HALF)


def prep(meta, latent, other, out_grad, orders):
    wide = shape((3, 8, 8, ROWS, HALF), BF)
    pre = shape((PRE_ROWS, C), F32)
    return call(
        prep_kernel, "prep", (wide, wide, wide, pre, pre), [SM] + [VM] * 4,
        [pltpu.VMEM((2, PAD_ROWS + 16, HALF), F32), pltpu.VMEM((2, PRE_ROWS, HALF), F32)],
        20, 2_000_000_000, 8_000_000,
    )(meta, latent, other, out_grad, orders)


def swap_halves(value, core):
    swapped = jnp.concatenate([value[:, HALF:], value[:, :HALF]], axis=1)
    return jnp.where(core == 1, swapped, value)


def cell_mask():
    cell = lax.broadcasted_iota(jnp.int32, (EDGE * ROWS, C), 0) % 8
    return (cell >= 1) & (cell <= EDGE)


def fetch_weights(quarters, place_of, weights, sems):
    copies = []
    for di in range(3):
        part = pl.ds(9 * di, 9)
        for k, source in enumerate(quarters):
            copies.append(
                pltpu.make_async_copy(
                    source.at[part],
                    weights.at[jnp.bitwise_xor(place_of, k), part],
                    sems.at[4 * di + k],
                )
            )
            copies[-1].start()
    return [copies[4 * di : 4 * di + 4] for di in range(3)]


def wait_all(copies):
    for copy in copies:
        copy.wait()


def half_weight(weights, t):
    return weights[:, t].reshape(HALF, C)


HALF_WEIGHTS = [pltpu.VMEM((4, *QUARTER), BF), pltpu.SemaphoreType.DMA((12,))]
WEIGHTS = HALF_WEIGHTS + HALF_WEIGHTS


def half_conv(x3, weights, copies, act, start):
    for first in range(0, TAPS, GROUP):
        taps = range(first, min(first + GROUP, TAPS))
        for di in range(3):
            if first <= 9 * di < first + GROUP or (first, di) == (0, 0):
                wait_all(copies[di])
        windows = [
            x3[t % 3, t // 9 : t // 9 + EDGE, t // 3 % 3 : t // 3 % 3 + EDGE] for t in taps
        ]
        total = dot(
            jnp.concatenate([window.reshape(ACT_ROWS, HALF) for window in windows], axis=1),
            jnp.concatenate([half_weight(weights, t) for t in taps], axis=0),
        )
        before = act if first else start
        act[...] = total if before is None else before[...] + total


def conv1_own_kernel(meta, x3a, q0, q1, q2, q3, act, weights, sems):
    copies = fetch_weights((q0, q1, q2, q3), meta[1], weights, sems)
    half_conv(x3a, weights, copies, act, None)


def conv1_own(meta, x3a, own):
    return call(
        conv1_own_kernel, "conv1_own", shape((ACT_ROWS, C), F32), [SM, VM] + [HB] * 4,
        HALF_WEIGHTS, 12, 2_000_000_000, 5_000_000,
    )(meta, x3a, *own)


def conv1_kernel(meta, x3b, part_act, q0, q1, q2, q3, act, hsel, hsend, weights, sems, hs):
    core = meta[0]
    copies = fetch_weights((q0, q1, q2, q3), meta[2], weights, sems)
    half_conv(x3b, weights, copies, act, part_act)

    hsel[:, 0] = jnp.zeros_like(hsel[:, 0])
    hsel[:, :, 0] = jnp.zeros_like(hsel[:, :, 0])
    hsend[:, 0] = jnp.zeros_like(hsend[:, 0])
    hsend[:, :, 0] = jnp.zeros_like(hsend[:, :, 0])
    store(hs, ACT_ROWS, 8, jnp.zeros((8, C), F32))
    inside = cell_mask()
    for i in range(EDGE):
        part = pl.ds(i * EDGE * ROWS, EDGE * ROWS)
        value = swap_halves(act[part, :], core)
        act[part, :] = value
        hidden = jnp.where(inside, value * sigmoid(value), 0.0)
        store(hs, i * EDGE * ROWS, EDGE * ROWS, hidden.astype(BF).astype(F32))
    for dl in range(3):
        for i in range(EDGE):
            rows = load(hs, i * EDGE * ROWS + dl, EDGE * OUT_ROWS, 2)
            rows = rows.astype(BF).reshape(EDGE, OUT_ROWS, C)
            hsel[dl, i + 1, 1:] = rows
            hsend[dl, i + 1, 1:] = rows[..., HALF:]


def conv1(meta, x3b, part_act, other):
    return call(
        conv1_kernel, "conv1",
        (
            shape((ACT_ROWS, C), F32),
            shape((3, 7, 7, OUT_ROWS, C), BF),
            shape((3, 7, 7, OUT_ROWS, HALF), BF),
        ),
        [SM, VM, VM] + [HB] * 4,
        HALF_WEIGHTS + [pltpu.VMEM((2, ACT_ROWS + 8, HALF), F32)],
        24, 2_000_000_000, 7_000_000,
    )(meta, x3b, part_act, *other)


def weight(wa, wb, t):
    return jnp.concatenate([half_weight(wa, t), half_weight(wb, t)], axis=0)


def strided_window(hsel, dl, di, dj, lanes=slice(None)):
    blocks = [
        hsel[dl, 2 * qi + di, 2 * qj + dj, :, lanes] for qi in range(OUTER) for qj in range(OUTER)
    ]
    return jnp.concatenate(blocks, axis=0)


def conv2_kernel(
    meta, skip, cot, hsel, q0, q1, q2, q3, p0, p1, p2, p3,
    block_out, grad_pre, grad_pre_t, wa, sa, wb, sb, bo,
):
    halves = (
        fetch_weights((q0, q1, q2, q3), meta[1], wa, sa),
        fetch_weights((p0, p1, p2, p3), meta[2], wb, sb),
    )
    pre = skip[...]
    for di in range(3):
        for copies in halves:
            wait_all(copies[di])
        for dj in range(3):
            for dl in range(3):
                pre = pre + dot(
                    strided_window(hsel, dl, di, dj), weight(wa, wb, di * 9 + dj * 3 + dl)
                )
    sigma = sigmoid(pre)
    store(bo, 0, PRE_ROWS, pre * sigma)
    for qi in range(OUTER):
        for qj in range(OUTER):
            for ql in range(OUTER):
                base = (qi * 3 + qj) * OUT_ROWS + ql
                block_out[qi, qj, ql] = load(bo, base, SAMP, 4).astype(BF)
    grad = (cot[...] * (sigma * (1.0 + pre * (1.0 - sigma)))).astype(BF)
    grad_pre[...] = grad
    grad_pre_t[...] = grad.astype(F32).T.astype(BF)


def conv2(meta, skip, cot, hsel, own, other):
    return call(
        conv2_kernel, "conv2",
        (
            shape((OUTER, OUTER, OUTER, SAMP, C), BF),
            shape((PRE_ROWS, C), BF),
            shape((C, PRE_ROWS), BF),
        ),
        [SM, VM, VM, VM] + [HB] * 8,
        WEIGHTS + [pltpu.VMEM((2, PRE_ROWS, HALF), F32)],
        16, 1_500_000_000, 6_000_000,
    )(meta, skip, cot, hsel, *own, *other)


def back_kernel(
    meta, act_far, grad_far, q0, q1, q2, q3, p0, p1, p2, p3,
    gat, wa, sa, wb, sb, y, gh, act, grad_pre, sems,
):
    core = meta[0]
    fetch_grad = pltpu.make_async_copy(grad_far, grad_pre, sems.at[0])
    fetch_act = pltpu.make_async_copy(act_far, act, sems.at[1])
    fetch_grad.start()
    halves = (
        fetch_weights((q0, q1, q2, q3), meta[1], wa, sa),
        fetch_weights((p0, p1, p2, p3), meta[2], wb, sb),
    )
    fetch_act.start()
    y[...] = jnp.zeros_like(y)
    fetch_grad.wait()
    grad = grad_pre[...]
    for di in range(3):
        for copies in halves:
            wait_all(copies[di])
        for dj in range(3):
            for dl in range(3):
                term = dot_t(grad, weight(wa, wb, di * 9 + dj * 3 + dl))
                term = term.reshape(9, OUT_ROWS, C)
                for qi in range(OUTER):
                    for qj in range(OUTER):
                        y[dl, 2 * qi + di, 2 * qj + dj] += term[qi * 3 + qj]
    store(gh, ACT_ROWS, 8, jnp.zeros((8, C), F32))
    count = EDGE * OUT_ROWS
    for i in range(EDGE):
        base = i * EDGE * ROWS
        store(gh, base, count, y[0, i + 1, 1:].reshape(count, C), 2)
        store(gh, base + 1, count, y[1, i + 1, 1:].reshape(count, C), 2)
    for i in range(EDGE):
        base = i * EDGE * ROWS + 2
        total = load(gh, base, count, 2) + y[2, i + 1, 1:].reshape(count, C)
        store(gh, base, count, total, 2)
    inside = cell_mask()
    fetch_act.wait()
    for i in range(EDGE):
        value = act[pl.ds(i * EDGE * ROWS, EDGE * ROWS), :]
        sigma = sigmoid(value)
        part = load(gh, i * EDGE * ROWS, EDGE * ROWS) * (sigma * (1.0 + value * (1.0 - sigma)))
        part = swap_halves(jnp.where(inside, part, 0.0), core)
        store(gh, i * EDGE * ROWS, EDGE * ROWS, part)
    for n in range(ACT_ROWS // HALF):
        gat[:, n * HALF : (n + 1) * HALF] = load(gh, n * HALF, HALF).T.astype(BF)


def back(meta, act, grad_pre, own, other):
    return call(
        back_kernel, "back", shape((C, ACT_ROWS), BF),
        [SM, HB, HB] + [HB] * 8,
        WEIGHTS
        + [
            pltpu.VMEM((3, 7, 7, OUT_ROWS, C), F32),
            pltpu.VMEM((2, ACT_ROWS + 8, HALF), F32),
            pltpu.VMEM((ACT_ROWS, C), F32),
            pltpu.VMEM((PRE_ROWS, C), BF),
            pltpu.SemaphoreType.DMA((2,)),
        ],
        20, 1_500_000_000, 8_000_000,
    )(meta, act, grad_pre, *own, *other)


def grad_loop(place_of, far, out, sems, left, windows):
    eye = (
        lax.broadcasted_iota(jnp.int32, (C, C), 0) == lax.broadcasted_iota(jnp.int32, (C, C), 1)
    ).astype(BF)

    def send(n, count):
        part = pl.ds(GROUP * n, count)
        return [
            pltpu.make_async_copy(
                out.at[jnp.bitwise_xor(place_of, k), part], quarter.at[part], sems.at[n, k]
            )
            for k, quarter in enumerate(far)
        ]

    def product(taps):
        right = [
            jnp.concatenate([window(t // 9, t // 3 % 3, t % 3) for t in taps], axis=1)
            for window in windows
        ]
        total = dot(left[...], jnp.concatenate(right, axis=0)).astype(BF)
        for n in range(0, len(taps), 2):
            two = taps[n : n + 2]
            width = HALF * len(two)
            turned = dot_t(eye[:width, :width], total[:, n * HALF : n * HALF + width]).astype(BF)
            for m, t in enumerate(two):
                out[:, t] = turned[m * HALF : (m + 1) * HALF].reshape(4, BLOCK, C)

    def step(n, carry):
        product([GROUP * n + k for k in range(GROUP)])
        for copy in send(n, GROUP):
            copy.start()
        return carry

    whole = TAPS // GROUP
    lax.fori_loop(0, whole, step, 0)
    product(list(range(GROUP * whole, TAPS)))
    for copy in send(whole, TAPS - GROUP * whole):
        copy.start()
    for n in range(whole):
        wait_all(send(n, GROUP))
    wait_all(send(whole, TAPS - GROUP * whole))


QUARTERS = (shape(QUARTER, BF),) * 4
STAGING = [pltpu.VMEM((4, *QUARTER), BF), pltpu.SemaphoreType.DMA((-(-TAPS // GROUP), 4))]


def grad2_kernel(
    meta, grad_t, grad_t_other, hsel, hsel_other, f0, f1, f2, f3, out, sems, left
):
    left[:, :PRE_ROWS] = grad_t[...]
    left[:, PRE_ROWS:] = grad_t_other[...]
    grad_loop(
        meta[1],
        (f0, f1, f2, f3),
        out,
        sems,
        left,
        (
            lambda di, dj, dl: strided_window(hsel, dl, di, dj, slice(0, HALF)),
            lambda di, dj, dl: strided_window(hsel_other, dl, di, dj),
        ),
    )


def grad2(meta, grad_t, grad_t_other, hsel, hsel_other):
    return call(
        grad2_kernel, "grad2", QUARTERS, [SM] + [VM] * 4,
        STAGING + [pltpu.VMEM((C, 2 * PRE_ROWS), BF)], 12, 1_000_000_000, 4_000_000, HB,
    )(meta, grad_t, grad_t_other, hsel, hsel_other)


def same_window(x3):
    def window(di, dj, dl):
        return x3[dl, pl.ds(di, EDGE), pl.ds(dj, EDGE)].reshape(ACT_ROWS, HALF)

    return window


def grad1_kernel(meta, gat, gat_other, x3a, x3o, f0, f1, f2, f3, out, sems, left):
    left[:, :ACT_ROWS] = gat[...]
    left[:, ACT_ROWS:] = gat_other[...]
    windows = (same_window(x3a), same_window(x3o))
    grad_loop(meta[1], (f0, f1, f2, f3), out, sems, left, windows)


def grad1(meta, gat, gat_other, x3a, x3o):
    return call(
        grad1_kernel, "grad1", QUARTERS, [SM] + [VM] * 4,
        STAGING + [pltpu.VMEM((C, 2 * ACT_ROWS), BF)], 16, 4_000_000_000, 7_000_000, HB,
    )(meta, gat, gat_other, x3a, x3o)


SHARD = (2 * TAPS, 2 * C)
FOUR = (4, *SHARD)


def pack_kernel(first, second, orders, out):
    perm = one_hot(orders[0])
    for i in range(2):
        lanes = slice(i * C, (i + 1) * C)
        one = dot(first[:, lanes].astype(BF), perm)
        out[:, lanes] = jnp.concatenate([one, second[:, lanes]], axis=0).astype(BF)


def pack(first, second, orders):
    return call(
        pack_kernel, "pack", shape(SHARD, BF), [VM] * 3, [], 56, 10_000_000, 300_000
    )(first, second, orders)


def join_kernel(meta, p0, p1, p2, p3, out):
    for k, part in enumerate((p0, p1, p2, p3)):
        out[jnp.bitwise_xor(meta[3], k)] = part[...]


def join(meta, parts):
    return call(
        join_kernel, "join", shape(FOUR, BF), [SM] + [VM] * 4, [], 4, 100_000, 500_000
    )(meta, *parts)


def spread_kernel(meta, p0, p1, p2, p3, out1, out2, stage, wide):
    for k, part in enumerate((p0, p1, p2, p3)):
        stage[jnp.bitwise_xor(meta[2], k)] = part[...]
    for m in range(4):
        for n in range(4):
            rows = stage[m, n].astype(F32)
            for i in range(2):
                start = 8 * m + 2 * n + i
                store(wide, start, 2 * TAPS, rows[:, i * C : (i + 1) * C], BLOCK)

    def step(t, carry):
        for k, out in enumerate((out1, out2)):
            start = pl.multiple_of((k * TAPS + t) * BLOCK, BLOCK)
            out[t] = load(wide, start, BLOCK).astype(BF)
        return carry

    lax.fori_loop(0, TAPS, step, 0)


def spread(meta, parts):
    return call(
        spread_kernel, "spread", (shape(QUARTER, BF),) * 2, [SM] + [VM] * 4,
        [pltpu.VMEM((4, *FOUR), BF), pltpu.VMEM((2, 2 * TAPS * BLOCK, HALF), F32)],
        8, 1_000_000, 2_000_000,
    )(meta, *parts)


def add_parts(p0, p1, p2, p3, wide):
    def step(t, carry):
        total = p0[t].astype(F32)
        for part in (p1, p2, p3):
            total = total + part[t].astype(F32)
        store(wide, pl.multiple_of(t * BLOCK, BLOCK), BLOCK, total)
        return carry

    lax.fori_loop(0, TAPS, step, 0)


def collect2(parts):
    return call(
        add_parts, "collect2", shape((2, TAPS * BLOCK, HALF), F32), [VM] * 4, [],
        4, 1_000_000, 3_000_000,
    )(*parts)


def collect_kernel(meta, p0, p1, p2, p3, second, f0, f1, f2, f3, wide, stage, sems):
    wide[:, TAPS * BLOCK :] = second[...]
    add_parts(p0, p1, p2, p3, wide)
    copies = []
    for k, far in enumerate((f0, f1, f2, f3)):
        m = jnp.bitwise_xor(meta[2], k)
        copies.append(pltpu.make_async_copy(stage.at[m], far, sems.at[k]))
    for m in range(4):
        for n in range(4):
            for i in range(2):
                rows = load(wide, 8 * m + 2 * n + i, 2 * TAPS, BLOCK)
                stage[m, n, :, i * C : (i + 1) * C] = rows.astype(BF)
    for copy in copies:
        copy.start()
    wait_all(copies)


def collect(meta, parts, second):
    return call(
        collect_kernel, "collect", (shape(FOUR, BF),) * 4, [SM] + [VM] * 5,
        [
            pltpu.VMEM((2, 2 * TAPS * BLOCK, HALF), F32),
            pltpu.VMEM((4, *FOUR), BF),
            pltpu.SemaphoreType.DMA((4,)),
        ],
        8, 1_000_000, 3_000_000, HB,
    )(meta, *parts, second)


def divide_kernel(meta, p0, p1, p2, p3, f0, f1, f2, f3):
    for k, far in enumerate((f0, f1, f2, f3)):
        n = jnp.bitwise_xor(meta[3], k)
        total = p0[n].astype(F32)
        for part in (p1, p2, p3):
            total = total + part[n].astype(F32)
        far[...] = total.astype(BF)


def divide(meta, parts):
    return call(
        divide_kernel, "divide", (shape(SHARD, BF),) * 4, [SM] + [VM] * 4, [],
        4, 1_000_000, 1_000_000,
    )(meta, *parts)


def adam_update(weight, first, second, grad):
    first_new = 0.9 * first + 0.1 * grad
    second_new = 0.999 * second + 0.001 * grad * grad
    fix_first = 1.0 - 0.9**10
    fix_second = 1.0 - 0.999**10
    weight_new = weight - 0.05 * (first_new / fix_first) / (
        jnp.sqrt(second_new / fix_second) + 1e-08
    )
    return (weight_new, first_new, second_new)


def adam_kernel(
    scale, p0, p1, p2, p3, orders, k1, m1, v1, k2, m2, v2, k1n, m1n, v1n, k2n, m2n, v2n
):
    back = one_hot(orders[0]).astype(F32)
    for i in range(2):
        lanes = slice(i * C, (i + 1) * C)
        total = p0[:, lanes].astype(F32)
        for part in (p1, p2, p3):
            total = total + part[:, lanes].astype(F32)
        total = total * scale
        grad = lax.dot_general(
            total[:TAPS],
            back,
            (((1,), (1,)), ((), ())),
            precision=lax.Precision.HIGHEST,
            preferred_element_type=F32,
        )
        k1n[:, lanes], m1n[:, lanes], v1n[:, lanes] = adam_update(
            k1[:, lanes], m1[:, lanes], v1[:, lanes], grad
        )
        k2n[:, lanes], m2n[:, lanes], v2n[:, lanes] = adam_update(
            k2[:, lanes], m2[:, lanes], v2[:, lanes], total[TAPS:]
        )


def adam(scale, parts, orders, *state):
    return call(
        functools.partial(adam_kernel, scale), "adam",
        (shape((TAPS, 2 * C), F32),) * 6, [VM] * 11, [], 6, 10_000_000, 1_000_000,
    )(*parts, orders, *state)


def place(x, y, z, c):
    return ((x * 4 + y) * 4 + z) * 2 + c


GRAY = [(0, 0), (1, 0), (1, 1), (0, 1)]
RING = {bits: at for at, bits in enumerate(GRAY)}


def label(bits):
    return bits[0] ^ 2 * bits[1] ^ 3 * bits[2]


def device(core, near, far):
    first, second = (near, far) if core == 0 else (far, near)
    return place(*(RING[pair] for pair in zip(first, second)), core)


TRIPLES = list(itertools.product(range(2), repeat=3))
DEVICES = list(itertools.product(range(2), TRIPLES, TRIPLES))


def turned(bits, which):
    return tuple(bit ^ (n in which) for n, bit in enumerate(bits))


def pairs(near=(), far=()):
    return [
        (device(c, u, v), device(c, turned(u, near), turned(v, far))) for c, u, v in DEVICES
    ]


EVERY = (0, 1, 2)
FIRST_ROUND = [pairs(far=EVERY), pairs(near=EVERY), pairs(near=EVERY, far=EVERY)]
SECOND_ROUND = [pairs(far=(k,)) for k in range(3)]
THIRD_ROUND = [pairs(near=(k,)) for k in range(3)]
PARTNERS = [(n, n ^ 1) for n in range(128)]


def tables():
    meta = np.zeros((128, 8), np.int32)
    at = {}
    for c, u, v in DEVICES:
        row = (c, label(u), label(v), 2 * u[2] + v[2])
        meta[device(c, u, v), :4] = row
        at[row] = device(c, u, v)
    halves = [
        [2 * at[(c, l, m, n)] + i for l in range(4) for m in range(4) for n in range(4) for i in range(2)]
        for c in range(2)
    ]
    orders = [halves[0] + halves[1], halves[1] + halves[0]]
    return meta, np.array(orders, np.int32).reshape(2, 1, C)


META, ORDERS = tables()


def swap(value):
    return lax.ppermute(value, "dp", PARTNERS)


def send_round(values, plan):
    return [values[0]] + [lax.ppermute(v, "dp", to) for v, to in zip(values[1:], plan)]


def gather_round(value, plan):
    return send_round([value] * 4, plan)


def after(value, *others):
    return lax.optimization_barrier((value, *others))[0]


def body(latent, out_grad, k1, m1, v1, k2, m2, v2):
    scale = 1.0 / (latent.shape[0] * lax.axis_size("dp"))
    meta = lax.dynamic_index_in_dim(jnp.asarray(META), lax.axis_index("dp"), keepdims=False)
    orders = jnp.asarray(ORDERS)

    shards = gather_round(pack(k1, k2, orders), FIRST_ROUND)
    latent = latent.transpose(1, 2, 3, 0, 4)
    x3a, x3b, x3o, skip, cot = prep(
        meta, latent, swap(latent), out_grad.transpose(1, 2, 3, 0, 4), orders
    )
    own1, own2 = spread(meta, gather_round(join(meta, shards), SECOND_ROUND))
    own1 = gather_round(own1, THIRD_ROUND)
    own2 = gather_round(after(own2, *own1[1:]), THIRD_ROUND)
    other1 = [swap(value) for value in own1]
    other2 = [swap(value) for value in own2]

    act, hsel, hsend = conv1(meta, x3b, conv1_own(meta, x3a, own1), other1)
    hsel_other = swap(hsend)
    block_out, grad_pre, grad_pre_t = conv2(meta, skip, cot, hsel, own2, other2)
    second = grad2(meta, grad_pre_t, swap(grad_pre_t), hsel, hsel_other)
    grad_pre = after(grad_pre, *second)
    second = send_round(second, THIRD_ROUND)
    gat = back(meta, act, grad_pre, own2, other2)
    first = send_round(grad1(meta, gat, swap(gat), x3a, x3o), THIRD_ROUND)
    parts = send_round(collect(meta, first, collect2(second)), SECOND_ROUND)
    parts = send_round(divide(meta, parts), FIRST_ROUND)
    new = adam(scale, parts, orders, k1, m1, v1, k2, m2, v2)
    return (block_out.transpose(3, 0, 1, 2, 4), *new)


def solution(mesh):
    wide = P("dp", None, None, None, None)
    flat = P(None, "dp")
    return jax.shard_map(
        body,
        mesh=mesh,
        in_specs=(wide, wide) + (flat,) * 6,
        out_specs=(wide,) + (flat,) * 6,
        check_vma=False,
    )
```

time: 131 us -> 146 us (1.11)
  blocking collectives: 42.9 us -> 0 us
  starting transfers between devices: 19.2 us -> 46.9 us
  Pallas kernels: 35.8 us -> 58.3 us
  waiting for transfers between devices: 23.6 us -> 37.4 us
  local copies, waits for them, and re-layouts: 6.25 us -> 2.56 us
    all_to_all x2 -> x0, blocking collectives: 42.9 us -> none  [exchange(): lax.all_to_all(value, 'dp', 0, 0, axis_index_groups=groups, tiled=True)]
    ppermute x0 -> x24, starting transfers between devices: none -> 42.4 us  [send_round(): lax.ppermute(v, 'dp', to)]
    ppermute x0 -> x24, waiting for transfers between devices: none -> 35.6 us  [send_round(): lax.ppermute(v, 'dp', to)]
    all_to_all x3 -> x0, waiting for transfers between devices: 19 us -> none  [exchange(): lax.all_to_all(value, 'dp', 0, 0, axis_index_groups=groups, tiled=True)]
    all_to_all x3 -> x0, starting transfers between devices: 17.8 us -> none  [exchange(): lax.all_to_all(value, 'dp', 0, 0, axis_index_groups=groups, tiled=True)]
    pallas_call x9 -> x11, Pallas kernels: 27.8 us -> 42.5 us  [the longest x1 9.87 us: grad1(): call(grad1_kernel, 'grad1', QUARTERS, [SM] + [VM] * 4, STAGING + [pltpu.V...]
    pallas_call x1, Pallas kernels: 2.19 us -> 7.21 us  [conv2(): call(conv2_kernel, 'conv2', (shape((OUTER, OUTER, OUTER, SAMP, C), BF), s...]
    unnamed x42 -> x20, local copies, waits for them, and re-layouts: 6.25 us -> 1.87 us
  transfers between devices with their start and end apart: 8 -> 36, of which waited for: 5 -> 17; matrix products, arithmetic and copies ran while one was open for 1% -> 0% of each run, Pallas kernels for 19% -> 23%
where the time goes in v5:
time: 146 us
  Pallas kernels  58.3 us (40%)
  starting transfers between devices  46.9 us (32%)
  waiting for transfers between devices  37.4 us (26%)
  local copies, waits for them, and re-layouts  2.56 us (2%)
    ppermute x24, starting transfers between devices, send_round(): lax.ppermute(v, 'dp', to)  42.4 us
    ppermute x24, waiting for transfers between devices, send_round(): lax.ppermute(v, 'dp', to)  35.6 us
    pallas_call x1, Pallas kernels, grad1(): call(grad1_kernel, 'grad1', QUARTERS, [SM] + [VM] * 4, STAGING + [pltpu.V...  9.87 us
    pallas_call x1, Pallas kernels, back(): call(back_kernel, 'back', shape((C, ACT_ROWS), BF), [SM, HB, HB] + [HB] *...  8.06 us
    pallas_call x1, Pallas kernels, conv1(): call(conv1_kernel, 'conv1', (shape((ACT_ROWS, C), F32), shape((3, 7, 7, O...  7.34 us
    pallas_call x1, Pallas kernels, conv2(): call(conv2_kernel, 'conv2', (shape((OUTER, OUTER, OUTER, SAMP, C), BF), s...  7.21 us
    pallas_call x1, Pallas kernels, conv1_own(): call(conv1_own_kernel, 'conv1_own', shape((ACT_ROWS, C), F32), [SM, VM] +...  6.98 us
    pallas_call x1, Pallas kernels, grad2(): call(grad2_kernel, 'grad2', QUARTERS, [SM] + [VM] * 4, STAGING + [pltpu.V...  6.18 us
  transfers between devices with their start and end apart: 36, of which 17 were waited for; matrix products, arithmetic and copies ran while one was open for 0% of the time, Pallas kernels for 23%

profile of v5, /device:TPU:0, one launch (start us, length us, event | category | flops | bytes accessed | tf_op | source)
XLA Modules:
  0.0 146.1 jit_solution(8562624625918944475)
XLA Ops:
  0.7 1.7 %pack.1.p0 = bf16[54,512]{1,0:T(8,128)(2,1)} custom-call(f32[27,512]{1,0:T(8,128)} %k1.1, f32[27,512]{1,0:T(8,128)} %k2.1, s32[2,1,256]{2,1,0:T(1,128)} %constant.15.clone.orders), custom_call_target="tpu_custom_call" | custom-call | flops 10000000 | bytes 300000 | tf_op jit(solution)/shard_map/pack/pallas_call | solution.py:459
  2.3 8.8 %collective-permute-start.1 = (bf16[54,512]{1,0:T(8,128)(2,1)}, bf16[54,512]{1,0:T(8,128)(2,1)S(1)}, u32[]{:S(2)}, u32[]{:S(2)}) collective-permute-start(bf16[54,512]{1,0:T(8,128)(2,1)} %pack.1.p0), channel_id=1, source_target_pairs={{0,126},{6,120},{24,102},{30,96},{96,30},{102,24},{120,6},{126,0},... | collective-permute-start | bytes 165896 | tf_op jit(solution)/shard_map/ppermute | solution.py:669
  11.1 3.3 %collective-permute-start.3 = (bf16[54,512]{1,0:T(8,128)(2,1)}, bf16[54,512]{1,0:T(8,128)(2,1)S(1)}, u32[]{:S(2)}, u32[]{:S(2)}) collective-permute-start(bf16[54,512]{1,0:T(8,128)(2,1)} %pack.1.p0), channel_id=1, source_target_pairs={{0,84},{6,82},{24,76},{30,74},{96,52},{102,50},{120,44},{126,42},{... | collective-permute-start | bytes 165896 | tf_op jit(solution)/shard_map/ppermute | solution.py:669
  14.4 0.7 dynamic-slice_bitcast_fusion.meta
  15.1 2.5 %collective-permute-done.2.p2 = bf16[54,512]{1,0:T(8,128)(2,1)S(1)} collective-permute-done((bf16[54,512]{1,0:T(8,128)(2,1)}, bf16[54,512]{1,0:T(8,128)(2,1)S(1)}, u32[]{:S(2)}, u32[]{:S(2)}) %collective-permute-start.2) | collective-permute-done | bytes 55328 | tf_op jit(solution)/shard_map/ppermute | solution.py:669
  17.5 4.3 %collective-permute-done.3.p3 = bf16[54,512]{1,0:T(8,128)(2,1)S(1)} collective-permute-done((bf16[54,512]{1,0:T(8,128)(2,1)}, bf16[54,512]{1,0:T(8,128)(2,1)S(1)}, u32[]{:S(2)}, u32[]{:S(2)}) %collective-permute-start.3) | collective-permute-done | bytes 55328 | tf_op jit(solution)/shard_map/ppermute | solution.py:669
  21.8 0.8 copy-done.2
  23.2 1.0 collective-permute-start.4
  24.2 0.8 collective-permute-start.5
  25.0 2.4 %collective-permute-start.6 = (bf16[4,54,512]{2,1,0:T(8,128)(2,1)S(1)}, bf16[4,54,512]{2,1,0:T(8,128)(2,1)S(1)}, u32[]{:S(2)}, u32[]{:S(2)}) collective-permute-start(bf16[4,54,512]{2,1,0:T(8,128)(2,1)S(1)} %join.1.p0), channel_id=1, source_target_pairs={{0,6},{6,0},{24,30},{30,24},{96,102},{102,96},{120,126},{126,120},... | collective-permute-start | bytes 663560 | tf_op jit(solution)/shard_map/ppermute | solution.py:669
  27.4 3.1 %collective-permute-done.4.p1 = bf16[4,54,512]{2,1,0:T(8,128)(2,1)S(1)} collective-permute-done((bf16[4,54,512]{2,1,0:T(8,128)(2,1)S(1)}, bf16[4,54,512]{2,1,0:T(8,128)(2,1)S(1)}, u32[]{:S(2)}, u32[]{:S(2)}) %collective-permute-start.4) | collective-permute-done | bytes 221216 | tf_op jit(solution)/shard_map/ppermute | solution.py:669
  30.5 0.9 collective-permute-done.5.p2
  31.4 0.8 collective-permute-done.6.p3
  32.2 2.2 %spread.1 = (bf16[27,32,256]{2,1,0:T(8,128)(2,1)S(1)}, bf16[27,32,256]{2,1,0:T(8,128)(2,1)S(1)}) custom-call(s32[8]{0:T(128)S(1)} %dynamic-slice_bitcast_fusion.meta, bf16[4,54,512]{2,1,0:T(8,128)(2,1)S(1)} %join.1.p0, bf16[4,54,512]{2,1,0:T(8,128)(2,1)S(1)} %collective-permute-done.4.p1, bf16[4,54,512]{2,1,0:T(8,128)(2,1)S(1)} %collective-permute-done.5.p2, ...), custom_call_target="tpu_custom_call" | custom-call | flops 1000000 | bytes 2000000 | tf_op jit(solution)/shard_map/spread/pallas_call | solution.py:495
  34.8 0.9 collective-permute-start.8
  35.7 1.0 collective-permute-start.9
  37.2 5.6 %collective-permute-done.7.q1 = bf16[27,32,256]{2,1,0:T(8,128)(2,1)S(1)} collective-permute-done((bf16[27,32,256]{2,1,0:T(8,128)(2,1)S(1)}, bf16[27,32,256]{2,1,0:T(8,128)(2,1)S(1)}, u32[]{:S(2)}, u32[]{:S(2)}) %collective-permute-start.7) | collective-permute-done | bytes 442400 | tf_op jit(solution)/shard_map/ppermute | solution.py:669
  43.1 0.9 collective-permute-done.9.q3
  44.0 1.2 collective-permute-start.14
  45.2 1.7 %collective-permute-start.15 = (bf16[27,32,256]{2,1,0:T(8,128)(2,1)S(1)}, bf16[27,32,256]{2,1,0:T(8,128)(2,1)S(1)}, u32[]{:S(2)}, u32[]{:S(2)}) collective-permute-start(bf16[27,32,256]{2,1,0:T(8,128)(2,1)S(1)} %get-tuple-element.51.q0), channel_id=1, source_target_pairs={{0,8},{6,14},{24,16},{30,22},{96,104},{102,110},{120,112},{126,118... | collective-permute-start | bytes 1327112 | tf_op jit(solution)/shard_map/ppermute | solution.py:669
  47.6 1.9 %collective-permute-start.13 = (bf16[27,32,256]{2,1,0:T(8,128)(2,1)S(1)}, bf16[27,32,256]{2,1,0:T(8,128)(2,1)S(1)}, u32[]{:S(2)}, u32[]{:S(2)}) collective-permute-start(bf16[27,32,256]{2,1,0:T(8,128)(2,1)S(1)} %collective-permute-done.9.q3), channel_id=1, source_target_pairs={{0,1},{1,0},{2,3},{3,2},{4,5},{5,4},{6,7},{7,6},{8,9},{9,8},{10,11... | collective-permute-start | bytes 1327112 | tf_op jit(solution)/shard_map/ppermute | solution.py:665
  49.5 1.0 copy-done.8
  50.5 2.5 %prep.1 = (bf16[3,8,8,32,128]{4,3,2,1,0:T(8,128)(2,1)S(1)}, bf16[3,8,8,32,128]{4,3,2,1,0:T(8,128)(2,1)S(1)}, bf16[3,8,8,32,128]{4,3,2,1,0:T(8,128)(2,1)S(1)}, f32[144,256]{1,0:T(8,128)S(1)}, f32[144,256]{1,0:T(8,128)S(1)}) custom-call(s32[8]{0:T(128)S(1)} %dynamic-slice_bitcast_fusion.meta, bf16[6,6,6,4,256]{4,3,2,1,0:T(4,128)(2,1)S(1)} %bitcast.6, ...), custom_call_target="tpu_custom_call" | custom-call | flops 2000000000 | bytes 8000000 | tf_op jit(solution)/shard_map/prep/pallas_call | solution.py:121
  53.0 7.0 %conv1_own.1.part_act = f32[1152,256]{1,0:T(8,128)S(1)} custom-call(s32[8]{0:T(128)S(1)} %dynamic-slice_bitcast_fusion.meta, bf16[3,8,8,32,128]{4,3,2,1,0:T(8,128)(2,1)S(1)} %get-tuple-element.47.x3a, bf16[27,32,256]{2,1,0:T(8,128)(2,1)S(1)} %get-tuple-element.48.q0, bf16[27,32,256]{2,1,0:T(8,128)(2,1)S(1)} %collective-permute-done.7.q1, ...), custom_call_target="tpu_custom_call" | custom-call | flops 2000000000 | bytes 5000000 | tf_op jit(solution)/shard_map/conv1_own/pallas_call | solution.py:190
  61.1 7.3 %conv1.1 = (f32[1152,256]{1,0:T(8,128)S(1)}, bf16[3,7,7,16,256]{4,3,2,1,0:T(8,128)(2,1)S(1)}, bf16[3,7,7,16,128]{4,3,2,1,0:T(8,128)(2,1)S(1)}) custom-call(s32[8]{0:T(128)S(1)} %dynamic-slice_bitcast_fusion.meta, bf16[3,8,8,32,128]{4,3,2,1,0:T(8,128)(2,1)S(1)} %get-tuple-element.46.x3b, f32[1152,256]{1,0:T(8,128)S(1)} %conv1_own.1.part_act, ...), custom_call_target="tpu_custom_call" | custom-call | flops 2000000000 | bytes 7000000 | tf_op jit(solution)/shard_map/conv1/pallas_call | solution.py:222
  68.8 7.2 %conv2.1 = (bf16[3,3,3,4,256]{4,3,2,1,0:T(4,128)(2,1)}, bf16[144,256]{1,0:T(8,128)(2,1)S(1)}, bf16[256,144]{1,0:T(8,128)(2,1)S(1)}) custom-call(s32[8]{0:T(128)S(1)} %dynamic-slice_bitcast_fusion.meta, f32[144,256]{1,0:T(8,128)S(1)} %get-tuple-element.44.skip, f32[144,256]{1,0:T(8,128)S(1)} %get-tuple-element.45.cot, ...), custom_call_target="tpu_custom_call" | custom-call | flops 1500000000 | bytes 6000000 | tf_op jit(solution)/shard_map/conv2/pallas_call | solution.py:276
  76.4 1.1 collective-permute-done.21.grad_t_other
  77.5 6.2 %grad2.1 = (bf16[27,32,256]{2,1,0:T(8,128)(2,1)S(1)}, bf16[27,32,256]{2,1,0:T(8,128)(2,1)S(1)}, bf16[27,32,256]{2,1,0:T(8,128)(2,1)S(1)}, bf16[27,32,256]{2,1,0:T(8,128)(2,1)S(1)}) custom-call(s32[8]{0:T(128)S(1)} %dynamic-slice_bitcast_fusion.meta, bf16[256,144]{1,0:T(8,128)(2,1)S(1)} %get-tuple-element.55.grad_t, ...), custom_call_target="tpu_custom_call" | custom-call | flops 1000000000 | bytes 4000000 | tf_op jit(solution)/shard_map/grad2/pallas_call | solution.py:419
  83.7 8.1 %back.1.gat = bf16[256,1152]{1,0:T(8,128)(2,1)S(1)} custom-call(s32[8]{0:T(128)S(1)} %dynamic-slice_bitcast_fusion.meta, f32[1152,256]{1,0:T(8,128)S(1)} %get-tuple-element.53.act_far, bf16[144,256]{1,0:T(8,128)(2,1)S(1)} %get-tuple-element.61.grad_far, bf16[27,32,256]{2,1,0:T(8,128)(2,1)S(1)} %get-tuple-element.51.q0, ...), custom_call_target="tpu_custom_call" | custom-call | flops 1500000000 | bytes 8000000 | tf_op jit(solution)/shard_map/back/pallas_call | solution.py:338
  92.3 0.8 collective-permute-start.28
  93.1 0.7 collective-permute-done.23.gat_other
  93.8 9.9 %grad1.1 = (bf16[27,32,256]{2,1,0:T(8,128)(2,1)S(1)}, bf16[27,32,256]{2,1,0:T(8,128)(2,1)S(1)}, bf16[27,32,256]{2,1,0:T(8,128)(2,1)S(1)}, bf16[27,32,256]{2,1,0:T(8,128)(2,1)S(1)}) custom-call(s32[8]{0:T(128)S(1)} %dynamic-slice_bitcast_fusion.meta, bf16[256,1152]{1,0:T(8,128)(2,1)S(1)} %back.1.gat, bf16[256,1152]{1,0:T(8,128)(2,1)S(1)} %collective-permute-done.23.gat_other, ...), custom_call_target="tpu_custom_call" | custom-call | flops 4000000000 | bytes 7000000 | tf_op jit(solution)/shard_map/grad1/pallas_call | solution.py:440
  103.7 1.2 collective-permute-start.24
  104.9 1.9 %collective-permute-start.25 = (bf16[27,32,256]{2,1,0:T(8,128)(2,1)S(1)}, bf16[27,32,256]{2,1,0:T(8,128)(2,1)S(1)}, u32[]{:S(2)}, u32[]{:S(2)}) collective-permute-start(bf16[27,32,256]{2,1,0:T(8,128)(2,1)S(1)} %get-tuple-element.65), channel_id=1, source_target_pairs={{0,8},{6,14},{24,16},{30,22},{96,104},{102,110},{120,112},{126,118... | collective-permute-start | bytes 1327112 | tf_op jit(solution)/shard_map/ppermute | solution.py:669
  106.8 1.3 collective-permute-start.26
  108.5 3.6 %collective-permute-done.24.p1 = bf16[27,32,256]{2,1,0:T(8,128)(2,1)S(1)} collective-permute-done((bf16[27,32,256]{2,1,0:T(8,128)(2,1)S(1)}, bf16[27,32,256]{2,1,0:T(8,128)(2,1)S(1)}, u32[]{:S(2)}, u32[]{:S(2)}) %collective-permute-start.24) | collective-permute-done | bytes 442400 | tf_op jit(solution)/shard_map/ppermute | solution.py:669
  112.1 1.1 collective-permute-done.25.p2
  113.2 1.9 %collective-permute-done.26.p3 = bf16[27,32,256]{2,1,0:T(8,128)(2,1)S(1)} collective-permute-done((bf16[27,32,256]{2,1,0:T(8,128)(2,1)S(1)}, bf16[27,32,256]{2,1,0:T(8,128)(2,1)S(1)}, u32[]{:S(2)}, u32[]{:S(2)}) %collective-permute-start.26) | collective-permute-done | bytes 442400 | tf_op jit(solution)/shard_map/ppermute | solution.py:669
  115.1 3.5 %collect.1 = (bf16[4,54,512]{2,1,0:T(8,128)(2,1)S(1)}, bf16[4,54,512]{2,1,0:T(8,128)(2,1)S(1)}, bf16[4,54,512]{2,1,0:T(8,128)(2,1)S(1)}, bf16[4,54,512]{2,1,0:T(8,128)(2,1)S(1)}) custom-call(s32[8]{0:T(128)S(1)} %dynamic-slice_bitcast_fusion.meta, bf16[27,32,256]{2,1,0:T(8,128)(2,1)S(1)} %get-tuple-element.63.p0, ...), custom_call_target="tpu_custom_call" | custom-call | flops 1000000 | bytes 3000000 | tf_op jit(solution)/shard_map/collect/pallas_call | solution.py:538
  118.6 1.4 collective-permute-start.30
  120.0 2.4 %collective-permute-start.31 = (bf16[4,54,512]{2,1,0:T(8,128)(2,1)S(1)}, bf16[4,54,512]{2,1,0:T(8,128)(2,1)S(1)}, u32[]{:S(2)}, u32[]{:S(2)}) collective-permute-start(bf16[4,54,512]{2,1,0:T(8,128)(2,1)S(1)} %get-tuple-element.69), channel_id=1, source_target_pairs={{0,24},{6,30},{24,0},{30,6},{96,120},{102,126},{120,96},{126,102},... | collective-permute-start | bytes 663560 | tf_op jit(solution)/shard_map/ppermute | solution.py:669
  122.7 3.2 %collective-permute-done.30.p1 = bf16[4,54,512]{2,1,0:T(8,128)(2,1)S(1)} collective-permute-done((bf16[4,54,512]{2,1,0:T(8,128)(2,1)S(1)}, bf16[4,54,512]{2,1,0:T(8,128)(2,1)S(1)}, u32[]{:S(2)}, u32[]{:S(2)}) %collective-permute-start.30) | collective-permute-done | bytes 221216 | tf_op jit(solution)/shard_map/ppermute | solution.py:669
  125.9 1.4 collective-permute-done.31.p2
  127.3 2.4 %collective-permute-done.32.p3 = bf16[4,54,512]{2,1,0:T(8,128)(2,1)S(1)} collective-permute-done((bf16[4,54,512]{2,1,0:T(8,128)(2,1)S(1)}, bf16[4,54,512]{2,1,0:T(8,128)(2,1)S(1)}, u32[]{:S(2)}, u32[]{:S(2)}) %collective-permute-start.32) | collective-permute-done | bytes 221216 | tf_op jit(solution)/shard_map/ppermute | solution.py:669
  130.4 3.9 %collective-permute-start.33 = (bf16[54,512]{1,0:T(8,128)(2,1)S(1)}, bf16[54,512]{1,0:T(8,128)(2,1)S(1)}, u32[]{:S(2)}, u32[]{:S(2)}) collective-permute-start(bf16[54,512]{1,0:T(8,128)(2,1)S(1)} %get-tuple-element.72), channel_id=1, source_target_pairs={{0,126},{6,120},{24,102},{30,96},{96,30},{102,24},{120,6},{126,0},... | collective-permute-start | bytes 165896 | tf_op jit(solution)/shard_map/ppermute | solution.py:669
  134.3 6.9 %collective-permute-start.35 = (bf16[54,512]{1,0:T(8,128)(2,1)S(1)}, bf16[54,512]{1,0:T(8,128)(2,1)S(1)}, u32[]{:S(2)}, u32[]{:S(2)}) collective-permute-start(bf16[54,512]{1,0:T(8,128)(2,1)S(1)} %get-tuple-element.74), channel_id=1, source_target_pairs={{0,84},{6,82},{24,76},{30,74},{96,52},{102,50},{120,44},{126,42},{... | collective-permute-start | bytes 165896 | tf_op jit(solution)/shard_map/ppermute | solution.py:669
  141.2 3.6 %collective-permute-done.35.p3 = bf16[54,512]{1,0:T(8,128)(2,1)S(1)} collective-permute-done((bf16[54,512]{1,0:T(8,128)(2,1)S(1)}, bf16[54,512]{1,0:T(8,128)(2,1)S(1)}, u32[]{:S(2)}, u32[]{:S(2)}) %collective-permute-start.35) | collective-permute-done | bytes 55328 | tf_op jit(solution)/shard_map/ppermute | solution.py:669
  144.8 1.3 adam.1
  (59 shorter events, 6.0 us)
Async XLA Ops:
  0.6 48.8 %copy-start.7 = (s32[2,1,256]{2,1,0:T(1,128)S(1)}, s32[2,1,256]{2,1,0:T(1,128)}, u32[]{:S(2)}) copy-start(s32[2,1,256]{2,1,0:T(1,128)} %constant.15.clone.orders) | copy-start | bytes 6148
  0.6 48.8 %copy-start.9 = (bf16[4,3,3,3,256]{4,0,3,2,1:T(4,128)(2,1)S(1)}, bf16[4,3,3,3,256]{4,0,3,2,1:T(4,128)(2,1)}, u32[]{:S(2)}) copy-start(bf16[4,3,3,3,256]{4,0,3,2,1:T(4,128)(2,1)} %param.11) | copy-start | bytes 165892
  2.3 12.7 %collective-permute-start.1 = (bf16[54,512]{1,0:T(8,128)(2,1)}, bf16[54,512]{1,0:T(8,128)(2,1)S(1)}, u32[]{:S(2)}, u32[]{:S(2)}) collective-permute-start(bf16[54,512]{1,0:T(8,128)(2,1)} %pack.1.p0), channel_id=1, source_target_pairs={{0,126},{6,120},{24,102},{30,96},{96,30},{102,24},{120,6},{126,0},... | collective-permute-start | bytes 165896 | tf_op jit(solution)/shard_map/ppermute | solution.py:669
  11.1 6.4 %collective-permute-start.2 = (bf16[54,512]{1,0:T(8,128)(2,1)}, bf16[54,512]{1,0:T(8,128)(2,1)S(1)}, u32[]{:S(2)}, u32[]{:S(2)}) collective-permute-start(bf16[54,512]{1,0:T(8,128)(2,1)} %pack.1.p0), channel_id=1, source_target_pairs={{0,42},{6,44},{24,50},{30,52},{96,74},{102,76},{120,82},{126,84},{... | collective-permute-start | bytes 165896 | tf_op jit(solution)/shard_map/ppermute | solution.py:669
  11.1 10.7 %collective-permute-start.3 = (bf16[54,512]{1,0:T(8,128)(2,1)}, bf16[54,512]{1,0:T(8,128)(2,1)S(1)}, u32[]{:S(2)}, u32[]{:S(2)}) collective-permute-start(bf16[54,512]{1,0:T(8,128)(2,1)} %pack.1.p0), channel_id=1, source_target_pairs={{0,84},{6,82},{24,76},{30,74},{96,52},{102,50},{120,44},{126,42},{... | collective-permute-start | bytes 165896 | tf_op jit(solution)/shard_map/ppermute | solution.py:669
  21.8 0.8 copy-start.2
  23.2 7.3 %collective-permute-start.4 = (bf16[4,54,512]{2,1,0:T(8,128)(2,1)S(1)}, bf16[4,54,512]{2,1,0:T(8,128)(2,1)S(1)}, u32[]{:S(2)}, u32[]{:S(2)}) collective-permute-start(bf16[4,54,512]{2,1,0:T(8,128)(2,1)S(1)} %join.1.p0), channel_id=1, source_target_pairs={{0,96},{6,102},{24,120},{30,126},{96,0},{102,6},{120,24},{126,30},... | collective-permute-start | bytes 663560 | tf_op jit(solution)/shard_map/ppermute | solution.py:669
  24.2 7.2 %collective-permute-start.5 = (bf16[4,54,512]{2,1,0:T(8,128)(2,1)S(1)}, bf16[4,54,512]{2,1,0:T(8,128)(2,1)S(1)}, u32[]{:S(2)}, u32[]{:S(2)}) collective-permute-start(bf16[4,54,512]{2,1,0:T(8,128)(2,1)S(1)} %join.1.p0), channel_id=1, source_target_pairs={{0,24},{6,30},{24,0},{30,6},{96,120},{102,126},{120,96},{126,102},... | collective-permute-start | bytes 663560 | tf_op jit(solution)/shard_map/ppermute | solution.py:669
  25.0 7.2 %collective-permute-start.6 = (bf16[4,54,512]{2,1,0:T(8,128)(2,1)S(1)}, bf16[4,54,512]{2,1,0:T(8,128)(2,1)S(1)}, u32[]{:S(2)}, u32[]{:S(2)}) collective-permute-start(bf16[4,54,512]{2,1,0:T(8,128)(2,1)S(1)} %join.1.p0), channel_id=1, source_target_pairs={{0,6},{6,0},{24,30},{30,24},{96,102},{102,96},{120,126},{126,120},... | collective-permute-start | bytes 663560 | tf_op jit(solution)/shard_map/ppermute | solution.py:669
  34.4 8.4 %collective-permute-start.7 = (bf16[27,32,256]{2,1,0:T(8,128)(2,1)S(1)}, bf16[27,32,256]{2,1,0:T(8,128)(2,1)S(1)}, u32[]{:S(2)}, u32[]{:S(2)}) collective-permute-start(bf16[27,32,256]{2,1,0:T(8,128)(2,1)S(1)} %get-tuple-element.48.q0), channel_id=1, source_target_pairs={{0,32},{6,38},{24,56},{30,62},{96,64},{102,70},{120,88},{126,94},{... | collective-permute-start | bytes 1327112 | tf_op jit(solution)/shard_map/ppermute | solution.py:669
  34.8 8.3 %collective-permute-start.8 = (bf16[27,32,256]{2,1,0:T(8,128)(2,1)S(1)}, bf16[27,32,256]{2,1,0:T(8,128)(2,1)S(1)}, u32[]{:S(2)}, u32[]{:S(2)}) collective-permute-start(bf16[27,32,256]{2,1,0:T(8,128)(2,1)S(1)} %get-tuple-element.48.q0), channel_id=1, source_target_pairs={{0,8},{6,14},{24,16},{30,22},{96,104},{102,110},{120,112},{126,118... | collective-permute-start | bytes 1327112 | tf_op jit(solution)/shard_map/ppermute | solution.py:669
  35.7 8.3 %collective-permute-start.9 = (bf16[27,32,256]{2,1,0:T(8,128)(2,1)S(1)}, bf16[27,32,256]{2,1,0:T(8,128)(2,1)S(1)}, u32[]{:S(2)}, u32[]{:S(2)}) collective-permute-start(bf16[27,32,256]{2,1,0:T(8,128)(2,1)S(1)} %get-tuple-element.48.q0), channel_id=1, source_target_pairs={{0,2},{6,4},{24,26},{30,28},{96,98},{102,100},{120,122},{126,124},... | collective-permute-start | bytes 1327112 | tf_op jit(solution)/shard_map/ppermute | solution.py:669
  36.7 8.5 %collective-permute-start = (bf16[6,6,6,4,256]{4,3,2,1,0:T(4,128)(2,1)}, bf16[6,6,6,4,256]{4,3,2,1,0:T(4,128)(2,1)S(1)}, u32[]{:S(2)}, u32[]{:S(2)}) collective-permute-start(bf16[6,6,6,4,256]{4,3,2,1,0:T(4,128)(2,1)} %bitcast.5), channel_id=1, source_target_pairs={{0,1},{1,0},{2,3},{3,2},{4,5},{5,4},{6,7},{7,6},{8,9},{9,8},{10,11... | collective-permute-start | bytes 1327112 | tf_op jit(solution)/shard_map/ppermute | solution.py:665
  36.7 10.2 %collective-permute-start.10 = (bf16[27,32,256]{2,1,0:T(8,128)(2,1)S(1)}, bf16[27,32,256]{2,1,0:T(8,128)(2,1)S(1)}, u32[]{:S(2)}, u32[]{:S(2)}) collective-permute-start(bf16[27,32,256]{2,1,0:T(8,128)(2,1)S(1)} %get-tuple-element.48.q0), channel_id=1, source_target_pairs={{0,1},{1,0},{2,3},{3,2},{4,5},{5,4},{6,7},{7,6},{8,9},{9,8},{10,11... | collective-permute-start | bytes 1327112 | tf_op jit(solution)/shard_map/ppermute | solution.py:665
  42.8 4.8 %collective-permute-start.11 = (bf16[27,32,256]{2,1,0:T(8,128)(2,1)S(1)}, bf16[27,32,256]{2,1,0:T(8,128)(2,1)S(1)}, u32[]{:S(2)}, u32[]{:S(2)}) collective-permute-start(bf16[27,32,256]{2,1,0:T(8,128)(2,1)S(1)} %collective-permute-done.7.q1), channel_id=1, source_target_pairs={{0,1},{1,0},{2,3},{3,2},{4,5},{5,4},{6,7},{7,6},{8,9},{9,8},{10,11... | collective-permute-start | bytes 1327112 | tf_op jit(solution)/shard_map/ppermute | solution.py:665
  44.0 16.0 %collective-permute-start.12 = (bf16[27,32,256]{2,1,0:T(8,128)(2,1)S(1)}, bf16[27,32,256]{2,1,0:T(8,128)(2,1)S(1)}, u32[]{:S(2)}, u32[]{:S(2)}) collective-permute-start(bf16[27,32,256]{2,1,0:T(8,128)(2,1)S(1)} %collective-permute-done.8.q2), channel_id=1, source_target_pairs={{0,1},{1,0},{2,3},{3,2},{4,5},{5,4},{6,7},{7,6},{8,9},{9,8},{10,11... | collective-permute-start | bytes 1327112 | tf_op jit(solution)/shard_map/ppermute | solution.py:665
  44.0 16.1 %collective-permute-start.14 = (bf16[27,32,256]{2,1,0:T(8,128)(2,1)S(1)}, bf16[27,32,256]{2,1,0:T(8,128)(2,1)S(1)}, u32[]{:S(2)}, u32[]{:S(2)}) collective-permute-start(bf16[27,32,256]{2,1,0:T(8,128)(2,1)S(1)} %get-tuple-element.51.q0), channel_id=1, source_target_pairs={{0,32},{6,38},{24,56},{30,62},{96,64},{102,70},{120,88},{126,94},{... | collective-permute-start | bytes 1327112 | tf_op jit(solution)/shard_map/ppermute | solution.py:669
  45.2 15.4 %collective-permute-start.15 = (bf16[27,32,256]{2,1,0:T(8,128)(2,1)S(1)}, bf16[27,32,256]{2,1,0:T(8,128)(2,1)S(1)}, u32[]{:S(2)}, u32[]{:S(2)}) collective-permute-start(bf16[27,32,256]{2,1,0:T(8,128)(2,1)S(1)} %get-tuple-element.51.q0), channel_id=1, source_target_pairs={{0,8},{6,14},{24,16},{30,22},{96,104},{102,110},{120,112},{126,118... | collective-permute-start | bytes 1327112 | tf_op jit(solution)/shard_map/ppermute | solution.py:669
  46.9 13.8 %collective-permute-start.16 = (bf16[27,32,256]{2,1,0:T(8,128)(2,1)S(1)}, bf16[27,32,256]{2,1,0:T(8,128)(2,1)S(1)}, u32[]{:S(2)}, u32[]{:S(2)}) collective-permute-start(bf16[27,32,256]{2,1,0:T(8,128)(2,1)S(1)} %get-tuple-element.51.q0), channel_id=1, source_target_pairs={{0,2},{6,4},{24,26},{30,28},{96,98},{102,100},{120,122},{126,124},... | collective-permute-start | bytes 1327112 | tf_op jit(solution)/shard_map/ppermute | solution.py:669
  47.6 13.6 %collective-permute-start.13 = (bf16[27,32,256]{2,1,0:T(8,128)(2,1)S(1)}, bf16[27,32,256]{2,1,0:T(8,128)(2,1)S(1)}, u32[]{:S(2)}, u32[]{:S(2)}) collective-permute-start(bf16[27,32,256]{2,1,0:T(8,128)(2,1)S(1)} %collective-permute-done.9.q3), channel_id=1, source_target_pairs={{0,1},{1,0},{2,3},{3,2},{4,5},{5,4},{6,7},{7,6},{8,9},{9,8},{10,11... | collective-permute-start | bytes 1327112 | tf_op jit(solution)/shard_map/ppermute | solution.py:665
  49.5 1.0 copy-start.8
  60.0 8.8 %collective-permute-start.17 = (bf16[27,32,256]{2,1,0:T(8,128)(2,1)S(1)}, bf16[27,32,256]{2,1,0:T(8,128)(2,1)S(1)}, u32[]{:S(2)}, u32[]{:S(2)}) collective-permute-start(bf16[27,32,256]{2,1,0:T(8,128)(2,1)S(1)} %get-tuple-element.51.q0), channel_id=1, source_target_pairs={{0,1},{1,0},{2,3},{3,2},{4,5},{5,4},{6,7},{7,6},{8,9},{9,8},{10,11... | collective-permute-start | bytes 1327112 | tf_op jit(solution)/shard_map/ppermute | solution.py:665
  60.1 8.7 %collective-permute-start.18 = (bf16[27,32,256]{2,1,0:T(8,128)(2,1)S(1)}, bf16[27,32,256]{2,1,0:T(8,128)(2,1)S(1)}, u32[]{:S(2)}, u32[]{:S(2)}) collective-permute-start(bf16[27,32,256]{2,1,0:T(8,128)(2,1)S(1)} %collective-permute-done.14.q1), channel_id=1, source_target_pairs={{0,1},{1,0},{2,3},{3,2},{4,5},{5,4},{6,7},{7,6},{8,9},{9,8},{10,11... | collective-permute-start | bytes 1327112 | tf_op jit(solution)/shard_map/ppermute | solution.py:665
  60.6 8.2 %collective-permute-start.19 = (bf16[27,32,256]{2,1,0:T(8,128)(2,1)S(1)}, bf16[27,32,256]{2,1,0:T(8,128)(2,1)S(1)}, u32[]{:S(2)}, u32[]{:S(2)}) collective-permute-start(bf16[27,32,256]{2,1,0:T(8,128)(2,1)S(1)} %collective-permute-done.15.q2), channel_id=1, source_target_pairs={{0,1},{1,0},{2,3},{3,2},{4,5},{5,4},{6,7},{7,6},{8,9},{9,8},{10,11... | collective-permute-start | bytes 1327112 | tf_op jit(solution)/shard_map/ppermute | solution.py:665
  60.7 8.1 %collective-permute-start.20 = (bf16[27,32,256]{2,1,0:T(8,128)(2,1)S(1)}, bf16[27,32,256]{2,1,0:T(8,128)(2,1)S(1)}, u32[]{:S(2)}, u32[]{:S(2)}) collective-permute-start(bf16[27,32,256]{2,1,0:T(8,128)(2,1)S(1)} %collective-permute-done.16.q3), channel_id=1, source_target_pairs={{0,1},{1,0},{2,3},{3,2},{4,5},{5,4},{6,7},{7,6},{8,9},{9,8},{10,11... | collective-permute-start | bytes 1327112 | tf_op jit(solution)/shard_map/ppermute | solution.py:665
  68.5 9.0 %collective-permute-start.22 = (bf16[3,7,7,16,128]{4,3,2,1,0:T(8,128)(2,1)S(1)}, bf16[3,7,7,16,128]{4,3,2,1,0:T(8,128)(2,1)S(1)}, u32[]{:S(2)}, u32[]{:S(2)}) collective-permute-start(bf16[3,7,7,16,128]{4,3,2,1,0:T(8,128)(2,1)S(1)} %get-tuple-element.56), channel_id=1, source_target_pairs={{0,1},{1,0},{2,3},{3,2},{4,5},{5,4},{6,7},{7,6},{8,9},{9,8},{10,11... | collective-permute-start | bytes 1806344 | tf_op jit(solution)/shard_map/ppermute | solution.py:665
  76.1 1.4 collective-permute-start.21
  91.7 2.1 %collective-permute-start.23 = (bf16[256,1152]{1,0:T(8,128)(2,1)S(1)}, bf16[256,1152]{1,0:T(8,128)(2,1)S(1)}, u32[]{:S(2)}, u32[]{:S(2)}) collective-permute-start(bf16[256,1152]{1,0:T(8,128)(2,1)S(1)} %back.1.gat), channel_id=1, source_target_pairs={{0,1},{1,0},{2,3},{3,2},{4,5},{5,4},{6,7},{7,6},{8,9},{9,8},{10,11... | collective-permute-start | bytes 1769480 | tf_op jit(solution)/shard_map/ppermute | solution.py:665
  92.1 14.7 %collective-permute-start.27 = (bf16[27,32,256]{2,1,0:T(8,128)(2,1)S(1)}, bf16[27,32,256]{2,1,0:T(8,128)(2,1)S(1)}, u32[]{:S(2)}, u32[]{:S(2)}) collective-permute-start(bf16[27,32,256]{2,1,0:T(8,128)(2,1)S(1)} %get-tuple-element.58), channel_id=1, source_target_pairs={{0,32},{6,38},{24,56},{30,62},{96,64},{102,70},{120,88},{126,94},{... | collective-permute-start | bytes 1327112 | tf_op jit(solution)/shard_map/ppermute | solution.py:669
  92.3 15.8 %collective-permute-start.28 = (bf16[27,32,256]{2,1,0:T(8,128)(2,1)S(1)}, bf16[27,32,256]{2,1,0:T(8,128)(2,1)S(1)}, u32[]{:S(2)}, u32[]{:S(2)}) collective-permute-start(bf16[27,32,256]{2,1,0:T(8,128)(2,1)S(1)} %get-tuple-element.59), channel_id=1, source_target_pairs={{0,8},{6,14},{24,16},{30,22},{96,104},{102,110},{120,112},{126,118... | collective-permute-start | bytes 1327112 | tf_op jit(solution)/shard_map/ppermute | solution.py:669
  93.1 15.1 %collective-permute-start.29 = (bf16[27,32,256]{2,1,0:T(8,128)(2,1)S(1)}, bf16[27,32,256]{2,1,0:T(8,128)(2,1)S(1)}, u32[]{:S(2)}, u32[]{:S(2)}) collective-permute-start(bf16[27,32,256]{2,1,0:T(8,128)(2,1)S(1)} %get-tuple-element.60), channel_id=1, source_target_pairs={{0,2},{6,4},{24,26},{30,28},{96,98},{102,100},{120,122},{126,124},... | collective-permute-start | bytes 1327112 | tf_op jit(solution)/shard_map/ppermute | solution.py:669
  103.7 8.4 %collective-permute-start.24 = (bf16[27,32,256]{2,1,0:T(8,128)(2,1)S(1)}, bf16[27,32,256]{2,1,0:T(8,128)(2,1)S(1)}, u32[]{:S(2)}, u32[]{:S(2)}) collective-permute-start(bf16[27,32,256]{2,1,0:T(8,128)(2,1)S(1)} %get-tuple-element.64), channel_id=1, source_target_pairs={{0,32},{6,38},{24,56},{30,62},{96,64},{102,70},{120,88},{126,94},{... | collective-permute-start | bytes 1327112 | tf_op jit(solution)/shard_map/ppermute | solution.py:669
  104.9 8.3 %collective-permute-start.25 = (bf16[27,32,256]{2,1,0:T(8,128)(2,1)S(1)}, bf16[27,32,256]{2,1,0:T(8,128)(2,1)S(1)}, u32[]{:S(2)}, u32[]{:S(2)}) collective-permute-start(bf16[27,32,256]{2,1,0:T(8,128)(2,1)S(1)} %get-tuple-element.65), channel_id=1, source_target_pairs={{0,8},{6,14},{24,16},{30,22},{96,104},{102,110},{120,112},{126,118... | collective-permute-start | bytes 1327112 | tf_op jit(solution)/shard_map/ppermute | solution.py:669
  106.8 8.3 %collective-permute-start.26 = (bf16[27,32,256]{2,1,0:T(8,128)(2,1)S(1)}, bf16[27,32,256]{2,1,0:T(8,128)(2,1)S(1)}, u32[]{:S(2)}, u32[]{:S(2)}) collective-permute-start(bf16[27,32,256]{2,1,0:T(8,128)(2,1)S(1)} %get-tuple-element.66), channel_id=1, source_target_pairs={{0,2},{6,4},{24,26},{30,28},{96,98},{102,100},{120,122},{126,124},... | collective-permute-start | bytes 1327112 | tf_op jit(solution)/shard_map/ppermute | solution.py:669
  115.1 29.7 %copy-start = (f32[27,512]{1,0:T(8,128)S(1)}, f32[27,512]{1,0:T(8,128)}, u32[]{:S(2)}) copy-start(f32[27,512]{1,0:T(8,128)} %k1.1) | copy-start | bytes 165892
  115.1 29.7 %copy-start.1 = (f32[27,512]{1,0:T(8,128)S(1)}, f32[27,512]{1,0:T(8,128)}, u32[]{:S(2)}) copy-start(f32[27,512]{1,0:T(8,128)} %k2.1) | copy-start | bytes 165892
  115.1 29.7 %copy-start.3 = (f32[27,512]{1,0:T(8,128)S(1)}, f32[27,512]{1,0:T(8,128)}, u32[]{:S(2)}) copy-start(f32[27,512]{1,0:T(8,128)} %m1.1) | copy-start | bytes 165892
  115.1 29.7 %copy-start.4 = (f32[27,512]{1,0:T(8,128)S(1)}, f32[27,512]{1,0:T(8,128)}, u32[]{:S(2)}) copy-start(f32[27,512]{1,0:T(8,128)} %v1.1) | copy-start | bytes 165892
  115.1 29.7 %copy-start.5 = (f32[27,512]{1,0:T(8,128)S(1)}, f32[27,512]{1,0:T(8,128)}, u32[]{:S(2)}) copy-start(f32[27,512]{1,0:T(8,128)} %m2.1) | copy-start | bytes 165892
  115.1 29.7 %copy-start.6 = (f32[27,512]{1,0:T(8,128)S(1)}, f32[27,512]{1,0:T(8,128)}, u32[]{:S(2)}) copy-start(f32[27,512]{1,0:T(8,128)} %v2.1) | copy-start | bytes 165892
  118.6 7.3 %collective-permute-start.30 = (bf16[4,54,512]{2,1,0:T(8,128)(2,1)S(1)}, bf16[4,54,512]{2,1,0:T(8,128)(2,1)S(1)}, u32[]{:S(2)}, u32[]{:S(2)}) collective-permute-start(bf16[4,54,512]{2,1,0:T(8,128)(2,1)S(1)} %get-tuple-element.68), channel_id=1, source_target_pairs={{0,96},{6,102},{24,120},{30,126},{96,0},{102,6},{120,24},{126,30},... | collective-permute-start | bytes 663560 | tf_op jit(solution)/shard_map/ppermute | solution.py:669
  120.0 7.2 %collective-permute-start.31 = (bf16[4,54,512]{2,1,0:T(8,128)(2,1)S(1)}, bf16[4,54,512]{2,1,0:T(8,128)(2,1)S(1)}, u32[]{:S(2)}, u32[]{:S(2)}) collective-permute-start(bf16[4,54,512]{2,1,0:T(8,128)(2,1)S(1)} %get-tuple-element.69), channel_id=1, source_target_pairs={{0,24},{6,30},{24,0},{30,6},{96,120},{102,126},{120,96},{126,102},... | collective-permute-start | bytes 663560 | tf_op jit(solution)/shard_map/ppermute | solution.py:669
  122.5 7.2 %collective-permute-start.32 = (bf16[4,54,512]{2,1,0:T(8,128)(2,1)S(1)}, bf16[4,54,512]{2,1,0:T(8,128)(2,1)S(1)}, u32[]{:S(2)}, u32[]{:S(2)}) collective-permute-start(bf16[4,54,512]{2,1,0:T(8,128)(2,1)S(1)} %get-tuple-element.70), channel_id=1, source_target_pairs={{0,6},{6,0},{24,30},{30,24},{96,102},{102,96},{120,126},{126,120},... | collective-permute-start | bytes 663560 | tf_op jit(solution)/shard_map/ppermute | solution.py:669
  130.4 10.8 %collective-permute-start.33 = (bf16[54,512]{1,0:T(8,128)(2,1)S(1)}, bf16[54,512]{1,0:T(8,128)(2,1)S(1)}, u32[]{:S(2)}, u32[]{:S(2)}) collective-permute-start(bf16[54,512]{1,0:T(8,128)(2,1)S(1)} %get-tuple-element.72), channel_id=1, source_target_pairs={{0,126},{6,120},{24,102},{30,96},{96,30},{102,24},{120,6},{126,0},... | collective-permute-start | bytes 165896 | tf_op jit(solution)/shard_map/ppermute | solution.py:669
  134.3 6.9 %collective-permute-start.34 = (bf16[54,512]{1,0:T(8,128)(2,1)S(1)}, bf16[54,512]{1,0:T(8,128)(2,1)S(1)}, u32[]{:S(2)}, u32[]{:S(2)}) collective-permute-start(bf16[54,512]{1,0:T(8,128)(2,1)S(1)} %get-tuple-element.73), channel_id=1, source_target_pairs={{0,42},{6,44},{24,50},{30,52},{96,74},{102,76},{120,82},{126,84},{... | collective-permute-start | bytes 165896 | tf_op jit(solution)/shard_map/ppermute | solution.py:669
  134.3 10.5 %collective-permute-start.35 = (bf16[54,512]{1,0:T(8,128)(2,1)S(1)}, bf16[54,512]{1,0:T(8,128)(2,1)S(1)}, u32[]{:S(2)}, u32[]{:S(2)}) collective-permute-start(bf16[54,512]{1,0:T(8,128)(2,1)S(1)} %get-tuple-element.74), channel_id=1, source_target_pairs={{0,84},{6,82},{24,76},{30,74},{96,52},{102,50},{120,44},{126,42},{... | collective-permute-start | bytes 165896 | tf_op jit(solution)/shard_map/ppermute | solution.py:669

commit v6 on v4

v6 whole, which is shorter than its diff:
```python
import functools
import itertools

import jax
import jax.numpy as jnp
import numpy as np
from jax import lax
from jax.experimental import pallas as pl
from jax.experimental.pallas import tpu as pltpu
from jax.sharding import PartitionSpec as P

C = 256
HALF = 128
EDGE = 6
OUTER = 3
TAPS = 27
SAMP = 4
ROWS = 32
ACT_ROWS = EDGE * EDGE * ROWS
PAD_ROWS = 64 * ROWS
OUT_ROWS = 16
PRE_ROWS = 9 * OUT_ROWS
MEMBERS = 16
MIB = 1024 * 1024
BF = jnp.bfloat16
F32 = jnp.float32

GROUP = 6
BLOCK = 32
QUARTER = (TAPS, BLOCK, C)

VM = pl.BlockSpec(memory_space=pltpu.VMEM)


def shape(dims, dtype):
    return jax.ShapeDtypeStruct(dims, dtype)


def call(kernel, name, out_shape, in_specs, scratch, mib, flops, moved):
    single = not isinstance(out_shape, tuple)
    return pl.pallas_call(
        kernel,
        out_shape=out_shape,
        in_specs=in_specs,
        out_specs=VM if single else (VM,) * len(out_shape),
        scratch_shapes=scratch,
        compiler_params=pltpu.CompilerParams(vmem_limit_bytes=mib * MIB),
        cost_estimate=pl.CostEstimate(flops=flops, bytes_accessed=moved, transcendentals=0),
        name=name,
    )


def dot(a, b):
    return jnp.dot(a, b, preferred_element_type=F32)


def dot_t(a, b):
    return lax.dot_general(a, b, (((1,), (1,)), ((), ())), preferred_element_type=F32)


def sigmoid(v):
    return 1.0 / (1.0 + jnp.exp(-v))


def load(ref, start, count, stride=1):
    return jnp.concatenate(
        [ref[half, pl.ds(start, count, stride=stride), :] for half in range(2)], axis=1
    )


def store(ref, start, count, value, stride=1):
    for half in range(2):
        ref[half, pl.ds(start, count, stride=stride), :] = value[
            :, half * HALF : (half + 1) * HALF
        ]


def one_hot(order_row):
    return (lax.broadcasted_iota(jnp.int32, (C, C), 0) == order_row).astype(BF)


def fill_cells(source, xs):
    for i in range(EDGE):
        for j in range(EDGE):
            value = source[i, j].astype(F32)
            base = 8 + ((i + 1) * 8 + j + 1) * ROWS + 1
            for l in range(EDGE):
                store(xs, base + l, SAMP, value[l], 8)


def prep_kernel(latent, other, out_grad, table, x3a, x3b, x3o, skip, cot, xs, og):
    perm = one_hot(table[0])
    xs[...] = jnp.zeros_like(xs)
    og[...] = jnp.zeros_like(og)
    fill_cells(latent, xs)
    for qi in range(OUTER):
        for qj in range(OUTER):
            q = (qi * 3 + qj) * OUT_ROWS
            value = out_grad[qi, qj].astype(F32)
            for ql in range(OUTER):
                store(og, q + ql, SAMP, value[ql], 4)
            base = 8 + ((2 * qi + 1) * 8 + 2 * qj + 1) * ROWS + 1
            skip[q : q + OUT_ROWS, :] = load(xs, base, OUT_ROWS, 2)
    cot[...] = load(og, 0, PRE_ROWS)
    for i in range(8):
        for dl in range(3):
            rows = dot(load(xs, 7 + dl + i * 256, 256).astype(BF), perm).astype(BF)
            x3a[dl, i] = rows[:, :HALF].reshape(8, ROWS, HALF)
            x3b[dl, i] = rows[:, HALF:].reshape(8, ROWS, HALF)
    fill_cells(other, xs)
    for i in range(8):
        for dl in range(3):
            rows = dot(load(xs, 7 + dl + i * 256, 256).astype(BF), perm[:, :HALF])
            x3o[dl, i] = rows.astype(BF).reshape(8, ROWS, HALF)


def prep(latent, other, out_grad, table):
    wide = shape((3, 8, 8, ROWS, HALF), BF)
    pre = shape((PRE_ROWS, C), F32)
    return call(
        prep_kernel, "prep", (wide, wide, wide, pre, pre), [VM] * 4,
        [pltpu.VMEM((2, PAD_ROWS + 16, HALF), F32), pltpu.VMEM((2, PRE_ROWS, HALF), F32)],
        20, 2_000_000_000, 8_000_000,
    )(latent, other, out_grad, table)


def cell_mask():
    cell = lax.broadcasted_iota(jnp.int32, (EDGE * ROWS, C), 0) % 8
    return (cell >= 1) & (cell <= EDGE)


def half_weight(quarters, t):
    return jnp.concatenate([quarter[t] for quarter in quarters], axis=0)


def half_conv(x3, quarters, act, start):
    for first in range(0, TAPS, GROUP):
        taps = range(first, min(first + GROUP, TAPS))
        windows = [
            x3[t % 3, t // 9 : t // 9 + EDGE, t // 3 % 3 : t // 3 % 3 + EDGE] for t in taps
        ]
        total = dot(
            jnp.concatenate([window.reshape(ACT_ROWS, HALF) for window in windows], axis=1),
            jnp.concatenate([half_weight(quarters, t) for t in taps], axis=0),
        )
        before = act if first else start
        act[...] = total if before is None else before[...] + total


def conv1_own_kernel(x3a, q0, q1, q2, q3, act):
    half_conv(x3a, (q0, q1, q2, q3), act, None)


def conv1_own(x3a, own):
    return call(
        conv1_own_kernel, "conv1_own", shape((ACT_ROWS, C), F32), [VM] * 5,
        [], 12, 2_000_000_000, 5_000_000,
    )(x3a, *own)


def permuted(value, lanes):
    high = value.astype(BF)
    rest = value - high.astype(F32)
    middle = rest.astype(BF)
    low = (rest - middle.astype(F32)).astype(BF)
    return dot(high, lanes) + (dot(middle, lanes) + dot(low, lanes))


def conv1_kernel(x3b, part_act, q0, q1, q2, q3, table, act, hsel, hsend, hs):
    half_conv(x3b, (q0, q1, q2, q3), act, part_act)

    hsel[:, 0] = jnp.zeros_like(hsel[:, 0])
    hsel[:, :, 0] = jnp.zeros_like(hsel[:, :, 0])
    hsend[:, 0] = jnp.zeros_like(hsend[:, 0])
    hsend[:, :, 0] = jnp.zeros_like(hsend[:, :, 0])
    store(hs, ACT_ROWS, 8, jnp.zeros((8, C), F32))
    inside = cell_mask()
    lanes = one_hot(table[1])
    for i in range(EDGE):
        part = pl.ds(i * EDGE * ROWS, EDGE * ROWS)
        value = permuted(act[part, :], lanes)
        act[part, :] = value
        hidden = jnp.where(inside, value * sigmoid(value), 0.0)
        store(hs, i * EDGE * ROWS, EDGE * ROWS, hidden.astype(BF).astype(F32))
    for dl in range(3):
        for i in range(EDGE):
            rows = load(hs, i * EDGE * ROWS + dl, EDGE * OUT_ROWS, 2)
            rows = rows.astype(BF).reshape(EDGE, OUT_ROWS, C)
            hsel[dl, i + 1, 1:] = rows
            hsend[dl, i + 1, 1:] = rows[..., HALF:]


def conv1(x3b, part_act, other, table):
    return call(
        conv1_kernel, "conv1",
        (
            shape((ACT_ROWS, C), F32),
            shape((3, 7, 7, OUT_ROWS, C), BF),
            shape((3, 7, 7, OUT_ROWS, HALF), BF),
        ),
        [VM] * 7,
        [pltpu.VMEM((2, ACT_ROWS + 8, HALF), F32)],
        24, 2_000_000_000, 7_000_000,
    )(x3b, part_act, *other, table)


def strided_window(hsel, dl, di, dj, lanes=slice(None)):
    blocks = [
        hsel[dl, 2 * qi + di, 2 * qj + dj, :, lanes] for qi in range(OUTER) for qj in range(OUTER)
    ]
    return jnp.concatenate(blocks, axis=0)


def conv2_kernel(
    skip, cot, hsel, q0, q1, q2, q3, p0, p1, p2, p3, block_out, grad_pre, grad_pre_t, bo
):
    quarters = (q0, q1, q2, q3, p0, p1, p2, p3)
    pre = skip[...]
    for di in range(3):
        for dj in range(3):
            for dl in range(3):
                pre = pre + dot(
                    strided_window(hsel, dl, di, dj), half_weight(quarters, di * 9 + dj * 3 + dl)
                )
    sigma = sigmoid(pre)
    store(bo, 0, PRE_ROWS, pre * sigma)
    for qi in range(OUTER):
        for qj in range(OUTER):
            for ql in range(OUTER):
                base = (qi * 3 + qj) * OUT_ROWS + ql
                block_out[qi, qj, ql] = load(bo, base, SAMP, 4).astype(BF)
    grad = (cot[...] * (sigma * (1.0 + pre * (1.0 - sigma)))).astype(BF)
    grad_pre[...] = grad
    grad_pre_t[...] = grad.astype(F32).T.astype(BF)


def conv2(skip, cot, hsel, own, other):
    return call(
        conv2_kernel, "conv2",
        (
            shape((OUTER, OUTER, OUTER, SAMP, C), BF),
            shape((PRE_ROWS, C), BF),
            shape((C, PRE_ROWS), BF),
        ),
        [VM] * 11,
        [pltpu.VMEM((2, PRE_ROWS, HALF), F32)],
        16, 1_500_000_000, 6_000_000,
    )(skip, cot, hsel, *own, *other)


def back_kernel(
    act, grad_pre, q0, q1, q2, q3, p0, p1, p2, p3, table, gat, y, gh
):
    quarters = (q0, q1, q2, q3, p0, p1, p2, p3)
    y[...] = jnp.zeros_like(y)
    grad = grad_pre[...]
    for di in range(3):
        for dj in range(3):
            for dl in range(3):
                term = dot_t(grad, half_weight(quarters, di * 9 + dj * 3 + dl))
                term = term.reshape(9, OUT_ROWS, C)
                for qi in range(OUTER):
                    for qj in range(OUTER):
                        y[dl, 2 * qi + di, 2 * qj + dj] += term[qi * 3 + qj]
    store(gh, ACT_ROWS, 8, jnp.zeros((8, C), F32))
    count = EDGE * OUT_ROWS
    for i in range(EDGE):
        base = i * EDGE * ROWS
        store(gh, base, count, y[0, i + 1, 1:].reshape(count, C), 2)
        store(gh, base + 1, count, y[1, i + 1, 1:].reshape(count, C), 2)
    for i in range(EDGE):
        base = i * EDGE * ROWS + 2
        total = load(gh, base, count, 2) + y[2, i + 1, 1:].reshape(count, C)
        store(gh, base, count, total, 2)
    inside = cell_mask()
    lanes = one_hot(table[1])
    for i in range(0, EDGE, 2):
        grads = []
        for start in (i * EDGE * ROWS, (i + 1) * EDGE * ROWS):
            value = act[pl.ds(start, EDGE * ROWS), :]
            sigma = sigmoid(value)
            grad = load(gh, start, EDGE * ROWS) * (sigma * (1.0 + value * (1.0 - sigma)))
            grads.append(jnp.where(inside, grad, 0.0).astype(BF))
        gat[i // 2] = dot_t(lanes, jnp.concatenate(grads, axis=0)).astype(BF)


def back(act, grad_pre, own, other, table):
    return call(
        back_kernel, "back", shape((EDGE // 2, C, 2 * EDGE * ROWS), BF), [VM] * 11,
        [
            pltpu.VMEM((3, 7, 7, OUT_ROWS, C), F32),
            pltpu.VMEM((2, ACT_ROWS + 8, HALF), F32),
        ],
        16, 1_500_000_000, 8_000_000,
    )(act, grad_pre, *own, *other, table)


def grad_loop(quarters, left, windows):
    eye = (
        lax.broadcasted_iota(jnp.int32, (C, C), 0) == lax.broadcasted_iota(jnp.int32, (C, C), 1)
    ).astype(BF)

    def product(taps):
        right = [
            jnp.concatenate([window(t // 9, t // 3 % 3, t % 3) for t in taps], axis=1)
            for window in windows
        ]
        total = dot(left[...], jnp.concatenate(right, axis=0)).astype(BF)
        for n in range(0, len(taps), 2):
            two = taps[n : n + 2]
            width = HALF * len(two)
            turned = dot_t(eye[:width, :width], total[:, n * HALF : n * HALF + width]).astype(BF)
            for m, t in enumerate(two):
                for k, quarter in enumerate(quarters):
                    first = m * HALF + k * BLOCK
                    quarter[t] = turned[first : first + BLOCK]

    def step(n, carry):
        product([GROUP * n + k for k in range(GROUP)])
        return carry

    whole = TAPS // GROUP
    lax.fori_loop(0, whole, step, 0)
    product(list(range(GROUP * whole, TAPS)))


QUARTERS = (shape(QUARTER, BF),) * 4


def grad2_kernel(
    grad_t, grad_t_other, hsel, hsel_other, f0, f1, f2, f3, left
):
    left[:, :PRE_ROWS] = grad_t[...]
    left[:, PRE_ROWS:] = grad_t_other[...]
    grad_loop(
        (f0, f1, f2, f3),
        left,
        (
            lambda di, dj, dl: strided_window(hsel, dl, di, dj, slice(0, HALF)),
            lambda di, dj, dl: strided_window(hsel_other, dl, di, dj),
        ),
    )


def grad2(grad_t, grad_t_other, hsel, hsel_other):
    return call(
        grad2_kernel, "grad2", QUARTERS, [VM] * 4,
        [pltpu.VMEM((C, 2 * PRE_ROWS), BF)], 12, 1_000_000_000, 4_000_000,
    )(grad_t, grad_t_other, hsel, hsel_other)


def same_window(x3):
    def window(di, dj, dl):
        return x3[dl, pl.ds(di, EDGE), pl.ds(dj, EDGE)].reshape(ACT_ROWS, HALF)

    return window


def grad1_kernel(gat, gat_other, x3a, x3o, f0, f1, f2, f3, left):
    for n, part in enumerate((gat, gat_other)):
        for i in range(EDGE // 2):
            first = n * ACT_ROWS + 2 * i * EDGE * ROWS
            left[:, first : first + 2 * EDGE * ROWS] = part[i]
    windows = (same_window(x3a), same_window(x3o))
    grad_loop((f0, f1, f2, f3), left, windows)


def grad1(gat, gat_other, x3a, x3o):
    return call(
        grad1_kernel, "grad1", QUARTERS, [VM] * 4,
        [pltpu.VMEM((C, 2 * ACT_ROWS), BF)], 16, 4_000_000_000, 7_000_000,
    )(gat, gat_other, x3a, x3o)


SHARDS = (MEMBERS, 2 * TAPS, 2 * C)


def pack_kernel(first, second, order, out):
    perm = one_hot(order[...])
    for i in range(2):
        lanes = slice(i * C, (i + 1) * C)
        one = dot(first[:, lanes].astype(BF), perm)
        both = jnp.concatenate([one, second[:, lanes]], axis=0).astype(BF)
        for n in range(MEMBERS):
            out[n, :, lanes] = both


def pack(first, second, order):
    return call(
        pack_kernel, "pack", shape(SHARDS, BF), [VM] * 3, [], 56, 10_000_000, 1_000_000
    )(first, second, order)


def spread_kernel(shards, out1, out2, wide):
    for m in range(MEMBERS):
        rows = shards[m].astype(F32)
        for i in range(2):
            store(wide, 2 * m + i, 2 * TAPS, rows[:, i * C : (i + 1) * C], BLOCK)

    def step(t, carry):
        for k, out in enumerate((out1, out2)):
            start = pl.multiple_of((k * TAPS + t) * BLOCK, BLOCK)
            out[t] = load(wide, start, BLOCK).astype(BF)
        return carry

    lax.fori_loop(0, TAPS, step, 0)


def spread(shards):
    return call(
        spread_kernel, "spread", (shape(QUARTER, BF),) * 2, [VM],
        [pltpu.VMEM((2, 2 * TAPS * BLOCK, HALF), F32)], 8, 1_000_000, 2_000_000,
    )(shards)


def add_parts(p0, p1, p2, p3, wide):
    def step(t, carry):
        total = p0[t].astype(F32)
        for part in (p1, p2, p3):
            total = total + part[t].astype(F32)
        store(wide, pl.multiple_of(t * BLOCK, BLOCK), BLOCK, total)
        return carry

    lax.fori_loop(0, TAPS, step, 0)


def collect2(parts):
    return call(
        add_parts, "collect2", shape((2, TAPS * BLOCK, HALF), F32), [VM] * 4, [],
        4, 1_000_000, 3_000_000,
    )(*parts)


def collect_kernel(p0, p1, p2, p3, second, out, wide):
    wide[:, TAPS * BLOCK :] = second[...]
    add_parts(p0, p1, p2, p3, wide)
    for m in range(MEMBERS):
        for i in range(2):
            rows = load(wide, 2 * m + i, 2 * TAPS, BLOCK)
            out[m, :, i * C : (i + 1) * C] = rows.astype(BF)


def collect(parts, second):
    return call(
        collect_kernel, "collect", shape(SHARDS, BF), [VM] * 5,
        [pltpu.VMEM((2, 2 * TAPS * BLOCK, HALF), F32)], 8, 1_000_000, 3_000_000,
    )(*parts, second)


def adam_update(weight, first, second, grad):
    first_new = 0.9 * first + 0.1 * grad
    second_new = 0.999 * second + 0.001 * grad * grad
    fix_first = 1.0 - 0.9**10
    fix_second = 1.0 - 0.999**10
    weight_new = weight - 0.05 * (first_new / fix_first) / (
        jnp.sqrt(second_new / fix_second) + 1e-08
    )
    return (weight_new, first_new, second_new)


def adam_kernel(
    scale, parts, order, k1, m1, v1, k2, m2, v2, k1n, m1n, v1n, k2n, m2n, v2n
):
    back = one_hot(order[...]).astype(F32)
    for i in range(2):
        lanes = slice(i * C, (i + 1) * C)
        total = parts[0, :, lanes].astype(F32)
        for n in range(1, MEMBERS):
            total = total + parts[n, :, lanes].astype(F32)
        total = total * scale
        grad = lax.dot_general(
            total[:TAPS],
            back,
            (((1,), (1,)), ((), ())),
            precision=lax.Precision.HIGHEST,
            preferred_element_type=F32,
        )
        k1n[:, lanes], m1n[:, lanes], v1n[:, lanes] = adam_update(
            k1[:, lanes], m1[:, lanes], v1[:, lanes], grad
        )
        k2n[:, lanes], m2n[:, lanes], v2n[:, lanes] = adam_update(
            k2[:, lanes], m2[:, lanes], v2[:, lanes], total[TAPS:]
        )


def adam(scale, parts, order, *state):
    return call(
        functools.partial(adam_kernel, scale), "adam",
        (shape((TAPS, 2 * C), F32),) * 6, [VM] * 8, [], 6, 10_000_000, 1_000_000,
    )(parts, order, *state)


def place(x, y, z, c):
    return ((x * 4 + y) * 4 + z) * 2 + c


GRAY = [(0, 0), (1, 0), (1, 1), (0, 1)]
RING = {bits: at for at, bits in enumerate(GRAY)}


def label(bits):
    return bits[0] ^ 2 * bits[1] ^ 3 * bits[2]


def device(core, near, far):
    first, second = (near, far) if core == 0 else (far, near)
    return place(*(RING[pair] for pair in zip(first, second)), core)


TRIPLES = list(itertools.product(range(2), repeat=3))
DEVICES = list(itertools.product(range(2), TRIPLES, TRIPLES))


def turned(bits, which):
    return tuple(bit ^ (n in which) for n, bit in enumerate(bits))


NEIGHBOURS = [
    [(device(c, u, v), device(c, turned(u, (k,)), v)) for c, u, v in DEVICES] for k in range(3)
]
PARTNERS = [(n, n ^ 1) for n in range(128)]
FAR = [
    sorted(device(*d) for d in DEVICES if d[0] == c and label(d[1]) == l)
    for c in range(2)
    for l in range(4)
]


def tables():
    half = lambda c, l: [
        2 * member + i for k in range(4) for member in FAR[4 * c + (l ^ k)] for i in range(2)
    ]
    columns = half(0, 0) + half(1, 0)
    at = {channel: n for n, channel in enumerate(columns)}
    table = np.zeros((128, 2, 1, C), np.int32)
    for c, u, v in DEVICES:
        channels = half(c, label(u)) + half(1 - c, label(v))
        table[device(c, u, v), 0, 0] = channels
        table[device(c, u, v), 1, 0] = [at[channel] for channel in channels]
    return np.array(columns, np.int32).reshape(1, C), table


COLUMNS, TABLE = tables()


def exchange(value):
    return lax.all_to_all(value, "dp", 0, 0, axis_index_groups=FAR, tiled=True)


def swap(value):
    return lax.ppermute(value, "dp", PARTNERS)


def send_round(values):
    return [values[0]] + [lax.ppermute(v, "dp", to) for v, to in zip(values[1:], NEIGHBOURS)]


def after(value, *others):
    return lax.optimization_barrier((value, *others))[0]


def body(latent, out_grad, k1, m1, v1, k2, m2, v2):
    scale = 1.0 / (latent.shape[0] * lax.axis_size("dp"))
    table = lax.dynamic_index_in_dim(jnp.asarray(TABLE), lax.axis_index("dp"), keepdims=False)
    columns = jnp.asarray(COLUMNS)

    shards = exchange(pack(k1, k2, columns))
    latent = latent.transpose(1, 2, 3, 0, 4)
    cells = prep(latent, swap(latent), out_grad.transpose(1, 2, 3, 0, 4), table)
    shards, cells = lax.optimization_barrier((shards, cells))
    x3a, x3b, x3o, skip, cot = cells
    own1, own2 = spread(shards)
    own1 = send_round([own1] * 4)
    own2 = send_round([after(own2, *own1[1:])] * 4)
    other1 = [swap(value) for value in own1]
    other2 = [swap(value) for value in own2]

    act, hsel, hsend = conv1(x3b, conv1_own(x3a, own1), other1, table)
    hsel_other = swap(hsend)
    block_out, grad_pre, grad_pre_t = conv2(skip, cot, hsel, own2, other2)
    second = grad2(grad_pre_t, swap(grad_pre_t), hsel, hsel_other)
    grad_pre = after(grad_pre, *second)
    second = send_round(second)
    gat = back(act, grad_pre, own2, other2, table)
    first = send_round(grad1(gat, swap(gat), x3a, x3o))
    parts = exchange(collect(first, collect2(second)))
    new = adam(scale, parts, columns, k1, m1, v1, k2, m2, v2)
    return (block_out.transpose(3, 0, 1, 2, 4), *new)


def solution(mesh):
    wide = P("dp", None, None, None, None)
    flat = P(None, "dp")
    return jax.shard_map(
        body,
        mesh=mesh,
        in_specs=(wide, wide) + (flat,) * 6,
        out_specs=(wide,) + (flat,) * 6,
        check_vma=False,
    )
```

time: 131 us -> 115 us (0.88)
  blocking collectives: 42.9 us -> 24.1 us
  Pallas kernels: 35.8 us -> 28.4 us
  starting transfers between devices: 19.2 us -> 25.3 us
  waiting for transfers between devices: 23.6 us -> 28.6 us
    all_to_all x2 -> x1, blocking collectives: 42.9 us -> 24.1 us  [exchange(): return lax.all_to_all(value, 'dp', 0, 0, axis_index_groups=FAR, tiled=True)]
    ppermute x0 -> x12, waiting for transfers between devices: none -> 16.2 us  [send_round(): lax.ppermute(v, 'dp', to)]
    ppermute x0 -> x12, starting transfers between devices: none -> 10.8 us  [send_round(): lax.ppermute(v, 'dp', to)]
    all_to_all x3 -> x1, waiting for transfers between devices: 19 us -> 10.3 us  [exchange(): return lax.all_to_all(value, 'dp', 0, 0, axis_index_groups=FAR, tiled=True)]
    all_to_all x3 -> x1, starting transfers between devices: 17.8 us -> 10.4 us  [exchange(): return lax.all_to_all(value, 'dp', 0, 0, axis_index_groups=FAR, tiled=True)]
    pallas_call x8, Pallas kernels: 23.2 us -> 20 us  [the longest x1 6.76 us: grad1(): call(grad1_kernel, 'grad1', QUARTERS, [VM] * 4, [pltpu.VMEM((C, 2 * ACT_R...]
    ppermute x5 -> x12, starting transfers between devices: 1.36 us -> 4 us  [swap(): return lax.ppermute(value, 'dp', PARTNERS)]
    pallas_call x1, Pallas kernels: 4.6 us -> 2 us  [prep(): call(prep_kernel, 'prep', (wide, wide, wide, pre, pre), [VM] * 4, [pltpu....]
  transfers between devices with their start and end apart: 8 -> 25, of which waited for: 5 -> 12; matrix products, arithmetic and copies ran while one was open for 1% -> 1% of each run, Pallas kernels for 19% -> 15%
where the time goes in v6:
time: 115 us; the launch traced here: 113 us
  waiting for transfers between devices  28.6 us (25%)
  Pallas kernels  28.4 us (25%)
  starting transfers between devices  25.3 us (22%)
  blocking collectives  24.1 us (21%)
  local copies, waits for them, and re-layouts  5.64 us (5%)
    all_to_all x1, blocking collectives, exchange(): return lax.all_to_all(value, 'dp', 0, 0, axis_index_groups=FAR, tiled=True)  24.1 us
    ppermute x12, waiting for transfers between devices, send_round(): lax.ppermute(v, 'dp', to)  16.2 us
    ppermute x12, starting transfers between devices, send_round(): lax.ppermute(v, 'dp', to)  10.8 us
    all_to_all x1, starting transfers between devices, exchange(): return lax.all_to_all(value, 'dp', 0, 0, axis_index_groups=FAR, tiled=True)  10.4 us
    all_to_all x1, waiting for transfers between devices, exchange(): return lax.all_to_all(value, 'dp', 0, 0, axis_index_groups=FAR, tiled=True)  10.3 us
    pallas_call x1, Pallas kernels, grad1(): call(grad1_kernel, 'grad1', QUARTERS, [VM] * 4, [pltpu.VMEM((C, 2 * ACT_R...  6.76 us
    unnamed x32, local copies, waits for them, and re-layouts  4.95 us
    ppermute x12, starting transfers between devices, swap(): return lax.ppermute(value, 'dp', PARTNERS)  4 us
  transfers between devices with their start and end apart: 25, of which 12 were waited for; matrix products, arithmetic and copies ran while one was open for 1% of the time, Pallas kernels for 15%

profile of v6, /device:TPU:0, one launch (start us, length us, event | category | flops | bytes accessed | tf_op | source)
XLA Modules:
  0.0 113.0 jit_solution(549643607013547063)
XLA Ops:
  0.7 2.1 %pack.1 = bf16[16,54,512]{2,1,0:T(8,128)(2,1)} custom-call(f32[27,512]{1,0:T(8,128)} %k1.1, f32[27,512]{1,0:T(8,128)} %k2.1, s32[1,256]{1,0:T(1,128)} %constant.15.clone.order), custom_call_target="tpu_custom_call" | custom-call | flops 10000000 | bytes 1000000 | tf_op jit(solution)/shard_map/pack/pallas_call | solution.py:389
  2.7 10.4 %all-to-all-start = ((bf16[16,54,512]{2,1,0:T(8,128)(2,1)}), bf16[16,54,512]{2,1,0:T(8,128)(2,1)S(1)}, u32[]{:S(2)}, u32[]{:S(2)}) async-start(bf16[16,54,512]{2,1,0:T(8,128)(2,1)} %pack.1), calls=%async_computation | async-start | bytes 1835008 | tf_op jit(solution)/shard_map/all_to_all | solution.py:547
  13.3 0.7 dynamic-slice_bitcast_fusion.table
  14.0 1.1 collective-permute-done.other
  15.0 2.0 %prep.1 = (bf16[3,8,8,32,128]{4,3,2,1,0:T(8,128)(2,1)S(1)}, bf16[3,8,8,32,128]{4,3,2,1,0:T(8,128)(2,1)S(1)}, bf16[3,8,8,32,128]{4,3,2,1,0:T(8,128)(2,1)S(1)}, f32[144,256]{1,0:T(8,128)S(1)}, f32[144,256]{1,0:T(8,128)S(1)}) custom-call(bf16[6,6,6,4,256]{4,3,2,1,0:T(4,128)(2,1)S(1)} %bitcast.6, bf16[6,6,6,4,256]{4,3,2,1,0:T(4,128)(2,1)S(1)} %collective-permute-done.other, ...), custom_call_target="tpu_custom_call" | custom-call | flops 2000000000 | bytes 8000000 | tf_op jit(solution)/shard_map/prep/pallas_call | solution.py:120
  17.1 1.2 %copy-done.9 = bf16[3,8,8,32,128]{4,3,2,1,0:T(8,128)(2,1)} copy-done((bf16[3,8,8,32,128]{4,3,2,1,0:T(8,128)(2,1)}, bf16[3,8,8,32,128]{4,3,2,1,0:T(8,128)(2,1)S(1)}, u32[]{:S(2)}) %copy-start.9) | copy-done | bytes 1572888
  18.2 1.2 %copy-done.11 = bf16[3,8,8,32,128]{4,3,2,1,0:T(8,128)(2,1)} copy-done((bf16[3,8,8,32,128]{4,3,2,1,0:T(8,128)(2,1)}, bf16[3,8,8,32,128]{4,3,2,1,0:T(8,128)(2,1)S(1)}, u32[]{:S(2)}) %copy-start.11) | copy-done | bytes 1572888
  19.4 1.2 %copy-done.14 = bf16[3,8,8,32,128]{4,3,2,1,0:T(8,128)(2,1)} copy-done((bf16[3,8,8,32,128]{4,3,2,1,0:T(8,128)(2,1)}, bf16[3,8,8,32,128]{4,3,2,1,0:T(8,128)(2,1)S(1)}, u32[]{:S(2)}) %copy-start.14) | copy-done | bytes 1572888
  20.5 10.3 %all-to-all-done.shards = bf16[16,54,512]{2,1,0:T(8,128)(2,1)S(1)} async-done(((bf16[16,54,512]{2,1,0:T(8,128)(2,1)}), bf16[16,54,512]{2,1,0:T(8,128)(2,1)S(1)}, u32[]{:S(2)}, u32[]{:S(2)}) %all-to-all-start) | async-done | bytes 884768 | tf_op jit(solution)/shard_map/all_to_all | solution.py:547
  30.8 2.0 %spread.1 = (bf16[27,32,256]{2,1,0:T(8,128)(2,1)S(1)}, bf16[27,32,256]{2,1,0:T(8,128)(2,1)S(1)}) custom-call(bf16[16,54,512]{2,1,0:T(8,128)(2,1)S(1)} %all-to-all-done.shards), custom_call_target="tpu_custom_call" | custom-call | flops 1000000 | bytes 2000000 | tf_op jit(solution)/shard_map/spread/pallas_call | solution.py:410
  32.8 1.0 collective-permute-start.1
  33.8 1.2 %collective-permute-start.2 = (bf16[27,32,256]{2,1,0:T(8,128)(2,1)S(1)}, bf16[27,32,256]{2,1,0:T(8,128)(2,1)S(1)}, u32[]{:S(2)}, u32[]{:S(2)}) collective-permute-start(bf16[27,32,256]{2,1,0:T(8,128)(2,1)S(1)} %get-tuple-element.52.q0), channel_id=1, source_target_pairs={{0,8},{6,14},{24,16},{30,22},{96,104},{102,110},{120,112},{126,118... | collective-permute-start | bytes 1327112 | tf_op jit(solution)/shard_map/ppermute | solution.py:555
  35.0 0.8 collective-permute-start.4
  35.8 5.4 %collective-permute-done.1.q1 = bf16[27,32,256]{2,1,0:T(8,128)(2,1)S(1)} collective-permute-done((bf16[27,32,256]{2,1,0:T(8,128)(2,1)S(1)}, bf16[27,32,256]{2,1,0:T(8,128)(2,1)S(1)}, u32[]{:S(2)}, u32[]{:S(2)}) %collective-permute-start.1) | collective-permute-done | bytes 442400 | tf_op jit(solution)/shard_map/ppermute | solution.py:555
  41.2 0.9 collective-permute-done.2.q2
  42.1 1.2 %collective-permute-done.3.q3 = bf16[27,32,256]{2,1,0:T(8,128)(2,1)S(1)} collective-permute-done((bf16[27,32,256]{2,1,0:T(8,128)(2,1)S(1)}, bf16[27,32,256]{2,1,0:T(8,128)(2,1)S(1)}, u32[]{:S(2)}, u32[]{:S(2)}) %collective-permute-start.3) | collective-permute-done | bytes 442400 | tf_op jit(solution)/shard_map/ppermute | solution.py:555
  43.3 0.9 collective-permute-start.8
  44.2 1.0 collective-permute-start.9
  45.2 0.6 collective-permute-start.10
  45.8 0.6 collective-permute-start.7
  46.4 1.4 %copy-done.12 = bf16[3,8,8,32,128]{4,3,2,1,0:T(8,128)(2,1)S(1)} copy-done((bf16[3,8,8,32,128]{4,3,2,1,0:T(8,128)(2,1)S(1)}, bf16[3,8,8,32,128]{4,3,2,1,0:T(8,128)(2,1)}, u32[]{:S(2)}) %copy-start.12) | copy-done | bytes 1572888
  47.8 2.3 %conv1_own.1.part_act = f32[1152,256]{1,0:T(8,128)S(1)} custom-call(bf16[3,8,8,32,128]{4,3,2,1,0:T(8,128)(2,1)S(1)} %copy-done.12, bf16[27,32,256]{2,1,0:T(8,128)(2,1)S(1)} %get-tuple-element.52.q0, bf16[27,32,256]{2,1,0:T(8,128)(2,1)S(1)} %collective-permute-done.1.q1, bf16[27,32,256]{2,1,0:T(8,128)(2,1)S(1)} %collective-permute-done.2.q2, ...), custom_call_target="tpu_custom_call" | custom-call | flops 2000000000 | bytes 5000000 | tf_op jit(solution)/shard_map/conv1_own/pallas_call | solution.py:155
  50.3 1.3 %collective-permute-done.8.q1 = bf16[27,32,256]{2,1,0:T(8,128)(2,1)S(1)} collective-permute-done((bf16[27,32,256]{2,1,0:T(8,128)(2,1)S(1)}, bf16[27,32,256]{2,1,0:T(8,128)(2,1)S(1)}, u32[]{:S(2)}, u32[]{:S(2)}) %collective-permute-start.8) | collective-permute-done | bytes 442400 | tf_op jit(solution)/shard_map/ppermute | solution.py:555
  51.6 0.6 collective-permute-start.12
  52.2 0.4 collective-permute-done.9.q2
  52.5 1.0 collective-permute-done.10.q3
  53.5 0.6 collective-permute-start.14
  54.2 3.7 %conv1.1 = (f32[1152,256]{1,0:T(8,128)S(1)}, bf16[3,7,7,16,256]{4,3,2,1,0:T(8,128)(2,1)S(1)}, bf16[3,7,7,16,128]{4,3,2,1,0:T(8,128)(2,1)S(1)}) custom-call(bf16[3,8,8,32,128]{4,3,2,1,0:T(8,128)(2,1)S(1)} %copy-done.10, f32[1152,256]{1,0:T(8,128)S(1)} %conv1_own.1.part_act, bf16[27,32,256]{2,1,0:T(8,128)(2,1)S(1)} %collective-permute-done.4.q0, ...), custom_call_target="tpu_custom_call" | custom-call | flops 2000000000 | bytes 7000000 | tf_op jit(solution)/shard_map/conv1/pallas_call | solution.py:194
  57.9 0.3 collective-permute-start.16
  58.2 1.4 %conv2.1 = (bf16[3,3,3,4,256]{4,3,2,1,0:T(4,128)(2,1)}, bf16[144,256]{1,0:T(8,128)(2,1)S(1)}, bf16[256,144]{1,0:T(8,128)(2,1)S(1)}) custom-call(f32[144,256]{1,0:T(8,128)S(1)} %get-tuple-element.47.skip, f32[144,256]{1,0:T(8,128)S(1)} %get-tuple-element.48.cot, bf16[3,7,7,16,256]{4,3,2,1,0:T(8,128)(2,1)S(1)} %get-tuple-element.53.hsel, ...), custom_call_target="tpu_custom_call" | custom-call | flops 1500000000 | bytes 6000000 | tf_op jit(solution)/shard_map/conv2/pallas_call | solution.py:238
  59.6 0.5 collective-permute-start.15
  60.0 1.0 collective-permute-done.15.grad_t_other
  61.0 3.1 %grad2.1 = (bf16[27,32,256]{2,1,0:T(8,128)(2,1)S(1)}, bf16[27,32,256]{2,1,0:T(8,128)(2,1)S(1)}, bf16[27,32,256]{2,1,0:T(8,128)(2,1)S(1)}, bf16[27,32,256]{2,1,0:T(8,128)(2,1)S(1)}) custom-call(bf16[256,144]{1,0:T(8,128)(2,1)S(1)} %get-tuple-element.59.grad_t, bf16[256,144]{1,0:T(8,128)(2,1)S(1)} %collective-permute-done.15.grad_t_other, ...), custom_call_target="tpu_custom_call" | custom-call | flops 1000000000 | bytes 4000000 | tf_op jit(solution)/shard_map/grad2/pallas_call | solution.py:346
  64.1 1.8 %back.1.gat = bf16[3,256,384]{2,1,0:T(8,128)(2,1)S(1)} custom-call(f32[1152,256]{1,0:T(8,128)S(1)} %get-tuple-element.57.act, bf16[144,256]{1,0:T(8,128)(2,1)S(1)} %get-tuple-element.65.grad_pre, bf16[27,32,256]{2,1,0:T(8,128)(2,1)S(1)} %get-tuple-element.55.q0, bf16[27,32,256]{2,1,0:T(8,128)(2,1)S(1)} %collective-permute-done.8.q1, ...), custom_call_target="tpu_custom_call" | custom-call | flops 1500000000 | bytes 8000000 | tf_op jit(solution)/shard_map/back/pallas_call | solution.py:288
  65.9 0.5 collective-permute-start.17
  66.3 0.5 collective-permute-start.21
  66.8 1.2 %collective-permute-start.22 = (bf16[27,32,256]{2,1,0:T(8,128)(2,1)S(1)}, bf16[27,32,256]{2,1,0:T(8,128)(2,1)S(1)}, u32[]{:S(2)}, u32[]{:S(2)}) collective-permute-start(bf16[27,32,256]{2,1,0:T(8,128)(2,1)S(1)} %get-tuple-element.63), channel_id=1, source_target_pairs={{0,8},{6,14},{24,16},{30,22},{96,104},{102,110},{120,112},{126,118... | collective-permute-start | bytes 1327112 | tf_op jit(solution)/shard_map/ppermute | solution.py:555
  68.0 6.8 %grad1.1 = (bf16[27,32,256]{2,1,0:T(8,128)(2,1)S(1)}, bf16[27,32,256]{2,1,0:T(8,128)(2,1)S(1)}, bf16[27,32,256]{2,1,0:T(8,128)(2,1)S(1)}, bf16[27,32,256]{2,1,0:T(8,128)(2,1)S(1)}) custom-call(bf16[3,256,384]{2,1,0:T(8,128)(2,1)S(1)} %back.1.gat, bf16[3,256,384]{2,1,0:T(8,128)(2,1)S(1)} %collective-permute-done.17.gat_other, ...), custom_call_target="tpu_custom_call" | custom-call | flops 4000000000 | bytes 7000000 | tf_op jit(solution)/shard_map/grad1/pallas_call | solution.py:369
  74.8 1.3 %collective-permute-start.18 = (bf16[27,32,256]{2,1,0:T(8,128)(2,1)S(1)}, bf16[27,32,256]{2,1,0:T(8,128)(2,1)S(1)}, u32[]{:S(2)}, u32[]{:S(2)}) collective-permute-start(bf16[27,32,256]{2,1,0:T(8,128)(2,1)S(1)} %get-tuple-element.68), channel_id=1, source_target_pairs={{0,32},{6,38},{24,56},{30,62},{96,64},{102,70},{120,88},{126,94},{... | collective-permute-start | bytes 1327112 | tf_op jit(solution)/shard_map/ppermute | solution.py:555
  76.1 1.2 %collective-permute-start.19 = (bf16[27,32,256]{2,1,0:T(8,128)(2,1)S(1)}, bf16[27,32,256]{2,1,0:T(8,128)(2,1)S(1)}, u32[]{:S(2)}, u32[]{:S(2)}) collective-permute-start(bf16[27,32,256]{2,1,0:T(8,128)(2,1)S(1)} %get-tuple-element.69), channel_id=1, source_target_pairs={{0,8},{6,14},{24,16},{30,22},{96,104},{102,110},{120,112},{126,118... | collective-permute-start | bytes 1327112 | tf_op jit(solution)/shard_map/ppermute | solution.py:555
  77.3 1.9 %collective-permute-start.20 = (bf16[27,32,256]{2,1,0:T(8,128)(2,1)S(1)}, bf16[27,32,256]{2,1,0:T(8,128)(2,1)S(1)}, u32[]{:S(2)}, u32[]{:S(2)}) collective-permute-start(bf16[27,32,256]{2,1,0:T(8,128)(2,1)S(1)} %get-tuple-element.70), channel_id=1, source_target_pairs={{0,2},{6,4},{24,26},{30,28},{96,98},{102,100},{120,122},{126,124},... | collective-permute-start | bytes 1327112 | tf_op jit(solution)/shard_map/ppermute | solution.py:555
  79.3 0.3 collect2.1.second
  79.6 3.5 %collective-permute-done.18.p1 = bf16[27,32,256]{2,1,0:T(8,128)(2,1)S(1)} collective-permute-done((bf16[27,32,256]{2,1,0:T(8,128)(2,1)S(1)}, bf16[27,32,256]{2,1,0:T(8,128)(2,1)S(1)}, u32[]{:S(2)}, u32[]{:S(2)}) %collective-permute-start.18) | collective-permute-done | bytes 442400 | tf_op jit(solution)/shard_map/ppermute | solution.py:555
  83.2 1.2 %collective-permute-done.19.p2 = bf16[27,32,256]{2,1,0:T(8,128)(2,1)S(1)} collective-permute-done((bf16[27,32,256]{2,1,0:T(8,128)(2,1)S(1)}, bf16[27,32,256]{2,1,0:T(8,128)(2,1)S(1)}, u32[]{:S(2)}, u32[]{:S(2)}) %collective-permute-start.19) | collective-permute-done | bytes 442400 | tf_op jit(solution)/shard_map/ppermute | solution.py:555
  84.4 1.2 %collective-permute-done.20.p3 = bf16[27,32,256]{2,1,0:T(8,128)(2,1)S(1)} collective-permute-done((bf16[27,32,256]{2,1,0:T(8,128)(2,1)S(1)}, bf16[27,32,256]{2,1,0:T(8,128)(2,1)S(1)}, u32[]{:S(2)}, u32[]{:S(2)}) %collective-permute-start.20) | collective-permute-done | bytes 442400 | tf_op jit(solution)/shard_map/ppermute | solution.py:555
  85.6 1.7 %collect.1 = bf16[16,54,512]{2,1,0:T(8,128)(2,1)S(1)} custom-call(bf16[27,32,256]{2,1,0:T(8,128)(2,1)S(1)} %get-tuple-element.67.p0, bf16[27,32,256]{2,1,0:T(8,128)(2,1)S(1)} %collective-permute-done.18.p1, bf16[27,32,256]{2,1,0:T(8,128)(2,1)S(1)} %collective-permute-done.19.p2, bf16[27,32,256]{2,1,0:T(8,128)(2,1)S(1)} %collective-permute-done.20.p3, ...), custom_call_target="tpu_custom_call" | custom-call | flops 1000000 | bytes 3000000 | tf_op jit(solution)/shard_map/collect/pallas_call | solution.py:444
  87.4 24.1 %all_to_all.10.parts = bf16[16,54,512]{2,1,0:T(8,128)(2,1)S(1)} all-to-all(bf16[16,54,512]{2,1,0:T(8,128)(2,1)S(1)} %collect.1), channel_id=1, replica_groups={{0,6,24,30,42,44,50,52,74,76,82,84,96,102,120,126},{10,12,18,20,32,38,5..., dimensions={0} | all-to-all | bytes 1769472 | tf_op jit(solution)/shard_map/all_to_all | solution.py:547
  111.6 1.4 %adam.1 = (f32[27,512]{1,0:T(8,128)}, f32[27,512]{1,0:T(8,128)}, f32[27,512]{1,0:T(8,128)}, f32[27,512]{1,0:T(8,128)}, f32[27,512]{1,0:T(8,128)}, /*index=5*/f32[27,512]{1,0:T(8,128)}) custom-call(bf16[16,54,512]{2,1,0:T(8,128)(2,1)S(1)} %all_to_all.10.parts, s32[1,256]{1,0:T(1,128)S(1)} %copy-done.6, f32[27,512]{1,0:T(8,128)S(1)} %copy-done, ...), custom_call_target="tpu_custom_call" | custom-call | flops 10000000 | bytes 1000000 | tf_op jit(solution)/shard_map/adam/pallas_call | solution.py:487
  (48 shorter events, 0.3 us)
Async XLA Ops:
  0.6 12.5 %copy-start.7 = (bf16[4,6,6,6,256]{4,0,3,2,1:T(4,128)(2,1)S(1)}, bf16[4,6,6,6,256]{4,0,3,2,1:T(4,128)(2,1)}, u32[]{:S(2)}) copy-start(bf16[4,6,6,6,256]{4,0,3,2,1:T(4,128)(2,1)} %param.10) | copy-start | bytes 1327108
  0.6 14.4 %copy-start.8 = (bf16[4,3,3,3,256]{4,0,3,2,1:T(4,128)(2,1)S(1)}, bf16[4,3,3,3,256]{4,0,3,2,1:T(4,128)(2,1)}, u32[]{:S(2)}) copy-start(bf16[4,3,3,3,256]{4,0,3,2,1:T(4,128)(2,1)} %param.11) | copy-start | bytes 165892
  2.7 28.1 %all-to-all-start = ((bf16[16,54,512]{2,1,0:T(8,128)(2,1)}), bf16[16,54,512]{2,1,0:T(8,128)(2,1)S(1)}, u32[]{:S(2)}, u32[]{:S(2)}) async-start(bf16[16,54,512]{2,1,0:T(8,128)(2,1)} %pack.1), calls=%async_computation | async-start | bytes 1835008 | tf_op jit(solution)/shard_map/all_to_all | solution.py:547
  13.2 1.9 %collective-permute-start = (bf16[6,6,6,4,256]{4,3,2,1,0:T(4,128)(2,1)S(1)}, bf16[6,6,6,4,256]{4,3,2,1,0:T(4,128)(2,1)S(1)}, u32[]{:S(2)}, u32[]{:S(2)}) collective-permute-start(bf16[6,6,6,4,256]{4,3,2,1,0:T(4,128)(2,1)S(1)} %bitcast.5), channel_id=1, source_target_pairs={{0,1},{1,0},{2,3},{3,2},{4,5},{5,4},{6,7},{7,6},{8,9},{9,8},{10,11... | collective-permute-start | bytes 1327112 | tf_op jit(solution)/shard_map/ppermute | solution.py:551
  17.0 1.2 %copy-start.9 = (bf16[3,8,8,32,128]{4,3,2,1,0:T(8,128)(2,1)}, bf16[3,8,8,32,128]{4,3,2,1,0:T(8,128)(2,1)S(1)}, u32[]{:S(2)}) copy-start(bf16[3,8,8,32,128]{4,3,2,1,0:T(8,128)(2,1)S(1)} %get-tuple-element.49.x3b) | copy-start | bytes 4718596
  18.2 1.2 %copy-start.11 = (bf16[3,8,8,32,128]{4,3,2,1,0:T(8,128)(2,1)}, bf16[3,8,8,32,128]{4,3,2,1,0:T(8,128)(2,1)S(1)}, u32[]{:S(2)}) copy-start(bf16[3,8,8,32,128]{4,3,2,1,0:T(8,128)(2,1)S(1)} %get-tuple-element.50.x3a) | copy-start | bytes 4718596
  19.4 1.2 %copy-start.14 = (bf16[3,8,8,32,128]{4,3,2,1,0:T(8,128)(2,1)}, bf16[3,8,8,32,128]{4,3,2,1,0:T(8,128)(2,1)S(1)}, u32[]{:S(2)}) copy-start(bf16[3,8,8,32,128]{4,3,2,1,0:T(8,128)(2,1)S(1)} %get-tuple-element.66.x3o) | copy-start | bytes 4718596
  32.8 8.4 %collective-permute-start.1 = (bf16[27,32,256]{2,1,0:T(8,128)(2,1)S(1)}, bf16[27,32,256]{2,1,0:T(8,128)(2,1)S(1)}, u32[]{:S(2)}, u32[]{:S(2)}) collective-permute-start(bf16[27,32,256]{2,1,0:T(8,128)(2,1)S(1)} %get-tuple-element.52.q0), channel_id=1, source_target_pairs={{0,32},{6,38},{24,56},{30,62},{96,64},{102,70},{120,88},{126,94},{... | collective-permute-start | bytes 1327112 | tf_op jit(solution)/shard_map/ppermute | solution.py:555
  33.8 8.3 %collective-permute-start.2 = (bf16[27,32,256]{2,1,0:T(8,128)(2,1)S(1)}, bf16[27,32,256]{2,1,0:T(8,128)(2,1)S(1)}, u32[]{:S(2)}, u32[]{:S(2)}) collective-permute-start(bf16[27,32,256]{2,1,0:T(8,128)(2,1)S(1)} %get-tuple-element.52.q0), channel_id=1, source_target_pairs={{0,8},{6,14},{24,16},{30,22},{96,104},{102,110},{120,112},{126,118... | collective-permute-start | bytes 1327112 | tf_op jit(solution)/shard_map/ppermute | solution.py:555
  35.0 8.3 %collective-permute-start.3 = (bf16[27,32,256]{2,1,0:T(8,128)(2,1)S(1)}, bf16[27,32,256]{2,1,0:T(8,128)(2,1)S(1)}, u32[]{:S(2)}, u32[]{:S(2)}) collective-permute-start(bf16[27,32,256]{2,1,0:T(8,128)(2,1)S(1)} %get-tuple-element.52.q0), channel_id=1, source_target_pairs={{0,2},{6,4},{24,26},{30,28},{96,98},{102,100},{120,122},{126,124},... | collective-permute-start | bytes 1327112 | tf_op jit(solution)/shard_map/ppermute | solution.py:555
  35.0 10.2 %collective-permute-start.4 = (bf16[27,32,256]{2,1,0:T(8,128)(2,1)S(1)}, bf16[27,32,256]{2,1,0:T(8,128)(2,1)S(1)}, u32[]{:S(2)}, u32[]{:S(2)}) collective-permute-start(bf16[27,32,256]{2,1,0:T(8,128)(2,1)S(1)} %get-tuple-element.52.q0), channel_id=1, source_target_pairs={{0,1},{1,0},{2,3},{3,2},{4,5},{5,4},{6,7},{7,6},{8,9},{9,8},{10,11... | collective-permute-start | bytes 1327112 | tf_op jit(solution)/shard_map/ppermute | solution.py:551
  41.2 4.6 %collective-permute-start.5 = (bf16[27,32,256]{2,1,0:T(8,128)(2,1)S(1)}, bf16[27,32,256]{2,1,0:T(8,128)(2,1)S(1)}, u32[]{:S(2)}, u32[]{:S(2)}) collective-permute-start(bf16[27,32,256]{2,1,0:T(8,128)(2,1)S(1)} %collective-permute-done.1.q1), channel_id=1, source_target_pairs={{0,1},{1,0},{2,3},{3,2},{4,5},{5,4},{6,7},{7,6},{8,9},{9,8},{10,11... | collective-permute-start | bytes 1327112 | tf_op jit(solution)/shard_map/ppermute | solution.py:551
  43.3 10.9 %copy-start.10 = (bf16[3,8,8,32,128]{4,3,2,1,0:T(8,128)(2,1)S(1)}, bf16[3,8,8,32,128]{4,3,2,1,0:T(8,128)(2,1)}, u32[]{:S(2)}) copy-start(bf16[3,8,8,32,128]{4,3,2,1,0:T(8,128)(2,1)} %copy-done.9) | copy-start | bytes 4718596
  43.3 6.9 %collective-permute-start.6 = (bf16[27,32,256]{2,1,0:T(8,128)(2,1)S(1)}, bf16[27,32,256]{2,1,0:T(8,128)(2,1)S(1)}, u32[]{:S(2)}, u32[]{:S(2)}) collective-permute-start(bf16[27,32,256]{2,1,0:T(8,128)(2,1)S(1)} %collective-permute-done.2.q2), channel_id=1, source_target_pairs={{0,1},{1,0},{2,3},{3,2},{4,5},{5,4},{6,7},{7,6},{8,9},{9,8},{10,11... | collective-permute-start | bytes 1327112 | tf_op jit(solution)/shard_map/ppermute | solution.py:551
  43.3 8.3 %collective-permute-start.8 = (bf16[27,32,256]{2,1,0:T(8,128)(2,1)S(1)}, bf16[27,32,256]{2,1,0:T(8,128)(2,1)S(1)}, u32[]{:S(2)}, u32[]{:S(2)}) collective-permute-start(bf16[27,32,256]{2,1,0:T(8,128)(2,1)S(1)} %get-tuple-element.55.q0), channel_id=1, source_target_pairs={{0,32},{6,38},{24,56},{30,62},{96,64},{102,70},{120,88},{126,94},{... | collective-permute-start | bytes 1327112 | tf_op jit(solution)/shard_map/ppermute | solution.py:555
  44.2 8.3 %collective-permute-start.9 = (bf16[27,32,256]{2,1,0:T(8,128)(2,1)S(1)}, bf16[27,32,256]{2,1,0:T(8,128)(2,1)S(1)}, u32[]{:S(2)}, u32[]{:S(2)}) collective-permute-start(bf16[27,32,256]{2,1,0:T(8,128)(2,1)S(1)} %get-tuple-element.55.q0), channel_id=1, source_target_pairs={{0,8},{6,14},{24,16},{30,22},{96,104},{102,110},{120,112},{126,118... | collective-permute-start | bytes 1327112 | tf_op jit(solution)/shard_map/ppermute | solution.py:555
  45.2 8.3 %collective-permute-start.10 = (bf16[27,32,256]{2,1,0:T(8,128)(2,1)S(1)}, bf16[27,32,256]{2,1,0:T(8,128)(2,1)S(1)}, u32[]{:S(2)}, u32[]{:S(2)}) collective-permute-start(bf16[27,32,256]{2,1,0:T(8,128)(2,1)S(1)} %get-tuple-element.55.q0), channel_id=1, source_target_pairs={{0,2},{6,4},{24,26},{30,28},{96,98},{102,100},{120,122},{126,124},... | collective-permute-start | bytes 1327112 | tf_op jit(solution)/shard_map/ppermute | solution.py:555
  45.8 8.4 %collective-permute-start.7 = (bf16[27,32,256]{2,1,0:T(8,128)(2,1)S(1)}, bf16[27,32,256]{2,1,0:T(8,128)(2,1)S(1)}, u32[]{:S(2)}, u32[]{:S(2)}) collective-permute-start(bf16[27,32,256]{2,1,0:T(8,128)(2,1)S(1)} %collective-permute-done.3.q3), channel_id=1, source_target_pairs={{0,1},{1,0},{2,3},{3,2},{4,5},{5,4},{6,7},{7,6},{8,9},{9,8},{10,11... | collective-permute-start | bytes 1327112 | tf_op jit(solution)/shard_map/ppermute | solution.py:551
  46.4 1.4 %copy-start.12 = (bf16[3,8,8,32,128]{4,3,2,1,0:T(8,128)(2,1)S(1)}, bf16[3,8,8,32,128]{4,3,2,1,0:T(8,128)(2,1)}, u32[]{:S(2)}) copy-start(bf16[3,8,8,32,128]{4,3,2,1,0:T(8,128)(2,1)} %copy-done.11) | copy-start | bytes 4718596
  50.2 8.0 %collective-permute-start.11 = (bf16[27,32,256]{2,1,0:T(8,128)(2,1)S(1)}, bf16[27,32,256]{2,1,0:T(8,128)(2,1)S(1)}, u32[]{:S(2)}, u32[]{:S(2)}) collective-permute-start(bf16[27,32,256]{2,1,0:T(8,128)(2,1)S(1)} %get-tuple-element.55.q0), channel_id=1, source_target_pairs={{0,1},{1,0},{2,3},{3,2},{4,5},{5,4},{6,7},{7,6},{8,9},{9,8},{10,11... | collective-permute-start | bytes 1327112 | tf_op jit(solution)/shard_map/ppermute | solution.py:551
  51.6 6.6 %collective-permute-start.12 = (bf16[27,32,256]{2,1,0:T(8,128)(2,1)S(1)}, bf16[27,32,256]{2,1,0:T(8,128)(2,1)S(1)}, u32[]{:S(2)}, u32[]{:S(2)}) collective-permute-start(bf16[27,32,256]{2,1,0:T(8,128)(2,1)S(1)} %collective-permute-done.8.q1), channel_id=1, source_target_pairs={{0,1},{1,0},{2,3},{3,2},{4,5},{5,4},{6,7},{7,6},{8,9},{9,8},{10,11... | collective-permute-start | bytes 1327112 | tf_op jit(solution)/shard_map/ppermute | solution.py:551
  52.5 5.6 %collective-permute-start.13 = (bf16[27,32,256]{2,1,0:T(8,128)(2,1)S(1)}, bf16[27,32,256]{2,1,0:T(8,128)(2,1)S(1)}, u32[]{:S(2)}, u32[]{:S(2)}) collective-permute-start(bf16[27,32,256]{2,1,0:T(8,128)(2,1)S(1)} %collective-permute-done.9.q2), channel_id=1, source_target_pairs={{0,1},{1,0},{2,3},{3,2},{4,5},{5,4},{6,7},{7,6},{8,9},{9,8},{10,11... | collective-permute-start | bytes 1327112 | tf_op jit(solution)/shard_map/ppermute | solution.py:551
  53.5 4.7 %collective-permute-start.14 = (bf16[27,32,256]{2,1,0:T(8,128)(2,1)S(1)}, bf16[27,32,256]{2,1,0:T(8,128)(2,1)S(1)}, u32[]{:S(2)}, u32[]{:S(2)}) collective-permute-start(bf16[27,32,256]{2,1,0:T(8,128)(2,1)S(1)} %collective-permute-done.10.q3), channel_id=1, source_target_pairs={{0,1},{1,0},{2,3},{3,2},{4,5},{5,4},{6,7},{7,6},{8,9},{9,8},{10,11... | collective-permute-start | bytes 1327112 | tf_op jit(solution)/shard_map/ppermute | solution.py:551
  57.9 3.2 %collective-permute-start.16 = (bf16[3,7,7,16,128]{4,3,2,1,0:T(8,128)(2,1)S(1)}, bf16[3,7,7,16,128]{4,3,2,1,0:T(8,128)(2,1)S(1)}, u32[]{:S(2)}, u32[]{:S(2)}) collective-permute-start(bf16[3,7,7,16,128]{4,3,2,1,0:T(8,128)(2,1)S(1)} %get-tuple-element.60), channel_id=1, source_target_pairs={{0,1},{1,0},{2,3},{3,2},{4,5},{5,4},{6,7},{7,6},{8,9},{9,8},{10,11... | collective-permute-start | bytes 1806344 | tf_op jit(solution)/shard_map/ppermute | solution.py:551
  59.6 1.5 %collective-permute-start.15 = (bf16[256,144]{1,0:T(8,128)(2,1)S(1)}, bf16[256,144]{1,0:T(8,128)(2,1)S(1)}, u32[]{:S(2)}, u32[]{:S(2)}) collective-permute-start(bf16[256,144]{1,0:T(8,128)(2,1)S(1)} %get-tuple-element.59.grad_t), channel_id=1, source_target_pairs={{0,1},{1,0},{2,3},{3,2},{4,5},{5,4},{6,7},{7,6},{8,9},{9,8},{10,11... | collective-permute-start | bytes 221192 | tf_op jit(solution)/shard_map/ppermute | solution.py:551
  64.1 3.9 %copy-start.13 = (bf16[3,8,8,32,128]{4,3,2,1,0:T(8,128)(2,1)S(1)}, bf16[3,8,8,32,128]{4,3,2,1,0:T(8,128)(2,1)}, u32[]{:S(2)}) copy-start(bf16[3,8,8,32,128]{4,3,2,1,0:T(8,128)(2,1)} %copy-done.11) | copy-start | bytes 4718596
  64.1 3.9 %copy-start.15 = (bf16[3,8,8,32,128]{4,3,2,1,0:T(8,128)(2,1)S(1)}, bf16[3,8,8,32,128]{4,3,2,1,0:T(8,128)(2,1)}, u32[]{:S(2)}) copy-start(bf16[3,8,8,32,128]{4,3,2,1,0:T(8,128)(2,1)} %copy-done.14) | copy-start | bytes 4718596
  65.9 2.1 %collective-permute-start.17 = (bf16[3,256,384]{2,1,0:T(8,128)(2,1)S(1)}, bf16[3,256,384]{2,1,0:T(8,128)(2,1)S(1)}, u32[]{:S(2)}, u32[]{:S(2)}) collective-permute-start(bf16[3,256,384]{2,1,0:T(8,128)(2,1)S(1)} %back.1.gat), channel_id=1, source_target_pairs={{0,1},{1,0},{2,3},{3,2},{4,5},{5,4},{6,7},{7,6},{8,9},{9,8},{10,11... | collective-permute-start | bytes 1769480 | tf_op jit(solution)/shard_map/ppermute | solution.py:551
  66.3 11.0 %collective-permute-start.21 = (bf16[27,32,256]{2,1,0:T(8,128)(2,1)S(1)}, bf16[27,32,256]{2,1,0:T(8,128)(2,1)S(1)}, u32[]{:S(2)}, u32[]{:S(2)}) collective-permute-start(bf16[27,32,256]{2,1,0:T(8,128)(2,1)S(1)} %get-tuple-element.62), channel_id=1, source_target_pairs={{0,32},{6,38},{24,56},{30,62},{96,64},{102,70},{120,88},{126,94},{... | collective-permute-start | bytes 1327112 | tf_op jit(solution)/shard_map/ppermute | solution.py:555
  66.8 12.5 %collective-permute-start.22 = (bf16[27,32,256]{2,1,0:T(8,128)(2,1)S(1)}, bf16[27,32,256]{2,1,0:T(8,128)(2,1)S(1)}, u32[]{:S(2)}, u32[]{:S(2)}) collective-permute-start(bf16[27,32,256]{2,1,0:T(8,128)(2,1)S(1)} %get-tuple-element.63), channel_id=1, source_target_pairs={{0,8},{6,14},{24,16},{30,22},{96,104},{102,110},{120,112},{126,118... | collective-permute-start | bytes 1327112 | tf_op jit(solution)/shard_map/ppermute | solution.py:555
  68.0 11.3 %collective-permute-start.23 = (bf16[27,32,256]{2,1,0:T(8,128)(2,1)S(1)}, bf16[27,32,256]{2,1,0:T(8,128)(2,1)S(1)}, u32[]{:S(2)}, u32[]{:S(2)}) collective-permute-start(bf16[27,32,256]{2,1,0:T(8,128)(2,1)S(1)} %get-tuple-element.64), channel_id=1, source_target_pairs={{0,2},{6,4},{24,26},{30,28},{96,98},{102,100},{120,122},{126,124},... | collective-permute-start | bytes 1327112 | tf_op jit(solution)/shard_map/ppermute | solution.py:555
  74.8 8.4 %collective-permute-start.18 = (bf16[27,32,256]{2,1,0:T(8,128)(2,1)S(1)}, bf16[27,32,256]{2,1,0:T(8,128)(2,1)S(1)}, u32[]{:S(2)}, u32[]{:S(2)}) collective-permute-start(bf16[27,32,256]{2,1,0:T(8,128)(2,1)S(1)} %get-tuple-element.68), channel_id=1, source_target_pairs={{0,32},{6,38},{24,56},{30,62},{96,64},{102,70},{120,88},{126,94},{... | collective-permute-start | bytes 1327112 | tf_op jit(solution)/shard_map/ppermute | solution.py:555
  76.1 8.3 %collective-permute-start.19 = (bf16[27,32,256]{2,1,0:T(8,128)(2,1)S(1)}, bf16[27,32,256]{2,1,0:T(8,128)(2,1)S(1)}, u32[]{:S(2)}, u32[]{:S(2)}) collective-permute-start(bf16[27,32,256]{2,1,0:T(8,128)(2,1)S(1)} %get-tuple-element.69), channel_id=1, source_target_pairs={{0,8},{6,14},{24,16},{30,22},{96,104},{102,110},{120,112},{126,118... | collective-permute-start | bytes 1327112 | tf_op jit(solution)/shard_map/ppermute | solution.py:555
  77.3 8.3 %collective-permute-start.20 = (bf16[27,32,256]{2,1,0:T(8,128)(2,1)S(1)}, bf16[27,32,256]{2,1,0:T(8,128)(2,1)S(1)}, u32[]{:S(2)}, u32[]{:S(2)}) collective-permute-start(bf16[27,32,256]{2,1,0:T(8,128)(2,1)S(1)} %get-tuple-element.70), channel_id=1, source_target_pairs={{0,2},{6,4},{24,26},{30,28},{96,98},{102,100},{120,122},{126,124},... | collective-permute-start | bytes 1327112 | tf_op jit(solution)/shard_map/ppermute | solution.py:555
  87.3 24.2 %copy-start = (f32[27,512]{1,0:T(8,128)S(1)}, f32[27,512]{1,0:T(8,128)}, u32[]{:S(2)}) copy-start(f32[27,512]{1,0:T(8,128)} %k1.1) | copy-start | bytes 165892
  87.4 24.2 %copy-start.1 = (f32[27,512]{1,0:T(8,128)S(1)}, f32[27,512]{1,0:T(8,128)}, u32[]{:S(2)}) copy-start(f32[27,512]{1,0:T(8,128)} %k2.1) | copy-start | bytes 165892
  87.4 24.2 %copy-start.2 = (f32[27,512]{1,0:T(8,128)S(1)}, f32[27,512]{1,0:T(8,128)}, u32[]{:S(2)}) copy-start(f32[27,512]{1,0:T(8,128)} %m1.1) | copy-start | bytes 165892
  87.4 24.2 %copy-start.3 = (f32[27,512]{1,0:T(8,128)S(1)}, f32[27,512]{1,0:T(8,128)}, u32[]{:S(2)}) copy-start(f32[27,512]{1,0:T(8,128)} %v1.1) | copy-start | bytes 165892
  87.4 24.2 %copy-start.4 = (f32[27,512]{1,0:T(8,128)S(1)}, f32[27,512]{1,0:T(8,128)}, u32[]{:S(2)}) copy-start(f32[27,512]{1,0:T(8,128)} %m2.1) | copy-start | bytes 165892
  87.4 24.2 %copy-start.5 = (f32[27,512]{1,0:T(8,128)S(1)}, f32[27,512]{1,0:T(8,128)}, u32[]{:S(2)}) copy-start(f32[27,512]{1,0:T(8,128)} %v2.1) | copy-start | bytes 165892
  87.4 24.2 %copy-start.6 = (s32[1,256]{1,0:T(1,128)S(1)}, s32[1,256]{1,0:T(1,128)}, u32[]{:S(2)}) copy-start(s32[1,256]{1,0:T(1,128)} %constant.15.clone.order) | copy-start | bytes 3076

commit v7 on v6

--- a/solution.py
+++ b/solution.py
@@ -220,7 +220,7 @@
         for dj in range(3):
             for dl in range(3):
                 pre = pre + dot(
-                    strided_window(hsel, dl, di, dj), half_weight(quarters, di * 9 + dj * 3 + dl)
+                    strided_window(hsel, dl, di, dj), half_weight(quarters, TAPS + di * 9 + dj * 3 + dl)
                 )
     sigma = sigmoid(pre)
     store(bo, 0, PRE_ROWS, pre * sigma)
@@ -257,7 +257,7 @@
     for di in range(3):
         for dj in range(3):
             for dl in range(3):
-                term = dot_t(grad, half_weight(quarters, di * 9 + dj * 3 + dl))
+                term = dot_t(grad, half_weight(quarters, TAPS + di * 9 + dj * 3 + dl))
                 term = term.reshape(9, OUT_ROWS, C)
                 for qi in range(OUTER):
                     for qj in range(OUTER):
@@ -391,24 +391,22 @@
     )(first, second, order)
 
 
-def spread_kernel(shards, out1, out2, wide):
+def spread_kernel(shards, out, wide):
     for m in range(MEMBERS):
         rows = shards[m].astype(F32)
         for i in range(2):
             store(wide, 2 * m + i, 2 * TAPS, rows[:, i * C : (i + 1) * C], BLOCK)
 
     def step(t, carry):
-        for k, out in enumerate((out1, out2)):
-            start = pl.multiple_of((k * TAPS + t) * BLOCK, BLOCK)
-            out[t] = load(wide, start, BLOCK).astype(BF)
+        out[t] = load(wide, pl.multiple_of(t * BLOCK, BLOCK), BLOCK).astype(BF)
         return carry
 
-    lax.fori_loop(0, TAPS, step, 0)
+    lax.fori_loop(0, 2 * TAPS, step, 0)
 
 
 def spread(shards):
     return call(
-        spread_kernel, "spread", (shape(QUARTER, BF),) * 2, [VM],
+        spread_kernel, "spread", shape((2 * TAPS, BLOCK, C), BF), [VM],
         [pltpu.VMEM((2, 2 * TAPS * BLOCK, HALF), F32)], 8, 1_000_000, 2_000_000,
     )(shards)
 
@@ -566,23 +564,25 @@
 
     shards = exchange(pack(k1, k2, columns))
     latent = latent.transpose(1, 2, 3, 0, 4)
-    cells = prep(latent, swap(latent), out_grad.transpose(1, 2, 3, 0, 4), table)
-    shards, cells = lax.optimization_barrier((shards, cells))
+    other = swap(latent)
+    own = spread(shards)
+    latent = after(latent, own)
+    cells = prep(latent, other, out_grad.transpose(1, 2, 3, 0, 4), table)
+    own = send_round([own] * 4)
+    other, own[1:], cells = lax.optimization_barrier((swap(own[0]), own[1:], cells))
+    other = [other] + [swap(value) for value in own[1:]]
     x3a, x3b, x3o, skip, cot = cells
-    own1, own2 = spread(shards)
-    own1 = send_round([own1] * 4)
-    own2 = send_round([after(own2, *own1[1:])] * 4)
-    other1 = [swap(value) for value in own1]
-    other2 = [swap(value) for value in own2]
-
-    act, hsel, hsend = conv1(x3b, conv1_own(x3a, own1), other1, table)
+
+    act, hsel, hsend = conv1(x3b, conv1_own(x3a, own), other, table)
     hsel_other = swap(hsend)
-    block_out, grad_pre, grad_pre_t = conv2(skip, cot, hsel, own2, other2)
-    second = grad2(grad_pre_t, swap(grad_pre_t), hsel, hsel_other)
-    grad_pre = after(grad_pre, *second)
+    block_out, grad_pre, grad_pre_t = conv2(skip, cot, hsel, own, other)
+    grad_pre_t_other = swap(grad_pre_t)
+    gat = back(act, grad_pre, own, other, table)
+    gat_other = swap(gat)
+    second = grad2(grad_pre_t, grad_pre_t_other, hsel, hsel_other)
+    gat = after(gat, *second)
     second = send_round(second)
-    gat = back(act, grad_pre, own2, other2, table)
-    first = send_round(grad1(gat, swap(gat), x3a, x3o))
+    first = send_round(grad1(gat, gat_other, x3a, x3o))
     parts = exchange(collect(first, collect2(second)))
     new = adam(scale, parts, columns, k1, m1, v1, k2, m2, v2)
     return (block_out.transpose(3, 0, 1, 2, 4), *new)

time: 115 us -> 117 us (1.017)
  blocking collectives: 24.1 us -> 51.5 us
  starting transfers between devices: 25.3 us -> 9.85 us
  waiting for transfers between devices: 28.6 us -> 18.7 us
  Pallas kernels: 28.4 us -> 33.2 us
  local copies, waits for them, and re-layouts: 5.64 us -> 1.54 us
    all_to_all x1 -> x2, blocking collectives: 24.1 us -> 51.5 us  [exchange(): return lax.all_to_all(value, 'dp', 0, 0, axis_index_groups=FAR, tiled=True)]
    all_to_all x1 -> x0, starting transfers between devices: 10.4 us -> none  [exchange(): return lax.all_to_all(value, 'dp', 0, 0, axis_index_groups=FAR, tiled=True)]
    all_to_all x1 -> x0, waiting for transfers between devices: 10.3 us -> none  [exchange(): return lax.all_to_all(value, 'dp', 0, 0, axis_index_groups=FAR, tiled=True)]
    unnamed x32 -> x16, local copies, waits for them, and re-layouts: 4.95 us -> 0.86 us
    ppermute x12 -> x8, waiting for transfers between devices: 2.1 us -> 6.01 us  [swap(): return lax.ppermute(value, 'dp', PARTNERS)]
    ppermute x12 -> x9, waiting for transfers between devices: 16.2 us -> 12.7 us  [send_round(): lax.ppermute(v, 'dp', to)]
    ppermute x12 -> x9, starting transfers between devices: 10.8 us -> 7.84 us  [send_round(): lax.ppermute(v, 'dp', to)]
    ppermute x12 -> x8, starting transfers between devices: 4 us -> 2.01 us  [swap(): return lax.ppermute(value, 'dp', PARTNERS)]
  transfers between devices with their start and end apart: 25 -> 17, of which waited for: 12 -> 10; matrix products, arithmetic and copies ran while one was open for 1% -> 1% of each run, Pallas kernels for 15% -> 18%
where the time goes in v7:
time: 117 us; the launch traced here: 116 us
  blocking collectives  51.5 us (44%)
  Pallas kernels  33.2 us (28%)
  waiting for transfers between devices  18.7 us (16%)
  starting transfers between devices  9.85 us (8%)
  local copies, waits for them, and re-layouts  1.54 us (1%)
    all_to_all x2, blocking collectives, exchange(): return lax.all_to_all(value, 'dp', 0, 0, axis_index_groups=FAR, tiled=True)  51.5 us
    ppermute x9, waiting for transfers between devices, send_round(): lax.ppermute(v, 'dp', to)  12.7 us
    ppermute x9, starting transfers between devices, send_round(): lax.ppermute(v, 'dp', to)  7.84 us
    pallas_call x1, Pallas kernels, grad1(): call(grad1_kernel, 'grad1', QUARTERS, [VM] * 4, [pltpu.VMEM((C, 2 * ACT_R...  6.75 us
    ppermute x8, waiting for transfers between devices, swap(): return lax.ppermute(value, 'dp', PARTNERS)  6.01 us
    pallas_call x1, Pallas kernels, conv1(): call(conv1_kernel, 'conv1', (shape((ACT_ROWS, C), F32), shape((3, 7, 7, O...  4.89 us
    pallas_call x1, Pallas kernels, prep(): call(prep_kernel, 'prep', (wide, wide, wide, pre, pre), [VM] * 4, [pltpu....  3.13 us
    pallas_call x1, Pallas kernels, grad2(): call(grad2_kernel, 'grad2', QUARTERS, [VM] * 4, [pltpu.VMEM((C, 2 * PRE_R...  3.06 us
  transfers between devices with their start and end apart: 17, of which 10 were waited for; matrix products, arithmetic and copies ran while one was open for 1% of the time, Pallas kernels for 18%

profile of v7, /device:TPU:0, one launch (start us, length us, event | category | flops | bytes accessed | tf_op | source)
XLA Modules:
  0.0 115.5 jit_solution(6043320895866106836)
XLA Ops:
  0.6 2.0 %pack.1 = bf16[16,54,512]{2,1,0:T(8,128)(2,1)} custom-call(f32[27,512]{1,0:T(8,128)} %k1.1, f32[27,512]{1,0:T(8,128)} %k2.1, s32[1,256]{1,0:T(1,128)} %constant.15.clone.order), custom_call_target="tpu_custom_call" | custom-call | flops 10000000 | bytes 1000000 | tf_op jit(solution)/shard_map/pack/pallas_call | solution.py:389
  2.6 28.5 %all_to_all.10.shards = bf16[16,54,512]{2,1,0:T(8,128)(2,1)S(1)} all-to-all(bf16[16,54,512]{2,1,0:T(8,128)(2,1)} %pack.1), channel_id=1, replica_groups={{0,6,24,30,42,44,50,52,74,76,82,84,96,102,120,126},{10,12,18,20,32,38,5..., dimensions={0} | all-to-all | bytes 1769472 | tf_op jit(solution)/shard_map/all_to_all | solution.py:545
  31.1 2.1 %spread.1.q0 = bf16[54,32,256]{2,1,0:T(8,128)(2,1)S(1)} custom-call(bf16[16,54,512]{2,1,0:T(8,128)(2,1)S(1)} %all_to_all.10.shards), custom_call_target="tpu_custom_call" | custom-call | flops 1000000 | bytes 2000000 | tf_op jit(solution)/shard_map/spread/pallas_call | solution.py:408
  33.2 0.6 collective-permute-start.3
  33.9 0.6 collective-permute-start.2
  34.4 0.4 collective-permute-start.1
  34.8 0.2 collective-permute-start
  35.0 0.3 collective-permute-start.4
  35.3 0.7 dynamic-slice_bitcast_fusion.table
  36.0 2.2 %collective-permute-done.4.other = bf16[6,6,6,4,256]{4,3,2,1,0:T(4,128)(2,1)} collective-permute-done((bf16[6,6,6,4,256]{4,3,2,1,0:T(4,128)(2,1)}, bf16[6,6,6,4,256]{4,3,2,1,0:T(4,128)(2,1)}, u32[]{:S(2)}, u32[]{:S(2)}) %collective-permute-start.4) | collective-permute-done | bytes 442400 | tf_op jit(solution)/shard_map/ppermute | solution.py:549
  38.2 0.8 copy-done.7
  39.0 3.1 %prep.1 = (bf16[3,8,8,32,128]{4,3,2,1,0:T(8,128)(2,1)S(1)}, bf16[3,8,8,32,128]{4,3,2,1,0:T(8,128)(2,1)S(1)}, bf16[3,8,8,32,128]{4,3,2,1,0:T(8,128)(2,1)S(1)}, f32[144,256]{1,0:T(8,128)S(1)}, f32[144,256]{1,0:T(8,128)S(1)}) custom-call(bf16[6,6,6,4,256]{4,3,2,1,0:T(4,128)(2,1)} %bitcast.latent, bf16[6,6,6,4,256]{4,3,2,1,0:T(4,128)(2,1)} %collective-permute-done.4.other, ...), custom_call_target="tpu_custom_call" | custom-call | flops 2000000000 | bytes 8000000 | tf_op jit(solution)/shard_map/prep/pallas_call | solution.py:120
  42.2 4.2 %collective-permute-done.3.q3 = bf16[54,32,256]{2,1,0:T(8,128)(2,1)S(1)} collective-permute-done((bf16[54,32,256]{2,1,0:T(8,128)(2,1)S(1)}, bf16[54,32,256]{2,1,0:T(8,128)(2,1)S(1)}, u32[]{:S(2)}, u32[]{:S(2)}) %collective-permute-start.3) | collective-permute-done | bytes 884768 | tf_op jit(solution)/shard_map/ppermute | solution.py:553
  46.3 0.6 collective-permute-done.2.q2
  46.9 0.6 collective-permute-done.1.q1
  47.5 0.5 collective-permute-start.6
  48.0 2.3 %conv1_own.1.part_act = f32[1152,256]{1,0:T(8,128)S(1)} custom-call(bf16[3,8,8,32,128]{4,3,2,1,0:T(8,128)(2,1)S(1)} %get-tuple-element.52.x3a, bf16[54,32,256]{2,1,0:T(8,128)(2,1)S(1)} %spread.1.q0, bf16[54,32,256]{2,1,0:T(8,128)(2,1)S(1)} %collective-permute-done.1.q1, bf16[54,32,256]{2,1,0:T(8,128)(2,1)S(1)} %collective-permute-done.2.q2, ...), custom_call_target="tpu_custom_call" | custom-call | flops 2000000000 | bytes 5000000 | tf_op jit(solution)/shard_map/conv1_own/pallas_call | solution.py:155
  50.3 0.8 collective-permute-done.6.q2.p2
  51.2 1.3 %collective-permute-done.7.q3.p3 = bf16[54,32,256]{2,1,0:T(8,128)(2,1)S(1)} collective-permute-done((bf16[54,32,256]{2,1,0:T(8,128)(2,1)S(1)}, bf16[54,32,256]{2,1,0:T(8,128)(2,1)S(1)}, u32[]{:S(2)}, u32[]{:S(2)}) %collective-permute-start.7) | collective-permute-done | bytes 884768 | tf_op jit(solution)/shard_map/ppermute | solution.py:549
  52.4 4.9 %conv1.1 = (f32[1152,256]{1,0:T(8,128)S(1)}, bf16[3,7,7,16,256]{4,3,2,1,0:T(8,128)(2,1)S(1)}, bf16[3,7,7,16,128]{4,3,2,1,0:T(8,128)(2,1)S(1)}) custom-call(bf16[3,8,8,32,128]{4,3,2,1,0:T(8,128)(2,1)S(1)} %get-tuple-element.51.x3b, f32[1152,256]{1,0:T(8,128)S(1)} %conv1_own.1.part_act, bf16[54,32,256]{2,1,0:T(8,128)(2,1)} %collective-permute-done.q0.p0, ...), custom_call_target="tpu_custom_call" | custom-call | flops 2000000000 | bytes 7000000 | tf_op jit(solution)/shard_map/conv1/pallas_call | solution.py:194
  57.3 0.4 collective-permute-start.9
  57.7 2.6 %conv2.1 = (bf16[3,3,3,4,256]{4,3,2,1,0:T(4,128)(2,1)}, bf16[144,256]{1,0:T(8,128)(2,1)S(1)}, bf16[256,144]{1,0:T(8,128)(2,1)S(1)}) custom-call(f32[144,256]{1,0:T(8,128)S(1)} %get-tuple-element.49.skip, f32[144,256]{1,0:T(8,128)S(1)} %get-tuple-element.50.cot, bf16[3,7,7,16,256]{4,3,2,1,0:T(8,128)(2,1)S(1)} %get-tuple-element.57.hsel, ...), custom_call_target="tpu_custom_call" | custom-call | flops 1500000000 | bytes 6000000 | tf_op jit(solution)/shard_map/conv2/pallas_call | solution.py:238
  60.3 2.9 %back.1.gat = bf16[3,256,384]{2,1,0:T(8,128)(2,1)S(1)} custom-call(f32[1152,256]{1,0:T(8,128)S(1)} %get-tuple-element.59.act, bf16[144,256]{1,0:T(8,128)(2,1)S(1)} %get-tuple-element.60.grad_pre, bf16[54,32,256]{2,1,0:T(8,128)(2,1)S(1)} %spread.1.q0, bf16[54,32,256]{2,1,0:T(8,128)(2,1)S(1)} %collective-permute-done.1.q1, ...), custom_call_target="tpu_custom_call" | custom-call | flops 1500000000 | bytes 8000000 | tf_op jit(solution)/shard_map/back/pallas_call | solution.py:288
  63.2 0.5 collective-permute-start.10
  63.7 0.1 collective-permute-start.8
  63.8 1.7 %collective-permute-done.8.grad_t_other = bf16[256,144]{1,0:T(8,128)(2,1)S(1)} collective-permute-done((bf16[256,144]{1,0:T(8,128)(2,1)S(1)}, bf16[256,144]{1,0:T(8,128)(2,1)S(1)}, u32[]{:S(2)}, u32[]{:S(2)}) %collective-permute-start.8) | collective-permute-done | bytes 73760 | tf_op jit(solution)/shard_map/ppermute | solution.py:549
  65.5 3.1 %grad2.1 = (bf16[27,32,256]{2,1,0:T(8,128)(2,1)S(1)}, bf16[27,32,256]{2,1,0:T(8,128)(2,1)S(1)}, bf16[27,32,256]{2,1,0:T(8,128)(2,1)S(1)}, bf16[27,32,256]{2,1,0:T(8,128)(2,1)S(1)}) custom-call(bf16[256,144]{1,0:T(8,128)(2,1)S(1)} %get-tuple-element.61.grad_t, bf16[256,144]{1,0:T(8,128)(2,1)S(1)} %collective-permute-done.8.grad_t_other, ...), custom_call_target="tpu_custom_call" | custom-call | flops 1000000000 | bytes 4000000 | tf_op jit(solution)/shard_map/grad2/pallas_call | solution.py:346
  68.6 0.5 collective-permute-start.14
  69.1 1.2 %collective-permute-start.15 = (bf16[27,32,256]{2,1,0:T(8,128)(2,1)S(1)}, bf16[27,32,256]{2,1,0:T(8,128)(2,1)S(1)}, u32[]{:S(2)}, u32[]{:S(2)}) collective-permute-start(bf16[27,32,256]{2,1,0:T(8,128)(2,1)S(1)} %get-tuple-element.65), channel_id=1, source_target_pairs={{0,8},{6,14},{24,16},{30,22},{96,104},{102,110},{120,112},{126,118... | collective-permute-start | bytes 1327112 | tf_op jit(solution)/shard_map/ppermute | solution.py:553
  70.2 1.5 %collective-permute-start.16 = (bf16[27,32,256]{2,1,0:T(8,128)(2,1)S(1)}, bf16[27,32,256]{2,1,0:T(8,128)(2,1)S(1)}, u32[]{:S(2)}, u32[]{:S(2)}) collective-permute-start(bf16[27,32,256]{2,1,0:T(8,128)(2,1)S(1)} %get-tuple-element.66), channel_id=1, source_target_pairs={{0,2},{6,4},{24,26},{30,28},{96,98},{102,100},{120,122},{126,124},... | collective-permute-start | bytes 1327112 | tf_op jit(solution)/shard_map/ppermute | solution.py:553
  71.7 6.7 %grad1.1 = (bf16[27,32,256]{2,1,0:T(8,128)(2,1)S(1)}, bf16[27,32,256]{2,1,0:T(8,128)(2,1)S(1)}, bf16[27,32,256]{2,1,0:T(8,128)(2,1)S(1)}, bf16[27,32,256]{2,1,0:T(8,128)(2,1)S(1)}) custom-call(bf16[3,256,384]{2,1,0:T(8,128)(2,1)S(1)} %back.1.gat, bf16[3,256,384]{2,1,0:T(8,128)(2,1)S(1)} %collective-permute-done.10.gat_other, ...), custom_call_target="tpu_custom_call" | custom-call | flops 4000000000 | bytes 7000000 | tf_op jit(solution)/shard_map/grad1/pallas_call | solution.py:369
  78.4 2.0 %collective-permute-start.11 = (bf16[27,32,256]{2,1,0:T(8,128)(2,1)S(1)}, bf16[27,32,256]{2,1,0:T(8,128)(2,1)S(1)}, u32[]{:S(2)}, u32[]{:S(2)}) collective-permute-start(bf16[27,32,256]{2,1,0:T(8,128)(2,1)S(1)} %get-tuple-element.70), channel_id=1, source_target_pairs={{0,32},{6,38},{24,56},{30,62},{96,64},{102,70},{120,88},{126,94},{... | collective-permute-start | bytes 1327112 | tf_op jit(solution)/shard_map/ppermute | solution.py:553
  80.5 0.6 collective-permute-start.12
  81.0 0.6 collective-permute-start.13
  81.6 0.3 collect2.1.second
  81.9 4.9 %collective-permute-done.11.p1 = bf16[27,32,256]{2,1,0:T(8,128)(2,1)S(1)} collective-permute-done((bf16[27,32,256]{2,1,0:T(8,128)(2,1)S(1)}, bf16[27,32,256]{2,1,0:T(8,128)(2,1)S(1)}, u32[]{:S(2)}, u32[]{:S(2)}) %collective-permute-start.11) | collective-permute-done | bytes 442400 | tf_op jit(solution)/shard_map/ppermute | solution.py:553
  86.8 1.9 %collective-permute-done.12.p2 = bf16[27,32,256]{2,1,0:T(8,128)(2,1)S(1)} collective-permute-done((bf16[27,32,256]{2,1,0:T(8,128)(2,1)S(1)}, bf16[27,32,256]{2,1,0:T(8,128)(2,1)S(1)}, u32[]{:S(2)}, u32[]{:S(2)}) %collective-permute-start.12) | collective-permute-done | bytes 442400 | tf_op jit(solution)/shard_map/ppermute | solution.py:553
  88.8 0.6 collective-permute-done.13.p3
  89.3 1.7 %collect.1 = bf16[16,54,512]{2,1,0:T(8,128)(2,1)S(1)} custom-call(bf16[27,32,256]{2,1,0:T(8,128)(2,1)S(1)} %get-tuple-element.69.p0, bf16[27,32,256]{2,1,0:T(8,128)(2,1)S(1)} %collective-permute-done.11.p1, bf16[27,32,256]{2,1,0:T(8,128)(2,1)S(1)} %collective-permute-done.12.p2, bf16[27,32,256]{2,1,0:T(8,128)(2,1)S(1)} %collective-permute-done.13.p3, ...), custom_call_target="tpu_custom_call" | custom-call | flops 1000000 | bytes 3000000 | tf_op jit(solution)/shard_map/collect/pallas_call | solution.py:442
  91.0 0.0 copy-start
  91.0 0.0 copy-start.1
  91.1 0.0 copy-start.2
  91.1 0.0 copy-start.3
  91.1 0.0 copy-start.4
  91.1 0.0 copy-start.5
  91.1 0.0 copy-start.6
  91.1 23.0 %all_to_all.11.parts = bf16[16,54,512]{2,1,0:T(8,128)(2,1)S(1)} all-to-all(bf16[16,54,512]{2,1,0:T(8,128)(2,1)S(1)} %collect.1), channel_id=1, replica_groups={{0,6,24,30,42,44,50,52,74,76,82,84,96,102,120,126},{10,12,18,20,32,38,5..., dimensions={0} | all-to-all | bytes 1769472 | tf_op jit(solution)/shard_map/all_to_all | solution.py:545
  114.2 1.4 %adam.1 = (f32[27,512]{1,0:T(8,128)}, f32[27,512]{1,0:T(8,128)}, f32[27,512]{1,0:T(8,128)}, f32[27,512]{1,0:T(8,128)}, f32[27,512]{1,0:T(8,128)}, /*index=5*/f32[27,512]{1,0:T(8,128)}) custom-call(bf16[16,54,512]{2,1,0:T(8,128)(2,1)S(1)} %all_to_all.11.parts, s32[1,256]{1,0:T(1,128)S(1)} %copy-done.6, f32[27,512]{1,0:T(8,128)S(1)} %copy-done, ...), custom_call_target="tpu_custom_call" | custom-call | flops 10000000 | bytes 1000000 | tf_op jit(solution)/shard_map/adam/pallas_call | solution.py:485
  (17 shorter events, 0.0 us)
Async XLA Ops:
  33.2 13.1 %collective-permute-start.3 = (bf16[54,32,256]{2,1,0:T(8,128)(2,1)S(1)}, bf16[54,32,256]{2,1,0:T(8,128)(2,1)S(1)}, u32[]{:S(2)}, u32[]{:S(2)}) collective-permute-start(bf16[54,32,256]{2,1,0:T(8,128)(2,1)S(1)} %spread.1.q0), channel_id=1, source_target_pairs={{0,2},{6,4},{24,26},{30,28},{96,98},{102,100},{120,122},{126,124},... | collective-permute-start | bytes 2654216 | tf_op jit(solution)/shard_map/ppermute | solution.py:553
  33.9 13.0 %collective-permute-start.2 = (bf16[54,32,256]{2,1,0:T(8,128)(2,1)S(1)}, bf16[54,32,256]{2,1,0:T(8,128)(2,1)S(1)}, u32[]{:S(2)}, u32[]{:S(2)}) collective-permute-start(bf16[54,32,256]{2,1,0:T(8,128)(2,1)S(1)} %spread.1.q0), channel_id=1, source_target_pairs={{0,8},{6,14},{24,16},{30,22},{96,104},{102,110},{120,112},{126,118... | collective-permute-start | bytes 2654216 | tf_op jit(solution)/shard_map/ppermute | solution.py:553
  34.4 13.0 %collective-permute-start.1 = (bf16[54,32,256]{2,1,0:T(8,128)(2,1)S(1)}, bf16[54,32,256]{2,1,0:T(8,128)(2,1)S(1)}, u32[]{:S(2)}, u32[]{:S(2)}) collective-permute-start(bf16[54,32,256]{2,1,0:T(8,128)(2,1)S(1)} %spread.1.q0), channel_id=1, source_target_pairs={{0,32},{6,38},{24,56},{30,62},{96,64},{102,70},{120,88},{126,94},{... | collective-permute-start | bytes 2654216 | tf_op jit(solution)/shard_map/ppermute | solution.py:553
  34.8 12.7 %collective-permute-start = (bf16[54,32,256]{2,1,0:T(8,128)(2,1)S(1)}, bf16[54,32,256]{2,1,0:T(8,128)(2,1)}, u32[]{:S(2)}, u32[]{:S(2)}) collective-permute-start(bf16[54,32,256]{2,1,0:T(8,128)(2,1)S(1)} %spread.1.q0), channel_id=1, source_target_pairs={{0,1},{1,0},{2,3},{3,2},{4,5},{5,4},{6,7},{7,6},{8,9},{9,8},{10,11... | collective-permute-start | bytes 2654216 | tf_op jit(solution)/shard_map/ppermute | solution.py:549
  35.0 3.2 %collective-permute-start.4 = (bf16[6,6,6,4,256]{4,3,2,1,0:T(4,128)(2,1)}, bf16[6,6,6,4,256]{4,3,2,1,0:T(4,128)(2,1)}, u32[]{:S(2)}, u32[]{:S(2)}) collective-permute-start(bf16[6,6,6,4,256]{4,3,2,1,0:T(4,128)(2,1)} %bitcast.latent), channel_id=1, source_target_pairs={{0,1},{1,0},{2,3},{3,2},{4,5},{5,4},{6,7},{7,6},{8,9},{9,8},{10,11... | collective-permute-start | bytes 1327112 | tf_op jit(solution)/shard_map/ppermute | solution.py:549
  38.2 0.8 copy-start.7
  47.5 2.8 %collective-permute-start.5 = (bf16[54,32,256]{2,1,0:T(8,128)(2,1)S(1)}, bf16[54,32,256]{2,1,0:T(8,128)(2,1)S(1)}, u32[]{:S(2)}, u32[]{:S(2)}) collective-permute-start(bf16[54,32,256]{2,1,0:T(8,128)(2,1)S(1)} %collective-permute-done.1.q1), channel_id=1, source_target_pairs={{0,1},{1,0},{2,3},{3,2},{4,5},{5,4},{6,7},{7,6},{8,9},{9,8},{10,11... | collective-permute-start | bytes 2654216 | tf_op jit(solution)/shard_map/ppermute | solution.py:549
  47.5 3.7 %collective-permute-start.6 = (bf16[54,32,256]{2,1,0:T(8,128)(2,1)S(1)}, bf16[54,32,256]{2,1,0:T(8,128)(2,1)S(1)}, u32[]{:S(2)}, u32[]{:S(2)}) collective-permute-start(bf16[54,32,256]{2,1,0:T(8,128)(2,1)S(1)} %collective-permute-done.2.q2), channel_id=1, source_target_pairs={{0,1},{1,0},{2,3},{3,2},{4,5},{5,4},{6,7},{7,6},{8,9},{9,8},{10,11... | collective-permute-start | bytes 2654216 | tf_op jit(solution)/shard_map/ppermute | solution.py:549
  48.0 4.4 %collective-permute-start.7 = (bf16[54,32,256]{2,1,0:T(8,128)(2,1)S(1)}, bf16[54,32,256]{2,1,0:T(8,128)(2,1)S(1)}, u32[]{:S(2)}, u32[]{:S(2)}) collective-permute-start(bf16[54,32,256]{2,1,0:T(8,128)(2,1)S(1)} %collective-permute-done.3.q3), channel_id=1, source_target_pairs={{0,1},{1,0},{2,3},{3,2},{4,5},{5,4},{6,7},{7,6},{8,9},{9,8},{10,11... | collective-permute-start | bytes 2654216 | tf_op jit(solution)/shard_map/ppermute | solution.py:549
  57.3 8.2 %collective-permute-start.9 = (bf16[3,7,7,16,128]{4,3,2,1,0:T(8,128)(2,1)S(1)}, bf16[3,7,7,16,128]{4,3,2,1,0:T(8,128)(2,1)S(1)}, u32[]{:S(2)}, u32[]{:S(2)}) collective-permute-start(bf16[3,7,7,16,128]{4,3,2,1,0:T(8,128)(2,1)S(1)} %get-tuple-element.62), channel_id=1, source_target_pairs={{0,1},{1,0},{2,3},{3,2},{4,5},{5,4},{6,7},{7,6},{8,9},{9,8},{10,11... | collective-permute-start | bytes 1806344 | tf_op jit(solution)/shard_map/ppermute | solution.py:549
  63.2 8.4 %collective-permute-start.10 = (bf16[3,256,384]{2,1,0:T(8,128)(2,1)S(1)}, bf16[3,256,384]{2,1,0:T(8,128)(2,1)S(1)}, u32[]{:S(2)}, u32[]{:S(2)}) collective-permute-start(bf16[3,256,384]{2,1,0:T(8,128)(2,1)S(1)} %back.1.gat), channel_id=1, source_target_pairs={{0,1},{1,0},{2,3},{3,2},{4,5},{5,4},{6,7},{7,6},{8,9},{9,8},{10,11... | collective-permute-start | bytes 1769480 | tf_op jit(solution)/shard_map/ppermute | solution.py:549
  63.7 1.8 %collective-permute-start.8 = (bf16[256,144]{1,0:T(8,128)(2,1)S(1)}, bf16[256,144]{1,0:T(8,128)(2,1)S(1)}, u32[]{:S(2)}, u32[]{:S(2)}) collective-permute-start(bf16[256,144]{1,0:T(8,128)(2,1)S(1)} %get-tuple-element.61.grad_t), channel_id=1, source_target_pairs={{0,1},{1,0},{2,3},{3,2},{4,5},{5,4},{6,7},{7,6},{8,9},{9,8},{10,11... | collective-permute-start | bytes 221192 | tf_op jit(solution)/shard_map/ppermute | solution.py:549
  68.6 12.4 %collective-permute-start.14 = (bf16[27,32,256]{2,1,0:T(8,128)(2,1)S(1)}, bf16[27,32,256]{2,1,0:T(8,128)(2,1)S(1)}, u32[]{:S(2)}, u32[]{:S(2)}) collective-permute-start(bf16[27,32,256]{2,1,0:T(8,128)(2,1)S(1)} %get-tuple-element.64), channel_id=1, source_target_pairs={{0,32},{6,38},{24,56},{30,62},{96,64},{102,70},{120,88},{126,94},{... | collective-permute-start | bytes 1327112 | tf_op jit(solution)/shard_map/ppermute | solution.py:553
  69.1 12.5 %collective-permute-start.15 = (bf16[27,32,256]{2,1,0:T(8,128)(2,1)S(1)}, bf16[27,32,256]{2,1,0:T(8,128)(2,1)S(1)}, u32[]{:S(2)}, u32[]{:S(2)}) collective-permute-start(bf16[27,32,256]{2,1,0:T(8,128)(2,1)S(1)} %get-tuple-element.65), channel_id=1, source_target_pairs={{0,8},{6,14},{24,16},{30,22},{96,104},{102,110},{120,112},{126,118... | collective-permute-start | bytes 1327112 | tf_op jit(solution)/shard_map/ppermute | solution.py:553
  70.2 11.4 %collective-permute-start.16 = (bf16[27,32,256]{2,1,0:T(8,128)(2,1)S(1)}, bf16[27,32,256]{2,1,0:T(8,128)(2,1)S(1)}, u32[]{:S(2)}, u32[]{:S(2)}) collective-permute-start(bf16[27,32,256]{2,1,0:T(8,128)(2,1)S(1)} %get-tuple-element.66), channel_id=1, source_target_pairs={{0,2},{6,4},{24,26},{30,28},{96,98},{102,100},{120,122},{126,124},... | collective-permute-start | bytes 1327112 | tf_op jit(solution)/shard_map/ppermute | solution.py:553
  78.4 8.4 %collective-permute-start.11 = (bf16[27,32,256]{2,1,0:T(8,128)(2,1)S(1)}, bf16[27,32,256]{2,1,0:T(8,128)(2,1)S(1)}, u32[]{:S(2)}, u32[]{:S(2)}) collective-permute-start(bf16[27,32,256]{2,1,0:T(8,128)(2,1)S(1)} %get-tuple-element.70), channel_id=1, source_target_pairs={{0,32},{6,38},{24,56},{30,62},{96,64},{102,70},{120,88},{126,94},{... | collective-permute-start | bytes 1327112 | tf_op jit(solution)/shard_map/ppermute | solution.py:553
  80.5 8.3 %collective-permute-start.12 = (bf16[27,32,256]{2,1,0:T(8,128)(2,1)S(1)}, bf16[27,32,256]{2,1,0:T(8,128)(2,1)S(1)}, u32[]{:S(2)}, u32[]{:S(2)}) collective-permute-start(bf16[27,32,256]{2,1,0:T(8,128)(2,1)S(1)} %get-tuple-element.71), channel_id=1, source_target_pairs={{0,8},{6,14},{24,16},{30,22},{96,104},{102,110},{120,112},{126,118... | collective-permute-start | bytes 1327112 | tf_op jit(solution)/shard_map/ppermute | solution.py:553
  81.0 8.3 %collective-permute-start.13 = (bf16[27,32,256]{2,1,0:T(8,128)(2,1)S(1)}, bf16[27,32,256]{2,1,0:T(8,128)(2,1)S(1)}, u32[]{:S(2)}, u32[]{:S(2)}) collective-permute-start(bf16[27,32,256]{2,1,0:T(8,128)(2,1)S(1)} %get-tuple-element.72), channel_id=1, source_target_pairs={{0,2},{6,4},{24,26},{30,28},{96,98},{102,100},{120,122},{126,124},... | collective-permute-start | bytes 1327112 | tf_op jit(solution)/shard_map/ppermute | solution.py:553
  91.0 23.1 %copy-start = (f32[27,512]{1,0:T(8,128)S(1)}, f32[27,512]{1,0:T(8,128)}, u32[]{:S(2)}) copy-start(f32[27,512]{1,0:T(8,128)} %k1.1) | copy-start | bytes 165892
  91.0 23.1 %copy-start.1 = (f32[27,512]{1,0:T(8,128)S(1)}, f32[27,512]{1,0:T(8,128)}, u32[]{:S(2)}) copy-start(f32[27,512]{1,0:T(8,128)} %k2.1) | copy-start | bytes 165892
  91.1 23.1 %copy-start.2 = (f32[27,512]{1,0:T(8,128)S(1)}, f32[27,512]{1,0:T(8,128)}, u32[]{:S(2)}) copy-start(f32[27,512]{1,0:T(8,128)} %m1.1) | copy-start | bytes 165892
  91.1 23.1 %copy-start.3 = (f32[27,512]{1,0:T(8,128)S(1)}, f32[27,512]{1,0:T(8,128)}, u32[]{:S(2)}) copy-start(f32[27,512]{1,0:T(8,128)} %v1.1) | copy-start | bytes 165892
  91.1 23.1 %copy-start.4 = (f32[27,512]{1,0:T(8,128)S(1)}, f32[27,512]{1,0:T(8,128)}, u32[]{:S(2)}) copy-start(f32[27,512]{1,0:T(8,128)} %m2.1) | copy-start | bytes 165892
  91.1 23.1 %copy-start.5 = (f32[27,512]{1,0:T(8,128)S(1)}, f32[27,512]{1,0:T(8,128)}, u32[]{:S(2)}) copy-start(f32[27,512]{1,0:T(8,128)} %v2.1) | copy-start | bytes 165892
  91.1 23.0 %copy-start.6 = (s32[1,256]{1,0:T(1,128)S(1)}, s32[1,256]{1,0:T(1,128)}, u32[]{:S(2)}) copy-start(s32[1,256]{1,0:T(1,128)} %constant.15.clone.order) | copy-start | bytes 3076

commit v8 on v7

--- a/solution.py
+++ b/solution.py
@@ -569,8 +569,8 @@
     latent = after(latent, own)
     cells = prep(latent, other, out_grad.transpose(1, 2, 3, 0, 4), table)
     own = send_round([own] * 4)
-    other, own[1:], cells = lax.optimization_barrier((swap(own[0]), own[1:], cells))
-    other = [other] + [swap(value) for value in own[1:]]
+    own[1:], cells = lax.optimization_barrier((own[1:], cells))
+    other = [swap(value) for value in own]
     x3a, x3b, x3o, skip, cot = cells
 
     act, hsel, hsend = conv1(x3b, conv1_own(x3a, own), other, table)

time: 117 us -> 113 us (0.966)
  Pallas kernels: 33.2 us -> 29.7 us
    ppermute x8, waiting for transfers between devices: 6.01 us -> 4.74 us  [swap(): return lax.ppermute(value, 'dp', PARTNERS)]
    ppermute x9, waiting for transfers between devices: 12.7 us -> 14 us  [send_round(): lax.ppermute(v, 'dp', to)]
    pallas_call x1, Pallas kernels: 4.89 us -> 3.71 us  [conv1(): call(conv1_kernel, 'conv1', (shape((ACT_ROWS, C), F32), shape((3, 7, 7, O...]
  transfers between devices with their start and end apart: 17 -> 17, of which waited for: 10 -> 10; matrix products, arithmetic and copies ran while one was open for 1% -> 1% of each run, Pallas kernels for 18% -> 17%
where the time goes in v8:
time: 113 us; the launch traced here: 112 us
  blocking collectives  51.5 us (46%)
  Pallas kernels  29.7 us (26%)
  waiting for transfers between devices  18.7 us (17%)
  starting transfers between devices  9.85 us (9%)
  local copies, waits for them, and re-layouts  1.54 us (1%)
    all_to_all x2, blocking collectives, exchange(): return lax.all_to_all(value, 'dp', 0, 0, axis_index_groups=FAR, tiled=True)  51.5 us
    ppermute x9, waiting for transfers between devices, send_round(): lax.ppermute(v, 'dp', to)  14 us
    ppermute x9, starting transfers between devices, send_round(): lax.ppermute(v, 'dp', to)  7.84 us
    pallas_call x1, Pallas kernels, grad1(): call(grad1_kernel, 'grad1', QUARTERS, [VM] * 4, [pltpu.VMEM((C, 2 * ACT_R...  6.75 us
    ppermute x8, waiting for transfers between devices, swap(): return lax.ppermute(value, 'dp', PARTNERS)  4.74 us
    pallas_call x1, Pallas kernels, conv1(): call(conv1_kernel, 'conv1', (shape((ACT_ROWS, C), F32), shape((3, 7, 7, O...  3.71 us
    pallas_call x1, Pallas kernels, prep(): call(prep_kernel, 'prep', (wide, wide, wide, pre, pre), [VM] * 4, [pltpu....  3.13 us
    pallas_call x1, Pallas kernels, grad2(): call(grad2_kernel, 'grad2', QUARTERS, [VM] * 4, [pltpu.VMEM((C, 2 * PRE_R...  3.07 us
  transfers between devices with their start and end apart: 17, of which 10 were waited for; matrix products, arithmetic and copies ran while one was open for 1% of the time, Pallas kernels for 17%

profile of v8, /device:TPU:0, one launch (start us, length us, event | category | flops | bytes accessed | tf_op | source)
XLA Modules:
  0.0 112.1 jit_solution(13989514116887044767)
XLA Ops:
  0.6 2.0 %pack.1 = bf16[16,54,512]{2,1,0:T(8,128)(2,1)} custom-call(f32[27,512]{1,0:T(8,128)} %k1.1, f32[27,512]{1,0:T(8,128)} %k2.1, s32[1,256]{1,0:T(1,128)} %constant.15.clone.order), custom_call_target="tpu_custom_call" | custom-call | flops 10000000 | bytes 1000000 | tf_op jit(solution)/shard_map/pack/pallas_call | solution.py:389
  2.6 28.5 %all_to_all.10.shards = bf16[16,54,512]{2,1,0:T(8,128)(2,1)S(1)} all-to-all(bf16[16,54,512]{2,1,0:T(8,128)(2,1)} %pack.1), channel_id=1, replica_groups={{0,6,24,30,42,44,50,52,74,76,82,84,96,102,120,126},{10,12,18,20,32,38,5..., dimensions={0} | all-to-all | bytes 1769472 | tf_op jit(solution)/shard_map/all_to_all | solution.py:545
  31.1 2.1 %spread.1.q0 = bf16[54,32,256]{2,1,0:T(8,128)(2,1)S(1)} custom-call(bf16[16,54,512]{2,1,0:T(8,128)(2,1)S(1)} %all_to_all.10.shards), custom_call_target="tpu_custom_call" | custom-call | flops 1000000 | bytes 2000000 | tf_op jit(solution)/shard_map/spread/pallas_call | solution.py:408
  33.2 0.6 collective-permute-start.2
  33.9 0.6 collective-permute-start.1
  34.4 0.4 collective-permute-start
  34.8 0.2 collective-permute-start.3
  35.0 0.7 dynamic-slice_bitcast_fusion.table
  35.7 0.3 collective-permute-start.4
  36.0 0.9 collective-permute-done.3.other
  37.0 0.8 copy-done.7
  37.8 3.1 %prep.1 = (bf16[3,8,8,32,128]{4,3,2,1,0:T(8,128)(2,1)S(1)}, bf16[3,8,8,32,128]{4,3,2,1,0:T(8,128)(2,1)S(1)}, bf16[3,8,8,32,128]{4,3,2,1,0:T(8,128)(2,1)S(1)}, f32[144,256]{1,0:T(8,128)S(1)}, f32[144,256]{1,0:T(8,128)S(1)}) custom-call(bf16[6,6,6,4,256]{4,3,2,1,0:T(4,128)(2,1)} %bitcast.latent, bf16[6,6,6,4,256]{4,3,2,1,0:T(4,128)(2,1)} %collective-permute-done.3.other, ...), custom_call_target="tpu_custom_call" | custom-call | flops 2000000000 | bytes 8000000 | tf_op jit(solution)/shard_map/prep/pallas_call | solution.py:120
  40.9 5.4 %collective-permute-done.2.q3 = bf16[54,32,256]{2,1,0:T(8,128)(2,1)S(1)} collective-permute-done((bf16[54,32,256]{2,1,0:T(8,128)(2,1)S(1)}, bf16[54,32,256]{2,1,0:T(8,128)(2,1)S(1)}, u32[]{:S(2)}, u32[]{:S(2)}) %collective-permute-start.2) | collective-permute-done | bytes 884768 | tf_op jit(solution)/shard_map/ppermute | solution.py:553
  46.3 0.6 collective-permute-done.1.q2
  46.9 0.6 collective-permute-done.q1
  47.5 0.5 collective-permute-start.6
  48.0 2.3 %conv1_own.1.part_act = f32[1152,256]{1,0:T(8,128)S(1)} custom-call(bf16[3,8,8,32,128]{4,3,2,1,0:T(8,128)(2,1)S(1)} %get-tuple-element.51.x3a, bf16[54,32,256]{2,1,0:T(8,128)(2,1)S(1)} %spread.1.q0, bf16[54,32,256]{2,1,0:T(8,128)(2,1)S(1)} %collective-permute-done.q1, bf16[54,32,256]{2,1,0:T(8,128)(2,1)S(1)} %collective-permute-done.1.q2, ...), custom_call_target="tpu_custom_call" | custom-call | flops 2000000000 | bytes 5000000 | tf_op jit(solution)/shard_map/conv1_own/pallas_call | solution.py:155
  50.3 0.8 collective-permute-done.6.q2.p2
  51.2 1.3 %collective-permute-done.7.q3.p3 = bf16[54,32,256]{2,1,0:T(8,128)(2,1)S(1)} collective-permute-done((bf16[54,32,256]{2,1,0:T(8,128)(2,1)S(1)}, bf16[54,32,256]{2,1,0:T(8,128)(2,1)S(1)}, u32[]{:S(2)}, u32[]{:S(2)}) %collective-permute-start.7) | collective-permute-done | bytes 884768 | tf_op jit(solution)/shard_map/ppermute | solution.py:549
  52.4 3.7 %conv1.1 = (f32[1152,256]{1,0:T(8,128)S(1)}, bf16[3,7,7,16,256]{4,3,2,1,0:T(8,128)(2,1)S(1)}, bf16[3,7,7,16,128]{4,3,2,1,0:T(8,128)(2,1)S(1)}) custom-call(bf16[3,8,8,32,128]{4,3,2,1,0:T(8,128)(2,1)S(1)} %get-tuple-element.50.x3b, f32[1152,256]{1,0:T(8,128)S(1)} %conv1_own.1.part_act, bf16[54,32,256]{2,1,0:T(8,128)(2,1)S(1)} %collective-permute-done.4.q0.p0, ...), custom_call_target="tpu_custom_call" | custom-call | flops 2000000000 | bytes 7000000 | tf_op jit(solution)/shard_map/conv1/pallas_call | solution.py:194
  56.1 0.2 collective-permute-start.9
  56.4 1.4 %conv2.1 = (bf16[3,3,3,4,256]{4,3,2,1,0:T(4,128)(2,1)}, bf16[144,256]{1,0:T(8,128)(2,1)S(1)}, bf16[256,144]{1,0:T(8,128)(2,1)S(1)}) custom-call(f32[144,256]{1,0:T(8,128)S(1)} %get-tuple-element.48.skip, f32[144,256]{1,0:T(8,128)S(1)} %get-tuple-element.49.cot, bf16[3,7,7,16,256]{4,3,2,1,0:T(8,128)(2,1)S(1)} %get-tuple-element.55.hsel, ...), custom_call_target="tpu_custom_call" | custom-call | flops 1500000000 | bytes 6000000 | tf_op jit(solution)/shard_map/conv2/pallas_call | solution.py:238
  57.8 1.8 %back.1.gat = bf16[3,256,384]{2,1,0:T(8,128)(2,1)S(1)} custom-call(f32[1152,256]{1,0:T(8,128)S(1)} %get-tuple-element.57.act, bf16[144,256]{1,0:T(8,128)(2,1)S(1)} %get-tuple-element.58.grad_pre, bf16[54,32,256]{2,1,0:T(8,128)(2,1)S(1)} %spread.1.q0, bf16[54,32,256]{2,1,0:T(8,128)(2,1)S(1)} %collective-permute-done.q1, ...), custom_call_target="tpu_custom_call" | custom-call | flops 1500000000 | bytes 8000000 | tf_op jit(solution)/shard_map/back/pallas_call | solution.py:288
  59.6 0.6 collective-permute-start.10
  60.2 0.1 collective-permute-start.8
  60.3 1.7 %collective-permute-done.8.grad_t_other = bf16[256,144]{1,0:T(8,128)(2,1)S(1)} collective-permute-done((bf16[256,144]{1,0:T(8,128)(2,1)S(1)}, bf16[256,144]{1,0:T(8,128)(2,1)S(1)}, u32[]{:S(2)}, u32[]{:S(2)}) %collective-permute-start.8) | collective-permute-done | bytes 73760 | tf_op jit(solution)/shard_map/ppermute | solution.py:549
  62.0 3.1 %grad2.1 = (bf16[27,32,256]{2,1,0:T(8,128)(2,1)S(1)}, bf16[27,32,256]{2,1,0:T(8,128)(2,1)S(1)}, bf16[27,32,256]{2,1,0:T(8,128)(2,1)S(1)}, bf16[27,32,256]{2,1,0:T(8,128)(2,1)S(1)}) custom-call(bf16[256,144]{1,0:T(8,128)(2,1)S(1)} %get-tuple-element.59.grad_t, bf16[256,144]{1,0:T(8,128)(2,1)S(1)} %collective-permute-done.8.grad_t_other, ...), custom_call_target="tpu_custom_call" | custom-call | flops 1000000000 | bytes 4000000 | tf_op jit(solution)/shard_map/grad2/pallas_call | solution.py:346
  65.1 0.5 collective-permute-start.14
  65.6 1.2 %collective-permute-start.15 = (bf16[27,32,256]{2,1,0:T(8,128)(2,1)S(1)}, bf16[27,32,256]{2,1,0:T(8,128)(2,1)S(1)}, u32[]{:S(2)}, u32[]{:S(2)}) collective-permute-start(bf16[27,32,256]{2,1,0:T(8,128)(2,1)S(1)} %get-tuple-element.63), channel_id=1, source_target_pairs={{0,8},{6,14},{24,16},{30,22},{96,104},{102,110},{120,112},{126,118... | collective-permute-start | bytes 1327112 | tf_op jit(solution)/shard_map/ppermute | solution.py:553
  66.7 1.5 %collective-permute-start.16 = (bf16[27,32,256]{2,1,0:T(8,128)(2,1)S(1)}, bf16[27,32,256]{2,1,0:T(8,128)(2,1)S(1)}, u32[]{:S(2)}, u32[]{:S(2)}) collective-permute-start(bf16[27,32,256]{2,1,0:T(8,128)(2,1)S(1)} %get-tuple-element.64), channel_id=1, source_target_pairs={{0,2},{6,4},{24,26},{30,28},{96,98},{102,100},{120,122},{126,124},... | collective-permute-start | bytes 1327112 | tf_op jit(solution)/shard_map/ppermute | solution.py:553
  68.2 6.7 %grad1.1 = (bf16[27,32,256]{2,1,0:T(8,128)(2,1)S(1)}, bf16[27,32,256]{2,1,0:T(8,128)(2,1)S(1)}, bf16[27,32,256]{2,1,0:T(8,128)(2,1)S(1)}, bf16[27,32,256]{2,1,0:T(8,128)(2,1)S(1)}) custom-call(bf16[3,256,384]{2,1,0:T(8,128)(2,1)S(1)} %back.1.gat, bf16[3,256,384]{2,1,0:T(8,128)(2,1)S(1)} %collective-permute-done.10.gat_other, ...), custom_call_target="tpu_custom_call" | custom-call | flops 4000000000 | bytes 7000000 | tf_op jit(solution)/shard_map/grad1/pallas_call | solution.py:369
  75.0 2.0 %collective-permute-start.11 = (bf16[27,32,256]{2,1,0:T(8,128)(2,1)S(1)}, bf16[27,32,256]{2,1,0:T(8,128)(2,1)S(1)}, u32[]{:S(2)}, u32[]{:S(2)}) collective-permute-start(bf16[27,32,256]{2,1,0:T(8,128)(2,1)S(1)} %get-tuple-element.68), channel_id=1, source_target_pairs={{0,32},{6,38},{24,56},{30,62},{96,64},{102,70},{120,88},{126,94},{... | collective-permute-start | bytes 1327112 | tf_op jit(solution)/shard_map/ppermute | solution.py:553
  77.0 0.6 collective-permute-start.12
  77.5 0.6 collective-permute-start.13
  78.1 0.3 collect2.1.second
  78.4 4.9 %collective-permute-done.11.p1 = bf16[27,32,256]{2,1,0:T(8,128)(2,1)S(1)} collective-permute-done((bf16[27,32,256]{2,1,0:T(8,128)(2,1)S(1)}, bf16[27,32,256]{2,1,0:T(8,128)(2,1)S(1)}, u32[]{:S(2)}, u32[]{:S(2)}) %collective-permute-start.11) | collective-permute-done | bytes 442400 | tf_op jit(solution)/shard_map/ppermute | solution.py:553
  83.3 1.9 %collective-permute-done.12.p2 = bf16[27,32,256]{2,1,0:T(8,128)(2,1)S(1)} collective-permute-done((bf16[27,32,256]{2,1,0:T(8,128)(2,1)S(1)}, bf16[27,32,256]{2,1,0:T(8,128)(2,1)S(1)}, u32[]{:S(2)}, u32[]{:S(2)}) %collective-permute-start.12) | collective-permute-done | bytes 442400 | tf_op jit(solution)/shard_map/ppermute | solution.py:553
  85.3 0.6 collective-permute-done.13.p3
  85.8 1.7 %collect.1 = bf16[16,54,512]{2,1,0:T(8,128)(2,1)S(1)} custom-call(bf16[27,32,256]{2,1,0:T(8,128)(2,1)S(1)} %get-tuple-element.67.p0, bf16[27,32,256]{2,1,0:T(8,128)(2,1)S(1)} %collective-permute-done.11.p1, bf16[27,32,256]{2,1,0:T(8,128)(2,1)S(1)} %collective-permute-done.12.p2, bf16[27,32,256]{2,1,0:T(8,128)(2,1)S(1)} %collective-permute-done.13.p3, ...), custom_call_target="tpu_custom_call" | custom-call | flops 1000000 | bytes 3000000 | tf_op jit(solution)/shard_map/collect/pallas_call | solution.py:442
  87.5 0.0 copy-start
  87.6 0.0 copy-start.1
  87.6 0.0 copy-start.2
  87.6 0.0 copy-start.3
  87.6 0.0 copy-start.4
  87.6 0.0 copy-start.5
  87.6 0.0 copy-start.6
  87.6 23.0 %all_to_all.11.parts = bf16[16,54,512]{2,1,0:T(8,128)(2,1)S(1)} all-to-all(bf16[16,54,512]{2,1,0:T(8,128)(2,1)S(1)} %collect.1), channel_id=1, replica_groups={{0,6,24,30,42,44,50,52,74,76,82,84,96,102,120,126},{10,12,18,20,32,38,5..., dimensions={0} | all-to-all | bytes 1769472 | tf_op jit(solution)/shard_map/all_to_all | solution.py:545
  110.7 1.4 %adam.1 = (f32[27,512]{1,0:T(8,128)}, f32[27,512]{1,0:T(8,128)}, f32[27,512]{1,0:T(8,128)}, f32[27,512]{1,0:T(8,128)}, f32[27,512]{1,0:T(8,128)}, /*index=5*/f32[27,512]{1,0:T(8,128)}) custom-call(bf16[16,54,512]{2,1,0:T(8,128)(2,1)S(1)} %all_to_all.11.parts, s32[1,256]{1,0:T(1,128)S(1)} %copy-done.6, f32[27,512]{1,0:T(8,128)S(1)} %copy-done, ...), custom_call_target="tpu_custom_call" | custom-call | flops 10000000 | bytes 1000000 | tf_op jit(solution)/shard_map/adam/pallas_call | solution.py:485
  (17 shorter events, 0.0 us)
Async XLA Ops:
  33.2 13.1 %collective-permute-start.2 = (bf16[54,32,256]{2,1,0:T(8,128)(2,1)S(1)}, bf16[54,32,256]{2,1,0:T(8,128)(2,1)S(1)}, u32[]{:S(2)}, u32[]{:S(2)}) collective-permute-start(bf16[54,32,256]{2,1,0:T(8,128)(2,1)S(1)} %spread.1.q0), channel_id=1, source_target_pairs={{0,2},{6,4},{24,26},{30,28},{96,98},{102,100},{120,122},{126,124},... | collective-permute-start | bytes 2654216 | tf_op jit(solution)/shard_map/ppermute | solution.py:553
  33.9 13.0 %collective-permute-start.1 = (bf16[54,32,256]{2,1,0:T(8,128)(2,1)S(1)}, bf16[54,32,256]{2,1,0:T(8,128)(2,1)S(1)}, u32[]{:S(2)}, u32[]{:S(2)}) collective-permute-start(bf16[54,32,256]{2,1,0:T(8,128)(2,1)S(1)} %spread.1.q0), channel_id=1, source_target_pairs={{0,8},{6,14},{24,16},{30,22},{96,104},{102,110},{120,112},{126,118... | collective-permute-start | bytes 2654216 | tf_op jit(solution)/shard_map/ppermute | solution.py:553
  34.4 13.0 %collective-permute-start = (bf16[54,32,256]{2,1,0:T(8,128)(2,1)S(1)}, bf16[54,32,256]{2,1,0:T(8,128)(2,1)S(1)}, u32[]{:S(2)}, u32[]{:S(2)}) collective-permute-start(bf16[54,32,256]{2,1,0:T(8,128)(2,1)S(1)} %spread.1.q0), channel_id=1, source_target_pairs={{0,32},{6,38},{24,56},{30,62},{96,64},{102,70},{120,88},{126,94},{... | collective-permute-start | bytes 2654216 | tf_op jit(solution)/shard_map/ppermute | solution.py:553
  34.8 2.1 %collective-permute-start.3 = (bf16[6,6,6,4,256]{4,3,2,1,0:T(4,128)(2,1)}, bf16[6,6,6,4,256]{4,3,2,1,0:T(4,128)(2,1)}, u32[]{:S(2)}, u32[]{:S(2)}) collective-permute-start(bf16[6,6,6,4,256]{4,3,2,1,0:T(4,128)(2,1)} %bitcast.latent), channel_id=1, source_target_pairs={{0,1},{1,0},{2,3},{3,2},{4,5},{5,4},{6,7},{7,6},{8,9},{9,8},{10,11... | collective-permute-start | bytes 1327112 | tf_op jit(solution)/shard_map/ppermute | solution.py:549
  35.7 14.6 %collective-permute-start.4 = (bf16[54,32,256]{2,1,0:T(8,128)(2,1)S(1)}, bf16[54,32,256]{2,1,0:T(8,128)(2,1)S(1)}, u32[]{:S(2)}, u32[]{:S(2)}) collective-permute-start(bf16[54,32,256]{2,1,0:T(8,128)(2,1)S(1)} %spread.1.q0), channel_id=1, source_target_pairs={{0,1},{1,0},{2,3},{3,2},{4,5},{5,4},{6,7},{7,6},{8,9},{9,8},{10,11... | collective-permute-start | bytes 2654216 | tf_op jit(solution)/shard_map/ppermute | solution.py:549
  37.0 0.8 copy-start.7
  47.5 2.9 %collective-permute-start.5 = (bf16[54,32,256]{2,1,0:T(8,128)(2,1)S(1)}, bf16[54,32,256]{2,1,0:T(8,128)(2,1)S(1)}, u32[]{:S(2)}, u32[]{:S(2)}) collective-permute-start(bf16[54,32,256]{2,1,0:T(8,128)(2,1)S(1)} %collective-permute-done.q1), channel_id=1, source_target_pairs={{0,1},{1,0},{2,3},{3,2},{4,5},{5,4},{6,7},{7,6},{8,9},{9,8},{10,11... | collective-permute-start | bytes 2654216 | tf_op jit(solution)/shard_map/ppermute | solution.py:549
  47.5 3.7 %collective-permute-start.6 = (bf16[54,32,256]{2,1,0:T(8,128)(2,1)S(1)}, bf16[54,32,256]{2,1,0:T(8,128)(2,1)S(1)}, u32[]{:S(2)}, u32[]{:S(2)}) collective-permute-start(bf16[54,32,256]{2,1,0:T(8,128)(2,1)S(1)} %collective-permute-done.1.q2), channel_id=1, source_target_pairs={{0,1},{1,0},{2,3},{3,2},{4,5},{5,4},{6,7},{7,6},{8,9},{9,8},{10,11... | collective-permute-start | bytes 2654216 | tf_op jit(solution)/shard_map/ppermute | solution.py:549
  48.0 4.4 %collective-permute-start.7 = (bf16[54,32,256]{2,1,0:T(8,128)(2,1)S(1)}, bf16[54,32,256]{2,1,0:T(8,128)(2,1)S(1)}, u32[]{:S(2)}, u32[]{:S(2)}) collective-permute-start(bf16[54,32,256]{2,1,0:T(8,128)(2,1)S(1)} %collective-permute-done.2.q3), channel_id=1, source_target_pairs={{0,1},{1,0},{2,3},{3,2},{4,5},{5,4},{6,7},{7,6},{8,9},{9,8},{10,11... | collective-permute-start | bytes 2654216 | tf_op jit(solution)/shard_map/ppermute | solution.py:549
  56.1 5.9 %collective-permute-start.9 = (bf16[3,7,7,16,128]{4,3,2,1,0:T(8,128)(2,1)S(1)}, bf16[3,7,7,16,128]{4,3,2,1,0:T(8,128)(2,1)S(1)}, u32[]{:S(2)}, u32[]{:S(2)}) collective-permute-start(bf16[3,7,7,16,128]{4,3,2,1,0:T(8,128)(2,1)S(1)} %get-tuple-element.60), channel_id=1, source_target_pairs={{0,1},{1,0},{2,3},{3,2},{4,5},{5,4},{6,7},{7,6},{8,9},{9,8},{10,11... | collective-permute-start | bytes 1806344 | tf_op jit(solution)/shard_map/ppermute | solution.py:549
  59.6 8.6 %collective-permute-start.10 = (bf16[3,256,384]{2,1,0:T(8,128)(2,1)S(1)}, bf16[3,256,384]{2,1,0:T(8,128)(2,1)S(1)}, u32[]{:S(2)}, u32[]{:S(2)}) collective-permute-start(bf16[3,256,384]{2,1,0:T(8,128)(2,1)S(1)} %back.1.gat), channel_id=1, source_target_pairs={{0,1},{1,0},{2,3},{3,2},{4,5},{5,4},{6,7},{7,6},{8,9},{9,8},{10,11... | collective-permute-start | bytes 1769480 | tf_op jit(solution)/shard_map/ppermute | solution.py:549
  60.2 1.8 %collective-permute-start.8 = (bf16[256,144]{1,0:T(8,128)(2,1)S(1)}, bf16[256,144]{1,0:T(8,128)(2,1)S(1)}, u32[]{:S(2)}, u32[]{:S(2)}) collective-permute-start(bf16[256,144]{1,0:T(8,128)(2,1)S(1)} %get-tuple-element.59.grad_t), channel_id=1, source_target_pairs={{0,1},{1,0},{2,3},{3,2},{4,5},{5,4},{6,7},{7,6},{8,9},{9,8},{10,11... | collective-permute-start | bytes 221192 | tf_op jit(solution)/shard_map/ppermute | solution.py:549
  65.1 12.4 %collective-permute-start.14 = (bf16[27,32,256]{2,1,0:T(8,128)(2,1)S(1)}, bf16[27,32,256]{2,1,0:T(8,128)(2,1)S(1)}, u32[]{:S(2)}, u32[]{:S(2)}) collective-permute-start(bf16[27,32,256]{2,1,0:T(8,128)(2,1)S(1)} %get-tuple-element.62), channel_id=1, source_target_pairs={{0,32},{6,38},{24,56},{30,62},{96,64},{102,70},{120,88},{126,94},{... | collective-permute-start | bytes 1327112 | tf_op jit(solution)/shard_map/ppermute | solution.py:553
  65.6 12.5 %collective-permute-start.15 = (bf16[27,32,256]{2,1,0:T(8,128)(2,1)S(1)}, bf16[27,32,256]{2,1,0:T(8,128)(2,1)S(1)}, u32[]{:S(2)}, u32[]{:S(2)}) collective-permute-start(bf16[27,32,256]{2,1,0:T(8,128)(2,1)S(1)} %get-tuple-element.63), channel_id=1, source_target_pairs={{0,8},{6,14},{24,16},{30,22},{96,104},{102,110},{120,112},{126,118... | collective-permute-start | bytes 1327112 | tf_op jit(solution)/shard_map/ppermute | solution.py:553
  66.7 11.4 %collective-permute-start.16 = (bf16[27,32,256]{2,1,0:T(8,128)(2,1)S(1)}, bf16[27,32,256]{2,1,0:T(8,128)(2,1)S(1)}, u32[]{:S(2)}, u32[]{:S(2)}) collective-permute-start(bf16[27,32,256]{2,1,0:T(8,128)(2,1)S(1)} %get-tuple-element.64), channel_id=1, source_target_pairs={{0,2},{6,4},{24,26},{30,28},{96,98},{102,100},{120,122},{126,124},... | collective-permute-start | bytes 1327112 | tf_op jit(solution)/shard_map/ppermute | solution.py:553
  75.0 8.4 %collective-permute-start.11 = (bf16[27,32,256]{2,1,0:T(8,128)(2,1)S(1)}, bf16[27,32,256]{2,1,0:T(8,128)(2,1)S(1)}, u32[]{:S(2)}, u32[]{:S(2)}) collective-permute-start(bf16[27,32,256]{2,1,0:T(8,128)(2,1)S(1)} %get-tuple-element.68), channel_id=1, source_target_pairs={{0,32},{6,38},{24,56},{30,62},{96,64},{102,70},{120,88},{126,94},{... | collective-permute-start | bytes 1327112 | tf_op jit(solution)/shard_map/ppermute | solution.py:553
  77.0 8.3 %collective-permute-start.12 = (bf16[27,32,256]{2,1,0:T(8,128)(2,1)S(1)}, bf16[27,32,256]{2,1,0:T(8,128)(2,1)S(1)}, u32[]{:S(2)}, u32[]{:S(2)}) collective-permute-start(bf16[27,32,256]{2,1,0:T(8,128)(2,1)S(1)} %get-tuple-element.69), channel_id=1, source_target_pairs={{0,8},{6,14},{24,16},{30,22},{96,104},{102,110},{120,112},{126,118... | collective-permute-start | bytes 1327112 | tf_op jit(solution)/shard_map/ppermute | solution.py:553
  77.5 8.3 %collective-permute-start.13 = (bf16[27,32,256]{2,1,0:T(8,128)(2,1)S(1)}, bf16[27,32,256]{2,1,0:T(8,128)(2,1)S(1)}, u32[]{:S(2)}, u32[]{:S(2)}) collective-permute-start(bf16[27,32,256]{2,1,0:T(8,128)(2,1)S(1)} %get-tuple-element.70), channel_id=1, source_target_pairs={{0,2},{6,4},{24,26},{30,28},{96,98},{102,100},{120,122},{126,124},... | collective-permute-start | bytes 1327112 | tf_op jit(solution)/shard_map/ppermute | solution.py:553
  87.5 23.1 %copy-start = (f32[27,512]{1,0:T(8,128)S(1)}, f32[27,512]{1,0:T(8,128)}, u32[]{:S(2)}) copy-start(f32[27,512]{1,0:T(8,128)} %k1.1) | copy-start | bytes 165892
  87.6 23.1 %copy-start.1 = (f32[27,512]{1,0:T(8,128)S(1)}, f32[27,512]{1,0:T(8,128)}, u32[]{:S(2)}) copy-start(f32[27,512]{1,0:T(8,128)} %k2.1) | copy-start | bytes 165892
  87.6 23.1 %copy-start.2 = (f32[27,512]{1,0:T(8,128)S(1)}, f32[27,512]{1,0:T(8,128)}, u32[]{:S(2)}) copy-start(f32[27,512]{1,0:T(8,128)} %m1.1) | copy-start | bytes 165892
  87.6 23.1 %copy-start.3 = (f32[27,512]{1,0:T(8,128)S(1)}, f32[27,512]{1,0:T(8,128)}, u32[]{:S(2)}) copy-start(f32[27,512]{1,0:T(8,128)} %v1.1) | copy-start | bytes 165892
  87.6 23.1 %copy-start.4 = (f32[27,512]{1,0:T(8,128)S(1)}, f32[27,512]{1,0:T(8,128)}, u32[]{:S(2)}) copy-start(f32[27,512]{1,0:T(8,128)} %m2.1) | copy-start | bytes 165892
  87.6 23.1 %copy-start.5 = (f32[27,512]{1,0:T(8,128)S(1)}, f32[27,512]{1,0:T(8,128)}, u32[]{:S(2)}) copy-start(f32[27,512]{1,0:T(8,128)} %v2.1) | copy-start | bytes 165892
  87.6 23.1 %copy-start.6 = (s32[1,256]{1,0:T(1,128)S(1)}, s32[1,256]{1,0:T(1,128)}, u32[]{:S(2)}) copy-start(s32[1,256]{1,0:T(1,128)} %constant.15.clone.order) | copy-start | bytes 3076

commit v9 on v8

--- a/solution.py
+++ b/solution.py
@@ -500,6 +500,16 @@
     return bits[0] ^ 2 * bits[1] ^ 3 * bits[2]
 
 
+TWIST = (0, 1, 2)
+
+
+def kind(near, far):
+    twist = 0
+    for bit, turn in zip(far, TWIST):
+        twist ^= bit * turn
+    return label(near) ^ twist
+
+
 def device(core, near, far):
     first, second = (near, far) if core == 0 else (far, near)
     return place(*(RING[pair] for pair in zip(first, second)), core)
@@ -518,7 +528,7 @@
 ]
 PARTNERS = [(n, n ^ 1) for n in range(128)]
 FAR = [
-    sorted(device(*d) for d in DEVICES if d[0] == c and label(d[1]) == l)
+    sorted(device(*d) for d in DEVICES if d[0] == c and kind(*d[1:]) == l)
     for c in range(2)
     for l in range(4)
 ]
@@ -532,7 +542,7 @@
     at = {channel: n for n, channel in enumerate(columns)}
     table = np.zeros((128, 2, 1, C), np.int32)
     for c, u, v in DEVICES:
-        channels = half(c, label(u)) + half(1 - c, label(v))
+        channels = half(c, kind(u, v)) + half(1 - c, kind(v, u))
         table[device(c, u, v), 0, 0] = channels
         table[device(c, u, v), 1, 0] = [at[channel] for channel in channels]
     return np.array(columns, np.int32).reshape(1, C), table
@@ -569,7 +579,7 @@
     latent = after(latent, own)
     cells = prep(latent, other, out_grad.transpose(1, 2, 3, 0, 4), table)
     own = send_round([own] * 4)
-    own[1:], cells = lax.optimization_barrier((own[1:], cells))
+    own[1:] = [after(value, cells[0]) for value in own[1:]]
     other = [swap(value) for value in own]
     x3a, x3b, x3o, skip, cot = cells
 

time: 113 us -> 112 us (level)
  waiting for transfers between devices: 18.7 us -> 17 us
  starting transfers between devices: 9.85 us -> 11.5 us
  blocking collectives: 51.5 us -> 49.9 us
    all_to_all x2, blocking collectives: 51.5 us -> 49.9 us  [exchange(): return lax.all_to_all(value, 'dp', 0, 0, axis_index_groups=FAR, tiled=True)]
    ppermute x9, waiting for transfers between devices: 14 us -> 12.5 us  [send_round(): lax.ppermute(v, 'dp', to)]
    ppermute x8, starting transfers between devices: 2.01 us -> 3.51 us  [swap(): return lax.ppermute(value, 'dp', PARTNERS)]
  transfers between devices with their start and end apart: 17 -> 17, of which waited for: 10 -> 9; matrix products, arithmetic and copies ran while one was open for 1% -> 1% of each run, Pallas kernels for 17% -> 17%
where the time goes in v9:
time: 112 us; the launch traced here: 110 us
  blocking collectives  49.9 us (45%)
  Pallas kernels  29.6 us (26%)
  waiting for transfers between devices  17 us (15%)
  starting transfers between devices  11.5 us (10%)
  local copies, waits for them, and re-layouts  1.54 us (1%)
    all_to_all x2, blocking collectives, exchange(): return lax.all_to_all(value, 'dp', 0, 0, axis_index_groups=FAR, tiled=True)  49.9 us
    ppermute x9, waiting for transfers between devices, send_round(): lax.ppermute(v, 'dp', to)  12.5 us
    ppermute x9, starting transfers between devices, send_round(): lax.ppermute(v, 'dp', to)  7.97 us
    pallas_call x1, Pallas kernels, grad1(): call(grad1_kernel, 'grad1', QUARTERS, [VM] * 4, [pltpu.VMEM((C, 2 * ACT_R...  6.75 us
    ppermute x8, waiting for transfers between devices, swap(): return lax.ppermute(value, 'dp', PARTNERS)  4.49 us
    pallas_call x1, Pallas kernels, conv1(): call(conv1_kernel, 'conv1', (shape((ACT_ROWS, C), F32), shape((3, 7, 7, O...  3.72 us
    ppermute x8, starting transfers between devices, swap(): return lax.ppermute(value, 'dp', PARTNERS)  3.51 us
    pallas_call x1, Pallas kernels, prep(): call(prep_kernel, 'prep', (wide, wide, wide, pre, pre), [VM] * 4, [pltpu....  3.13 us
  transfers between devices with their start and end apart: 17, of which 9 were waited for; matrix products, arithmetic and copies ran while one was open for 1% of the time, Pallas kernels for 17%

profile of v9, /device:TPU:0, one launch (start us, length us, event | category | flops | bytes accessed | tf_op | source)
XLA Modules:
  0.0 110.3 jit_solution(17963254095975040083)
XLA Ops:
  0.6 2.0 %pack.1 = bf16[16,54,512]{2,1,0:T(8,128)(2,1)} custom-call(f32[27,512]{1,0:T(8,128)} %k1.1, f32[27,512]{1,0:T(8,128)} %k2.1, s32[1,256]{1,0:T(1,128)} %constant.15.clone.order), custom_call_target="tpu_custom_call" | custom-call | flops 10000000 | bytes 1000000 | tf_op jit(solution)/shard_map/pack/pallas_call | solution.py:389
  2.6 26.6 %all_to_all.10.shards = bf16[16,54,512]{2,1,0:T(8,128)(2,1)S(1)} all-to-all(bf16[16,54,512]{2,1,0:T(8,128)(2,1)} %pack.1), channel_id=1, replica_groups={{0,14,18,28,36,42,54,56,68,74,86,88,96,110,114,124},{4,10,22,24,32,46,5..., dimensions={0} | all-to-all | bytes 1769472 | tf_op jit(solution)/shard_map/all_to_all | solution.py:555
  29.2 2.1 %spread.1.q0 = bf16[54,32,256]{2,1,0:T(8,128)(2,1)S(1)} custom-call(bf16[16,54,512]{2,1,0:T(8,128)(2,1)S(1)} %all_to_all.10.shards), custom_call_target="tpu_custom_call" | custom-call | flops 1000000 | bytes 2000000 | tf_op jit(solution)/shard_map/spread/pallas_call | solution.py:408
  31.3 1.7 %collective-permute-start.3 = (bf16[54,32,256]{2,1,0:T(8,128)(2,1)S(1)}, bf16[54,32,256]{2,1,0:T(8,128)(2,1)S(1)}, u32[]{:S(2)}, u32[]{:S(2)}) collective-permute-start(bf16[54,32,256]{2,1,0:T(8,128)(2,1)S(1)} %spread.1.q0), channel_id=1, source_target_pairs={{0,2},{6,4},{24,26},{30,28},{96,98},{102,100},{120,122},{126,124},... | collective-permute-start | bytes 2654216 | tf_op jit(solution)/shard_map/ppermute | solution.py:563
  33.0 1.1 %collective-permute-start = (bf16[6,6,6,4,256]{4,3,2,1,0:T(4,128)(2,1)}, bf16[6,6,6,4,256]{4,3,2,1,0:T(4,128)(2,1)}, u32[]{:S(2)}, u32[]{:S(2)}) collective-permute-start(bf16[6,6,6,4,256]{4,3,2,1,0:T(4,128)(2,1)} %bitcast.latent), channel_id=1, source_target_pairs={{0,1},{1,0},{2,3},{3,2},{4,5},{5,4},{6,7},{7,6},{8,9},{9,8},{10,11... | collective-permute-start | bytes 1327112 | tf_op jit(solution)/shard_map/ppermute | solution.py:559
  34.2 0.7 dynamic-slice_bitcast_fusion.table
  34.9 0.0 collective-permute-start.4
  34.9 1.1 collective-permute-done.other
  35.9 0.8 copy-done.7
  36.8 3.1 %prep.1 = (bf16[3,8,8,32,128]{4,3,2,1,0:T(8,128)(2,1)S(1)}, bf16[3,8,8,32,128]{4,3,2,1,0:T(8,128)(2,1)S(1)}, bf16[3,8,8,32,128]{4,3,2,1,0:T(8,128)(2,1)S(1)}, f32[144,256]{1,0:T(8,128)S(1)}, f32[144,256]{1,0:T(8,128)S(1)}) custom-call(bf16[6,6,6,4,256]{4,3,2,1,0:T(4,128)(2,1)} %bitcast.latent, bf16[6,6,6,4,256]{4,3,2,1,0:T(4,128)(2,1)} %collective-permute-done.other, ...), custom_call_target="tpu_custom_call" | custom-call | flops 2000000000 | bytes 8000000 | tf_op jit(solution)/shard_map/prep/pallas_call | solution.py:120
  39.9 4.5 %collective-permute-done.3.q3 = bf16[54,32,256]{2,1,0:T(8,128)(2,1)S(1)} collective-permute-done((bf16[54,32,256]{2,1,0:T(8,128)(2,1)S(1)}, bf16[54,32,256]{2,1,0:T(8,128)(2,1)S(1)}, u32[]{:S(2)}, u32[]{:S(2)}) %collective-permute-start.3) | collective-permute-done | bytes 884768 | tf_op jit(solution)/shard_map/ppermute | solution.py:563
  44.4 1.7 %collective-permute-done.2.q2 = bf16[54,32,256]{2,1,0:T(8,128)(2,1)S(1)} collective-permute-done((bf16[54,32,256]{2,1,0:T(8,128)(2,1)S(1)}, bf16[54,32,256]{2,1,0:T(8,128)(2,1)S(1)}, u32[]{:S(2)}, u32[]{:S(2)}) %collective-permute-start.2) | collective-permute-done | bytes 884768 | tf_op jit(solution)/shard_map/ppermute | solution.py:563
  46.1 0.0 collective-permute-done.1.q1
  46.1 0.6 collective-permute-start.5
  46.7 0.0 collective-permute-start.6
  46.7 0.5 collective-permute-start.7
  47.2 2.3 %conv1_own.1.part_act = f32[1152,256]{1,0:T(8,128)S(1)} custom-call(bf16[3,8,8,32,128]{4,3,2,1,0:T(8,128)(2,1)S(1)} %get-tuple-element.41.x3a, bf16[54,32,256]{2,1,0:T(8,128)(2,1)S(1)} %spread.1.q0, bf16[54,32,256]{2,1,0:T(8,128)(2,1)S(1)} %collective-permute-done.1.q1, bf16[54,32,256]{2,1,0:T(8,128)(2,1)S(1)} %collective-permute-done.2.q2, ...), custom_call_target="tpu_custom_call" | custom-call | flops 2000000000 | bytes 5000000 | tf_op jit(solution)/shard_map/conv1_own/pallas_call | solution.py:155
  49.6 0.5 collective-permute-done.6.q2.p2
  50.1 1.3 %collective-permute-done.7.q3.p3 = bf16[54,32,256]{2,1,0:T(8,128)(2,1)S(1)} collective-permute-done((bf16[54,32,256]{2,1,0:T(8,128)(2,1)S(1)}, bf16[54,32,256]{2,1,0:T(8,128)(2,1)S(1)}, u32[]{:S(2)}, u32[]{:S(2)}) %collective-permute-start.7) | collective-permute-done | bytes 884768 | tf_op jit(solution)/shard_map/ppermute | solution.py:559
  51.3 3.7 %conv1.1 = (f32[1152,256]{1,0:T(8,128)S(1)}, bf16[3,7,7,16,256]{4,3,2,1,0:T(8,128)(2,1)S(1)}, bf16[3,7,7,16,128]{4,3,2,1,0:T(8,128)(2,1)S(1)}) custom-call(bf16[3,8,8,32,128]{4,3,2,1,0:T(8,128)(2,1)S(1)} %get-tuple-element.40.x3b, f32[1152,256]{1,0:T(8,128)S(1)} %conv1_own.1.part_act, bf16[54,32,256]{2,1,0:T(8,128)(2,1)S(1)} %collective-permute-done.4.q0.p0, ...), custom_call_target="tpu_custom_call" | custom-call | flops 2000000000 | bytes 7000000 | tf_op jit(solution)/shard_map/conv1/pallas_call | solution.py:194
  55.0 0.5 collective-permute-start.9
  55.5 1.4 %conv2.1 = (bf16[3,3,3,4,256]{4,3,2,1,0:T(4,128)(2,1)}, bf16[144,256]{1,0:T(8,128)(2,1)S(1)}, bf16[256,144]{1,0:T(8,128)(2,1)S(1)}) custom-call(f32[144,256]{1,0:T(8,128)S(1)} %get-tuple-element.38.skip, f32[144,256]{1,0:T(8,128)S(1)} %get-tuple-element.39.cot, bf16[3,7,7,16,256]{4,3,2,1,0:T(8,128)(2,1)S(1)} %get-tuple-element.45.hsel, ...), custom_call_target="tpu_custom_call" | custom-call | flops 1500000000 | bytes 6000000 | tf_op jit(solution)/shard_map/conv2/pallas_call | solution.py:238
  56.9 1.8 %back.1.gat = bf16[3,256,384]{2,1,0:T(8,128)(2,1)S(1)} custom-call(f32[1152,256]{1,0:T(8,128)S(1)} %get-tuple-element.47.act, bf16[144,256]{1,0:T(8,128)(2,1)S(1)} %get-tuple-element.48.grad_pre, bf16[54,32,256]{2,1,0:T(8,128)(2,1)S(1)} %spread.1.q0, bf16[54,32,256]{2,1,0:T(8,128)(2,1)S(1)} %collective-permute-done.1.q1, ...), custom_call_target="tpu_custom_call" | custom-call | flops 1500000000 | bytes 8000000 | tf_op jit(solution)/shard_map/back/pallas_call | solution.py:288
  58.7 0.4 collective-permute-start.10
  59.1 0.4 collective-permute-start.8
  59.5 1.7 %collective-permute-done.8.grad_t_other = bf16[256,144]{1,0:T(8,128)(2,1)S(1)} collective-permute-done((bf16[256,144]{1,0:T(8,128)(2,1)S(1)}, bf16[256,144]{1,0:T(8,128)(2,1)S(1)}, u32[]{:S(2)}, u32[]{:S(2)}) %collective-permute-start.8) | collective-permute-done | bytes 73760 | tf_op jit(solution)/shard_map/ppermute | solution.py:559
  61.1 3.1 %grad2.1 = (bf16[27,32,256]{2,1,0:T(8,128)(2,1)S(1)}, bf16[27,32,256]{2,1,0:T(8,128)(2,1)S(1)}, bf16[27,32,256]{2,1,0:T(8,128)(2,1)S(1)}, bf16[27,32,256]{2,1,0:T(8,128)(2,1)S(1)}) custom-call(bf16[256,144]{1,0:T(8,128)(2,1)S(1)} %get-tuple-element.49.grad_t, bf16[256,144]{1,0:T(8,128)(2,1)S(1)} %collective-permute-done.8.grad_t_other, ...), custom_call_target="tpu_custom_call" | custom-call | flops 1000000000 | bytes 4000000 | tf_op jit(solution)/shard_map/grad2/pallas_call | solution.py:346
  64.2 0.1 collective-permute-start.14
  64.3 1.6 %collective-permute-start.15 = (bf16[27,32,256]{2,1,0:T(8,128)(2,1)S(1)}, bf16[27,32,256]{2,1,0:T(8,128)(2,1)S(1)}, u32[]{:S(2)}, u32[]{:S(2)}) collective-permute-start(bf16[27,32,256]{2,1,0:T(8,128)(2,1)S(1)} %get-tuple-element.53), channel_id=1, source_target_pairs={{0,8},{6,14},{24,16},{30,22},{96,104},{102,110},{120,112},{126,118... | collective-permute-start | bytes 1327112 | tf_op jit(solution)/shard_map/ppermute | solution.py:563
  65.9 1.6 %collective-permute-start.16 = (bf16[27,32,256]{2,1,0:T(8,128)(2,1)S(1)}, bf16[27,32,256]{2,1,0:T(8,128)(2,1)S(1)}, u32[]{:S(2)}, u32[]{:S(2)}) collective-permute-start(bf16[27,32,256]{2,1,0:T(8,128)(2,1)S(1)} %get-tuple-element.54), channel_id=1, source_target_pairs={{0,2},{6,4},{24,26},{30,28},{96,98},{102,100},{120,122},{126,124},... | collective-permute-start | bytes 1327112 | tf_op jit(solution)/shard_map/ppermute | solution.py:563
  67.6 6.7 %grad1.1 = (bf16[27,32,256]{2,1,0:T(8,128)(2,1)S(1)}, bf16[27,32,256]{2,1,0:T(8,128)(2,1)S(1)}, bf16[27,32,256]{2,1,0:T(8,128)(2,1)S(1)}, bf16[27,32,256]{2,1,0:T(8,128)(2,1)S(1)}) custom-call(bf16[3,256,384]{2,1,0:T(8,128)(2,1)S(1)} %back.1.gat, bf16[3,256,384]{2,1,0:T(8,128)(2,1)S(1)} %collective-permute-done.10.gat_other, ...), custom_call_target="tpu_custom_call" | custom-call | flops 4000000000 | bytes 7000000 | tf_op jit(solution)/shard_map/grad1/pallas_call | solution.py:369
  74.3 0.7 collective-permute-start.11
  75.0 0.4 collective-permute-start.12
  75.5 1.7 %collective-permute-start.13 = (bf16[27,32,256]{2,1,0:T(8,128)(2,1)S(1)}, bf16[27,32,256]{2,1,0:T(8,128)(2,1)S(1)}, u32[]{:S(2)}, u32[]{:S(2)}) collective-permute-start(bf16[27,32,256]{2,1,0:T(8,128)(2,1)S(1)} %get-tuple-element.60), channel_id=1, source_target_pairs={{0,2},{6,4},{24,26},{30,28},{96,98},{102,100},{120,122},{126,124},... | collective-permute-start | bytes 1327112 | tf_op jit(solution)/shard_map/ppermute | solution.py:563
  77.2 0.3 collect2.1.second
  77.5 5.1 %collective-permute-done.11.p1 = bf16[27,32,256]{2,1,0:T(8,128)(2,1)S(1)} collective-permute-done((bf16[27,32,256]{2,1,0:T(8,128)(2,1)S(1)}, bf16[27,32,256]{2,1,0:T(8,128)(2,1)S(1)}, u32[]{:S(2)}, u32[]{:S(2)}) %collective-permute-start.11) | collective-permute-done | bytes 442400 | tf_op jit(solution)/shard_map/ppermute | solution.py:563
  82.7 0.7 collective-permute-done.12.p2
  83.3 0.5 collective-permute-done.13.p3
  83.8 1.7 %collect.1 = bf16[16,54,512]{2,1,0:T(8,128)(2,1)S(1)} custom-call(bf16[27,32,256]{2,1,0:T(8,128)(2,1)S(1)} %get-tuple-element.57.p0, bf16[27,32,256]{2,1,0:T(8,128)(2,1)S(1)} %collective-permute-done.11.p1, bf16[27,32,256]{2,1,0:T(8,128)(2,1)S(1)} %collective-permute-done.12.p2, bf16[27,32,256]{2,1,0:T(8,128)(2,1)S(1)} %collective-permute-done.13.p3, ...), custom_call_target="tpu_custom_call" | custom-call | flops 1000000 | bytes 3000000 | tf_op jit(solution)/shard_map/collect/pallas_call | solution.py:442
  85.5 0.0 copy-start
  85.5 0.0 copy-start.1
  85.5 0.0 copy-start.2
  85.5 0.0 copy-start.3
  85.6 0.0 copy-start.4
  85.6 0.0 copy-start.5
  85.6 0.0 copy-start.6
  85.6 23.3 %all_to_all.11.parts = bf16[16,54,512]{2,1,0:T(8,128)(2,1)S(1)} all-to-all(bf16[16,54,512]{2,1,0:T(8,128)(2,1)S(1)} %collect.1), channel_id=1, replica_groups={{0,14,18,28,36,42,54,56,68,74,86,88,96,110,114,124},{4,10,22,24,32,46,5..., dimensions={0} | all-to-all | bytes 1769472 | tf_op jit(solution)/shard_map/all_to_all | solution.py:555
  109.0 1.4 %adam.1 = (f32[27,512]{1,0:T(8,128)}, f32[27,512]{1,0:T(8,128)}, f32[27,512]{1,0:T(8,128)}, f32[27,512]{1,0:T(8,128)}, f32[27,512]{1,0:T(8,128)}, /*index=5*/f32[27,512]{1,0:T(8,128)}) custom-call(bf16[16,54,512]{2,1,0:T(8,128)(2,1)S(1)} %all_to_all.11.parts, s32[1,256]{1,0:T(1,128)S(1)} %copy-done.6, f32[27,512]{1,0:T(8,128)S(1)} %copy-done, ...), custom_call_target="tpu_custom_call" | custom-call | flops 10000000 | bytes 1000000 | tf_op jit(solution)/shard_map/adam/pallas_call | solution.py:485
  (17 shorter events, 0.0 us)
Async XLA Ops:
  31.3 13.1 %collective-permute-start.3 = (bf16[54,32,256]{2,1,0:T(8,128)(2,1)S(1)}, bf16[54,32,256]{2,1,0:T(8,128)(2,1)S(1)}, u32[]{:S(2)}, u32[]{:S(2)}) collective-permute-start(bf16[54,32,256]{2,1,0:T(8,128)(2,1)S(1)} %spread.1.q0), channel_id=1, source_target_pairs={{0,2},{6,4},{24,26},{30,28},{96,98},{102,100},{120,122},{126,124},... | collective-permute-start | bytes 2654216 | tf_op jit(solution)/shard_map/ppermute | solution.py:563
  33.0 13.0 %collective-permute-start.2 = (bf16[54,32,256]{2,1,0:T(8,128)(2,1)S(1)}, bf16[54,32,256]{2,1,0:T(8,128)(2,1)S(1)}, u32[]{:S(2)}, u32[]{:S(2)}) collective-permute-start(bf16[54,32,256]{2,1,0:T(8,128)(2,1)S(1)} %spread.1.q0), channel_id=1, source_target_pairs={{0,8},{6,14},{24,16},{30,22},{96,104},{102,110},{120,112},{126,118... | collective-permute-start | bytes 2654216 | tf_op jit(solution)/shard_map/ppermute | solution.py:563
  33.0 13.0 %collective-permute-start.1 = (bf16[54,32,256]{2,1,0:T(8,128)(2,1)S(1)}, bf16[54,32,256]{2,1,0:T(8,128)(2,1)S(1)}, u32[]{:S(2)}, u32[]{:S(2)}) collective-permute-start(bf16[54,32,256]{2,1,0:T(8,128)(2,1)S(1)} %spread.1.q0), channel_id=1, source_target_pairs={{0,32},{6,38},{24,56},{30,62},{96,64},{102,70},{120,88},{126,94},{... | collective-permute-start | bytes 2654216 | tf_op jit(solution)/shard_map/ppermute | solution.py:563
  33.0 2.9 %collective-permute-start = (bf16[6,6,6,4,256]{4,3,2,1,0:T(4,128)(2,1)}, bf16[6,6,6,4,256]{4,3,2,1,0:T(4,128)(2,1)}, u32[]{:S(2)}, u32[]{:S(2)}) collective-permute-start(bf16[6,6,6,4,256]{4,3,2,1,0:T(4,128)(2,1)} %bitcast.latent), channel_id=1, source_target_pairs={{0,1},{1,0},{2,3},{3,2},{4,5},{5,4},{6,7},{7,6},{8,9},{9,8},{10,11... | collective-permute-start | bytes 1327112 | tf_op jit(solution)/shard_map/ppermute | solution.py:559
  34.9 14.7 %collective-permute-start.4 = (bf16[54,32,256]{2,1,0:T(8,128)(2,1)S(1)}, bf16[54,32,256]{2,1,0:T(8,128)(2,1)S(1)}, u32[]{:S(2)}, u32[]{:S(2)}) collective-permute-start(bf16[54,32,256]{2,1,0:T(8,128)(2,1)S(1)} %spread.1.q0), channel_id=1, source_target_pairs={{0,1},{1,0},{2,3},{3,2},{4,5},{5,4},{6,7},{7,6},{8,9},{9,8},{10,11... | collective-permute-start | bytes 2654216 | tf_op jit(solution)/shard_map/ppermute | solution.py:559
  35.9 0.8 copy-start.7
  46.1 3.5 %collective-permute-start.5 = (bf16[54,32,256]{2,1,0:T(8,128)(2,1)S(1)}, bf16[54,32,256]{2,1,0:T(8,128)(2,1)S(1)}, u32[]{:S(2)}, u32[]{:S(2)}) collective-permute-start(bf16[54,32,256]{2,1,0:T(8,128)(2,1)S(1)} %collective-permute-done.1.q1), channel_id=1, source_target_pairs={{0,1},{1,0},{2,3},{3,2},{4,5},{5,4},{6,7},{7,6},{8,9},{9,8},{10,11... | collective-permute-start | bytes 2654216 | tf_op jit(solution)/shard_map/ppermute | solution.py:559
  46.7 3.3 %collective-permute-start.6 = (bf16[54,32,256]{2,1,0:T(8,128)(2,1)S(1)}, bf16[54,32,256]{2,1,0:T(8,128)(2,1)S(1)}, u32[]{:S(2)}, u32[]{:S(2)}) collective-permute-start(bf16[54,32,256]{2,1,0:T(8,128)(2,1)S(1)} %collective-permute-done.2.q2), channel_id=1, source_target_pairs={{0,1},{1,0},{2,3},{3,2},{4,5},{5,4},{6,7},{7,6},{8,9},{9,8},{10,11... | collective-permute-start | bytes 2654216 | tf_op jit(solution)/shard_map/ppermute | solution.py:559
  46.7 4.6 %collective-permute-start.7 = (bf16[54,32,256]{2,1,0:T(8,128)(2,1)S(1)}, bf16[54,32,256]{2,1,0:T(8,128)(2,1)S(1)}, u32[]{:S(2)}, u32[]{:S(2)}) collective-permute-start(bf16[54,32,256]{2,1,0:T(8,128)(2,1)S(1)} %collective-permute-done.3.q3), channel_id=1, source_target_pairs={{0,1},{1,0},{2,3},{3,2},{4,5},{5,4},{6,7},{7,6},{8,9},{9,8},{10,11... | collective-permute-start | bytes 2654216 | tf_op jit(solution)/shard_map/ppermute | solution.py:559
  55.0 6.1 %collective-permute-start.9 = (bf16[3,7,7,16,128]{4,3,2,1,0:T(8,128)(2,1)S(1)}, bf16[3,7,7,16,128]{4,3,2,1,0:T(8,128)(2,1)S(1)}, u32[]{:S(2)}, u32[]{:S(2)}) collective-permute-start(bf16[3,7,7,16,128]{4,3,2,1,0:T(8,128)(2,1)S(1)} %get-tuple-element.50), channel_id=1, source_target_pairs={{0,1},{1,0},{2,3},{3,2},{4,5},{5,4},{6,7},{7,6},{8,9},{9,8},{10,11... | collective-permute-start | bytes 1806344 | tf_op jit(solution)/shard_map/ppermute | solution.py:559
  58.7 8.9 %collective-permute-start.10 = (bf16[3,256,384]{2,1,0:T(8,128)(2,1)S(1)}, bf16[3,256,384]{2,1,0:T(8,128)(2,1)S(1)}, u32[]{:S(2)}, u32[]{:S(2)}) collective-permute-start(bf16[3,256,384]{2,1,0:T(8,128)(2,1)S(1)} %back.1.gat), channel_id=1, source_target_pairs={{0,1},{1,0},{2,3},{3,2},{4,5},{5,4},{6,7},{7,6},{8,9},{9,8},{10,11... | collective-permute-start | bytes 1769480 | tf_op jit(solution)/shard_map/ppermute | solution.py:559
  59.1 2.1 %collective-permute-start.8 = (bf16[256,144]{1,0:T(8,128)(2,1)S(1)}, bf16[256,144]{1,0:T(8,128)(2,1)S(1)}, u32[]{:S(2)}, u32[]{:S(2)}) collective-permute-start(bf16[256,144]{1,0:T(8,128)(2,1)S(1)} %get-tuple-element.49.grad_t), channel_id=1, source_target_pairs={{0,1},{1,0},{2,3},{3,2},{4,5},{5,4},{6,7},{7,6},{8,9},{9,8},{10,11... | collective-permute-start | bytes 221192 | tf_op jit(solution)/shard_map/ppermute | solution.py:559
  64.2 11.3 %collective-permute-start.14 = (bf16[27,32,256]{2,1,0:T(8,128)(2,1)S(1)}, bf16[27,32,256]{2,1,0:T(8,128)(2,1)S(1)}, u32[]{:S(2)}, u32[]{:S(2)}) collective-permute-start(bf16[27,32,256]{2,1,0:T(8,128)(2,1)S(1)} %get-tuple-element.52), channel_id=1, source_target_pairs={{0,32},{6,38},{24,56},{30,62},{96,64},{102,70},{120,88},{126,94},{... | collective-permute-start | bytes 1327112 | tf_op jit(solution)/shard_map/ppermute | solution.py:563
  64.3 12.9 %collective-permute-start.15 = (bf16[27,32,256]{2,1,0:T(8,128)(2,1)S(1)}, bf16[27,32,256]{2,1,0:T(8,128)(2,1)S(1)}, u32[]{:S(2)}, u32[]{:S(2)}) collective-permute-start(bf16[27,32,256]{2,1,0:T(8,128)(2,1)S(1)} %get-tuple-element.53), channel_id=1, source_target_pairs={{0,8},{6,14},{24,16},{30,22},{96,104},{102,110},{120,112},{126,118... | collective-permute-start | bytes 1327112 | tf_op jit(solution)/shard_map/ppermute | solution.py:563
  65.9 11.3 %collective-permute-start.16 = (bf16[27,32,256]{2,1,0:T(8,128)(2,1)S(1)}, bf16[27,32,256]{2,1,0:T(8,128)(2,1)S(1)}, u32[]{:S(2)}, u32[]{:S(2)}) collective-permute-start(bf16[27,32,256]{2,1,0:T(8,128)(2,1)S(1)} %get-tuple-element.54), channel_id=1, source_target_pairs={{0,2},{6,4},{24,26},{30,28},{96,98},{102,100},{120,122},{126,124},... | collective-permute-start | bytes 1327112 | tf_op jit(solution)/shard_map/ppermute | solution.py:563
  74.3 8.4 %collective-permute-start.11 = (bf16[27,32,256]{2,1,0:T(8,128)(2,1)S(1)}, bf16[27,32,256]{2,1,0:T(8,128)(2,1)S(1)}, u32[]{:S(2)}, u32[]{:S(2)}) collective-permute-start(bf16[27,32,256]{2,1,0:T(8,128)(2,1)S(1)} %get-tuple-element.58), channel_id=1, source_target_pairs={{0,32},{6,38},{24,56},{30,62},{96,64},{102,70},{120,88},{126,94},{... | collective-permute-start | bytes 1327112 | tf_op jit(solution)/shard_map/ppermute | solution.py:563
  75.0 8.3 %collective-permute-start.12 = (bf16[27,32,256]{2,1,0:T(8,128)(2,1)S(1)}, bf16[27,32,256]{2,1,0:T(8,128)(2,1)S(1)}, u32[]{:S(2)}, u32[]{:S(2)}) collective-permute-start(bf16[27,32,256]{2,1,0:T(8,128)(2,1)S(1)} %get-tuple-element.59), channel_id=1, source_target_pairs={{0,8},{6,14},{24,16},{30,22},{96,104},{102,110},{120,112},{126,118... | collective-permute-start | bytes 1327112 | tf_op jit(solution)/shard_map/ppermute | solution.py:563
  75.5 8.3 %collective-permute-start.13 = (bf16[27,32,256]{2,1,0:T(8,128)(2,1)S(1)}, bf16[27,32,256]{2,1,0:T(8,128)(2,1)S(1)}, u32[]{:S(2)}, u32[]{:S(2)}) collective-permute-start(bf16[27,32,256]{2,1,0:T(8,128)(2,1)S(1)} %get-tuple-element.60), channel_id=1, source_target_pairs={{0,2},{6,4},{24,26},{30,28},{96,98},{102,100},{120,122},{126,124},... | collective-permute-start | bytes 1327112 | tf_op jit(solution)/shard_map/ppermute | solution.py:563
  85.5 23.4 %copy-start = (f32[27,512]{1,0:T(8,128)S(1)}, f32[27,512]{1,0:T(8,128)}, u32[]{:S(2)}) copy-start(f32[27,512]{1,0:T(8,128)} %k1.1) | copy-start | bytes 165892
  85.5 23.4 %copy-start.1 = (f32[27,512]{1,0:T(8,128)S(1)}, f32[27,512]{1,0:T(8,128)}, u32[]{:S(2)}) copy-start(f32[27,512]{1,0:T(8,128)} %k2.1) | copy-start | bytes 165892
  85.5 23.4 %copy-start.2 = (f32[27,512]{1,0:T(8,128)S(1)}, f32[27,512]{1,0:T(8,128)}, u32[]{:S(2)}) copy-start(f32[27,512]{1,0:T(8,128)} %m1.1) | copy-start | bytes 165892
  85.5 23.4 %copy-start.3 = (f32[27,512]{1,0:T(8,128)S(1)}, f32[27,512]{1,0:T(8,128)}, u32[]{:S(2)}) copy-start(f32[27,512]{1,0:T(8,128)} %v1.1) | copy-start | bytes 165892
  85.6 23.4 %copy-start.4 = (f32[27,512]{1,0:T(8,128)S(1)}, f32[27,512]{1,0:T(8,128)}, u32[]{:S(2)}) copy-start(f32[27,512]{1,0:T(8,128)} %m2.1) | copy-start | bytes 165892
  85.6 23.4 %copy-start.5 = (f32[27,512]{1,0:T(8,128)S(1)}, f32[27,512]{1,0:T(8,128)}, u32[]{:S(2)}) copy-start(f32[27,512]{1,0:T(8,128)} %v2.1) | copy-start | bytes 165892
  85.6 23.4 %copy-start.6 = (s32[1,256]{1,0:T(1,128)S(1)}, s32[1,256]{1,0:T(1,128)}, u32[]{:S(2)}) copy-start(s32[1,256]{1,0:T(1,128)} %constant.15.clone.order) | copy-start | bytes 3076

commit v10 on v9

--- a/solution.py
+++ b/solution.py
@@ -300,28 +300,22 @@
         lax.broadcasted_iota(jnp.int32, (C, C), 0) == lax.broadcasted_iota(jnp.int32, (C, C), 1)
     ).astype(BF)
 
-    def product(taps):
-        right = [
-            jnp.concatenate([window(t // 9, t // 3 % 3, t % 3) for t in taps], axis=1)
-            for window in windows
-        ]
-        total = dot(left[...], jnp.concatenate(right, axis=0)).astype(BF)
-        for n in range(0, len(taps), 2):
-            two = taps[n : n + 2]
-            width = HALF * len(two)
-            turned = dot_t(eye[:width, :width], total[:, n * HALF : n * HALF + width]).astype(BF)
-            for m, t in enumerate(two):
-                for k, quarter in enumerate(quarters):
-                    first = m * HALF + k * BLOCK
-                    quarter[t] = turned[first : first + BLOCK]
-
-    def step(n, carry):
-        product([GROUP * n + k for k in range(GROUP)])
-        return carry
-
-    whole = TAPS // GROUP
-    lax.fori_loop(0, whole, step, 0)
-    product(list(range(GROUP * whole, TAPS)))
+    right = [
+        jnp.concatenate(
+            [window(t // 9, t // 3 % 3, t % 3) for t in range(TAPS)], axis=1
+        )
+        for window in windows
+    ]
+    total = dot(left[...], jnp.concatenate(right, axis=0)).astype(BF)
+    for first in range(0, TAPS, 2):
+        taps = range(first, min(first + 2, TAPS))
+        width = HALF * len(taps)
+        part = total[:, first * HALF : first * HALF + width]
+        turned = dot_t(eye[:width, :width], part).astype(BF)
+        for t in taps:
+            for k, quarter in enumerate(quarters):
+                row = (t - first) * HALF + k * BLOCK
+                quarter[t] = turned[row : row + BLOCK]
 
 
 QUARTERS = (shape(QUARTER, BF),) * 4
@@ -345,7 +339,7 @@
 def grad2(grad_t, grad_t_other, hsel, hsel_other):
     return call(
         grad2_kernel, "grad2", QUARTERS, [VM] * 4,
-        [pltpu.VMEM((C, 2 * PRE_ROWS), BF)], 12, 1_000_000_000, 4_000_000,
+        [pltpu.VMEM((C, 2 * PRE_ROWS), BF)], 20, 1_000_000_000, 4_000_000,
     )(grad_t, grad_t_other, hsel, hsel_other)
 
 
@@ -368,7 +362,7 @@
 def grad1(gat, gat_other, x3a, x3o):
     return call(
         grad1_kernel, "grad1", QUARTERS, [VM] * 4,
-        [pltpu.VMEM((C, 2 * ACT_ROWS), BF)], 16, 4_000_000_000, 7_000_000,
+        [pltpu.VMEM((C, 2 * ACT_ROWS), BF)], 24, 4_000_000_000, 7_000_000,
     )(gat, gat_other, x3a, x3o)
 
 
@@ -397,11 +391,13 @@
         for i in range(2):
             store(wide, 2 * m + i, 2 * TAPS, rows[:, i * C : (i + 1) * C], BLOCK)
 
-    def step(t, carry):
-        out[t] = load(wide, pl.multiple_of(t * BLOCK, BLOCK), BLOCK).astype(BF)
+    def step(n, carry):
+        for k in range(GROUP):
+            t = n * GROUP + k
+            out[t] = load(wide, pl.multiple_of(t * BLOCK, BLOCK), BLOCK).astype(BF)
         return carry
 
-    lax.fori_loop(0, 2 * TAPS, step, 0)
+    lax.fori_loop(0, 2 * TAPS // GROUP, step, 0)
 
 
 def spread(shards):
@@ -412,14 +408,16 @@
 
 
 def add_parts(p0, p1, p2, p3, wide):
-    def step(t, carry):
-        total = p0[t].astype(F32)
-        for part in (p1, p2, p3):
-            total = total + part[t].astype(F32)
-        store(wide, pl.multiple_of(t * BLOCK, BLOCK), BLOCK, total)
+    def step(n, carry):
+        for k in range(3):
+            t = n * 3 + k
+            total = p0[t].astype(F32)
+            for part in (p1, p2, p3):
+                total = total + part[t].astype(F32)
+            store(wide, pl.multiple_of(t * BLOCK, BLOCK), BLOCK, total)
         return carry
 
-    lax.fori_loop(0, TAPS, step, 0)
+    lax.fori_loop(0, TAPS // 3, step, 0)
 
 
 def collect2(parts):

time: 112 us -> 108 us (0.964)
  Pallas kernels: 29.6 us -> 26 us
    pallas_call x1, Pallas kernels: 6.75 us -> 4.91 us  [grad1(): call(grad1_kernel, 'grad1', QUARTERS, [VM] * 4, [pltpu.VMEM((C, 2 * ACT_R...]
    pallas_call x1, Pallas kernels: 3.06 us -> 1.64 us  [grad2(): call(grad2_kernel, 'grad2', QUARTERS, [VM] * 4, [pltpu.VMEM((C, 2 * PRE_R...]
  transfers between devices with their start and end apart: 17 -> 17, of which waited for: 9 -> 9; matrix products, arithmetic and copies ran while one was open for 1% -> 1% of each run, Pallas kernels for 17% -> 14%
where the time goes in v10:
time: 108 us; the launch traced here: 107 us
  blocking collectives  49.9 us (46%)
  Pallas kernels  26 us (24%)
  waiting for transfers between devices  17 us (16%)
  starting transfers between devices  11.5 us (11%)
  local copies, waits for them, and re-layouts  1.54 us (1%)
    all_to_all x2, blocking collectives, exchange(): return lax.all_to_all(value, 'dp', 0, 0, axis_index_groups=FAR, tiled=True)  49.9 us
    ppermute x9, waiting for transfers between devices, send_round(): lax.ppermute(v, 'dp', to)  12.5 us
    ppermute x9, starting transfers between devices, send_round(): lax.ppermute(v, 'dp', to)  7.97 us
    pallas_call x1, Pallas kernels, grad1(): call(grad1_kernel, 'grad1', QUARTERS, [VM] * 4, [pltpu.VMEM((C, 2 * ACT_R...  4.91 us
    ppermute x8, waiting for transfers between devices, swap(): return lax.ppermute(value, 'dp', PARTNERS)  4.49 us
    pallas_call x1, Pallas kernels, conv1(): call(conv1_kernel, 'conv1', (shape((ACT_ROWS, C), F32), shape((3, 7, 7, O...  3.72 us
    ppermute x8, starting transfers between devices, swap(): return lax.ppermute(value, 'dp', PARTNERS)  3.51 us
    pallas_call x1, Pallas kernels, prep(): call(prep_kernel, 'prep', (wide, wide, wide, pre, pre), [VM] * 4, [pltpu....  3.13 us
  transfers between devices with their start and end apart: 17, of which 9 were waited for; matrix products, arithmetic and copies ran while one was open for 1% of the time, Pallas kernels for 14%

profile of v10, /device:TPU:0, one launch (start us, length us, event | category | flops | bytes accessed | tf_op | source)
XLA Modules:
  0.0 106.8 jit_solution(17683550640415145512)
XLA Ops:
  0.6 2.0 %pack.1 = bf16[16,54,512]{2,1,0:T(8,128)(2,1)} custom-call(f32[27,512]{1,0:T(8,128)} %k1.1, f32[27,512]{1,0:T(8,128)} %k2.1, s32[1,256]{1,0:T(1,128)} %constant.15.clone.order), custom_call_target="tpu_custom_call" | custom-call | flops 10000000 | bytes 1000000 | tf_op jit(solution)/shard_map/pack/pallas_call | solution.py:383
  2.6 26.6 %all_to_all.10.shards = bf16[16,54,512]{2,1,0:T(8,128)(2,1)S(1)} all-to-all(bf16[16,54,512]{2,1,0:T(8,128)(2,1)} %pack.1), channel_id=1, replica_groups={{0,14,18,28,36,42,54,56,68,74,86,88,96,110,114,124},{4,10,22,24,32,46,5..., dimensions={0} | all-to-all | bytes 1769472 | tf_op jit(solution)/shard_map/all_to_all | solution.py:553
  29.2 1.9 %spread.1.q0 = bf16[54,32,256]{2,1,0:T(8,128)(2,1)S(1)} custom-call(bf16[16,54,512]{2,1,0:T(8,128)(2,1)S(1)} %all_to_all.10.shards), custom_call_target="tpu_custom_call" | custom-call | flops 1000000 | bytes 2000000 | tf_op jit(solution)/shard_map/spread/pallas_call | solution.py:404
  31.1 1.7 %collective-permute-start.3 = (bf16[54,32,256]{2,1,0:T(8,128)(2,1)S(1)}, bf16[54,32,256]{2,1,0:T(8,128)(2,1)S(1)}, u32[]{:S(2)}, u32[]{:S(2)}) collective-permute-start(bf16[54,32,256]{2,1,0:T(8,128)(2,1)S(1)} %spread.1.q0), channel_id=1, source_target_pairs={{0,2},{6,4},{24,26},{30,28},{96,98},{102,100},{120,122},{126,124},... | collective-permute-start | bytes 2654216 | tf_op jit(solution)/shard_map/ppermute | solution.py:561
  32.8 0.0 collective-permute-start.2
  32.9 1.1 %collective-permute-start = (bf16[6,6,6,4,256]{4,3,2,1,0:T(4,128)(2,1)}, bf16[6,6,6,4,256]{4,3,2,1,0:T(4,128)(2,1)}, u32[]{:S(2)}, u32[]{:S(2)}) collective-permute-start(bf16[6,6,6,4,256]{4,3,2,1,0:T(4,128)(2,1)} %bitcast.latent), channel_id=1, source_target_pairs={{0,1},{1,0},{2,3},{3,2},{4,5},{5,4},{6,7},{7,6},{8,9},{9,8},{10,11... | collective-permute-start | bytes 1327112 | tf_op jit(solution)/shard_map/ppermute | solution.py:557
  34.0 0.7 dynamic-slice_bitcast_fusion.table
  34.7 0.0 collective-permute-start.4
  34.7 1.1 %collective-permute-done.other = bf16[6,6,6,4,256]{4,3,2,1,0:T(4,128)(2,1)} collective-permute-done((bf16[6,6,6,4,256]{4,3,2,1,0:T(4,128)(2,1)}, bf16[6,6,6,4,256]{4,3,2,1,0:T(4,128)(2,1)}, u32[]{:S(2)}, u32[]{:S(2)}) %collective-permute-start) | collective-permute-done | bytes 442400 | tf_op jit(solution)/shard_map/ppermute | solution.py:557
  35.7 0.8 copy-done.7
  36.6 3.1 %prep.1 = (bf16[3,8,8,32,128]{4,3,2,1,0:T(8,128)(2,1)S(1)}, bf16[3,8,8,32,128]{4,3,2,1,0:T(8,128)(2,1)S(1)}, bf16[3,8,8,32,128]{4,3,2,1,0:T(8,128)(2,1)S(1)}, f32[144,256]{1,0:T(8,128)S(1)}, f32[144,256]{1,0:T(8,128)S(1)}) custom-call(bf16[6,6,6,4,256]{4,3,2,1,0:T(4,128)(2,1)} %bitcast.latent, bf16[6,6,6,4,256]{4,3,2,1,0:T(4,128)(2,1)} %collective-permute-done.other, ...), custom_call_target="tpu_custom_call" | custom-call | flops 2000000000 | bytes 8000000 | tf_op jit(solution)/shard_map/prep/pallas_call | solution.py:120
  39.7 4.5 %collective-permute-done.3.q3 = bf16[54,32,256]{2,1,0:T(8,128)(2,1)S(1)} collective-permute-done((bf16[54,32,256]{2,1,0:T(8,128)(2,1)S(1)}, bf16[54,32,256]{2,1,0:T(8,128)(2,1)S(1)}, u32[]{:S(2)}, u32[]{:S(2)}) %collective-permute-start.3) | collective-permute-done | bytes 884768 | tf_op jit(solution)/shard_map/ppermute | solution.py:561
  44.2 1.7 %collective-permute-done.2.q2 = bf16[54,32,256]{2,1,0:T(8,128)(2,1)S(1)} collective-permute-done((bf16[54,32,256]{2,1,0:T(8,128)(2,1)S(1)}, bf16[54,32,256]{2,1,0:T(8,128)(2,1)S(1)}, u32[]{:S(2)}, u32[]{:S(2)}) %collective-permute-start.2) | collective-permute-done | bytes 884768 | tf_op jit(solution)/shard_map/ppermute | solution.py:561
  45.9 0.6 collective-permute-start.5
  46.5 0.0 collective-permute-start.6
  46.5 0.5 collective-permute-start.7
  47.1 2.3 %conv1_own.1.part_act = f32[1152,256]{1,0:T(8,128)S(1)} custom-call(bf16[3,8,8,32,128]{4,3,2,1,0:T(8,128)(2,1)S(1)} %get-tuple-element.41.x3a, bf16[54,32,256]{2,1,0:T(8,128)(2,1)S(1)} %spread.1.q0, bf16[54,32,256]{2,1,0:T(8,128)(2,1)S(1)} %collective-permute-done.1.q1, bf16[54,32,256]{2,1,0:T(8,128)(2,1)S(1)} %collective-permute-done.2.q2, ...), custom_call_target="tpu_custom_call" | custom-call | flops 2000000000 | bytes 5000000 | tf_op jit(solution)/shard_map/conv1_own/pallas_call | solution.py:155
  49.4 0.5 collective-permute-done.6.q2.p2
  49.9 1.3 %collective-permute-done.7.q3.p3 = bf16[54,32,256]{2,1,0:T(8,128)(2,1)S(1)} collective-permute-done((bf16[54,32,256]{2,1,0:T(8,128)(2,1)S(1)}, bf16[54,32,256]{2,1,0:T(8,128)(2,1)S(1)}, u32[]{:S(2)}, u32[]{:S(2)}) %collective-permute-start.7) | collective-permute-done | bytes 884768 | tf_op jit(solution)/shard_map/ppermute | solution.py:557
  51.1 3.7 %conv1.1 = (f32[1152,256]{1,0:T(8,128)S(1)}, bf16[3,7,7,16,256]{4,3,2,1,0:T(8,128)(2,1)S(1)}, bf16[3,7,7,16,128]{4,3,2,1,0:T(8,128)(2,1)S(1)}) custom-call(bf16[3,8,8,32,128]{4,3,2,1,0:T(8,128)(2,1)S(1)} %get-tuple-element.40.x3b, f32[1152,256]{1,0:T(8,128)S(1)} %conv1_own.1.part_act, bf16[54,32,256]{2,1,0:T(8,128)(2,1)S(1)} %collective-permute-done.4.q0.p0, ...), custom_call_target="tpu_custom_call" | custom-call | flops 2000000000 | bytes 7000000 | tf_op jit(solution)/shard_map/conv1/pallas_call | solution.py:194
  54.9 0.5 collective-permute-start.9
  55.3 1.4 %conv2.1 = (bf16[3,3,3,4,256]{4,3,2,1,0:T(4,128)(2,1)}, bf16[144,256]{1,0:T(8,128)(2,1)S(1)}, bf16[256,144]{1,0:T(8,128)(2,1)S(1)}) custom-call(f32[144,256]{1,0:T(8,128)S(1)} %get-tuple-element.38.skip, f32[144,256]{1,0:T(8,128)S(1)} %get-tuple-element.39.cot, bf16[3,7,7,16,256]{4,3,2,1,0:T(8,128)(2,1)S(1)} %get-tuple-element.45.hsel, ...), custom_call_target="tpu_custom_call" | custom-call | flops 1500000000 | bytes 6000000 | tf_op jit(solution)/shard_map/conv2/pallas_call | solution.py:238
  56.7 1.8 %back.1.gat = bf16[3,256,384]{2,1,0:T(8,128)(2,1)S(1)} custom-call(f32[1152,256]{1,0:T(8,128)S(1)} %get-tuple-element.47.act, bf16[144,256]{1,0:T(8,128)(2,1)S(1)} %get-tuple-element.48.grad_pre, bf16[54,32,256]{2,1,0:T(8,128)(2,1)S(1)} %spread.1.q0, bf16[54,32,256]{2,1,0:T(8,128)(2,1)S(1)} %collective-permute-done.1.q1, ...), custom_call_target="tpu_custom_call" | custom-call | flops 1500000000 | bytes 8000000 | tf_op jit(solution)/shard_map/back/pallas_call | solution.py:288
  58.5 0.4 collective-permute-start.10
  58.9 0.4 collective-permute-start.8
  59.3 1.7 %collective-permute-done.8.grad_t_other = bf16[256,144]{1,0:T(8,128)(2,1)S(1)} collective-permute-done((bf16[256,144]{1,0:T(8,128)(2,1)S(1)}, bf16[256,144]{1,0:T(8,128)(2,1)S(1)}, u32[]{:S(2)}, u32[]{:S(2)}) %collective-permute-start.8) | collective-permute-done | bytes 73760 | tf_op jit(solution)/shard_map/ppermute | solution.py:557
  61.0 1.6 %grad2.1 = (bf16[27,32,256]{2,1,0:T(8,128)(2,1)S(1)}, bf16[27,32,256]{2,1,0:T(8,128)(2,1)S(1)}, bf16[27,32,256]{2,1,0:T(8,128)(2,1)S(1)}, bf16[27,32,256]{2,1,0:T(8,128)(2,1)S(1)}) custom-call(bf16[256,144]{1,0:T(8,128)(2,1)S(1)} %get-tuple-element.49.grad_t, bf16[256,144]{1,0:T(8,128)(2,1)S(1)} %collective-permute-done.8.grad_t_other, ...), custom_call_target="tpu_custom_call" | custom-call | flops 1000000000 | bytes 4000000 | tf_op jit(solution)/shard_map/grad2/pallas_call | solution.py:340
  62.6 0.1 collective-permute-start.14
  62.7 1.6 %collective-permute-start.15 = (bf16[27,32,256]{2,1,0:T(8,128)(2,1)S(1)}, bf16[27,32,256]{2,1,0:T(8,128)(2,1)S(1)}, u32[]{:S(2)}, u32[]{:S(2)}) collective-permute-start(bf16[27,32,256]{2,1,0:T(8,128)(2,1)S(1)} %get-tuple-element.53), channel_id=1, source_target_pairs={{0,8},{6,14},{24,16},{30,22},{96,104},{102,110},{120,112},{126,118... | collective-permute-start | bytes 1327112 | tf_op jit(solution)/shard_map/ppermute | solution.py:561
  64.3 1.6 %collective-permute-start.16 = (bf16[27,32,256]{2,1,0:T(8,128)(2,1)S(1)}, bf16[27,32,256]{2,1,0:T(8,128)(2,1)S(1)}, u32[]{:S(2)}, u32[]{:S(2)}) collective-permute-start(bf16[27,32,256]{2,1,0:T(8,128)(2,1)S(1)} %get-tuple-element.54), channel_id=1, source_target_pairs={{0,2},{6,4},{24,26},{30,28},{96,98},{102,100},{120,122},{126,124},... | collective-permute-start | bytes 1327112 | tf_op jit(solution)/shard_map/ppermute | solution.py:561
  65.9 4.9 %grad1.1 = (bf16[27,32,256]{2,1,0:T(8,128)(2,1)S(1)}, bf16[27,32,256]{2,1,0:T(8,128)(2,1)S(1)}, bf16[27,32,256]{2,1,0:T(8,128)(2,1)S(1)}, bf16[27,32,256]{2,1,0:T(8,128)(2,1)S(1)}) custom-call(bf16[3,256,384]{2,1,0:T(8,128)(2,1)S(1)} %back.1.gat, bf16[3,256,384]{2,1,0:T(8,128)(2,1)S(1)} %collective-permute-done.10.gat_other, ...), custom_call_target="tpu_custom_call" | custom-call | flops 4000000000 | bytes 7000000 | tf_op jit(solution)/shard_map/grad1/pallas_call | solution.py:363
  70.9 0.7 collective-permute-start.11
  71.6 0.4 collective-permute-start.12
  72.0 1.7 %collective-permute-start.13 = (bf16[27,32,256]{2,1,0:T(8,128)(2,1)S(1)}, bf16[27,32,256]{2,1,0:T(8,128)(2,1)S(1)}, u32[]{:S(2)}, u32[]{:S(2)}) collective-permute-start(bf16[27,32,256]{2,1,0:T(8,128)(2,1)S(1)} %get-tuple-element.60), channel_id=1, source_target_pairs={{0,2},{6,4},{24,26},{30,28},{96,98},{102,100},{120,122},{126,124},... | collective-permute-start | bytes 1327112 | tf_op jit(solution)/shard_map/ppermute | solution.py:561
  73.8 0.2 collect2.1.second
  74.0 5.2 %collective-permute-done.11.p1 = bf16[27,32,256]{2,1,0:T(8,128)(2,1)S(1)} collective-permute-done((bf16[27,32,256]{2,1,0:T(8,128)(2,1)S(1)}, bf16[27,32,256]{2,1,0:T(8,128)(2,1)S(1)}, u32[]{:S(2)}, u32[]{:S(2)}) %collective-permute-start.11) | collective-permute-done | bytes 442400 | tf_op jit(solution)/shard_map/ppermute | solution.py:561
  79.2 0.7 collective-permute-done.12.p2
  79.9 0.4 collective-permute-done.13.p3
  80.3 1.6 %collect.1 = bf16[16,54,512]{2,1,0:T(8,128)(2,1)S(1)} custom-call(bf16[27,32,256]{2,1,0:T(8,128)(2,1)S(1)} %get-tuple-element.57.p0, bf16[27,32,256]{2,1,0:T(8,128)(2,1)S(1)} %collective-permute-done.11.p1, bf16[27,32,256]{2,1,0:T(8,128)(2,1)S(1)} %collective-permute-done.12.p2, bf16[27,32,256]{2,1,0:T(8,128)(2,1)S(1)} %collective-permute-done.13.p3, ...), custom_call_target="tpu_custom_call" | custom-call | flops 1000000 | bytes 3000000 | tf_op jit(solution)/shard_map/collect/pallas_call | solution.py:440
  82.0 0.0 copy-start
  82.0 0.0 copy-start.1
  82.0 0.0 copy-start.2
  82.0 0.0 copy-start.3
  82.0 0.0 copy-start.4
  82.0 0.0 copy-start.5
  82.0 0.0 copy-start.6
  82.0 23.4 %all_to_all.11.parts = bf16[16,54,512]{2,1,0:T(8,128)(2,1)S(1)} all-to-all(bf16[16,54,512]{2,1,0:T(8,128)(2,1)S(1)} %collect.1), channel_id=1, replica_groups={{0,14,18,28,36,42,54,56,68,74,86,88,96,110,114,124},{4,10,22,24,32,46,5..., dimensions={0} | all-to-all | bytes 1769472 | tf_op jit(solution)/shard_map/all_to_all | solution.py:553
  105.5 1.4 %adam.1 = (f32[27,512]{1,0:T(8,128)}, f32[27,512]{1,0:T(8,128)}, f32[27,512]{1,0:T(8,128)}, f32[27,512]{1,0:T(8,128)}, f32[27,512]{1,0:T(8,128)}, /*index=5*/f32[27,512]{1,0:T(8,128)}) custom-call(bf16[16,54,512]{2,1,0:T(8,128)(2,1)S(1)} %all_to_all.11.parts, s32[1,256]{1,0:T(1,128)S(1)} %copy-done.6, f32[27,512]{1,0:T(8,128)S(1)} %copy-done, ...), custom_call_target="tpu_custom_call" | custom-call | flops 10000000 | bytes 1000000 | tf_op jit(solution)/shard_map/adam/pallas_call | solution.py:483
  (17 shorter events, 0.0 us)
Async XLA Ops:
  31.1 13.1 %collective-permute-start.3 = (bf16[54,32,256]{2,1,0:T(8,128)(2,1)S(1)}, bf16[54,32,256]{2,1,0:T(8,128)(2,1)S(1)}, u32[]{:S(2)}, u32[]{:S(2)}) collective-permute-start(bf16[54,32,256]{2,1,0:T(8,128)(2,1)S(1)} %spread.1.q0), channel_id=1, source_target_pairs={{0,2},{6,4},{24,26},{30,28},{96,98},{102,100},{120,122},{126,124},... | collective-permute-start | bytes 2654216 | tf_op jit(solution)/shard_map/ppermute | solution.py:561
  32.8 13.0 %collective-permute-start.2 = (bf16[54,32,256]{2,1,0:T(8,128)(2,1)S(1)}, bf16[54,32,256]{2,1,0:T(8,128)(2,1)S(1)}, u32[]{:S(2)}, u32[]{:S(2)}) collective-permute-start(bf16[54,32,256]{2,1,0:T(8,128)(2,1)S(1)} %spread.1.q0), channel_id=1, source_target_pairs={{0,8},{6,14},{24,16},{30,22},{96,104},{102,110},{120,112},{126,118... | collective-permute-start | bytes 2654216 | tf_op jit(solution)/shard_map/ppermute | solution.py:561
  32.9 13.0 %collective-permute-start.1 = (bf16[54,32,256]{2,1,0:T(8,128)(2,1)S(1)}, bf16[54,32,256]{2,1,0:T(8,128)(2,1)S(1)}, u32[]{:S(2)}, u32[]{:S(2)}) collective-permute-start(bf16[54,32,256]{2,1,0:T(8,128)(2,1)S(1)} %spread.1.q0), channel_id=1, source_target_pairs={{0,32},{6,38},{24,56},{30,62},{96,64},{102,70},{120,88},{126,94},{... | collective-permute-start | bytes 2654216 | tf_op jit(solution)/shard_map/ppermute | solution.py:561
  32.9 2.9 %collective-permute-start = (bf16[6,6,6,4,256]{4,3,2,1,0:T(4,128)(2,1)}, bf16[6,6,6,4,256]{4,3,2,1,0:T(4,128)(2,1)}, u32[]{:S(2)}, u32[]{:S(2)}) collective-permute-start(bf16[6,6,6,4,256]{4,3,2,1,0:T(4,128)(2,1)} %bitcast.latent), channel_id=1, source_target_pairs={{0,1},{1,0},{2,3},{3,2},{4,5},{5,4},{6,7},{7,6},{8,9},{9,8},{10,11... | collective-permute-start | bytes 1327112 | tf_op jit(solution)/shard_map/ppermute | solution.py:557
  34.7 14.7 %collective-permute-start.4 = (bf16[54,32,256]{2,1,0:T(8,128)(2,1)S(1)}, bf16[54,32,256]{2,1,0:T(8,128)(2,1)S(1)}, u32[]{:S(2)}, u32[]{:S(2)}) collective-permute-start(bf16[54,32,256]{2,1,0:T(8,128)(2,1)S(1)} %spread.1.q0), channel_id=1, source_target_pairs={{0,1},{1,0},{2,3},{3,2},{4,5},{5,4},{6,7},{7,6},{8,9},{9,8},{10,11... | collective-permute-start | bytes 2654216 | tf_op jit(solution)/shard_map/ppermute | solution.py:557
  35.7 0.8 copy-start.7
  45.9 3.5 %collective-permute-start.5 = (bf16[54,32,256]{2,1,0:T(8,128)(2,1)S(1)}, bf16[54,32,256]{2,1,0:T(8,128)(2,1)S(1)}, u32[]{:S(2)}, u32[]{:S(2)}) collective-permute-start(bf16[54,32,256]{2,1,0:T(8,128)(2,1)S(1)} %collective-permute-done.1.q1), channel_id=1, source_target_pairs={{0,1},{1,0},{2,3},{3,2},{4,5},{5,4},{6,7},{7,6},{8,9},{9,8},{10,11... | collective-permute-start | bytes 2654216 | tf_op jit(solution)/shard_map/ppermute | solution.py:557
  46.5 3.3 %collective-permute-start.6 = (bf16[54,32,256]{2,1,0:T(8,128)(2,1)S(1)}, bf16[54,32,256]{2,1,0:T(8,128)(2,1)S(1)}, u32[]{:S(2)}, u32[]{:S(2)}) collective-permute-start(bf16[54,32,256]{2,1,0:T(8,128)(2,1)S(1)} %collective-permute-done.2.q2), channel_id=1, source_target_pairs={{0,1},{1,0},{2,3},{3,2},{4,5},{5,4},{6,7},{7,6},{8,9},{9,8},{10,11... | collective-permute-start | bytes 2654216 | tf_op jit(solution)/shard_map/ppermute | solution.py:557
  46.5 4.6 %collective-permute-start.7 = (bf16[54,32,256]{2,1,0:T(8,128)(2,1)S(1)}, bf16[54,32,256]{2,1,0:T(8,128)(2,1)S(1)}, u32[]{:S(2)}, u32[]{:S(2)}) collective-permute-start(bf16[54,32,256]{2,1,0:T(8,128)(2,1)S(1)} %collective-permute-done.3.q3), channel_id=1, source_target_pairs={{0,1},{1,0},{2,3},{3,2},{4,5},{5,4},{6,7},{7,6},{8,9},{9,8},{10,11... | collective-permute-start | bytes 2654216 | tf_op jit(solution)/shard_map/ppermute | solution.py:557
  54.9 6.1 %collective-permute-start.9 = (bf16[3,7,7,16,128]{4,3,2,1,0:T(8,128)(2,1)S(1)}, bf16[3,7,7,16,128]{4,3,2,1,0:T(8,128)(2,1)S(1)}, u32[]{:S(2)}, u32[]{:S(2)}) collective-permute-start(bf16[3,7,7,16,128]{4,3,2,1,0:T(8,128)(2,1)S(1)} %get-tuple-element.50), channel_id=1, source_target_pairs={{0,1},{1,0},{2,3},{3,2},{4,5},{5,4},{6,7},{7,6},{8,9},{9,8},{10,11... | collective-permute-start | bytes 1806344 | tf_op jit(solution)/shard_map/ppermute | solution.py:557
  58.5 7.4 %collective-permute-start.10 = (bf16[3,256,384]{2,1,0:T(8,128)(2,1)S(1)}, bf16[3,256,384]{2,1,0:T(8,128)(2,1)S(1)}, u32[]{:S(2)}, u32[]{:S(2)}) collective-permute-start(bf16[3,256,384]{2,1,0:T(8,128)(2,1)S(1)} %back.1.gat), channel_id=1, source_target_pairs={{0,1},{1,0},{2,3},{3,2},{4,5},{5,4},{6,7},{7,6},{8,9},{9,8},{10,11... | collective-permute-start | bytes 1769480 | tf_op jit(solution)/shard_map/ppermute | solution.py:557
  58.9 2.1 %collective-permute-start.8 = (bf16[256,144]{1,0:T(8,128)(2,1)S(1)}, bf16[256,144]{1,0:T(8,128)(2,1)S(1)}, u32[]{:S(2)}, u32[]{:S(2)}) collective-permute-start(bf16[256,144]{1,0:T(8,128)(2,1)S(1)} %get-tuple-element.49.grad_t), channel_id=1, source_target_pairs={{0,1},{1,0},{2,3},{3,2},{4,5},{5,4},{6,7},{7,6},{8,9},{9,8},{10,11... | collective-permute-start | bytes 221192 | tf_op jit(solution)/shard_map/ppermute | solution.py:557
  62.6 9.4 %collective-permute-start.14 = (bf16[27,32,256]{2,1,0:T(8,128)(2,1)S(1)}, bf16[27,32,256]{2,1,0:T(8,128)(2,1)S(1)}, u32[]{:S(2)}, u32[]{:S(2)}) collective-permute-start(bf16[27,32,256]{2,1,0:T(8,128)(2,1)S(1)} %get-tuple-element.52), channel_id=1, source_target_pairs={{0,32},{6,38},{24,56},{30,62},{96,64},{102,70},{120,88},{126,94},{... | collective-permute-start | bytes 1327112 | tf_op jit(solution)/shard_map/ppermute | solution.py:561
  62.7 11.1 %collective-permute-start.15 = (bf16[27,32,256]{2,1,0:T(8,128)(2,1)S(1)}, bf16[27,32,256]{2,1,0:T(8,128)(2,1)S(1)}, u32[]{:S(2)}, u32[]{:S(2)}) collective-permute-start(bf16[27,32,256]{2,1,0:T(8,128)(2,1)S(1)} %get-tuple-element.53), channel_id=1, source_target_pairs={{0,8},{6,14},{24,16},{30,22},{96,104},{102,110},{120,112},{126,118... | collective-permute-start | bytes 1327112 | tf_op jit(solution)/shard_map/ppermute | solution.py:561
  64.3 9.5 %collective-permute-start.16 = (bf16[27,32,256]{2,1,0:T(8,128)(2,1)S(1)}, bf16[27,32,256]{2,1,0:T(8,128)(2,1)S(1)}, u32[]{:S(2)}, u32[]{:S(2)}) collective-permute-start(bf16[27,32,256]{2,1,0:T(8,128)(2,1)S(1)} %get-tuple-element.54), channel_id=1, source_target_pairs={{0,2},{6,4},{24,26},{30,28},{96,98},{102,100},{120,122},{126,124},... | collective-permute-start | bytes 1327112 | tf_op jit(solution)/shard_map/ppermute | solution.py:561
  70.9 8.4 %collective-permute-start.11 = (bf16[27,32,256]{2,1,0:T(8,128)(2,1)S(1)}, bf16[27,32,256]{2,1,0:T(8,128)(2,1)S(1)}, u32[]{:S(2)}, u32[]{:S(2)}) collective-permute-start(bf16[27,32,256]{2,1,0:T(8,128)(2,1)S(1)} %get-tuple-element.58), channel_id=1, source_target_pairs={{0,32},{6,38},{24,56},{30,62},{96,64},{102,70},{120,88},{126,94},{... | collective-permute-start | bytes 1327112 | tf_op jit(solution)/shard_map/ppermute | solution.py:561
  71.6 8.3 %collective-permute-start.12 = (bf16[27,32,256]{2,1,0:T(8,128)(2,1)S(1)}, bf16[27,32,256]{2,1,0:T(8,128)(2,1)S(1)}, u32[]{:S(2)}, u32[]{:S(2)}) collective-permute-start(bf16[27,32,256]{2,1,0:T(8,128)(2,1)S(1)} %get-tuple-element.59), channel_id=1, source_target_pairs={{0,8},{6,14},{24,16},{30,22},{96,104},{102,110},{120,112},{126,118... | collective-permute-start | bytes 1327112 | tf_op jit(solution)/shard_map/ppermute | solution.py:561
  72.0 8.3 %collective-permute-start.13 = (bf16[27,32,256]{2,1,0:T(8,128)(2,1)S(1)}, bf16[27,32,256]{2,1,0:T(8,128)(2,1)S(1)}, u32[]{:S(2)}, u32[]{:S(2)}) collective-permute-start(bf16[27,32,256]{2,1,0:T(8,128)(2,1)S(1)} %get-tuple-element.60), channel_id=1, source_target_pairs={{0,2},{6,4},{24,26},{30,28},{96,98},{102,100},{120,122},{126,124},... | collective-permute-start | bytes 1327112 | tf_op jit(solution)/shard_map/ppermute | solution.py:561
  82.0 23.5 %copy-start = (f32[27,512]{1,0:T(8,128)S(1)}, f32[27,512]{1,0:T(8,128)}, u32[]{:S(2)}) copy-start(f32[27,512]{1,0:T(8,128)} %k1.1) | copy-start | bytes 165892
  82.0 23.4 %copy-start.1 = (f32[27,512]{1,0:T(8,128)S(1)}, f32[27,512]{1,0:T(8,128)}, u32[]{:S(2)}) copy-start(f32[27,512]{1,0:T(8,128)} %k2.1) | copy-start | bytes 165892
  82.0 23.4 %copy-start.2 = (f32[27,512]{1,0:T(8,128)S(1)}, f32[27,512]{1,0:T(8,128)}, u32[]{:S(2)}) copy-start(f32[27,512]{1,0:T(8,128)} %m1.1) | copy-start | bytes 165892
  82.0 23.4 %copy-start.3 = (f32[27,512]{1,0:T(8,128)S(1)}, f32[27,512]{1,0:T(8,128)}, u32[]{:S(2)}) copy-start(f32[27,512]{1,0:T(8,128)} %v1.1) | copy-start | bytes 165892
  82.0 23.4 %copy-start.4 = (f32[27,512]{1,0:T(8,128)S(1)}, f32[27,512]{1,0:T(8,128)}, u32[]{:S(2)}) copy-start(f32[27,512]{1,0:T(8,128)} %m2.1) | copy-start | bytes 165892
  82.0 23.4 %copy-start.5 = (f32[27,512]{1,0:T(8,128)S(1)}, f32[27,512]{1,0:T(8,128)}, u32[]{:S(2)}) copy-start(f32[27,512]{1,0:T(8,128)} %v2.1) | copy-start | bytes 165892
  82.0 23.4 %copy-start.6 = (s32[1,256]{1,0:T(1,128)S(1)}, s32[1,256]{1,0:T(1,128)}, u32[]{:S(2)}) copy-start(s32[1,256]{1,0:T(1,128)} %constant.15.clone.order) | copy-start | bytes 3076

commit v11 on v10

--- a/solution.py
+++ b/solution.py
@@ -211,8 +211,9 @@
     return jnp.concatenate(blocks, axis=0)
 
 
-def conv2_kernel(
-    skip, cot, hsel, q0, q1, q2, q3, p0, p1, p2, p3, block_out, grad_pre, grad_pre_t, bo
+def middle_kernel(
+    skip, cot, hsel, act, q0, q1, q2, q3, p0, p1, p2, p3, table,
+    block_out, grad_pre_t, gat, bo, y, gh,
 ):
     quarters = (q0, q1, q2, q3, p0, p1, p2, p3)
     pre = skip[...]
@@ -230,30 +231,9 @@
                 base = (qi * 3 + qj) * OUT_ROWS + ql
                 block_out[qi, qj, ql] = load(bo, base, SAMP, 4).astype(BF)
     grad = (cot[...] * (sigma * (1.0 + pre * (1.0 - sigma)))).astype(BF)
-    grad_pre[...] = grad
     grad_pre_t[...] = grad.astype(F32).T.astype(BF)
 
-
-def conv2(skip, cot, hsel, own, other):
-    return call(
-        conv2_kernel, "conv2",
-        (
-            shape((OUTER, OUTER, OUTER, SAMP, C), BF),
-            shape((PRE_ROWS, C), BF),
-            shape((C, PRE_ROWS), BF),
-        ),
-        [VM] * 11,
-        [pltpu.VMEM((2, PRE_ROWS, HALF), F32)],
-        16, 1_500_000_000, 6_000_000,
-    )(skip, cot, hsel, *own, *other)
-
-
-def back_kernel(
-    act, grad_pre, q0, q1, q2, q3, p0, p1, p2, p3, table, gat, y, gh
-):
-    quarters = (q0, q1, q2, q3, p0, p1, p2, p3)
     y[...] = jnp.zeros_like(y)
-    grad = grad_pre[...]
     for di in range(3):
         for dj in range(3):
             for dl in range(3):
@@ -284,15 +264,22 @@
         gat[i // 2] = dot_t(lanes, jnp.concatenate(grads, axis=0)).astype(BF)
 
 
-def back(act, grad_pre, own, other, table):
-    return call(
-        back_kernel, "back", shape((EDGE // 2, C, 2 * EDGE * ROWS), BF), [VM] * 11,
+def middle(skip, cot, hsel, act, own, other, table):
+    return call(
+        middle_kernel, "middle",
+        (
+            shape((OUTER, OUTER, OUTER, SAMP, C), BF),
+            shape((C, PRE_ROWS), BF),
+            shape((EDGE // 2, C, 2 * EDGE * ROWS), BF),
+        ),
+        [VM] * 13,
         [
+            pltpu.VMEM((2, PRE_ROWS, HALF), F32),
             pltpu.VMEM((3, 7, 7, OUT_ROWS, C), F32),
             pltpu.VMEM((2, ACT_ROWS + 8, HALF), F32),
         ],
-        16, 1_500_000_000, 8_000_000,
-    )(act, grad_pre, *own, *other, table)
+        16, 3_000_000_000, 14_000_000,
+    )(skip, cot, hsel, act, *own, *other, table)
 
 
 def grad_loop(quarters, left, windows):
@@ -583,9 +570,8 @@
 
     act, hsel, hsend = conv1(x3b, conv1_own(x3a, own), other, table)
     hsel_other = swap(hsend)
-    block_out, grad_pre, grad_pre_t = conv2(skip, cot, hsel, own, other)
+    block_out, grad_pre_t, gat = middle(skip, cot, hsel, act, own, other, table)
     grad_pre_t_other = swap(grad_pre_t)
-    gat = back(act, grad_pre, own, other, table)
     gat_other = swap(gat)
     second = grad2(grad_pre_t, grad_pre_t_other, hsel, hsel_other)
     gat = after(gat, *second)

time: 108 us -> 109 us (level)
    pallas_call x2 -> x1, Pallas kernels: 3.19 us -> 3.55 us  [middle(): call(middle_kernel, 'middle', (shape((OUTER, OUTER, OUTER, SAMP, C), BF),...]
  transfers between devices with their start and end apart: 17 -> 17, of which waited for: 9 -> 9; matrix products, arithmetic and copies ran while one was open for 1% -> 1% of each run, Pallas kernels for 14% -> 15%
where the time goes in v11:
time: 109 us; the launch traced here: 107 us
  blocking collectives  49.9 us (46%)
  Pallas kernels  26.4 us (24%)
  waiting for transfers between devices  17 us (16%)
  starting transfers between devices  11.5 us (11%)
  local copies, waits for them, and re-layouts  1.54 us (1%)
    all_to_all x2, blocking collectives, exchange(): return lax.all_to_all(value, 'dp', 0, 0, axis_index_groups=FAR, tiled=True)  49.9 us
    ppermute x9, waiting for transfers between devices, send_round(): lax.ppermute(v, 'dp', to)  12.5 us
    ppermute x9, starting transfers between devices, send_round(): lax.ppermute(v, 'dp', to)  7.97 us
    pallas_call x1, Pallas kernels, grad1(): call(grad1_kernel, 'grad1', QUARTERS, [VM] * 4, [pltpu.VMEM((C, 2 * ACT_R...  4.89 us
    ppermute x8, waiting for transfers between devices, swap(): return lax.ppermute(value, 'dp', PARTNERS)  4.5 us
    pallas_call x1, Pallas kernels, conv1(): call(conv1_kernel, 'conv1', (shape((ACT_ROWS, C), F32), shape((3, 7, 7, O...  3.72 us
    pallas_call x1, Pallas kernels, middle(): call(middle_kernel, 'middle', (shape((OUTER, OUTER, OUTER, SAMP, C), BF),...  3.55 us
    ppermute x8, starting transfers between devices, swap(): return lax.ppermute(value, 'dp', PARTNERS)  3.5 us
  transfers between devices with their start and end apart: 17, of which 9 were waited for; matrix products, arithmetic and copies ran while one was open for 1% of the time, Pallas kernels for 15%

profile of v11, /device:TPU:0, one launch (start us, length us, event | category | flops | bytes accessed | tf_op | source)
XLA Modules:
  0.0 107.1 jit_solution(1950529505453966099)
XLA Ops:
  0.6 2.0 %pack.1 = bf16[16,54,512]{2,1,0:T(8,128)(2,1)} custom-call(f32[27,512]{1,0:T(8,128)} %k1.1, f32[27,512]{1,0:T(8,128)} %k2.1, s32[1,256]{1,0:T(1,128)} %constant.15.clone.order), custom_call_target="tpu_custom_call" | custom-call | flops 10000000 | bytes 1000000 | tf_op jit(solution)/shard_map/pack/pallas_call | solution.py:370
  2.6 26.6 %all_to_all.10.shards = bf16[16,54,512]{2,1,0:T(8,128)(2,1)S(1)} all-to-all(bf16[16,54,512]{2,1,0:T(8,128)(2,1)} %pack.1), channel_id=1, replica_groups={{0,14,18,28,36,42,54,56,68,74,86,88,96,110,114,124},{4,10,22,24,32,46,5..., dimensions={0} | all-to-all | bytes 1769472 | tf_op jit(solution)/shard_map/all_to_all | solution.py:540
  29.2 1.9 %spread.1.q0 = bf16[54,32,256]{2,1,0:T(8,128)(2,1)S(1)} custom-call(bf16[16,54,512]{2,1,0:T(8,128)(2,1)S(1)} %all_to_all.10.shards), custom_call_target="tpu_custom_call" | custom-call | flops 1000000 | bytes 2000000 | tf_op jit(solution)/shard_map/spread/pallas_call | solution.py:391
  31.1 1.7 %collective-permute-start.3 = (bf16[54,32,256]{2,1,0:T(8,128)(2,1)S(1)}, bf16[54,32,256]{2,1,0:T(8,128)(2,1)S(1)}, u32[]{:S(2)}, u32[]{:S(2)}) collective-permute-start(bf16[54,32,256]{2,1,0:T(8,128)(2,1)S(1)} %spread.1.q0), channel_id=1, source_target_pairs={{0,2},{6,4},{24,26},{30,28},{96,98},{102,100},{120,122},{126,124},... | collective-permute-start | bytes 2654216 | tf_op jit(solution)/shard_map/ppermute | solution.py:548
  32.9 1.1 %collective-permute-start = (bf16[6,6,6,4,256]{4,3,2,1,0:T(4,128)(2,1)}, bf16[6,6,6,4,256]{4,3,2,1,0:T(4,128)(2,1)}, u32[]{:S(2)}, u32[]{:S(2)}) collective-permute-start(bf16[6,6,6,4,256]{4,3,2,1,0:T(4,128)(2,1)} %bitcast.latent), channel_id=1, source_target_pairs={{0,1},{1,0},{2,3},{3,2},{4,5},{5,4},{6,7},{7,6},{8,9},{9,8},{10,11... | collective-permute-start | bytes 1327112 | tf_op jit(solution)/shard_map/ppermute | solution.py:544
  34.0 0.7 dynamic-slice_bitcast_fusion.table
  34.7 0.0 collective-permute-start.4
  34.7 1.1 %collective-permute-done.other = bf16[6,6,6,4,256]{4,3,2,1,0:T(4,128)(2,1)} collective-permute-done((bf16[6,6,6,4,256]{4,3,2,1,0:T(4,128)(2,1)}, bf16[6,6,6,4,256]{4,3,2,1,0:T(4,128)(2,1)}, u32[]{:S(2)}, u32[]{:S(2)}) %collective-permute-start) | collective-permute-done | bytes 442400 | tf_op jit(solution)/shard_map/ppermute | solution.py:544
  35.7 0.8 copy-done.7
  36.6 3.1 %prep.1 = (bf16[3,8,8,32,128]{4,3,2,1,0:T(8,128)(2,1)S(1)}, bf16[3,8,8,32,128]{4,3,2,1,0:T(8,128)(2,1)S(1)}, bf16[3,8,8,32,128]{4,3,2,1,0:T(8,128)(2,1)S(1)}, f32[144,256]{1,0:T(8,128)S(1)}, f32[144,256]{1,0:T(8,128)S(1)}) custom-call(bf16[6,6,6,4,256]{4,3,2,1,0:T(4,128)(2,1)} %bitcast.latent, bf16[6,6,6,4,256]{4,3,2,1,0:T(4,128)(2,1)} %collective-permute-done.other, ...), custom_call_target="tpu_custom_call" | custom-call | flops 2000000000 | bytes 8000000 | tf_op jit(solution)/shard_map/prep/pallas_call | solution.py:120
  39.7 4.5 %collective-permute-done.3.q3 = bf16[54,32,256]{2,1,0:T(8,128)(2,1)S(1)} collective-permute-done((bf16[54,32,256]{2,1,0:T(8,128)(2,1)S(1)}, bf16[54,32,256]{2,1,0:T(8,128)(2,1)S(1)}, u32[]{:S(2)}, u32[]{:S(2)}) %collective-permute-start.3) | collective-permute-done | bytes 884768 | tf_op jit(solution)/shard_map/ppermute | solution.py:548
  44.2 1.7 %collective-permute-done.2.q2 = bf16[54,32,256]{2,1,0:T(8,128)(2,1)S(1)} collective-permute-done((bf16[54,32,256]{2,1,0:T(8,128)(2,1)S(1)}, bf16[54,32,256]{2,1,0:T(8,128)(2,1)S(1)}, u32[]{:S(2)}, u32[]{:S(2)}) %collective-permute-start.2) | collective-permute-done | bytes 884768 | tf_op jit(solution)/shard_map/ppermute | solution.py:548
  45.9 0.6 collective-permute-start.5
  46.5 0.0 collective-permute-start.6
  46.5 0.5 collective-permute-start.7
  47.1 2.3 %conv1_own.1.part_act = f32[1152,256]{1,0:T(8,128)S(1)} custom-call(bf16[3,8,8,32,128]{4,3,2,1,0:T(8,128)(2,1)S(1)} %get-tuple-element.41.x3a, bf16[54,32,256]{2,1,0:T(8,128)(2,1)S(1)} %spread.1.q0, bf16[54,32,256]{2,1,0:T(8,128)(2,1)S(1)} %collective-permute-done.1.q1, bf16[54,32,256]{2,1,0:T(8,128)(2,1)S(1)} %collective-permute-done.2.q2, ...), custom_call_target="tpu_custom_call" | custom-call | flops 2000000000 | bytes 5000000 | tf_op jit(solution)/shard_map/conv1_own/pallas_call | solution.py:155
  49.4 0.0 collective-permute-done.4.q0.p0
  49.4 0.0 collective-permute-done.5.q1.p1
  49.4 0.5 collective-permute-done.6.q2.p2
  49.9 1.3 %collective-permute-done.7.q3.p3 = bf16[54,32,256]{2,1,0:T(8,128)(2,1)S(1)} collective-permute-done((bf16[54,32,256]{2,1,0:T(8,128)(2,1)S(1)}, bf16[54,32,256]{2,1,0:T(8,128)(2,1)S(1)}, u32[]{:S(2)}, u32[]{:S(2)}) %collective-permute-start.7) | collective-permute-done | bytes 884768 | tf_op jit(solution)/shard_map/ppermute | solution.py:544
  51.1 3.7 %conv1.1 = (f32[1152,256]{1,0:T(8,128)S(1)}, bf16[3,7,7,16,256]{4,3,2,1,0:T(8,128)(2,1)S(1)}, bf16[3,7,7,16,128]{4,3,2,1,0:T(8,128)(2,1)S(1)}) custom-call(bf16[3,8,8,32,128]{4,3,2,1,0:T(8,128)(2,1)S(1)} %get-tuple-element.40.x3b, f32[1152,256]{1,0:T(8,128)S(1)} %conv1_own.1.part_act, bf16[54,32,256]{2,1,0:T(8,128)(2,1)S(1)} %collective-permute-done.4.q0.p0, ...), custom_call_target="tpu_custom_call" | custom-call | flops 2000000000 | bytes 7000000 | tf_op jit(solution)/shard_map/conv1/pallas_call | solution.py:194
  54.9 0.6 collective-permute-start.9
  55.5 3.5 %middle.1 = (bf16[3,3,3,4,256]{4,3,2,1,0:T(4,128)(2,1)}, bf16[256,144]{1,0:T(8,128)(2,1)S(1)}, bf16[3,256,384]{2,1,0:T(8,128)(2,1)S(1)}) custom-call(f32[144,256]{1,0:T(8,128)S(1)} %get-tuple-element.38.skip, f32[144,256]{1,0:T(8,128)S(1)} %get-tuple-element.39.cot, bf16[3,7,7,16,256]{4,3,2,1,0:T(8,128)(2,1)S(1)} %get-tuple-element.45.hsel, ...), custom_call_target="tpu_custom_call" | custom-call | flops 3000000000 | bytes 14000000 | tf_op jit(solution)/shard_map/middle/pallas_call | solution.py:268
  59.0 0.2 collective-permute-start.10
  59.3 0.4 collective-permute-start.8
  59.6 1.7 %collective-permute-done.8.grad_t_other = bf16[256,144]{1,0:T(8,128)(2,1)S(1)} collective-permute-done((bf16[256,144]{1,0:T(8,128)(2,1)S(1)}, bf16[256,144]{1,0:T(8,128)(2,1)S(1)}, u32[]{:S(2)}, u32[]{:S(2)}) %collective-permute-start.8) | collective-permute-done | bytes 73760 | tf_op jit(solution)/shard_map/ppermute | solution.py:544
  61.3 1.6 %grad2.1 = (bf16[27,32,256]{2,1,0:T(8,128)(2,1)S(1)}, bf16[27,32,256]{2,1,0:T(8,128)(2,1)S(1)}, bf16[27,32,256]{2,1,0:T(8,128)(2,1)S(1)}, bf16[27,32,256]{2,1,0:T(8,128)(2,1)S(1)}) custom-call(bf16[256,144]{1,0:T(8,128)(2,1)S(1)} %get-tuple-element.49.grad_t, bf16[256,144]{1,0:T(8,128)(2,1)S(1)} %collective-permute-done.8.grad_t_other, ...), custom_call_target="tpu_custom_call" | custom-call | flops 1000000000 | bytes 4000000 | tf_op jit(solution)/shard_map/grad2/pallas_call | solution.py:327
  62.9 0.1 collective-permute-start.14
  63.0 1.6 %collective-permute-start.15 = (bf16[27,32,256]{2,1,0:T(8,128)(2,1)S(1)}, bf16[27,32,256]{2,1,0:T(8,128)(2,1)S(1)}, u32[]{:S(2)}, u32[]{:S(2)}) collective-permute-start(bf16[27,32,256]{2,1,0:T(8,128)(2,1)S(1)} %get-tuple-element.53), channel_id=1, source_target_pairs={{0,8},{6,14},{24,16},{30,22},{96,104},{102,110},{120,112},{126,118... | collective-permute-start | bytes 1327112 | tf_op jit(solution)/shard_map/ppermute | solution.py:548
  64.6 1.6 %collective-permute-start.16 = (bf16[27,32,256]{2,1,0:T(8,128)(2,1)S(1)}, bf16[27,32,256]{2,1,0:T(8,128)(2,1)S(1)}, u32[]{:S(2)}, u32[]{:S(2)}) collective-permute-start(bf16[27,32,256]{2,1,0:T(8,128)(2,1)S(1)} %get-tuple-element.54), channel_id=1, source_target_pairs={{0,2},{6,4},{24,26},{30,28},{96,98},{102,100},{120,122},{126,124},... | collective-permute-start | bytes 1327112 | tf_op jit(solution)/shard_map/ppermute | solution.py:548
  66.3 4.9 %grad1.1 = (bf16[27,32,256]{2,1,0:T(8,128)(2,1)S(1)}, bf16[27,32,256]{2,1,0:T(8,128)(2,1)S(1)}, bf16[27,32,256]{2,1,0:T(8,128)(2,1)S(1)}, bf16[27,32,256]{2,1,0:T(8,128)(2,1)S(1)}) custom-call(bf16[3,256,384]{2,1,0:T(8,128)(2,1)S(1)} %get-tuple-element.55.gat, bf16[3,256,384]{2,1,0:T(8,128)(2,1)S(1)} %collective-permute-done.10.gat_other, ...), custom_call_target="tpu_custom_call" | custom-call | flops 4000000000 | bytes 7000000 | tf_op jit(solution)/shard_map/grad1/pallas_call | solution.py:350
  71.2 0.7 collective-permute-start.11
  71.9 0.4 collective-permute-start.12
  72.4 1.7 %collective-permute-start.13 = (bf16[27,32,256]{2,1,0:T(8,128)(2,1)S(1)}, bf16[27,32,256]{2,1,0:T(8,128)(2,1)S(1)}, u32[]{:S(2)}, u32[]{:S(2)}) collective-permute-start(bf16[27,32,256]{2,1,0:T(8,128)(2,1)S(1)} %get-tuple-element.60), channel_id=1, source_target_pairs={{0,2},{6,4},{24,26},{30,28},{96,98},{102,100},{120,122},{126,124},... | collective-permute-start | bytes 1327112 | tf_op jit(solution)/shard_map/ppermute | solution.py:548
  74.1 0.2 collect2.1.second
  74.3 5.2 %collective-permute-done.11.p1 = bf16[27,32,256]{2,1,0:T(8,128)(2,1)S(1)} collective-permute-done((bf16[27,32,256]{2,1,0:T(8,128)(2,1)S(1)}, bf16[27,32,256]{2,1,0:T(8,128)(2,1)S(1)}, u32[]{:S(2)}, u32[]{:S(2)}) %collective-permute-start.11) | collective-permute-done | bytes 442400 | tf_op jit(solution)/shard_map/ppermute | solution.py:548
  79.6 0.7 collective-permute-done.12.p2
  80.2 0.5 collective-permute-done.13.p3
  80.7 1.6 %collect.1 = bf16[16,54,512]{2,1,0:T(8,128)(2,1)S(1)} custom-call(bf16[27,32,256]{2,1,0:T(8,128)(2,1)S(1)} %get-tuple-element.57.p0, bf16[27,32,256]{2,1,0:T(8,128)(2,1)S(1)} %collective-permute-done.11.p1, bf16[27,32,256]{2,1,0:T(8,128)(2,1)S(1)} %collective-permute-done.12.p2, bf16[27,32,256]{2,1,0:T(8,128)(2,1)S(1)} %collective-permute-done.13.p3, ...), custom_call_target="tpu_custom_call" | custom-call | flops 1000000 | bytes 3000000 | tf_op jit(solution)/shard_map/collect/pallas_call | solution.py:427
  82.3 0.0 copy-start
  82.3 0.0 copy-start.1
  82.3 0.0 copy-start.2
  82.3 0.0 copy-start.3
  82.4 0.0 copy-start.4
  82.4 0.0 copy-start.5
  82.4 0.0 copy-start.6
  82.4 23.4 %all_to_all.11.parts = bf16[16,54,512]{2,1,0:T(8,128)(2,1)S(1)} all-to-all(bf16[16,54,512]{2,1,0:T(8,128)(2,1)S(1)} %collect.1), channel_id=1, replica_groups={{0,14,18,28,36,42,54,56,68,74,86,88,96,110,114,124},{4,10,22,24,32,46,5..., dimensions={0} | all-to-all | bytes 1769472 | tf_op jit(solution)/shard_map/all_to_all | solution.py:540
  105.8 1.4 %adam.1 = (f32[27,512]{1,0:T(8,128)}, f32[27,512]{1,0:T(8,128)}, f32[27,512]{1,0:T(8,128)}, f32[27,512]{1,0:T(8,128)}, f32[27,512]{1,0:T(8,128)}, /*index=5*/f32[27,512]{1,0:T(8,128)}) custom-call(bf16[16,54,512]{2,1,0:T(8,128)(2,1)S(1)} %all_to_all.11.parts, s32[1,256]{1,0:T(1,128)S(1)} %copy-done.6, f32[27,512]{1,0:T(8,128)S(1)} %copy-done, ...), custom_call_target="tpu_custom_call" | custom-call | flops 10000000 | bytes 1000000 | tf_op jit(solution)/shard_map/adam/pallas_call | solution.py:470
  (16 shorter events, 0.0 us)
Async XLA Ops:
  31.1 13.1 %collective-permute-start.3 = (bf16[54,32,256]{2,1,0:T(8,128)(2,1)S(1)}, bf16[54,32,256]{2,1,0:T(8,128)(2,1)S(1)}, u32[]{:S(2)}, u32[]{:S(2)}) collective-permute-start(bf16[54,32,256]{2,1,0:T(8,128)(2,1)S(1)} %spread.1.q0), channel_id=1, source_target_pairs={{0,2},{6,4},{24,26},{30,28},{96,98},{102,100},{120,122},{126,124},... | collective-permute-start | bytes 2654216 | tf_op jit(solution)/shard_map/ppermute | solution.py:548
  32.8 13.0 %collective-permute-start.2 = (bf16[54,32,256]{2,1,0:T(8,128)(2,1)S(1)}, bf16[54,32,256]{2,1,0:T(8,128)(2,1)S(1)}, u32[]{:S(2)}, u32[]{:S(2)}) collective-permute-start(bf16[54,32,256]{2,1,0:T(8,128)(2,1)S(1)} %spread.1.q0), channel_id=1, source_target_pairs={{0,8},{6,14},{24,16},{30,22},{96,104},{102,110},{120,112},{126,118... | collective-permute-start | bytes 2654216 | tf_op jit(solution)/shard_map/ppermute | solution.py:548
  32.9 13.0 %collective-permute-start.1 = (bf16[54,32,256]{2,1,0:T(8,128)(2,1)S(1)}, bf16[54,32,256]{2,1,0:T(8,128)(2,1)S(1)}, u32[]{:S(2)}, u32[]{:S(2)}) collective-permute-start(bf16[54,32,256]{2,1,0:T(8,128)(2,1)S(1)} %spread.1.q0), channel_id=1, source_target_pairs={{0,32},{6,38},{24,56},{30,62},{96,64},{102,70},{120,88},{126,94},{... | collective-permute-start | bytes 2654216 | tf_op jit(solution)/shard_map/ppermute | solution.py:548
  32.9 2.9 %collective-permute-start = (bf16[6,6,6,4,256]{4,3,2,1,0:T(4,128)(2,1)}, bf16[6,6,6,4,256]{4,3,2,1,0:T(4,128)(2,1)}, u32[]{:S(2)}, u32[]{:S(2)}) collective-permute-start(bf16[6,6,6,4,256]{4,3,2,1,0:T(4,128)(2,1)} %bitcast.latent), channel_id=1, source_target_pairs={{0,1},{1,0},{2,3},{3,2},{4,5},{5,4},{6,7},{7,6},{8,9},{9,8},{10,11... | collective-permute-start | bytes 1327112 | tf_op jit(solution)/shard_map/ppermute | solution.py:544
  34.7 14.7 %collective-permute-start.4 = (bf16[54,32,256]{2,1,0:T(8,128)(2,1)S(1)}, bf16[54,32,256]{2,1,0:T(8,128)(2,1)S(1)}, u32[]{:S(2)}, u32[]{:S(2)}) collective-permute-start(bf16[54,32,256]{2,1,0:T(8,128)(2,1)S(1)} %spread.1.q0), channel_id=1, source_target_pairs={{0,1},{1,0},{2,3},{3,2},{4,5},{5,4},{6,7},{7,6},{8,9},{9,8},{10,11... | collective-permute-start | bytes 2654216 | tf_op jit(solution)/shard_map/ppermute | solution.py:544
  35.7 0.8 copy-start.7
  45.9 3.5 %collective-permute-start.5 = (bf16[54,32,256]{2,1,0:T(8,128)(2,1)S(1)}, bf16[54,32,256]{2,1,0:T(8,128)(2,1)S(1)}, u32[]{:S(2)}, u32[]{:S(2)}) collective-permute-start(bf16[54,32,256]{2,1,0:T(8,128)(2,1)S(1)} %collective-permute-done.1.q1), channel_id=1, source_target_pairs={{0,1},{1,0},{2,3},{3,2},{4,5},{5,4},{6,7},{7,6},{8,9},{9,8},{10,11... | collective-permute-start | bytes 2654216 | tf_op jit(solution)/shard_map/ppermute | solution.py:544
  46.5 3.3 %collective-permute-start.6 = (bf16[54,32,256]{2,1,0:T(8,128)(2,1)S(1)}, bf16[54,32,256]{2,1,0:T(8,128)(2,1)S(1)}, u32[]{:S(2)}, u32[]{:S(2)}) collective-permute-start(bf16[54,32,256]{2,1,0:T(8,128)(2,1)S(1)} %collective-permute-done.2.q2), channel_id=1, source_target_pairs={{0,1},{1,0},{2,3},{3,2},{4,5},{5,4},{6,7},{7,6},{8,9},{9,8},{10,11... | collective-permute-start | bytes 2654216 | tf_op jit(solution)/shard_map/ppermute | solution.py:544
  46.5 4.6 %collective-permute-start.7 = (bf16[54,32,256]{2,1,0:T(8,128)(2,1)S(1)}, bf16[54,32,256]{2,1,0:T(8,128)(2,1)S(1)}, u32[]{:S(2)}, u32[]{:S(2)}) collective-permute-start(bf16[54,32,256]{2,1,0:T(8,128)(2,1)S(1)} %collective-permute-done.3.q3), channel_id=1, source_target_pairs={{0,1},{1,0},{2,3},{3,2},{4,5},{5,4},{6,7},{7,6},{8,9},{9,8},{10,11... | collective-permute-start | bytes 2654216 | tf_op jit(solution)/shard_map/ppermute | solution.py:544
  54.9 6.5 %collective-permute-start.9 = (bf16[3,7,7,16,128]{4,3,2,1,0:T(8,128)(2,1)S(1)}, bf16[3,7,7,16,128]{4,3,2,1,0:T(8,128)(2,1)S(1)}, u32[]{:S(2)}, u32[]{:S(2)}) collective-permute-start(bf16[3,7,7,16,128]{4,3,2,1,0:T(8,128)(2,1)S(1)} %get-tuple-element.50), channel_id=1, source_target_pairs={{0,1},{1,0},{2,3},{3,2},{4,5},{5,4},{6,7},{7,6},{8,9},{9,8},{10,11... | collective-permute-start | bytes 1806344 | tf_op jit(solution)/shard_map/ppermute | solution.py:544
  59.0 7.3 %collective-permute-start.10 = (bf16[3,256,384]{2,1,0:T(8,128)(2,1)S(1)}, bf16[3,256,384]{2,1,0:T(8,128)(2,1)S(1)}, u32[]{:S(2)}, u32[]{:S(2)}) collective-permute-start(bf16[3,256,384]{2,1,0:T(8,128)(2,1)S(1)} %get-tuple-element.55.gat), channel_id=1, source_target_pairs={{0,1},{1,0},{2,3},{3,2},{4,5},{5,4},{6,7},{7,6},{8,9},{9,8},{10,11... | collective-permute-start | bytes 1769480 | tf_op jit(solution)/shard_map/ppermute | solution.py:544
  59.3 2.0 %collective-permute-start.8 = (bf16[256,144]{1,0:T(8,128)(2,1)S(1)}, bf16[256,144]{1,0:T(8,128)(2,1)S(1)}, u32[]{:S(2)}, u32[]{:S(2)}) collective-permute-start(bf16[256,144]{1,0:T(8,128)(2,1)S(1)} %get-tuple-element.49.grad_t), channel_id=1, source_target_pairs={{0,1},{1,0},{2,3},{3,2},{4,5},{5,4},{6,7},{7,6},{8,9},{9,8},{10,11... | collective-permute-start | bytes 221192 | tf_op jit(solution)/shard_map/ppermute | solution.py:544
  62.9 9.4 %collective-permute-start.14 = (bf16[27,32,256]{2,1,0:T(8,128)(2,1)S(1)}, bf16[27,32,256]{2,1,0:T(8,128)(2,1)S(1)}, u32[]{:S(2)}, u32[]{:S(2)}) collective-permute-start(bf16[27,32,256]{2,1,0:T(8,128)(2,1)S(1)} %get-tuple-element.52), channel_id=1, source_target_pairs={{0,32},{6,38},{24,56},{30,62},{96,64},{102,70},{120,88},{126,94},{... | collective-permute-start | bytes 1327112 | tf_op jit(solution)/shard_map/ppermute | solution.py:548
  63.0 11.1 %collective-permute-start.15 = (bf16[27,32,256]{2,1,0:T(8,128)(2,1)S(1)}, bf16[27,32,256]{2,1,0:T(8,128)(2,1)S(1)}, u32[]{:S(2)}, u32[]{:S(2)}) collective-permute-start(bf16[27,32,256]{2,1,0:T(8,128)(2,1)S(1)} %get-tuple-element.53), channel_id=1, source_target_pairs={{0,8},{6,14},{24,16},{30,22},{96,104},{102,110},{120,112},{126,118... | collective-permute-start | bytes 1327112 | tf_op jit(solution)/shard_map/ppermute | solution.py:548
  64.6 9.5 %collective-permute-start.16 = (bf16[27,32,256]{2,1,0:T(8,128)(2,1)S(1)}, bf16[27,32,256]{2,1,0:T(8,128)(2,1)S(1)}, u32[]{:S(2)}, u32[]{:S(2)}) collective-permute-start(bf16[27,32,256]{2,1,0:T(8,128)(2,1)S(1)} %get-tuple-element.54), channel_id=1, source_target_pairs={{0,2},{6,4},{24,26},{30,28},{96,98},{102,100},{120,122},{126,124},... | collective-permute-start | bytes 1327112 | tf_op jit(solution)/shard_map/ppermute | solution.py:548
  71.2 8.4 %collective-permute-start.11 = (bf16[27,32,256]{2,1,0:T(8,128)(2,1)S(1)}, bf16[27,32,256]{2,1,0:T(8,128)(2,1)S(1)}, u32[]{:S(2)}, u32[]{:S(2)}) collective-permute-start(bf16[27,32,256]{2,1,0:T(8,128)(2,1)S(1)} %get-tuple-element.58), channel_id=1, source_target_pairs={{0,32},{6,38},{24,56},{30,62},{96,64},{102,70},{120,88},{126,94},{... | collective-permute-start | bytes 1327112 | tf_op jit(solution)/shard_map/ppermute | solution.py:548
  71.9 8.3 %collective-permute-start.12 = (bf16[27,32,256]{2,1,0:T(8,128)(2,1)S(1)}, bf16[27,32,256]{2,1,0:T(8,128)(2,1)S(1)}, u32[]{:S(2)}, u32[]{:S(2)}) collective-permute-start(bf16[27,32,256]{2,1,0:T(8,128)(2,1)S(1)} %get-tuple-element.59), channel_id=1, source_target_pairs={{0,8},{6,14},{24,16},{30,22},{96,104},{102,110},{120,112},{126,118... | collective-permute-start | bytes 1327112 | tf_op jit(solution)/shard_map/ppermute | solution.py:548
  72.4 8.3 %collective-permute-start.13 = (bf16[27,32,256]{2,1,0:T(8,128)(2,1)S(1)}, bf16[27,32,256]{2,1,0:T(8,128)(2,1)S(1)}, u32[]{:S(2)}, u32[]{:S(2)}) collective-permute-start(bf16[27,32,256]{2,1,0:T(8,128)(2,1)S(1)} %get-tuple-element.60), channel_id=1, source_target_pairs={{0,2},{6,4},{24,26},{30,28},{96,98},{102,100},{120,122},{126,124},... | collective-permute-start | bytes 1327112 | tf_op jit(solution)/shard_map/ppermute | solution.py:548
  82.3 23.4 %copy-start = (f32[27,512]{1,0:T(8,128)S(1)}, f32[27,512]{1,0:T(8,128)}, u32[]{:S(2)}) copy-start(f32[27,512]{1,0:T(8,128)} %k1.1) | copy-start | bytes 165892
  82.3 23.4 %copy-start.1 = (f32[27,512]{1,0:T(8,128)S(1)}, f32[27,512]{1,0:T(8,128)}, u32[]{:S(2)}) copy-start(f32[27,512]{1,0:T(8,128)} %k2.1) | copy-start | bytes 165892
  82.3 23.4 %copy-start.2 = (f32[27,512]{1,0:T(8,128)S(1)}, f32[27,512]{1,0:T(8,128)}, u32[]{:S(2)}) copy-start(f32[27,512]{1,0:T(8,128)} %m1.1) | copy-start | bytes 165892
  82.3 23.4 %copy-start.3 = (f32[27,512]{1,0:T(8,128)S(1)}, f32[27,512]{1,0:T(8,128)}, u32[]{:S(2)}) copy-start(f32[27,512]{1,0:T(8,128)} %v1.1) | copy-start | bytes 165892
  82.4 23.4 %copy-start.4 = (f32[27,512]{1,0:T(8,128)S(1)}, f32[27,512]{1,0:T(8,128)}, u32[]{:S(2)}) copy-start(f32[27,512]{1,0:T(8,128)} %m2.1) | copy-start | bytes 165892
  82.4 23.4 %copy-start.5 = (f32[27,512]{1,0:T(8,128)S(1)}, f32[27,512]{1,0:T(8,128)}, u32[]{:S(2)}) copy-start(f32[27,512]{1,0:T(8,128)} %v2.1) | copy-start | bytes 165892
  82.4 23.4 %copy-start.6 = (s32[1,256]{1,0:T(1,128)S(1)}, s32[1,256]{1,0:T(1,128)}, u32[]{:S(2)}) copy-start(s32[1,256]{1,0:T(1,128)} %constant.15.clone.order) | copy-start | bytes 3076

commit v12 on v10

--- a/solution.py
+++ b/solution.py
@@ -215,13 +215,11 @@
     skip, cot, hsel, q0, q1, q2, q3, p0, p1, p2, p3, block_out, grad_pre, grad_pre_t, bo
 ):
     quarters = (q0, q1, q2, q3, p0, p1, p2, p3)
-    pre = skip[...]
-    for di in range(3):
-        for dj in range(3):
-            for dl in range(3):
-                pre = pre + dot(
-                    strided_window(hsel, dl, di, dj), half_weight(quarters, TAPS + di * 9 + dj * 3 + dl)
-                )
+    windows = [strided_window(hsel, t % 3, t // 9, t // 3 % 3) for t in range(TAPS)]
+    weights = [half_weight(quarters, TAPS + t) for t in range(TAPS)]
+    pre = skip[...] + dot(
+        jnp.concatenate(windows, axis=1), jnp.concatenate(weights, axis=0)
+    )
     sigma = sigmoid(pre)
     store(bo, 0, PRE_ROWS, pre * sigma)
     for qi in range(OUTER):
@@ -253,15 +251,14 @@
 ):
     quarters = (q0, q1, q2, q3, p0, p1, p2, p3)
     y[...] = jnp.zeros_like(y)
-    grad = grad_pre[...]
-    for di in range(3):
-        for dj in range(3):
-            for dl in range(3):
-                term = dot_t(grad, half_weight(quarters, TAPS + di * 9 + dj * 3 + dl))
-                term = term.reshape(9, OUT_ROWS, C)
-                for qi in range(OUTER):
-                    for qj in range(OUTER):
-                        y[dl, 2 * qi + di, 2 * qj + dj] += term[qi * 3 + qj]
+    weights = [half_weight(quarters, TAPS + t) for t in range(TAPS)]
+    terms = dot_t(grad_pre[...], jnp.concatenate(weights, axis=0))
+    for t in range(TAPS):
+        di, dj, dl = t // 9, t // 3 % 3, t % 3
+        term = terms[:, t * C : (t + 1) * C].reshape(9, OUT_ROWS, C)
+        for qi in range(OUTER):
+            for qj in range(OUTER):
+                y[dl, 2 * qi + di, 2 * qj + dj] += term[qi * 3 + qj]
     store(gh, ACT_ROWS, 8, jnp.zeros((8, C), F32))
     count = EDGE * OUT_ROWS
     for i in range(EDGE):

time: 108 us -> 108 us (level)
  no operation moved by 1% of the time
where the time goes in v12:
time: 108 us; the launch traced here: 107 us
  blocking collectives  49.9 us (46%)
  Pallas kernels  26 us (24%)
  waiting for transfers between devices  17 us (16%)
  starting transfers between devices  11.5 us (11%)
  local copies, waits for them, and re-layouts  1.54 us (1%)
    all_to_all x2, blocking collectives, exchange(): return lax.all_to_all(value, 'dp', 0, 0, axis_index_groups=FAR, tiled=True)  49.9 us
    ppermute x9, waiting for transfers between devices, send_round(): lax.ppermute(v, 'dp', to)  12.5 us
    ppermute x9, starting transfers between devices, send_round(): lax.ppermute(v, 'dp', to)  7.97 us
    pallas_call x1, Pallas kernels, grad1(): call(grad1_kernel, 'grad1', QUARTERS, [VM] * 4, [pltpu.VMEM((C, 2 * ACT_R...  4.91 us
    ppermute x8, waiting for transfers between devices, swap(): return lax.ppermute(value, 'dp', PARTNERS)  4.49 us
    pallas_call x1, Pallas kernels, conv1(): call(conv1_kernel, 'conv1', (shape((ACT_ROWS, C), F32), shape((3, 7, 7, O...  3.72 us
    ppermute x8, starting transfers between devices, swap(): return lax.ppermute(value, 'dp', PARTNERS)  3.51 us
    pallas_call x1, Pallas kernels, prep(): call(prep_kernel, 'prep', (wide, wide, wide, pre, pre), [VM] * 4, [pltpu....  3.13 us
  transfers between devices with their start and end apart: 17, of which 9 were waited for; matrix products, arithmetic and copies ran while one was open for 1% of the time, Pallas kernels for 14%

profile of v12, /device:TPU:0, one launch (start us, length us, event | category | flops | bytes accessed | tf_op | source)
XLA Modules:
  0.0 106.8 jit_solution(16272136022796597358)
XLA Ops:
  0.6 2.0 %pack.1 = bf16[16,54,512]{2,1,0:T(8,128)(2,1)} custom-call(f32[27,512]{1,0:T(8,128)} %k1.1, f32[27,512]{1,0:T(8,128)} %k2.1, s32[1,256]{1,0:T(1,128)} %constant.15.clone.order), custom_call_target="tpu_custom_call" | custom-call | flops 10000000 | bytes 1000000 | tf_op jit(solution)/shard_map/pack/pallas_call | solution.py:380
  2.6 26.6 %all_to_all.10.shards = bf16[16,54,512]{2,1,0:T(8,128)(2,1)S(1)} all-to-all(bf16[16,54,512]{2,1,0:T(8,128)(2,1)} %pack.1), channel_id=1, replica_groups={{0,14,18,28,36,42,54,56,68,74,86,88,96,110,114,124},{4,10,22,24,32,46,5..., dimensions={0} | all-to-all | bytes 1769472 | tf_op jit(solution)/shard_map/all_to_all | solution.py:550
  29.2 1.9 %spread.1.q0 = bf16[54,32,256]{2,1,0:T(8,128)(2,1)S(1)} custom-call(bf16[16,54,512]{2,1,0:T(8,128)(2,1)S(1)} %all_to_all.10.shards), custom_call_target="tpu_custom_call" | custom-call | flops 1000000 | bytes 2000000 | tf_op jit(solution)/shard_map/spread/pallas_call | solution.py:401
  31.1 1.7 %collective-permute-start.3 = (bf16[54,32,256]{2,1,0:T(8,128)(2,1)S(1)}, bf16[54,32,256]{2,1,0:T(8,128)(2,1)S(1)}, u32[]{:S(2)}, u32[]{:S(2)}) collective-permute-start(bf16[54,32,256]{2,1,0:T(8,128)(2,1)S(1)} %spread.1.q0), channel_id=1, source_target_pairs={{0,2},{6,4},{24,26},{30,28},{96,98},{102,100},{120,122},{126,124},... | collective-permute-start | bytes 2654216 | tf_op jit(solution)/shard_map/ppermute | solution.py:558
  32.8 0.0 collective-permute-start.2
  32.9 1.1 %collective-permute-start = (bf16[6,6,6,4,256]{4,3,2,1,0:T(4,128)(2,1)}, bf16[6,6,6,4,256]{4,3,2,1,0:T(4,128)(2,1)}, u32[]{:S(2)}, u32[]{:S(2)}) collective-permute-start(bf16[6,6,6,4,256]{4,3,2,1,0:T(4,128)(2,1)} %bitcast.latent), channel_id=1, source_target_pairs={{0,1},{1,0},{2,3},{3,2},{4,5},{5,4},{6,7},{7,6},{8,9},{9,8},{10,11... | collective-permute-start | bytes 1327112 | tf_op jit(solution)/shard_map/ppermute | solution.py:554
  34.0 0.7 dynamic-slice_bitcast_fusion.table
  34.7 0.0 collective-permute-start.4
  34.7 1.1 %collective-permute-done.other = bf16[6,6,6,4,256]{4,3,2,1,0:T(4,128)(2,1)} collective-permute-done((bf16[6,6,6,4,256]{4,3,2,1,0:T(4,128)(2,1)}, bf16[6,6,6,4,256]{4,3,2,1,0:T(4,128)(2,1)}, u32[]{:S(2)}, u32[]{:S(2)}) %collective-permute-start) | collective-permute-done | bytes 442400 | tf_op jit(solution)/shard_map/ppermute | solution.py:554
  35.7 0.8 copy-done.7
  36.6 3.1 %prep.1 = (bf16[3,8,8,32,128]{4,3,2,1,0:T(8,128)(2,1)S(1)}, bf16[3,8,8,32,128]{4,3,2,1,0:T(8,128)(2,1)S(1)}, bf16[3,8,8,32,128]{4,3,2,1,0:T(8,128)(2,1)S(1)}, f32[144,256]{1,0:T(8,128)S(1)}, f32[144,256]{1,0:T(8,128)S(1)}) custom-call(bf16[6,6,6,4,256]{4,3,2,1,0:T(4,128)(2,1)} %bitcast.latent, bf16[6,6,6,4,256]{4,3,2,1,0:T(4,128)(2,1)} %collective-permute-done.other, ...), custom_call_target="tpu_custom_call" | custom-call | flops 2000000000 | bytes 8000000 | tf_op jit(solution)/shard_map/prep/pallas_call | solution.py:120
  39.7 4.5 %collective-permute-done.3.q3 = bf16[54,32,256]{2,1,0:T(8,128)(2,1)S(1)} collective-permute-done((bf16[54,32,256]{2,1,0:T(8,128)(2,1)S(1)}, bf16[54,32,256]{2,1,0:T(8,128)(2,1)S(1)}, u32[]{:S(2)}, u32[]{:S(2)}) %collective-permute-start.3) | collective-permute-done | bytes 884768 | tf_op jit(solution)/shard_map/ppermute | solution.py:558
  44.2 1.7 %collective-permute-done.2.q2 = bf16[54,32,256]{2,1,0:T(8,128)(2,1)S(1)} collective-permute-done((bf16[54,32,256]{2,1,0:T(8,128)(2,1)S(1)}, bf16[54,32,256]{2,1,0:T(8,128)(2,1)S(1)}, u32[]{:S(2)}, u32[]{:S(2)}) %collective-permute-start.2) | collective-permute-done | bytes 884768 | tf_op jit(solution)/shard_map/ppermute | solution.py:558
  45.9 0.6 collective-permute-start.5
  46.5 0.0 collective-permute-start.6
  46.5 0.5 collective-permute-start.7
  47.1 2.3 %conv1_own.1.part_act = f32[1152,256]{1,0:T(8,128)S(1)} custom-call(bf16[3,8,8,32,128]{4,3,2,1,0:T(8,128)(2,1)S(1)} %get-tuple-element.41.x3a, bf16[54,32,256]{2,1,0:T(8,128)(2,1)S(1)} %spread.1.q0, bf16[54,32,256]{2,1,0:T(8,128)(2,1)S(1)} %collective-permute-done.1.q1, bf16[54,32,256]{2,1,0:T(8,128)(2,1)S(1)} %collective-permute-done.2.q2, ...), custom_call_target="tpu_custom_call" | custom-call | flops 2000000000 | bytes 5000000 | tf_op jit(solution)/shard_map/conv1_own/pallas_call | solution.py:155
  49.4 0.5 collective-permute-done.6.q2.p2
  49.9 1.3 %collective-permute-done.7.q3.p3 = bf16[54,32,256]{2,1,0:T(8,128)(2,1)S(1)} collective-permute-done((bf16[54,32,256]{2,1,0:T(8,128)(2,1)S(1)}, bf16[54,32,256]{2,1,0:T(8,128)(2,1)S(1)}, u32[]{:S(2)}, u32[]{:S(2)}) %collective-permute-start.7) | collective-permute-done | bytes 884768 | tf_op jit(solution)/shard_map/ppermute | solution.py:554
  51.1 3.7 %conv1.1 = (f32[1152,256]{1,0:T(8,128)S(1)}, bf16[3,7,7,16,256]{4,3,2,1,0:T(8,128)(2,1)S(1)}, bf16[3,7,7,16,128]{4,3,2,1,0:T(8,128)(2,1)S(1)}) custom-call(bf16[3,8,8,32,128]{4,3,2,1,0:T(8,128)(2,1)S(1)} %get-tuple-element.40.x3b, f32[1152,256]{1,0:T(8,128)S(1)} %conv1_own.1.part_act, bf16[54,32,256]{2,1,0:T(8,128)(2,1)S(1)} %collective-permute-done.4.q0.p0, ...), custom_call_target="tpu_custom_call" | custom-call | flops 2000000000 | bytes 7000000 | tf_op jit(solution)/shard_map/conv1/pallas_call | solution.py:194
  54.9 0.5 collective-permute-start.9
  55.3 1.4 %conv2.1 = (bf16[3,3,3,4,256]{4,3,2,1,0:T(4,128)(2,1)}, bf16[144,256]{1,0:T(8,128)(2,1)S(1)}, bf16[256,144]{1,0:T(8,128)(2,1)S(1)}) custom-call(f32[144,256]{1,0:T(8,128)S(1)} %get-tuple-element.38.skip, f32[144,256]{1,0:T(8,128)S(1)} %get-tuple-element.39.cot, bf16[3,7,7,16,256]{4,3,2,1,0:T(8,128)(2,1)S(1)} %get-tuple-element.45.hsel, ...), custom_call_target="tpu_custom_call" | custom-call | flops 1500000000 | bytes 6000000 | tf_op jit(solution)/shard_map/conv2/pallas_call | solution.py:236
  56.7 1.8 %back.1.gat = bf16[3,256,384]{2,1,0:T(8,128)(2,1)S(1)} custom-call(f32[1152,256]{1,0:T(8,128)S(1)} %get-tuple-element.47.act, bf16[144,256]{1,0:T(8,128)(2,1)S(1)} %get-tuple-element.48.grad_pre, bf16[54,32,256]{2,1,0:T(8,128)(2,1)S(1)} %spread.1.q0, bf16[54,32,256]{2,1,0:T(8,128)(2,1)S(1)} %collective-permute-done.1.q1, ...), custom_call_target="tpu_custom_call" | custom-call | flops 1500000000 | bytes 8000000 | tf_op jit(solution)/shard_map/back/pallas_call | solution.py:285
  58.5 0.4 collective-permute-start.10
  58.9 0.4 collective-permute-start.8
  59.3 1.7 %collective-permute-done.8.grad_t_other = bf16[256,144]{1,0:T(8,128)(2,1)S(1)} collective-permute-done((bf16[256,144]{1,0:T(8,128)(2,1)S(1)}, bf16[256,144]{1,0:T(8,128)(2,1)S(1)}, u32[]{:S(2)}, u32[]{:S(2)}) %collective-permute-start.8) | collective-permute-done | bytes 73760 | tf_op jit(solution)/shard_map/ppermute | solution.py:554
  60.9 1.6 %grad2.1 = (bf16[27,32,256]{2,1,0:T(8,128)(2,1)S(1)}, bf16[27,32,256]{2,1,0:T(8,128)(2,1)S(1)}, bf16[27,32,256]{2,1,0:T(8,128)(2,1)S(1)}, bf16[27,32,256]{2,1,0:T(8,128)(2,1)S(1)}) custom-call(bf16[256,144]{1,0:T(8,128)(2,1)S(1)} %get-tuple-element.49.grad_t, bf16[256,144]{1,0:T(8,128)(2,1)S(1)} %collective-permute-done.8.grad_t_other, ...), custom_call_target="tpu_custom_call" | custom-call | flops 1000000000 | bytes 4000000 | tf_op jit(solution)/shard_map/grad2/pallas_call | solution.py:337
  62.6 0.1 collective-permute-start.14
  62.7 1.6 %collective-permute-start.15 = (bf16[27,32,256]{2,1,0:T(8,128)(2,1)S(1)}, bf16[27,32,256]{2,1,0:T(8,128)(2,1)S(1)}, u32[]{:S(2)}, u32[]{:S(2)}) collective-permute-start(bf16[27,32,256]{2,1,0:T(8,128)(2,1)S(1)} %get-tuple-element.53), channel_id=1, source_target_pairs={{0,8},{6,14},{24,16},{30,22},{96,104},{102,110},{120,112},{126,118... | collective-permute-start | bytes 1327112 | tf_op jit(solution)/shard_map/ppermute | solution.py:558
  64.3 1.6 %collective-permute-start.16 = (bf16[27,32,256]{2,1,0:T(8,128)(2,1)S(1)}, bf16[27,32,256]{2,1,0:T(8,128)(2,1)S(1)}, u32[]{:S(2)}, u32[]{:S(2)}) collective-permute-start(bf16[27,32,256]{2,1,0:T(8,128)(2,1)S(1)} %get-tuple-element.54), channel_id=1, source_target_pairs={{0,2},{6,4},{24,26},{30,28},{96,98},{102,100},{120,122},{126,124},... | collective-permute-start | bytes 1327112 | tf_op jit(solution)/shard_map/ppermute | solution.py:558
  65.9 4.9 %grad1.1 = (bf16[27,32,256]{2,1,0:T(8,128)(2,1)S(1)}, bf16[27,32,256]{2,1,0:T(8,128)(2,1)S(1)}, bf16[27,32,256]{2,1,0:T(8,128)(2,1)S(1)}, bf16[27,32,256]{2,1,0:T(8,128)(2,1)S(1)}) custom-call(bf16[3,256,384]{2,1,0:T(8,128)(2,1)S(1)} %back.1.gat, bf16[3,256,384]{2,1,0:T(8,128)(2,1)S(1)} %collective-permute-done.10.gat_other, ...), custom_call_target="tpu_custom_call" | custom-call | flops 4000000000 | bytes 7000000 | tf_op jit(solution)/shard_map/grad1/pallas_call | solution.py:360
  70.9 0.7 collective-permute-start.11
  71.6 0.4 collective-permute-start.12
  72.0 1.7 %collective-permute-start.13 = (bf16[27,32,256]{2,1,0:T(8,128)(2,1)S(1)}, bf16[27,32,256]{2,1,0:T(8,128)(2,1)S(1)}, u32[]{:S(2)}, u32[]{:S(2)}) collective-permute-start(bf16[27,32,256]{2,1,0:T(8,128)(2,1)S(1)} %get-tuple-element.60), channel_id=1, source_target_pairs={{0,2},{6,4},{24,26},{30,28},{96,98},{102,100},{120,122},{126,124},... | collective-permute-start | bytes 1327112 | tf_op jit(solution)/shard_map/ppermute | solution.py:558
  73.8 0.2 collect2.1.second
  74.0 5.2 %collective-permute-done.11.p1 = bf16[27,32,256]{2,1,0:T(8,128)(2,1)S(1)} collective-permute-done((bf16[27,32,256]{2,1,0:T(8,128)(2,1)S(1)}, bf16[27,32,256]{2,1,0:T(8,128)(2,1)S(1)}, u32[]{:S(2)}, u32[]{:S(2)}) %collective-permute-start.11) | collective-permute-done | bytes 442400 | tf_op jit(solution)/shard_map/ppermute | solution.py:558
  79.2 0.7 collective-permute-done.12.p2
  79.9 0.5 collective-permute-done.13.p3
  80.3 1.6 %collect.1 = bf16[16,54,512]{2,1,0:T(8,128)(2,1)S(1)} custom-call(bf16[27,32,256]{2,1,0:T(8,128)(2,1)S(1)} %get-tuple-element.57.p0, bf16[27,32,256]{2,1,0:T(8,128)(2,1)S(1)} %collective-permute-done.11.p1, bf16[27,32,256]{2,1,0:T(8,128)(2,1)S(1)} %collective-permute-done.12.p2, bf16[27,32,256]{2,1,0:T(8,128)(2,1)S(1)} %collective-permute-done.13.p3, ...), custom_call_target="tpu_custom_call" | custom-call | flops 1000000 | bytes 3000000 | tf_op jit(solution)/shard_map/collect/pallas_call | solution.py:437
  82.0 0.0 copy-start
  82.0 0.0 copy-start.1
  82.0 0.0 copy-start.2
  82.0 0.0 copy-start.3
  82.0 0.0 copy-start.4
  82.0 0.0 copy-start.5
  82.0 0.0 copy-start.6
  82.1 23.4 %all_to_all.11.parts = bf16[16,54,512]{2,1,0:T(8,128)(2,1)S(1)} all-to-all(bf16[16,54,512]{2,1,0:T(8,128)(2,1)S(1)} %collect.1), channel_id=1, replica_groups={{0,14,18,28,36,42,54,56,68,74,86,88,96,110,114,124},{4,10,22,24,32,46,5..., dimensions={0} | all-to-all | bytes 1769472 | tf_op jit(solution)/shard_map/all_to_all | solution.py:550
  105.5 1.4 %adam.1 = (f32[27,512]{1,0:T(8,128)}, f32[27,512]{1,0:T(8,128)}, f32[27,512]{1,0:T(8,128)}, f32[27,512]{1,0:T(8,128)}, f32[27,512]{1,0:T(8,128)}, /*index=5*/f32[27,512]{1,0:T(8,128)}) custom-call(bf16[16,54,512]{2,1,0:T(8,128)(2,1)S(1)} %all_to_all.11.parts, s32[1,256]{1,0:T(1,128)S(1)} %copy-done.6, f32[27,512]{1,0:T(8,128)S(1)} %copy-done, ...), custom_call_target="tpu_custom_call" | custom-call | flops 10000000 | bytes 1000000 | tf_op jit(solution)/shard_map/adam/pallas_call | solution.py:480
  (17 shorter events, 0.0 us)
Async XLA Ops:
  31.1 13.1 %collective-permute-start.3 = (bf16[54,32,256]{2,1,0:T(8,128)(2,1)S(1)}, bf16[54,32,256]{2,1,0:T(8,128)(2,1)S(1)}, u32[]{:S(2)}, u32[]{:S(2)}) collective-permute-start(bf16[54,32,256]{2,1,0:T(8,128)(2,1)S(1)} %spread.1.q0), channel_id=1, source_target_pairs={{0,2},{6,4},{24,26},{30,28},{96,98},{102,100},{120,122},{126,124},... | collective-permute-start | bytes 2654216 | tf_op jit(solution)/shard_map/ppermute | solution.py:558
  32.8 13.0 %collective-permute-start.2 = (bf16[54,32,256]{2,1,0:T(8,128)(2,1)S(1)}, bf16[54,32,256]{2,1,0:T(8,128)(2,1)S(1)}, u32[]{:S(2)}, u32[]{:S(2)}) collective-permute-start(bf16[54,32,256]{2,1,0:T(8,128)(2,1)S(1)} %spread.1.q0), channel_id=1, source_target_pairs={{0,8},{6,14},{24,16},{30,22},{96,104},{102,110},{120,112},{126,118... | collective-permute-start | bytes 2654216 | tf_op jit(solution)/shard_map/ppermute | solution.py:558
  32.9 13.0 %collective-permute-start.1 = (bf16[54,32,256]{2,1,0:T(8,128)(2,1)S(1)}, bf16[54,32,256]{2,1,0:T(8,128)(2,1)S(1)}, u32[]{:S(2)}, u32[]{:S(2)}) collective-permute-start(bf16[54,32,256]{2,1,0:T(8,128)(2,1)S(1)} %spread.1.q0), channel_id=1, source_target_pairs={{0,32},{6,38},{24,56},{30,62},{96,64},{102,70},{120,88},{126,94},{... | collective-permute-start | bytes 2654216 | tf_op jit(solution)/shard_map/ppermute | solution.py:558
  32.9 2.9 %collective-permute-start = (bf16[6,6,6,4,256]{4,3,2,1,0:T(4,128)(2,1)}, bf16[6,6,6,4,256]{4,3,2,1,0:T(4,128)(2,1)}, u32[]{:S(2)}, u32[]{:S(2)}) collective-permute-start(bf16[6,6,6,4,256]{4,3,2,1,0:T(4,128)(2,1)} %bitcast.latent), channel_id=1, source_target_pairs={{0,1},{1,0},{2,3},{3,2},{4,5},{5,4},{6,7},{7,6},{8,9},{9,8},{10,11... | collective-permute-start | bytes 1327112 | tf_op jit(solution)/shard_map/ppermute | solution.py:554
  34.7 14.7 %collective-permute-start.4 = (bf16[54,32,256]{2,1,0:T(8,128)(2,1)S(1)}, bf16[54,32,256]{2,1,0:T(8,128)(2,1)S(1)}, u32[]{:S(2)}, u32[]{:S(2)}) collective-permute-start(bf16[54,32,256]{2,1,0:T(8,128)(2,1)S(1)} %spread.1.q0), channel_id=1, source_target_pairs={{0,1},{1,0},{2,3},{3,2},{4,5},{5,4},{6,7},{7,6},{8,9},{9,8},{10,11... | collective-permute-start | bytes 2654216 | tf_op jit(solution)/shard_map/ppermute | solution.py:554
  35.7 0.8 copy-start.7
  45.9 3.5 %collective-permute-start.5 = (bf16[54,32,256]{2,1,0:T(8,128)(2,1)S(1)}, bf16[54,32,256]{2,1,0:T(8,128)(2,1)S(1)}, u32[]{:S(2)}, u32[]{:S(2)}) collective-permute-start(bf16[54,32,256]{2,1,0:T(8,128)(2,1)S(1)} %collective-permute-done.1.q1), channel_id=1, source_target_pairs={{0,1},{1,0},{2,3},{3,2},{4,5},{5,4},{6,7},{7,6},{8,9},{9,8},{10,11... | collective-permute-start | bytes 2654216 | tf_op jit(solution)/shard_map/ppermute | solution.py:554
  46.5 3.3 %collective-permute-start.6 = (bf16[54,32,256]{2,1,0:T(8,128)(2,1)S(1)}, bf16[54,32,256]{2,1,0:T(8,128)(2,1)S(1)}, u32[]{:S(2)}, u32[]{:S(2)}) collective-permute-start(bf16[54,32,256]{2,1,0:T(8,128)(2,1)S(1)} %collective-permute-done.2.q2), channel_id=1, source_target_pairs={{0,1},{1,0},{2,3},{3,2},{4,5},{5,4},{6,7},{7,6},{8,9},{9,8},{10,11... | collective-permute-start | bytes 2654216 | tf_op jit(solution)/shard_map/ppermute | solution.py:554
  46.5 4.6 %collective-permute-start.7 = (bf16[54,32,256]{2,1,0:T(8,128)(2,1)S(1)}, bf16[54,32,256]{2,1,0:T(8,128)(2,1)S(1)}, u32[]{:S(2)}, u32[]{:S(2)}) collective-permute-start(bf16[54,32,256]{2,1,0:T(8,128)(2,1)S(1)} %collective-permute-done.3.q3), channel_id=1, source_target_pairs={{0,1},{1,0},{2,3},{3,2},{4,5},{5,4},{6,7},{7,6},{8,9},{9,8},{10,11... | collective-permute-start | bytes 2654216 | tf_op jit(solution)/shard_map/ppermute | solution.py:554
  54.9 6.1 %collective-permute-start.9 = (bf16[3,7,7,16,128]{4,3,2,1,0:T(8,128)(2,1)S(1)}, bf16[3,7,7,16,128]{4,3,2,1,0:T(8,128)(2,1)S(1)}, u32[]{:S(2)}, u32[]{:S(2)}) collective-permute-start(bf16[3,7,7,16,128]{4,3,2,1,0:T(8,128)(2,1)S(1)} %get-tuple-element.50), channel_id=1, source_target_pairs={{0,1},{1,0},{2,3},{3,2},{4,5},{5,4},{6,7},{7,6},{8,9},{9,8},{10,11... | collective-permute-start | bytes 1806344 | tf_op jit(solution)/shard_map/ppermute | solution.py:554
  58.5 7.5 %collective-permute-start.10 = (bf16[3,256,384]{2,1,0:T(8,128)(2,1)S(1)}, bf16[3,256,384]{2,1,0:T(8,128)(2,1)S(1)}, u32[]{:S(2)}, u32[]{:S(2)}) collective-permute-start(bf16[3,256,384]{2,1,0:T(8,128)(2,1)S(1)} %back.1.gat), channel_id=1, source_target_pairs={{0,1},{1,0},{2,3},{3,2},{4,5},{5,4},{6,7},{7,6},{8,9},{9,8},{10,11... | collective-permute-start | bytes 1769480 | tf_op jit(solution)/shard_map/ppermute | solution.py:554
  58.9 2.0 %collective-permute-start.8 = (bf16[256,144]{1,0:T(8,128)(2,1)S(1)}, bf16[256,144]{1,0:T(8,128)(2,1)S(1)}, u32[]{:S(2)}, u32[]{:S(2)}) collective-permute-start(bf16[256,144]{1,0:T(8,128)(2,1)S(1)} %get-tuple-element.49.grad_t), channel_id=1, source_target_pairs={{0,1},{1,0},{2,3},{3,2},{4,5},{5,4},{6,7},{7,6},{8,9},{9,8},{10,11... | collective-permute-start | bytes 221192 | tf_op jit(solution)/shard_map/ppermute | solution.py:554
  62.6 9.4 %collective-permute-start.14 = (bf16[27,32,256]{2,1,0:T(8,128)(2,1)S(1)}, bf16[27,32,256]{2,1,0:T(8,128)(2,1)S(1)}, u32[]{:S(2)}, u32[]{:S(2)}) collective-permute-start(bf16[27,32,256]{2,1,0:T(8,128)(2,1)S(1)} %get-tuple-element.52), channel_id=1, source_target_pairs={{0,32},{6,38},{24,56},{30,62},{96,64},{102,70},{120,88},{126,94},{... | collective-permute-start | bytes 1327112 | tf_op jit(solution)/shard_map/ppermute | solution.py:558
  62.7 11.1 %collective-permute-start.15 = (bf16[27,32,256]{2,1,0:T(8,128)(2,1)S(1)}, bf16[27,32,256]{2,1,0:T(8,128)(2,1)S(1)}, u32[]{:S(2)}, u32[]{:S(2)}) collective-permute-start(bf16[27,32,256]{2,1,0:T(8,128)(2,1)S(1)} %get-tuple-element.53), channel_id=1, source_target_pairs={{0,8},{6,14},{24,16},{30,22},{96,104},{102,110},{120,112},{126,118... | collective-permute-start | bytes 1327112 | tf_op jit(solution)/shard_map/ppermute | solution.py:558
  64.3 9.5 %collective-permute-start.16 = (bf16[27,32,256]{2,1,0:T(8,128)(2,1)S(1)}, bf16[27,32,256]{2,1,0:T(8,128)(2,1)S(1)}, u32[]{:S(2)}, u32[]{:S(2)}) collective-permute-start(bf16[27,32,256]{2,1,0:T(8,128)(2,1)S(1)} %get-tuple-element.54), channel_id=1, source_target_pairs={{0,2},{6,4},{24,26},{30,28},{96,98},{102,100},{120,122},{126,124},... | collective-permute-start | bytes 1327112 | tf_op jit(solution)/shard_map/ppermute | solution.py:558
  70.9 8.4 %collective-permute-start.11 = (bf16[27,32,256]{2,1,0:T(8,128)(2,1)S(1)}, bf16[27,32,256]{2,1,0:T(8,128)(2,1)S(1)}, u32[]{:S(2)}, u32[]{:S(2)}) collective-permute-start(bf16[27,32,256]{2,1,0:T(8,128)(2,1)S(1)} %get-tuple-element.58), channel_id=1, source_target_pairs={{0,32},{6,38},{24,56},{30,62},{96,64},{102,70},{120,88},{126,94},{... | collective-permute-start | bytes 1327112 | tf_op jit(solution)/shard_map/ppermute | solution.py:558
  71.6 8.3 %collective-permute-start.12 = (bf16[27,32,256]{2,1,0:T(8,128)(2,1)S(1)}, bf16[27,32,256]{2,1,0:T(8,128)(2,1)S(1)}, u32[]{:S(2)}, u32[]{:S(2)}) collective-permute-start(bf16[27,32,256]{2,1,0:T(8,128)(2,1)S(1)} %get-tuple-element.59), channel_id=1, source_target_pairs={{0,8},{6,14},{24,16},{30,22},{96,104},{102,110},{120,112},{126,118... | collective-permute-start | bytes 1327112 | tf_op jit(solution)/shard_map/ppermute | solution.py:558
  72.0 8.3 %collective-permute-start.13 = (bf16[27,32,256]{2,1,0:T(8,128)(2,1)S(1)}, bf16[27,32,256]{2,1,0:T(8,128)(2,1)S(1)}, u32[]{:S(2)}, u32[]{:S(2)}) collective-permute-start(bf16[27,32,256]{2,1,0:T(8,128)(2,1)S(1)} %get-tuple-element.60), channel_id=1, source_target_pairs={{0,2},{6,4},{24,26},{30,28},{96,98},{102,100},{120,122},{126,124},... | collective-permute-start | bytes 1327112 | tf_op jit(solution)/shard_map/ppermute | solution.py:558
  82.0 23.5 %copy-start = (f32[27,512]{1,0:T(8,128)S(1)}, f32[27,512]{1,0:T(8,128)}, u32[]{:S(2)}) copy-start(f32[27,512]{1,0:T(8,128)} %k1.1) | copy-start | bytes 165892
  82.0 23.4 %copy-start.1 = (f32[27,512]{1,0:T(8,128)S(1)}, f32[27,512]{1,0:T(8,128)}, u32[]{:S(2)}) copy-start(f32[27,512]{1,0:T(8,128)} %k2.1) | copy-start | bytes 165892
  82.0 23.4 %copy-start.2 = (f32[27,512]{1,0:T(8,128)S(1)}, f32[27,512]{1,0:T(8,128)}, u32[]{:S(2)}) copy-start(f32[27,512]{1,0:T(8,128)} %m1.1) | copy-start | bytes 165892
  82.0 23.4 %copy-start.3 = (f32[27,512]{1,0:T(8,128)S(1)}, f32[27,512]{1,0:T(8,128)}, u32[]{:S(2)}) copy-start(f32[27,512]{1,0:T(8,128)} %v1.1) | copy-start | bytes 165892
  82.0 23.4 %copy-start.4 = (f32[27,512]{1,0:T(8,128)S(1)}, f32[27,512]{1,0:T(8,128)}, u32[]{:S(2)}) copy-start(f32[27,512]{1,0:T(8,128)} %m2.1) | copy-start | bytes 165892
  82.0 23.4 %copy-start.5 = (f32[27,512]{1,0:T(8,128)S(1)}, f32[27,512]{1,0:T(8,128)}, u32[]{:S(2)}) copy-start(f32[27,512]{1,0:T(8,128)} %v2.1) | copy-start | bytes 165892
  82.0 23.4 %copy-start.6 = (s32[1,256]{1,0:T(1,128)S(1)}, s32[1,256]{1,0:T(1,128)}, u32[]{:S(2)}) copy-start(s32[1,256]{1,0:T(1,128)} %constant.15.clone.order) | copy-start | bytes 3076
